TPU v7x, 32 devices: a whole 2x2x4 slice. The times are simulated.
32 devices in a mesh: band: 8 (over y, x, core), chan: 4 (over z).
Axes of the slice: x: 2, y: 2, z: 4, core: 2. Of those that a mesh axis runs over, the one named last changes fastest.
Arguments:
- image: bfloat16 [512, 32, 512], P('chan', 'band'), may hold values from -6 to 6
- filters: bfloat16 [9, 512, 512], P(None, None, 'chan'), may hold values from -0.09375 to 0.09375
- bias: bfloat16 [512], P('chan'), may hold values from -3 to 3
- upstream: bfloat16 [512, 32, 512], P('chan', 'band'), may hold values from -6 to 6
Outputs:
- features: bfloat16 [512, 32, 512], P('chan', 'band')
- image_grad: bfloat16 [512, 32, 512], P('chan', 'band')
All inputs are finite; a program needn't handle non-finite values.
Results may differ from a plain program's by a relative error of at most 0.001.
Values may be sent and summed in bfloat16 or wider, within the bound.
No kernel may reach another device: no remote copies, remote signals or barrier semaphores. Data moves between devices by JAX's collectives and lax.ppermute only.
A program may use at most 64 MiB of HBM per device.

v0:
```python
import jax
import jax.numpy as jnp
from jax import lax
from jax.sharding import PartitionSpec as P


def with_halo(value, sides, width):
    for axis, dim in sides:
        size, length = (lax.axis_size(axis), value.shape[dim])
        up = [(i, (i + 1) % size) for i in range(size - 1)]
        down = [(j, i) for i, j in up]
        last = lax.slice_in_dim(value, length - width, length, axis=dim)
        first = lax.slice_in_dim(value, 0, width, axis=dim)
        before = lax.ppermute(last, axis, up)
        after = lax.ppermute(first, axis, down)
        value = jnp.concatenate([before, value, after], axis=dim)
    return value


def tap_forward(weights, source, row_count, col_count):
    result = None
    for tap_row in range(3):
        for tap_col in range(3):
            term = jnp.einsum(
                "oi,irc->orc",
                weights[tap_row * 3 + tap_col],
                source[:, tap_row : tap_row + row_count, tap_col : tap_col + col_count],
                preferred_element_type=jnp.float32,
            )
            result = term if result is None else result + term
    return result


def tap_backward(weights, source, row_count, col_count):
    result = None
    for tap_row in range(3):
        for tap_col in range(3):
            term = jnp.einsum(
                "oi,orc->irc",
                weights[tap_row * 3 + tap_col],
                source[
                    :, 2 - tap_row : 2 - tap_row + row_count, 2 - tap_col : 2 - tap_col + col_count
                ],
                preferred_element_type=jnp.float32,
            )
            result = term if result is None else result + term
    return result


def per_device(image, filters, bias, upstream):
    row_count = image.shape[1]
    col_count = image.shape[2]
    stacked = jnp.stack([image, upstream])
    with_rims = with_halo(stacked, (("band", 2),), 1)
    padded = jnp.pad(with_rims, ((0, 0), (0, 0), (0, 0), (1, 1)))
    outward = lax.all_to_all(filters, "chan", split_axis=1, concat_axis=2, tiled=True)
    w_part = outward
    forward_sum = tap_forward(
        w_part, lax.all_gather(padded[0], "chan", axis=0, tiled=True), row_count, col_count
    )
    w_part = filters
    grad_sum = tap_backward(
        w_part, lax.all_gather(padded[1], "chan", axis=0, tiled=True), row_count, col_count
    )
    features = (forward_sum + bias.astype(jnp.float32)[:, None, None]).astype(jnp.bfloat16)
    image_grad = grad_sum.astype(jnp.bfloat16)
    return (features, image_grad)


def solution(mesh):
    return jax.shard_map(
        per_device,
        mesh=mesh,
        in_specs=(
            P("chan", "band", None),
            P(None, None, "chan"),
            P("chan"),
            P("chan", "band", None),
        ),
        out_specs=(P("chan", "band", None), P("chan", "band", None)),
        check_vma=False,
    )
```

profile of v0, /device:TPU:0, one launch (start us, length us, event | category | flops | bytes accessed | tf_op | source)
XLA Modules:
  0.0 213.0 jit_solution(11126061056946139895)
XLA Ops:
  7.2 0.0 all-gather.7.cloned.1.call-start
  7.2 1.5 copy.11
  8.7 1.5 copy.12
  10.2 2.4 %collective-permute-start = (bf16[2,128,1,512]{1,3,2,0:T(8,128)(2,1)S(1)}, bf16[2,128,1,512]{1,3,2,0:T(8,128)(2,1)S(1)}, u32[]{:S(2)}, u32[]{:S(2)}) collective-permute-start(bf16[2,128,1,512]{1,3,2,0:T(8,128)(2,1)S(1)} %get-tuple-element.17), channel_id=1, source_target_pairs={{0,4},{4,8},{8,12},{12,16},{16,20},{20,24},{24,28},{1,5},{5,9},{9,... | collective-permute-start | bytes 786440 | tf_op jit(solution)/shard_map/ppermute | solution.py:14
  12.6 1.3 collective-permute-start.1
  13.9 0.0 collective-permute-done
  13.9 4.2 %collective-permute-done.1 = bf16[2,128,1,512]{1,3,2,0:T(8,128)(2,1)S(1)} collective-permute-done((bf16[2,128,1,512]{1,3,2,0:T(8,128)(2,1)S(1)}, bf16[2,128,1,512]{1,3,2,0:T(8,128)(2,1)S(1)}, u32[]{:S(2)}, u32[]{:S(2)}) %collective-permute-start.1) | collective-permute-done | bytes 262176 | tf_op jit(solution)/shard_map/ppermute | solution.py:15
  18.1 0.4 select_maximum_fusion
  18.5 0.0 copy-start.1
  18.5 1.3 fusion.121
  19.9 0.0 all-gather.7.cloned.1.call-update
  19.9 0.5 copy-done.1
  20.3 2.2 %copy.13 = bf16[9,512,128]{2,0,1:T(8,128)(2,1)} copy(bf16[9,512,128]{2,1,0:T(8,128)(2,1)S(1)} %copy-done.1) | data formatting | bytes 2359296 | tf_op args[1]
  22.6 0.0 copy-start.3
  22.6 5.0 %all-to-all-start = ((bf16[9,512,128]{2,0,1:T(8,128)(2,1)}), bf16[9,512,128]{2,0,1:T(8,128)(2,1)S(1)}, u32[]{:S(2)}, u32[]{:S(2)}) async-start(bf16[9,512,128]{2,0,1:T(8,128)(2,1)} %copy.13), calls=%async_computation | async-start | bytes 4194304 | tf_op jit(solution)/shard_map/all_to_all | solution.py:56
  27.6 0.0 all-gather.5.cloned.1.call-start
  27.6 0.7 all-gather.5.cloned.1.call-update
  28.3 0.0 copy-done.3
  28.3 92.6 %all-to-all-done = bf16[9,512,128]{2,0,1:T(8,128)(2,1)S(1)} async-done(((bf16[9,512,128]{2,0,1:T(8,128)(2,1)}), bf16[9,512,128]{2,0,1:T(8,128)(2,1)S(1)}, u32[]{:S(2)}, u32[]{:S(2)}) %all-to-all-start) | async-done | bytes 1179680 | tf_op jit(solution)/shard_map/all_to_all | solution.py:56
  120.9 1.0 copy.18
  121.9 0.4 fusion.122
  122.3 0.1 reshape.27
  122.4 0.1 reshape.26
  122.5 0.1 reshape.25
  122.5 0.1 reshape.29
  122.6 0.1 reshape.28
  122.6 0.1 reshape.31
  122.7 0.1 reshape.30
  122.8 0.1 reshape.33
  122.8 0.1 reshape.32
  122.9 5.9 %all-gather.7.cloned.1.call-done = bf16[1,512,6,514]{1,3,2,0:T(8,128)(2,1)} async-done(((bf16[1,128,6,514]{1,3,2,0:T(8,128)(2,1)}), bf16[1,512,6,514]{1,3,2,0:T(8,128)(2,1)}) %all-gather.7.cloned.1.call-update) | async-done | bytes 3158032 | tf_op jit(solution)/shard_map/all_gather | solution.py:63
  128.8 0.0 copy-start.2
  128.8 2.4 %fusion.13 = f32[4,512,128]{2,1,0:T(8,128)S(1)} fusion(bf16[512,6,514]{0,2,1:T(8,128)(2,1)} %bitcast.72, bf16[9,512,128]{2,1,0:T(8,128)(2,1)S(1)} %copy-done.1), kind=kOutput, calls=%fused_computation.15 | convolution fusion | flops 268435456 | bytes 3276800 | tf_op jit(solution)/shard_map/oi,orc->irc/dot_general | solution.py:38
  131.2 0.1 copy-done.2
  131.3 0.7 fusion.15
  132.0 0.7 fusion.9
  132.8 0.7 fusion.5
  133.5 0.7 fusion.1
  134.2 0.7 fusion.73
  134.9 0.7 fusion.70
  135.6 0.7 fusion.67
  136.4 0.8 fusion.97
  137.1 1.2 copy.16
  138.3 58.0 %all-gather.5.cloned.1.call-done = bf16[1,512,6,514]{1,3,2,0:T(8,128)(2,1)} async-done(((bf16[1,128,6,514]{1,3,2,0:T(8,128)(2,1)}), bf16[1,512,6,514]{1,3,2,0:T(8,128)(2,1)}) %all-gather.5.cloned.1.call-update) | async-done | bytes 3158032 | tf_op jit(solution)/shard_map/all_gather | solution.py:59
  196.3 0.0 copy-start
  196.3 2.5 %fusion.31 = f32[4,512,128]{2,1,0:T(8,128)S(1)} fusion(bf16[128,512,1]{1,0,2:T(8,128)(2,1)S(1)} %reshape.27, bf16[512,6,514]{0,2,1:T(8,128)(2,1)} %bitcast.58), kind=kOutput, calls=%fused_computation.33 | convolution fusion | flops 268435456 | bytes 3276800 | tf_op jit(solution)/shard_map/oi,irc->orc/dot_general | solution.py:24
  198.8 0.1 copy-done
  198.8 0.7 fusion.33
  199.6 0.7 fusion.27
  200.3 0.7 fusion.23
  201.0 0.7 fusion.19
  201.7 1.0 fusion.88
  202.7 0.7 fusion.85
  203.4 0.7 fusion.82
  204.1 0.8 fusion.100
  204.9 1.2 copy.15
  (2 shorter events, 0.1 us)
Async XLA Ops:
  7.2 121.6 %all-gather.7.cloned.1.call-start = ((), (), s32[]{:S(2)}) async-start(), calls=%async_computation.2 | async-start | bytes 3993600 | tf_op jit(solution)/shard_map/all_gather | solution.py:63
  10.2 3.7 %collective-permute-start = (bf16[2,128,1,512]{1,3,2,0:T(8,128)(2,1)S(1)}, bf16[2,128,1,512]{1,3,2,0:T(8,128)(2,1)S(1)}, u32[]{:S(2)}, u32[]{:S(2)}) collective-permute-start(bf16[2,128,1,512]{1,3,2,0:T(8,128)(2,1)S(1)} %get-tuple-element.17), channel_id=1, source_target_pairs={{0,4},{4,8},{8,12},{12,16},{16,20},{20,24},{24,28},{1,5},{5,9},{9,... | collective-permute-start | bytes 786440 | tf_op jit(solution)/shard_map/ppermute | solution.py:14
  12.6 5.5 %collective-permute-start.1 = (bf16[2,128,1,512]{1,3,2,0:T(8,128)(2,1)S(1)}, bf16[2,128,1,512]{1,3,2,0:T(8,128)(2,1)S(1)}, u32[]{:S(2)}, u32[]{:S(2)}) collective-permute-start(bf16[2,128,1,512]{1,3,2,0:T(8,128)(2,1)S(1)} %get-tuple-element.18), channel_id=1, source_target_pairs={{4,0},{8,4},{12,8},{16,12},{20,16},{24,20},{28,24},{5,1},{9,5},{13... | collective-permute-start | bytes 786440 | tf_op jit(solution)/shard_map/ppermute | solution.py:15
  18.5 1.8 copy-start.1
  22.6 5.7 %copy-start.3 = (bf16[128]{0:T(256)(128)(2,1)S(1)}, bf16[128]{0:T(256)(128)(2,1)}, u32[]{:S(2)}) copy-start(bf16[128]{0:T(256)(128)(2,1)} %param.6) | copy-start | bytes 772
  22.6 98.3 %all-to-all-start = ((bf16[9,512,128]{2,0,1:T(8,128)(2,1)}), bf16[9,512,128]{2,0,1:T(8,128)(2,1)S(1)}, u32[]{:S(2)}, u32[]{:S(2)}) async-start(bf16[9,512,128]{2,0,1:T(8,128)(2,1)} %copy.13), calls=%async_computation | async-start | bytes 4194304 | tf_op jit(solution)/shard_map/all_to_all | solution.py:56
  27.6 168.7 %all-gather.5.cloned.1.call-start = ((), (), s32[]{:S(2)}) async-start(), calls=%async_computation.1 | async-start | bytes 3993600 | tf_op jit(solution)/shard_map/all_gather | solution.py:59
  128.8 2.5 %copy-start.2 = (bf16[1,512,6,514]{1,3,2,0:T(8,128)(2,1)S(1)}, bf16[1,512,6,514]{1,3,2,0:T(8,128)(2,1)}, u32[]{:S(2)}) copy-start(bf16[1,512,6,514]{1,3,2,0:T(8,128)(2,1)} %all-gather.7.cloned.1.call-done) | copy-start | bytes 9474052
  196.3 2.5 %copy-start = (bf16[1,512,6,514]{1,3,2,0:T(8,128)(2,1)S(1)}, bf16[1,512,6,514]{1,3,2,0:T(8,128)(2,1)}, u32[]{:S(2)}) copy-start(bf16[1,512,6,514]{1,3,2,0:T(8,128)(2,1)} %all-gather.5.cloned.1.call-done) | copy-start | bytes 9474052
Sparse Core Ops, SparseCore 0:
  20.0 108.7 all-gather.6
  130.3 65.9 all-gather.4
where the time goes:
time: 213 us
  waiting for transfers between devices  161 us (76%)
  matrix products  16.8 us (8%)
  between operations  14.2 us (7%)
  local copies, waits for them, and re-layouts  11.4 us (5%)
  starting transfers between devices  8.71 us (4%)
    all_to_all x1, waiting for transfers between devices, per_device(): lax.all_to_all(filters, 'chan', split_axis=1, concat_axis=2, tiled=True)  92.6 us
    all_gather x1, waiting for transfers between devices, per_device(): lax.all_gather(padded[0], 'chan', axis=0, tiled=True)  58 us
    dot_general x9, matrix products, tap_forward(): jnp.einsum('oi,irc->orc', weights[tap_row * 3 + tap_col], source[:, tap_r...  8.54 us
    dot_general x9, matrix products, tap_backward(): jnp.einsum('oi,orc->irc', weights[tap_row * 3 + tap_col], source[:, 2 - t...  8.23 us
    unnamed x13, local copies, waits for them, and re-layouts  8.18 us
    all_gather x1, waiting for transfers between devices, per_device(): lax.all_gather(padded[1], 'chan', axis=0, tiled=True)  5.88 us
    all_to_all x1, starting transfers between devices, per_device(): lax.all_to_all(filters, 'chan', split_axis=1, concat_axis=2, tiled=True)  5 us
  transfers between devices with their start and end apart: 5, of which 4 were waited for; matrix products, arithmetic and copies ran while one was open for 6% of the time, Pallas kernels for 0%

commit v1 on v0

v1 whole, which is shorter than its diff:
```python
import jax
import jax.numpy as jnp
from jax import lax
from jax.sharding import PartitionSpec as P


def swap(value, axis, step):
    size = lax.axis_size(axis)
    return lax.ppermute(value, axis, [(j, j ^ step) for j in range(size)])


def neighbours(first, last):
    size = lax.axis_size("band")
    up = [(j, j + 1) for j in range(size - 1)]
    down = [(j + 1, j) for j in range(size - 1)]
    return lax.ppermute(last, "band", up), lax.ppermute(first, "band", down)


def pick(pieces, index, axis):
    stacked = jnp.stack(pieces)
    return jnp.concatenate(
        [lax.dynamic_index_in_dim(stacked, i, 0, keepdims=False) for i in index], axis=axis
    )


def spread(value, me, width):
    n = lax.axis_size("chan")
    padded = jnp.pad(value, ((0, 0), (1, 1), (0, 0)))
    pieces = []
    for k in range(n):
        piece = lax.dynamic_slice_in_dim(padded, (me ^ k) * width, width + 2, axis=1)
        pieces.append(swap(piece, "chan", k) if k else piece)
    return pieces


def add_rows(value):
    before, after = neighbours(value[:1], value[-1:])
    return jnp.concatenate([before, value, after], axis=0)


def conv(source, taps):
    return lax.conv_general_dilated(
        source[None],
        taps,
        (1, 1),
        "VALID",
        dimension_numbers=("NHWC", "HWIO", "NHWC"),
        preferred_element_type=jnp.float32,
    )[0]


def per_device(image, filters, bias, upstream):
    n = lax.axis_size("chan")
    bands = lax.axis_size("band")
    me = lax.axis_index("chan")
    row = lax.axis_index("band")
    local = filters.shape[2]
    outs = filters.shape[1]
    width = image.shape[2] // n

    flat = filters.reshape(-1, local)
    share = flat.shape[0] // bands
    part = lax.dynamic_slice_in_dim(flat, row * share, share, axis=0)
    held = [jnp.concatenate([part, jnp.tile(bias[None], (16, 1))], axis=0)]
    step = n // 2
    while step:
        stacked = jnp.stack(held)
        there = swap(stacked, "chan", step)
        held = held + [there[j] for j in range(len(held))]
        step //= 2
    order = [0]
    step = n // 2
    while step:
        order = order + [o ^ step for o in order]
        step //= 2
    held = [held[order.index(k)] for k in range(n)]
    biases = [h[share] for h in held]
    whole = lax.all_gather(
        jnp.stack([h[:share] for h in held]), "band", axis=1, tiled=True
    ).reshape(n, 3, 3, outs, local)

    x_pieces = spread(jnp.transpose(image, (1, 2, 0)), me, width)
    u_pieces = spread(jnp.transpose(upstream, (1, 2, 0)), me, width)

    natural = [me ^ k for k in range(n)]
    x = add_rows(jnp.concatenate(x_pieces, axis=2))
    forward_taps = jnp.transpose(whole, (1, 2, 0, 4, 3)).reshape(3, 3, n * local, outs)
    total = conv(x, forward_taps) + pick(biases, natural, 0).astype(jnp.float32)
    features = back(total.astype(jnp.bfloat16), me, local, True)

    u = add_rows(pick(u_pieces, natural, 2))
    backward_taps = jnp.transpose(whole[:, ::-1, ::-1], (1, 2, 3, 0, 4)).reshape(
        3, 3, outs, n * local
    )
    image_grad = back(conv(u, backward_taps).astype(jnp.bfloat16), me, local, False)
    return features, image_grad


def back(value, me, local, is_natural):
    n = lax.axis_size("chan")
    pieces = []
    for k in range(n):
        start = (me ^ k) * local if is_natural else k * local
        piece = lax.dynamic_slice_in_dim(value, start, local, axis=2)
        pieces.append(swap(piece, "chan", k) if k else piece)
    whole = pick(pieces, [me ^ k for k in range(n)], 1)
    return jnp.transpose(whole, (2, 0, 1))


def solution(mesh):
    return jax.shard_map(
        per_device,
        mesh=mesh,
        in_specs=(
            P("chan", "band", None),
            P(None, None, "chan"),
            P("chan"),
            P("chan", "band", None),
        ),
        out_specs=(P("chan", "band", None), P("chan", "band", None)),
        check_vma=False,
    )
```

time: 213 us -> 137 us (0.64)
  waiting for transfers between devices: 161 us -> 48 us
  starting transfers between devices: 8.71 us -> 36.6 us
  local copies, waits for them, and re-layouts: 11.4 us -> 25.1 us
  matrix products: 16.8 us -> 8.03 us
  other arithmetic: 0.48 us -> 4.23 us
    all_to_all x1 -> x0, waiting for transfers between devices: 92.6 us -> none  [per_device(): lax.all_to_all(filters, 'chan', split_axis=1, concat_axis=2, tiled=True)]
    all_gather x2 -> x1, waiting for transfers between devices: 63.8 us -> 5.44 us  [per_device(): lax.all_gather(jnp.stack([h[:share] for h in held]), 'band', axis=1, tile...]
    ppermute x2 -> x18, waiting for transfers between devices: 4.21 us -> 42.5 us  [the longest x14 41.1 us: swap(): return lax.ppermute(value, axis, [(j, j ^ step) for j in range(size)])]
    ppermute x2 -> x18, starting transfers between devices: 3.66 us -> 36.5 us  [the longest x14 30.6 us: swap(): return lax.ppermute(value, axis, [(j, j ^ step) for j in range(size)])]
    dot_general x18 -> x0, matrix products: 16.8 us -> none  [the longest x9 8.54 us: tap_forward(): jnp.einsum('oi,irc->orc', weights[tap_row * 3 + tap_col], source[:, tap_r...]
    conv_general_dilated x0 -> x2, matrix products: none -> 8.03 us  [conv(): lax.conv_general_dilated(source[None], taps, (1, 1), 'VALID', dimension_n...]
    reshape x0 -> x1, local copies, waits for them, and re-layouts: none -> 6.65 us  [per_device(): whole = lax.all_gather(jnp.stack([h[:share] for h in held]), 'band', axis...]
    all_to_all x1 -> x0, starting transfers between devices: 5 us -> none  [per_device(): lax.all_to_all(filters, 'chan', split_axis=1, concat_axis=2, tiled=True)]
  transfers between devices with their start and end apart: 5 -> 19, of which waited for: 4 -> 8; matrix products, arithmetic and copies ran while one was open for 6% -> 6% of each run, Pallas kernels for 0% -> 0%
where the time goes in v1:
time: 137 us; the launch traced here: 136 us
  waiting for transfers between devices  48 us (35%)
  starting transfers between devices  36.6 us (27%)
  local copies, waits for them, and re-layouts  25.1 us (18%)
  between operations  14.5 us (11%)
  matrix products  8.03 us (6%)
  other arithmetic  4.23 us (3%)
    ppermute x14, waiting for transfers between devices, swap(): return lax.ppermute(value, axis, [(j, j ^ step) for j in range(size)])  41.1 us
    ppermute x14, starting transfers between devices, swap(): return lax.ppermute(value, axis, [(j, j ^ step) for j in range(size)])  30.6 us
    unnamed x33, local copies, waits for them, and re-layouts  11.1 us
    conv_general_dilated x2, matrix products, conv(): lax.conv_general_dilated(source[None], taps, (1, 1), 'VALID', dimension_n...  8.03 us
    reshape x1, local copies, waits for them, and re-layouts, per_device(): whole = lax.all_gather(jnp.stack([h[:share] for h in held]), 'band', axis...  6.65 us
    ppermute x4, starting transfers between devices, neighbours(): return (lax.ppermute(last, 'band', up), lax.ppermute(first, 'band', down))  5.99 us
    all_gather x1, waiting for transfers between devices, per_device(): lax.all_gather(jnp.stack([h[:share] for h in held]), 'band', axis=1, tile...  5.44 us
  transfers between devices with their start and end apart: 19, of which 8 were waited for; matrix products, arithmetic and copies ran while one was open for 6% of the time, Pallas kernels for 0%

profile of v1, /device:TPU:0, one launch (start us, length us, event | category | flops | bytes accessed | tf_op | source)
XLA Modules:
  0.0 136.4 jit_solution(3570369068166311153)
XLA Ops:
  7.2 0.0 copy-start
  7.2 0.0 all-gather.2.cloned.1.call-start
  7.2 1.2 copy-done
  8.5 0.7 tile.2
  9.1 4.1 %collective-permute-start.5 = (bf16[1,592,128]{2,1,0:T(8,128)(2,1)S(1)}, bf16[1,592,128]{2,1,0:T(8,128)(2,1)S(1)}, u32[]{:S(2)}, u32[]{:S(2)}) collective-permute-start(bf16[1,592,128]{2,1,0:T(8,128)(2,1)S(1)} %maximum_bitcast_fusion.4), channel_id=1, source_target_pairs={{0,2},{1,3},{2,0},{3,1},{4,6},{5,7},{6,4},{7,5},{8,10},{9,11},{10,... | collective-permute-start | bytes 454664 | tf_op jit(solution)/shard_map/ppermute | solution.py:9
  13.2 7.2 %collective-permute-done.5 = bf16[1,592,128]{2,1,0:T(8,128)(2,1)S(1)} collective-permute-done((bf16[1,592,128]{2,1,0:T(8,128)(2,1)S(1)}, bf16[1,592,128]{2,1,0:T(8,128)(2,1)S(1)}, u32[]{:S(2)}, u32[]{:S(2)}) %collective-permute-start.5) | collective-permute-done | bytes 151584 | tf_op jit(solution)/shard_map/ppermute | solution.py:9
  20.5 0.8 collective-permute-start.6
  21.3 7.6 %collective-permute-done.6 = bf16[2,592,128]{2,1,0:T(8,128)(2,1)S(1)} collective-permute-done((bf16[2,592,128]{2,1,0:T(8,128)(2,1)S(1)}, bf16[2,592,128]{2,1,0:T(8,128)(2,1)S(1)}, u32[]{:S(2)}, u32[]{:S(2)}) %collective-permute-start.6) | collective-permute-done | bytes 303136 | tf_op jit(solution)/shard_map/ppermute | solution.py:9
  28.9 0.7 copy-done.10
  29.6 0.9 pad_maximum_fusion
  30.6 0.0 all-gather.2.cloned.1.call-update
  30.6 0.4 copy.37
  31.1 0.9 pad_dynamic-slice_fusion.7
  32.0 1.5 %collective-permute-start = (bf16[4,130,128]{2,1,0:T(8,128)(2,1)}, bf16[4,130,128]{2,1,0:T(8,128)(2,1)S(1)}, u32[]{:S(2)}, u32[]{:S(2)}) collective-permute-start(bf16[4,130,128]{2,1,0:T(8,128)(2,1)} %get-tuple-element.35), channel_id=1, source_target_pairs={{0,1},{1,0},{2,3},{3,2},{4,5},{5,4},{6,7},{7,6},{8,9},{9,8},{10,11... | collective-permute-start | bytes 399368 | tf_op jit(solution)/shard_map/ppermute | solution.py:9
  33.4 3.4 %collective-permute-start.1 = (bf16[4,130,128]{2,1,0:T(8,128)(2,1)}, bf16[4,130,128]{2,1,0:T(8,128)(2,1)S(1)}, u32[]{:S(2)}, u32[]{:S(2)}) collective-permute-start(bf16[4,130,128]{2,1,0:T(8,128)(2,1)} %get-tuple-element.36), channel_id=1, source_target_pairs={{0,2},{1,3},{2,0},{3,1},{4,6},{5,7},{6,4},{7,5},{8,10},{9,11},{10,... | collective-permute-start | bytes 399368 | tf_op jit(solution)/shard_map/ppermute | solution.py:9
  36.8 0.4 copy.46
  37.2 0.8 fusion.27
  38.1 0.6 collective-permute-start.10
  38.6 3.8 %collective-permute-start.11 = (bf16[4,130,128]{2,1,0:T(8,128)(2,1)S(1)}, bf16[4,130,128]{2,1,0:T(8,128)(2,1)S(1)}, u32[]{:S(2)}, u32[]{:S(2)}) collective-permute-start(bf16[4,130,128]{2,1,0:T(8,128)(2,1)S(1)} %get-tuple-element.24), channel_id=1, source_target_pairs={{0,2},{1,3},{2,0},{3,1},{4,6},{5,7},{6,4},{7,5},{8,10},{9,11},{10,... | collective-permute-start | bytes 399368 | tf_op jit(solution)/shard_map/ppermute | solution.py:9
  42.5 0.6 collective-permute-start.12
  43.0 4.6 %collective-permute-done.1 = bf16[4,130,128]{2,1,0:T(8,128)(2,1)S(1)} collective-permute-done((bf16[4,130,128]{2,1,0:T(8,128)(2,1)}, bf16[4,130,128]{2,1,0:T(8,128)(2,1)S(1)}, u32[]{:S(2)}, u32[]{:S(2)}) %collective-permute-start.1) | collective-permute-done | bytes 133152 | tf_op jit(solution)/shard_map/ppermute | solution.py:9
  47.7 1.3 collective-permute-start.3
  49.0 1.3 collective-permute-start.4
  50.3 8.9 %collective-permute-done.11 = bf16[4,130,128]{2,1,0:T(8,128)(2,1)S(1)} collective-permute-done((bf16[4,130,128]{2,1,0:T(8,128)(2,1)S(1)}, bf16[4,130,128]{2,1,0:T(8,128)(2,1)S(1)}, u32[]{:S(2)}, u32[]{:S(2)}) %collective-permute-start.11) | collective-permute-done | bytes 133152 | tf_op jit(solution)/shard_map/ppermute | solution.py:9
  59.2 0.1 pad_maximum_fusion.1
  59.3 0.1 dynamic-slice_bitcast_fusion.3
  59.4 0.8 pad_maximum_fusion.8
  60.1 1.9 %collective-permute-start.13 = (bf16[1,130,512]{2,1,0:T(8,128)(2,1)}, bf16[1,130,512]{2,1,0:T(8,128)(2,1)}, u32[]{:S(2)}, u32[]{:S(2)}) collective-permute-start(bf16[1,130,512]{2,1,0:T(8,128)(2,1)} %get-tuple-element.6), channel_id=1, source_target_pairs={{0,4},{4,8},{8,12},{12,16},{16,20},{20,24},{24,28},{1,5},{5,9},{9,... | collective-permute-start | bytes 399368 | tf_op jit(solution)/shard_map/ppermute | solution.py:16
  62.1 1.5 %collective-permute-start.14 = (bf16[1,130,512]{2,1,0:T(8,128)(2,1)}, bf16[1,130,512]{2,1,0:T(8,128)(2,1)}, u32[]{:S(2)}, u32[]{:S(2)}) collective-permute-start(bf16[1,130,512]{2,1,0:T(8,128)(2,1)} %get-tuple-element.7), channel_id=1, source_target_pairs={{4,0},{8,4},{12,8},{16,12},{20,16},{24,20},{28,24},{5,1},{9,5},{13... | collective-permute-start | bytes 399368 | tf_op jit(solution)/shard_map/ppermute | solution.py:16
  63.6 0.1 maximum_bitcast_fusion
  63.7 0.1 pad.9
  63.7 0.3 reshape.69
  64.1 0.3 copy.39
  64.4 0.7 slice.69
  65.1 0.2 copy-done.6
  65.3 1.4 %collective-permute-done.14 = bf16[1,130,512]{2,1,0:T(8,128)(2,1)} collective-permute-done((bf16[1,130,512]{2,1,0:T(8,128)(2,1)}, bf16[1,130,512]{2,1,0:T(8,128)(2,1)}, u32[]{:S(2)}, u32[]{:S(2)}) %collective-permute-start.14) | collective-permute-done | bytes 133152 | tf_op jit(solution)/shard_map/ppermute | solution.py:16
  66.7 1.1 maximum_bitcast_fusion.1
  67.8 0.1 pad.11
  67.9 0.3 reshape.76
  68.2 0.3 copy.48
  68.5 0.7 slice_bitcast_fusion.5
  69.3 5.4 %all-gather.2.cloned.1.call-done = bf16[4,4608,128]{2,1,0:T(8,128)(2,1)} async-done(((bf16[4,576,128]{2,1,0:T(8,128)(2,1)}), bf16[4,4608,128]{2,1,0:T(8,128)(2,1)}) %all-gather.2.cloned.1.call-update) | async-done | bytes 4718608 | tf_op jit(solution)/shard_map/all_gather | solution.py:78
  74.7 5.0 %reverse_bitcast_fusion = bf16[4,3,3,64,8,128]{5,4,3,2,1,0:T(8,128)(2,1)} fusion(bf16[4,3,3,512,128]{4,3,2,1,0:T(8,128)(2,1)} %bitcast.118), kind=kLoop, calls=%fused_computation.3 | loop fusion | bytes 9437184
  79.7 6.7 %copy.40 = bf16[4,3,3,512,128]{3,4,0,2,1:T(8,128)(2,1)} copy(bf16[4,3,3,512,128]{4,3,2,1,0:T(8,128)(2,1)} %bitcast.119) | data formatting | bytes 9437184 | tf_op jit(solution)/shard_map/reshape | solution.py:80
  86.4 5.2 %fusion.8 = bf16[4,8,17,512]{3,1,2,0:T(8,128)(2,1)S(1)} fusion(bf16[4,3,3,64,8,128]{5,4,3,2,1,0:T(8,128)(2,1)} %reverse_bitcast_fusion, bf16[6,1,7,2,512]{4,2,3,0,1:T(8,128)(2,1)S(1)} %slice.77, bf16[6,1,8,17,512]{4,2,3,0,1:T(8,128)(2,1)S(1)} %copy.48, pred[8,17]{0,1:T(8,128)(4,1)S(1)} %copy-done.13), kind=kOutput, calls=%fused_computation.9 | convolution fusion | flops 2570272768 | bytes 6197384 | tf_op jit(solution)/shard_map/conv_general_dilated | solution.py:42
  91.6 0.3 copy.50
  91.9 0.2 slice_bitcast_fusion.1
  92.1 0.6 copy-done.7
  92.8 2.8 %convolution_select_fusion = f32[4,8,17,512]{3,1,2,0:T(8,128)S(1)} fusion(bf16[3,3,512,512]{3,2,1,0:T(8,128)(2,1)S(1)} %bitcast.120, bf16[6,1,7,2,512]{4,2,3,0,1:T(8,128)(2,1)S(1)} %copy-done.11, bf16[6,1,8,17,512]{4,2,3,0,1:T(8,128)(2,1)S(1)} %copy-done.7, pred[8,17]{0,1:T(8,128)(4,1)S(1)} %copy-done.13), kind=kOutput, calls=%fused_computation.8 | convolution fusion | flops 2569994240 | bytes 6754440 | tf_op jit(solution)/shard_map/conv_general_dilated | solution.py:42
  95.6 0.7 copy.41
  96.3 0.2 slice_bitcast_fusion.2
  96.5 6.1 %collective-permute-start.17 = (bf16[4,128,128]{2,0,1:T(4,128)(2,1)S(1)}, bf16[4,128,128]{2,0,1:T(4,128)(2,1)S(1)}, u32[]{:S(2)}, u32[]{:S(2)}) collective-permute-start(bf16[4,128,128]{2,0,1:T(4,128)(2,1)S(1)} %get-tuple-element.19), channel_id=1, source_target_pairs={{0,3},{1,2},{2,1},{3,0},{4,7},{5,6},{6,5},{7,4},{8,11},{9,10},{10,... | collective-permute-start | bytes 393224 | tf_op jit(solution)/shard_map/ppermute | solution.py:9
  102.6 0.6 collective-permute-start.15
  103.2 0.2 fusion.12
  103.4 0.2 dynamic-slice_bitcast_fusion.4
  103.6 3.8 %collective-permute-start.9 = (bf16[4,128,128]{2,0,1:T(4,128)(2,1)S(1)}, bf16[4,128,128]{2,0,1:T(4,128)(2,1)S(1)}, u32[]{:S(2)}, u32[]{:S(2)}) collective-permute-start(bf16[4,128,128]{2,0,1:T(4,128)(2,1)S(1)} %get-tuple-element.31), channel_id=1, source_target_pairs={{0,3},{1,2},{2,1},{3,0},{4,7},{5,6},{6,5},{7,4},{8,11},{9,10},{10,... | collective-permute-start | bytes 393224 | tf_op jit(solution)/shard_map/ppermute | solution.py:9
  107.4 5.3 %collective-permute-start.7 = (bf16[4,128,128]{2,0,1:T(4,128)(2,1)S(1)}, bf16[4,128,128]{2,0,1:T(4,128)(2,1)S(1)}, u32[]{:S(2)}, u32[]{:S(2)}) collective-permute-start(bf16[4,128,128]{2,0,1:T(4,128)(2,1)S(1)} %get-tuple-element.33), channel_id=1, source_target_pairs={{0,1},{1,0},{2,3},{3,2},{4,5},{5,4},{6,7},{7,6},{8,9},{9,8},{10,11... | collective-permute-start | bytes 393224 | tf_op jit(solution)/shard_map/ppermute | solution.py:9
  112.8 7.7 %collective-permute-done.16 = bf16[4,128,128]{2,0,1:T(4,128)(2,1)S(1)} collective-permute-done((bf16[4,128,128]{2,0,1:T(4,128)(2,1)S(1)}, bf16[4,128,128]{2,0,1:T(4,128)(2,1)S(1)}, u32[]{:S(2)}, u32[]{:S(2)}) %collective-permute-start.16) | collective-permute-done | bytes 131104 | tf_op jit(solution)/shard_map/ppermute | solution.py:9
  120.4 0.5 pad_maximum_fusion.3
  120.9 5.1 %collective-permute-done.8 = bf16[4,128,128]{2,0,1:T(4,128)(2,1)S(1)} collective-permute-done((bf16[4,128,128]{2,0,1:T(4,128)(2,1)S(1)}, bf16[4,128,128]{2,0,1:T(4,128)(2,1)S(1)}, u32[]{:S(2)}, u32[]{:S(2)}) %collective-permute-start.8) | collective-permute-done | bytes 131104 | tf_op jit(solution)/shard_map/ppermute | solution.py:9
  126.0 0.5 pad_maximum_fusion.2
  126.5 0.4 constant_dynamic-slice_fusion.3
  127.0 1.2 copy.56
  128.4 1.2 copy.55
  (59 shorter events, 0.5 us)
Async XLA Ops:
  7.2 1.3 copy-start
  7.2 67.5 %all-gather.2.cloned.1.call-start = ((), (), s32[]{:S(2)}) async-start(), calls=%async_computation | async-start | bytes 5308416 | tf_op jit(solution)/shard_map/all_gather | solution.py:78
  9.1 21.5 %copy-start.8 = (bf16[128,4,512]{2,1,0:T(4,128)(2,1)S(1)}, bf16[128,4,512]{2,1,0:T(4,128)(2,1)}, u32[]{:S(2)}) copy-start(bf16[128,4,512]{2,1,0:T(4,128)(2,1)} %param.4) | copy-start | bytes 1572868
  9.1 11.3 %collective-permute-start.5 = (bf16[1,592,128]{2,1,0:T(8,128)(2,1)S(1)}, bf16[1,592,128]{2,1,0:T(8,128)(2,1)S(1)}, u32[]{:S(2)}, u32[]{:S(2)}) collective-permute-start(bf16[1,592,128]{2,1,0:T(8,128)(2,1)S(1)} %maximum_bitcast_fusion.4), channel_id=1, source_target_pairs={{0,2},{1,3},{2,0},{3,1},{4,6},{5,7},{6,4},{7,5},{8,10},{9,11},{10,... | collective-permute-start | bytes 454664 | tf_op jit(solution)/shard_map/ppermute | solution.py:9
  20.5 8.4 %collective-permute-start.6 = (bf16[2,592,128]{2,1,0:T(8,128)(2,1)S(1)}, bf16[2,592,128]{2,1,0:T(8,128)(2,1)S(1)}, u32[]{:S(2)}, u32[]{:S(2)}) collective-permute-start(bf16[2,592,128]{2,1,0:T(8,128)(2,1)S(1)} %pad_maximum_fusion.4), channel_id=1, source_target_pairs={{0,1},{1,0},{2,3},{3,2},{4,5},{5,4},{6,7},{7,6},{8,9},{9,8},{10,11... | collective-permute-start | bytes 909320 | tf_op jit(solution)/shard_map/ppermute | solution.py:9
  28.9 0.7 copy-start.10
  30.6 6.2 %copy-start.9 = (bf16[128,4,512]{2,1,0:T(4,128)(2,1)S(1)}, bf16[128,4,512]{2,1,0:T(4,128)(2,1)}, u32[]{:S(2)}) copy-start(bf16[128,4,512]{2,1,0:T(4,128)(2,1)} %param.7) | copy-start | bytes 1572868
  32.0 10.5 %collective-permute-start = (bf16[4,130,128]{2,1,0:T(8,128)(2,1)}, bf16[4,130,128]{2,1,0:T(8,128)(2,1)S(1)}, u32[]{:S(2)}, u32[]{:S(2)}) collective-permute-start(bf16[4,130,128]{2,1,0:T(8,128)(2,1)} %get-tuple-element.35), channel_id=1, source_target_pairs={{0,1},{1,0},{2,3},{3,2},{4,5},{5,4},{6,7},{7,6},{8,9},{9,8},{10,11... | collective-permute-start | bytes 399368 | tf_op jit(solution)/shard_map/ppermute | solution.py:9
  33.4 14.2 %collective-permute-start.1 = (bf16[4,130,128]{2,1,0:T(8,128)(2,1)}, bf16[4,130,128]{2,1,0:T(8,128)(2,1)S(1)}, u32[]{:S(2)}, u32[]{:S(2)}) collective-permute-start(bf16[4,130,128]{2,1,0:T(8,128)(2,1)} %get-tuple-element.36), channel_id=1, source_target_pairs={{0,2},{1,3},{2,0},{3,1},{4,6},{5,7},{6,4},{7,5},{8,10},{9,11},{10,... | collective-permute-start | bytes 399368 | tf_op jit(solution)/shard_map/ppermute | solution.py:9
  36.8 10.8 %collective-permute-start.2 = (bf16[4,130,128]{2,1,0:T(8,128)(2,1)S(1)}, bf16[4,130,128]{2,1,0:T(8,128)(2,1)S(1)}, u32[]{:S(2)}, u32[]{:S(2)}) collective-permute-start(bf16[4,130,128]{2,1,0:T(8,128)(2,1)S(1)} %get-tuple-element.37), channel_id=1, source_target_pairs={{0,3},{1,2},{2,1},{3,0},{4,7},{5,6},{6,5},{7,4},{8,11},{9,10},{10,... | collective-permute-start | bytes 399368 | tf_op jit(solution)/shard_map/ppermute | solution.py:9
  38.1 12.2 %collective-permute-start.10 = (bf16[4,130,128]{2,1,0:T(8,128)(2,1)}, bf16[4,130,128]{2,1,0:T(8,128)(2,1)S(1)}, u32[]{:S(2)}, u32[]{:S(2)}) collective-permute-start(bf16[4,130,128]{2,1,0:T(8,128)(2,1)} %get-tuple-element.23), channel_id=1, source_target_pairs={{0,1},{1,0},{2,3},{3,2},{4,5},{5,4},{6,7},{7,6},{8,9},{9,8},{10,11... | collective-permute-start | bytes 399368 | tf_op jit(solution)/shard_map/ppermute | solution.py:9
  38.6 20.6 %collective-permute-start.11 = (bf16[4,130,128]{2,1,0:T(8,128)(2,1)S(1)}, bf16[4,130,128]{2,1,0:T(8,128)(2,1)S(1)}, u32[]{:S(2)}, u32[]{:S(2)}) collective-permute-start(bf16[4,130,128]{2,1,0:T(8,128)(2,1)S(1)} %get-tuple-element.24), channel_id=1, source_target_pairs={{0,2},{1,3},{2,0},{3,1},{4,6},{5,7},{6,4},{7,5},{8,10},{9,11},{10,... | collective-permute-start | bytes 399368 | tf_op jit(solution)/shard_map/ppermute | solution.py:9
  42.5 16.7 %collective-permute-start.12 = (bf16[4,130,128]{2,1,0:T(8,128)(2,1)S(1)}, bf16[4,130,128]{2,1,0:T(8,128)(2,1)S(1)}, u32[]{:S(2)}, u32[]{:S(2)}) collective-permute-start(bf16[4,130,128]{2,1,0:T(8,128)(2,1)S(1)} %get-tuple-element.25), channel_id=1, source_target_pairs={{0,3},{1,2},{2,1},{3,0},{4,7},{5,6},{6,5},{7,4},{8,11},{9,10},{10,... | collective-permute-start | bytes 399368 | tf_op jit(solution)/shard_map/ppermute | solution.py:9
  47.7 15.9 %collective-permute-start.3 = (bf16[1,130,512]{2,1,0:T(8,128)(2,1)S(1)}, bf16[1,130,512]{2,1,0:T(8,128)(2,1)S(1)}, u32[]{:S(2)}, u32[]{:S(2)}) collective-permute-start(bf16[1,130,512]{2,1,0:T(8,128)(2,1)S(1)} %get-tuple-element.12), channel_id=1, source_target_pairs={{0,4},{4,8},{8,12},{12,16},{16,20},{20,24},{24,28},{1,5},{5,9},{9,... | collective-permute-start | bytes 399368 | tf_op jit(solution)/shard_map/ppermute | solution.py:16
  49.0 14.6 %collective-permute-start.4 = (bf16[1,130,512]{2,1,0:T(8,128)(2,1)S(1)}, bf16[1,130,512]{2,1,0:T(8,128)(2,1)S(1)}, u32[]{:S(2)}, u32[]{:S(2)}) collective-permute-start(bf16[1,130,512]{2,1,0:T(8,128)(2,1)S(1)} %get-tuple-element.13), channel_id=1, source_target_pairs={{4,0},{8,4},{12,8},{16,12},{20,16},{24,20},{28,24},{5,1},{9,5},{13... | collective-permute-start | bytes 399368 | tf_op jit(solution)/shard_map/ppermute | solution.py:16
  59.3 4.2 %copy-start.2 = (bf16[4,130,128]{2,1,0:T(8,128)(2,1)}, bf16[4,130,128]{2,1,0:T(8,128)(2,1)S(1)}, u32[]{:S(2)}) copy-start(bf16[4,130,128]{2,1,0:T(8,128)(2,1)S(1)} %get-tuple-element.10) | copy-start | bytes 399364
  59.3 4.2 %copy-start.4 = (bf16[4,130,128]{2,1,0:T(8,128)(2,1)}, bf16[4,130,128]{2,1,0:T(8,128)(2,1)S(1)}, u32[]{:S(2)}) copy-start(bf16[4,130,128]{2,1,0:T(8,128)(2,1)S(1)} %get-tuple-element.11) | copy-start | bytes 399364
  60.1 5.0 %collective-permute-start.13 = (bf16[1,130,512]{2,1,0:T(8,128)(2,1)}, bf16[1,130,512]{2,1,0:T(8,128)(2,1)}, u32[]{:S(2)}, u32[]{:S(2)}) collective-permute-start(bf16[1,130,512]{2,1,0:T(8,128)(2,1)} %get-tuple-element.6), channel_id=1, source_target_pairs={{0,4},{4,8},{8,12},{12,16},{16,20},{20,24},{24,28},{1,5},{5,9},{9,... | collective-permute-start | bytes 399368 | tf_op jit(solution)/shard_map/ppermute | solution.py:16
  62.1 4.7 %collective-permute-start.14 = (bf16[1,130,512]{2,1,0:T(8,128)(2,1)}, bf16[1,130,512]{2,1,0:T(8,128)(2,1)}, u32[]{:S(2)}, u32[]{:S(2)}) collective-permute-start(bf16[1,130,512]{2,1,0:T(8,128)(2,1)} %get-tuple-element.7), channel_id=1, source_target_pairs={{4,0},{8,4},{12,8},{16,12},{20,16},{24,20},{28,24},{5,1},{9,5},{13... | collective-permute-start | bytes 399368 | tf_op jit(solution)/shard_map/ppermute | solution.py:16
  64.0 2.7 %copy-start.3 = (bf16[4,130,128]{2,1,0:T(8,128)(2,1)S(1)}, bf16[4,130,128]{2,1,0:T(8,128)(2,1)}, u32[]{:S(2)}) copy-start(bf16[4,130,128]{2,1,0:T(8,128)(2,1)} %copy-done.2) | copy-start | bytes 399364
  64.1 2.7 %copy-start.5 = (bf16[4,130,128]{2,1,0:T(8,128)(2,1)S(1)}, bf16[4,130,128]{2,1,0:T(8,128)(2,1)}, u32[]{:S(2)}) copy-start(bf16[4,130,128]{2,1,0:T(8,128)(2,1)} %copy-done.4) | copy-start | bytes 399364
  64.3 1.0 copy-start.6
  67.9 1.3 copy-start.12
  79.7 6.7 %copy-start.13 = (pred[8,17]{0,1:T(8,128)(4,1)S(1)}, pred[8,17]{0,1:T(8,128)(4,1)}, u32[]{:S(2)}) copy-start(pred[8,17]{0,1:T(8,128)(4,1)} %constant.82) | copy-start | bytes 412
  86.4 5.8 %copy-start.1 = (bf16[4,3,3,512,128]{3,4,0,2,1:T(8,128)(2,1)S(1)}, bf16[4,3,3,512,128]{3,4,0,2,1:T(8,128)(2,1)}, u32[]{:S(2)}) copy-start(bf16[4,3,3,512,128]{3,4,0,2,1:T(8,128)(2,1)} %copy.40) | copy-start | bytes 14155780
  91.6 1.2 copy-start.7
  91.6 1.1 copy-start.11
  96.5 10.9 %collective-permute-start.17 = (bf16[4,128,128]{2,0,1:T(4,128)(2,1)S(1)}, bf16[4,128,128]{2,0,1:T(4,128)(2,1)S(1)}, u32[]{:S(2)}, u32[]{:S(2)}) collective-permute-start(bf16[4,128,128]{2,0,1:T(4,128)(2,1)S(1)} %get-tuple-element.19), channel_id=1, source_target_pairs={{0,3},{1,2},{2,1},{3,0},{4,7},{5,6},{6,5},{7,4},{8,11},{9,10},{10,... | collective-permute-start | bytes 393224 | tf_op jit(solution)/shard_map/ppermute | solution.py:9
  102.6 17.8 %collective-permute-start.16 = (bf16[4,128,128]{2,0,1:T(4,128)(2,1)S(1)}, bf16[4,128,128]{2,0,1:T(4,128)(2,1)S(1)}, u32[]{:S(2)}, u32[]{:S(2)}) collective-permute-start(bf16[4,128,128]{2,0,1:T(4,128)(2,1)S(1)} %get-tuple-element.20), channel_id=1, source_target_pairs={{0,2},{1,3},{2,0},{3,1},{4,6},{5,7},{6,4},{7,5},{8,10},{9,11},{10,... | collective-permute-start | bytes 393224 | tf_op jit(solution)/shard_map/ppermute | solution.py:9
  102.6 17.8 %collective-permute-start.15 = (bf16[4,128,128]{2,0,1:T(4,128)(2,1)S(1)}, bf16[4,128,128]{2,0,1:T(4,128)(2,1)S(1)}, u32[]{:S(2)}, u32[]{:S(2)}) collective-permute-start(bf16[4,128,128]{2,0,1:T(4,128)(2,1)S(1)} %get-tuple-element.21), channel_id=1, source_target_pairs={{0,1},{1,0},{2,3},{3,2},{4,5},{5,4},{6,7},{7,6},{8,9},{9,8},{10,11... | collective-permute-start | bytes 393224 | tf_op jit(solution)/shard_map/ppermute | solution.py:9
  103.6 17.3 %collective-permute-start.9 = (bf16[4,128,128]{2,0,1:T(4,128)(2,1)S(1)}, bf16[4,128,128]{2,0,1:T(4,128)(2,1)S(1)}, u32[]{:S(2)}, u32[]{:S(2)}) collective-permute-start(bf16[4,128,128]{2,0,1:T(4,128)(2,1)S(1)} %get-tuple-element.31), channel_id=1, source_target_pairs={{0,3},{1,2},{2,1},{3,0},{4,7},{5,6},{6,5},{7,4},{8,11},{9,10},{10,... | collective-permute-start | bytes 393224 | tf_op jit(solution)/shard_map/ppermute | solution.py:9
  107.4 18.6 %collective-permute-start.8 = (bf16[4,128,128]{2,0,1:T(4,128)(2,1)S(1)}, bf16[4,128,128]{2,0,1:T(4,128)(2,1)S(1)}, u32[]{:S(2)}, u32[]{:S(2)}) collective-permute-start(bf16[4,128,128]{2,0,1:T(4,128)(2,1)S(1)} %get-tuple-element.32), channel_id=1, source_target_pairs={{0,2},{1,3},{2,0},{3,1},{4,6},{5,7},{6,4},{7,5},{8,10},{9,11},{10,... | collective-permute-start | bytes 393224 | tf_op jit(solution)/shard_map/ppermute | solution.py:9
  107.4 18.6 %collective-permute-start.7 = (bf16[4,128,128]{2,0,1:T(4,128)(2,1)S(1)}, bf16[4,128,128]{2,0,1:T(4,128)(2,1)S(1)}, u32[]{:S(2)}, u32[]{:S(2)}) collective-permute-start(bf16[4,128,128]{2,0,1:T(4,128)(2,1)S(1)} %get-tuple-element.33), channel_id=1, source_target_pairs={{0,1},{1,0},{2,3},{3,2},{4,5},{5,4},{6,7},{7,6},{8,9},{9,8},{10,11... | collective-permute-start | bytes 393224 | tf_op jit(solution)/shard_map/ppermute | solution.py:9
Sparse Core Ops, SparseCore 0:
  30.7 43.9 all-gather.1

commit v2 on v1

--- a/solution.py
+++ b/solution.py
@@ -1,6 +1,8 @@
 import jax
 import jax.numpy as jnp
 from jax import lax
+from jax.experimental import pallas as pl
+from jax.experimental.pallas import tpu as pltpu
 from jax.sharding import PartitionSpec as P
 
 
@@ -49,7 +51,7 @@
     )[0]
 
 
-def per_device(image, filters, bias, upstream):
+def plain(image, filters, bias, upstream):
     n = lax.axis_size("chan")
     bands = lax.axis_size("band")
     me = lax.axis_index("chan")
@@ -107,6 +109,202 @@
     return jnp.transpose(whole, (2, 0, 1))
 
 
+def fill_rows(target, piece, row, lanes, width):
+    for shift in range(3):
+        target[shift, pl.ds(row * width, width), lanes] = piece[shift : shift + width, :]
+
+
+def fill_source(target, pieces, before, after, blocks, local, width):
+    rows = pieces[0].shape[0]
+    for k, block in enumerate(blocks):
+        lanes = pl.ds(pl.multiple_of(block * local, local), local)
+        mine = slice(k * local, (k + 1) * local)
+        fill_rows(target, before[0, :, mine], 0, lanes, width)
+        for row in range(rows):
+            fill_rows(target, pieces[k][row], row + 1, lanes, width)
+        fill_rows(target, after[0, :, mine], rows + 1, lanes, width)
+
+
+def forward_kernel(n, bands, halves, place, *refs):
+    pieces, refs = refs[:n], refs[n:]
+    before, after, filters, bias = refs[:4]
+    shares, refs = refs[4 : 4 + 2 * len(halves)], refs[4 + 2 * len(halves) :]
+    outs, (weights, source, total) = refs[:n], refs[n:]
+    me, band = place[0], place[1]
+    taps, channels, local = filters.shape
+    rows, padded, _ = pieces[0].shape
+    width = padded - 2
+    share = taps * channels // bands
+    part = share // len(halves)
+    for tap in range(taps):
+        weights[pl.ds(tap * channels, channels), :local] = filters[tap]
+    for h, order in enumerate(halves):
+        for side in range(2):
+            held = shares[2 * h + side]
+            for j, d in enumerate(order):
+                start = pl.multiple_of((band ^ (d | side)) * share + h * part, 32)
+                for k in range(1, n):
+                    weights[pl.ds(start, part), pl.ds(k * local, local)] = held[j, k - 1]
+    fill_source(source, pieces, before, after, range(n), local, width)
+    acc = None
+    for a in range(3):
+        for b in range(3):
+            term = lax.dot_general(
+                source[b, pl.ds(a * width, rows * width), :],
+                weights[pl.ds((3 * a + b) * channels, channels), :],
+                (((1,), (1,)), ((), ())),
+                preferred_element_type=jnp.float32,
+            )
+            acc = term if acc is None else acc + term
+    for j in range(n):
+        total[j] = acc[:, j * local : (j + 1) * local]
+    for k in range(n):
+        value = total[me ^ k] + bias[k : k + 1, :].astype(jnp.float32)
+        outs[k][...] = value.astype(jnp.bfloat16)
+
+
+def backward_kernel(n, place, *refs):
+    pieces, refs = refs[:n], refs[n:]
+    before, after, weights = refs[:3]
+    outs, (source,) = refs[3 : 3 + n], refs[3 + n :]
+    me = place[0]
+    rows, padded, local = pieces[0].shape
+    width = padded - 2
+    channels = n * local
+    fill_source(source, pieces, before, after, [me ^ k for k in range(n)], local, width)
+    acc = None
+    for a in range(3):
+        for b in range(3):
+            term = jnp.dot(
+                source[2 - b, pl.ds((2 - a) * width, rows * width), :],
+                weights[pl.ds((3 * a + b) * channels, channels), :],
+                preferred_element_type=jnp.float32,
+            )
+            acc = term if acc is None else acc + term
+    for k in range(n):
+        outs[k][...] = acc[:, k * local : (k + 1) * local].astype(jnp.bfloat16)
+
+
+SMEM = pl.BlockSpec(memory_space=pltpu.SMEM)
+VMEM = pl.BlockSpec(memory_space=pltpu.VMEM)
+PARAMS = pltpu.CompilerParams(vmem_limit_bytes=40 * 2**20)
+
+
+def forward(place, pieces, before, after, filters, bias, shares, halves, bands):
+    n = len(pieces)
+    rows, padded, local = pieces[0].shape
+    width = padded - 2
+    channels = filters.shape[1]
+    args = [*pieces, before, after, filters, bias, *shares]
+    out = jax.ShapeDtypeStruct((rows * width, local), jnp.bfloat16)
+    return pl.pallas_call(
+        lambda *refs: forward_kernel(n, bands, halves, *refs),
+        out_shape=[out] * n
+        + [jax.ShapeDtypeStruct((9 * channels, n * local), jnp.bfloat16)],
+        in_specs=[SMEM] + [VMEM] * len(args),
+        out_specs=[VMEM] * (n + 1),
+        scratch_shapes=[
+            pltpu.VMEM((3, (rows + 2) * width, n * local), jnp.bfloat16),
+            pltpu.VMEM((n, rows * width, local), jnp.float32),
+        ],
+        compiler_params=PARAMS,
+        cost_estimate=pl.CostEstimate(
+            flops=18 * rows * width * channels * n * local,
+            bytes_accessed=10 * 2**20,
+            transcendentals=0,
+        ),
+        name="forward",
+    )(place, *args)
+
+
+def backward(place, pieces, before, after, weights):
+    n = len(pieces)
+    rows, padded, local = pieces[0].shape
+    width = padded - 2
+    args = [*pieces, before, after, weights]
+    out = jax.ShapeDtypeStruct((rows * width, local), jnp.bfloat16)
+    return pl.pallas_call(
+        lambda *refs: backward_kernel(n, *refs),
+        out_shape=[out] * n,
+        in_specs=[SMEM] + [VMEM] * len(args),
+        out_specs=[VMEM] * n,
+        scratch_shapes=[pltpu.VMEM((3, (rows + 2) * width, n * local), jnp.bfloat16)],
+        compiler_params=PARAMS,
+        cost_estimate=pl.CostEstimate(
+            flops=18 * rows * width * weights.shape[0] // 9 * n * local,
+            bytes_accessed=6 * 2**20,
+            transcendentals=0,
+        ),
+        name="backward",
+    )(place, *args)
+
+
+def xor_gather(value, axis, steps):
+    held, order = [value], [0]
+    for step in steps:
+        there = swap(jnp.stack(held) if len(held) > 1 else held[0][None], axis, step)
+        held = held + [there[j] for j in range(len(held))]
+        order = order + [o ^ step for o in order]
+    return held, order
+
+
+def halving(size):
+    steps = []
+    while size > 1:
+        size //= 2
+        steps.append(size)
+    return steps
+
+
+def rims(pieces):
+    first = jnp.concatenate([p[:1] for p in pieces], axis=2)
+    last = jnp.concatenate([p[-1:] for p in pieces], axis=2)
+    return neighbours(first, last)
+
+
+def home(pieces, me, rows, width):
+    whole = pick([p.reshape(rows, width, -1) for p in pieces], [me ^ k for k in range(len(pieces))], 1)
+    return jnp.transpose(whole, (2, 0, 1))
+
+
+def per_device(image, filters, bias, upstream):
+    n = lax.axis_size("chan")
+    bands = lax.axis_size("band")
+    taps, outs, local = filters.shape
+    rows = image.shape[1]
+    width = image.shape[2] // n
+    share = taps * outs // bands
+    if local % 128 or width % 128 or share % 32 or bands < 4:
+        return plain(image, filters, bias, upstream)
+    me = lax.axis_index("chan")
+    band = lax.axis_index("band")
+    place = jnp.stack([me, band]).astype(jnp.int32)
+
+    part = lax.dynamic_slice_in_dim(filters.reshape(-1, local), band * share, share, axis=0)
+    part = jnp.concatenate([part, jnp.tile(bias[None], (16, 1))], axis=0)
+    held, order = xor_gather(part, "chan", halving(n))
+    held = [held[order.index(k)] for k in range(n)]
+    biases = jnp.concatenate([h[share : share + 1] for h in held], axis=0)
+
+    steps = halving(bands)[:-1]
+    shares, halves = [], []
+    for h, path in enumerate((steps, steps[::-1])):
+        half = jnp.stack([p[h * share // 2 : (h + 1) * share // 2] for p in held[1:]])
+        got, order = xor_gather(half, "band", path)
+        got = jnp.stack(got)
+        shares += [got, swap(got, "band", 1)]
+        halves.append(order)
+
+    x = spread(jnp.transpose(image, (1, 2, 0)), me, width)
+    u = spread(jnp.transpose(upstream, (1, 2, 0)), me, width)
+
+    *sent, weights = forward(place, x, *rims(x), filters, biases, shares, halves, bands)
+    features = [swap(p, "chan", k) if k else p for k, p in enumerate(sent)]
+    sent = backward(place, u, *rims(u), weights)
+    image_grad = [swap(p, "chan", k) if k else p for k, p in enumerate(sent)]
+    return home(features, me, rows, width), home(image_grad, me, rows, width)
+
+
 def solution(mesh):
     return jax.shard_map(
         per_device,

time: 137 us -> 105 us (0.77)
  the two profiles are of different devices: /device:TPU:0 before, /device:TPU:10 now
where the time goes in v2:
time: 105 us; the launch traced here: 104 us
  waiting for transfers between devices  52.4 us (50%)
  starting transfers between devices  34.8 us (33%)
  Pallas kernels  8.04 us (8%)
  local copies, waits for them, and re-layouts  5.18 us (5%)
  other arithmetic  2.87 us (3%)
  between operations  1.07 us (1%)
    ppermute x20, waiting for transfers between devices, swap(): return lax.ppermute(value, axis, [(j, j ^ step) for j in range(size)])  52.4 us
    ppermute x20, starting transfers between devices, swap(): return lax.ppermute(value, axis, [(j, j ^ step) for j in range(size)])  25.4 us
    ppermute x4, starting transfers between devices, neighbours(): return (lax.ppermute(last, 'band', up), lax.ppermute(first, 'band', down))  9.4 us
    pallas_call x1, Pallas kernels, forward(): pl.pallas_call(lambda *refs: forward_kernel(n, bands, halves, *refs), out...  4.19 us
    pallas_call x1, Pallas kernels, backward(): pl.pallas_call(lambda *refs: backward_kernel(n, *refs), out_shape=[out] *...  3.85 us
    transpose x2, other arithmetic, home(): return jnp.transpose(whole, (2, 0, 1))  2.21 us
  transfers between devices with their start and end apart: 24, of which 11 were waited for; matrix products, arithmetic and copies ran while one was open for 3% of the time, Pallas kernels for 4%

profile of v2, /device:TPU:10, one launch (start us, length us, event | category | flops | bytes accessed | tf_op | source)
XLA Modules:
  0.0 104.3 jit_solution(9848497606948276936)
XLA Ops:
  0.6 0.9 constant_dynamic-slice_fusion.8
  1.6 0.7 tile.2
  2.2 2.7 %collective-permute-start.5 = (bf16[1,592,128]{2,1,0:T(8,128)(2,1)S(1)}, bf16[1,592,128]{2,1,0:T(8,128)(2,1)S(1)}, u32[]{:S(2)}, u32[]{:S(2)}) collective-permute-start(bf16[1,592,128]{2,1,0:T(8,128)(2,1)S(1)} %maximum_bitcast_fusion.4), channel_id=1, source_target_pairs={{0,2},{1,3},{2,0},{3,1},{4,6},{5,7},{6,4},{7,5},{8,10},{9,11},{10,... | collective-permute-start | bytes 454664 | tf_op jit(solution)/shard_map/ppermute | solution.py:11
  4.9 1.5 %copy.6 = bf16[128,4,512]{0,2,1:T(8,128)(2,1)S(1)} copy(bf16[128,4,512]{2,1,0:T(4,128)(2,1)} %param.4) | data formatting | bytes 1048576 | tf_op args[0]
  6.4 0.2 pad_dynamic-slice_fusion.8
  6.6 0.5 collective-permute-start
  7.1 0.3 collective-permute-start.1
  7.4 2.7 %collective-permute-start.2 = (bf16[4,130,128]{2,1,0:T(8,128)(2,1)S(1)}, bf16[4,130,128]{2,1,0:T(8,128)(2,1)S(1)}, u32[]{:S(2)}, u32[]{:S(2)}) collective-permute-start(bf16[4,130,128]{2,1,0:T(8,128)(2,1)S(1)} %get-tuple-element.36), channel_id=1, source_target_pairs={{0,3},{1,2},{2,1},{3,0},{4,7},{5,6},{6,5},{7,4},{8,11},{9,10},{10,... | collective-permute-start | bytes 399368 | tf_op jit(solution)/shard_map/ppermute | solution.py:11
  10.1 0.4 copy.11
  10.5 0.2 pad_dynamic-slice_fusion.2
  10.7 1.4 %collective-permute-start.16 = (bf16[4,130,128]{2,1,0:T(8,128)(2,1)S(1)}, bf16[4,130,128]{2,1,0:T(8,128)(2,1)S(1)}, u32[]{:S(2)}, u32[]{:S(2)}) collective-permute-start(bf16[4,130,128]{2,1,0:T(8,128)(2,1)S(1)} %get-tuple-element.27), channel_id=1, source_target_pairs={{0,1},{1,0},{2,3},{3,2},{4,5},{5,4},{6,7},{7,6},{8,9},{9,8},{10,11... | collective-permute-start | bytes 399368 | tf_op jit(solution)/shard_map/ppermute | solution.py:11
  12.1 0.1 pad_add_fusion.refs_0_
  12.3 1.6 %collective-permute-done.refs_2_ = bf16[4,130,128]{2,1,0:T(8,128)(2,1)S(1)} collective-permute-done((bf16[4,130,128]{2,1,0:T(8,128)(2,1)S(1)}, bf16[4,130,128]{2,1,0:T(8,128)(2,1)S(1)}, u32[]{:S(2)}, u32[]{:S(2)}) %collective-permute-start) | collective-permute-done | bytes 133152 | tf_op jit(solution)/shard_map/ppermute | solution.py:11
  13.8 1.6 %collective-permute-start.17 = (bf16[4,130,128]{2,1,0:T(8,128)(2,1)S(1)}, bf16[4,130,128]{2,1,0:T(8,128)(2,1)S(1)}, u32[]{:S(2)}, u32[]{:S(2)}) collective-permute-start(bf16[4,130,128]{2,1,0:T(8,128)(2,1)S(1)} %get-tuple-element.28), channel_id=1, source_target_pairs={{0,2},{1,3},{2,0},{3,1},{4,6},{5,7},{6,4},{7,5},{8,10},{9,11},{10,... | collective-permute-start | bytes 399368 | tf_op jit(solution)/shard_map/ppermute | solution.py:11
  15.4 6.1 %collective-permute-done.1.refs_3_ = bf16[4,130,128]{2,1,0:T(8,128)(2,1)S(1)} collective-permute-done((bf16[4,130,128]{2,1,0:T(8,128)(2,1)S(1)}, bf16[4,130,128]{2,1,0:T(8,128)(2,1)S(1)}, u32[]{:S(2)}, u32[]{:S(2)}) %collective-permute-start.1) | collective-permute-done | bytes 133152 | tf_op jit(solution)/shard_map/ppermute | solution.py:11
  21.5 0.1 collective-permute-start.18
  21.6 5.5 %collective-permute-done.2.refs_4_ = bf16[4,130,128]{2,1,0:T(8,128)(2,1)S(1)} collective-permute-done((bf16[4,130,128]{2,1,0:T(8,128)(2,1)S(1)}, bf16[4,130,128]{2,1,0:T(8,128)(2,1)S(1)}, u32[]{:S(2)}, u32[]{:S(2)}) %collective-permute-start.2) | collective-permute-done | bytes 133152 | tf_op jit(solution)/shard_map/ppermute | solution.py:11
  27.2 1.1 %collective-permute-start.6 = (bf16[2,592,128]{2,1,0:T(8,128)(2,1)S(1)}, bf16[2,592,128]{2,1,0:T(8,128)(2,1)S(1)}, u32[]{:S(2)}, u32[]{:S(2)}) collective-permute-start(bf16[2,592,128]{2,1,0:T(8,128)(2,1)S(1)} %pad_maximum_fusion.6), channel_id=1, source_target_pairs={{0,1},{1,0},{2,3},{3,2},{4,5},{5,4},{6,7},{7,6},{8,9},{9,8},{10,11... | collective-permute-start | bytes 909320 | tf_op jit(solution)/shard_map/ppermute | solution.py:11
  28.4 1.9 %collective-permute-start.4 = (bf16[1,130,512]{2,1,0:T(8,128)(2,1)S(1)}, bf16[1,130,512]{2,1,0:T(8,128)(2,1)S(1)}, u32[]{:S(2)}, u32[]{:S(2)}) collective-permute-start(bf16[1,130,512]{2,1,0:T(8,128)(2,1)S(1)} %pad_maximum_fusion.8), channel_id=1, source_target_pairs={{4,0},{8,4},{12,8},{16,12},{20,16},{24,20},{28,24},{5,1},{9,5},{13... | collective-permute-start | bytes 399368 | tf_op jit(solution)/shard_map/ppermute | solution.py:18
  30.3 7.9 %collective-permute-done.6 = bf16[2,592,128]{2,1,0:T(8,128)(2,1)S(1)} collective-permute-done((bf16[2,592,128]{2,1,0:T(8,128)(2,1)S(1)}, bf16[2,592,128]{2,1,0:T(8,128)(2,1)S(1)}, u32[]{:S(2)}, u32[]{:S(2)}) %collective-permute-start.6) | collective-permute-done | bytes 303136 | tf_op jit(solution)/shard_map/ppermute | solution.py:11
  38.3 0.6 collective-permute-start.10
  38.9 1.6 %collective-permute-start.7 = (bf16[1,3,288,128]{3,2,1,0:T(8,128)(2,1)S(1)}, bf16[1,3,288,128]{3,2,1,0:T(8,128)(2,1)S(1)}, u32[]{:S(2)}, u32[]{:S(2)}) collective-permute-start(bf16[1,3,288,128]{3,2,1,0:T(8,128)(2,1)S(1)} %maximum_bitcast_fusion.2), channel_id=1, source_target_pairs={{0,16},{4,20},{8,24},{12,28},{16,0},{20,4},{24,8},{28,12},{1,17},{... | collective-permute-start | bytes 663560 | tf_op jit(solution)/shard_map/ppermute | solution.py:11
  40.5 4.5 %collective-permute-done.10 = bf16[1,3,288,128]{3,2,1,0:T(8,128)(2,1)S(1)} collective-permute-done((bf16[1,3,288,128]{3,2,1,0:T(8,128)(2,1)S(1)}, bf16[1,3,288,128]{3,2,1,0:T(8,128)(2,1)S(1)}, u32[]{:S(2)}, u32[]{:S(2)}) %collective-permute-start.10) | collective-permute-done | bytes 221216 | tf_op jit(solution)/shard_map/ppermute | solution.py:11
  45.1 1.6 %collective-permute-start.11 = (bf16[2,3,288,128]{3,2,1,0:T(8,128)(2,1)S(1)}, bf16[2,3,288,128]{3,2,1,0:T(8,128)(2,1)S(1)}, u32[]{:S(2)}, u32[]{:S(2)}) collective-permute-start(bf16[2,3,288,128]{3,2,1,0:T(8,128)(2,1)S(1)} %pad_maximum_fusion.5), channel_id=1, source_target_pairs={{0,16},{4,20},{8,24},{12,28},{16,0},{20,4},{24,8},{28,12},{1,17},{... | collective-permute-start | bytes 1327112 | tf_op jit(solution)/shard_map/ppermute | solution.py:11
  46.6 0.0 collective-permute-done.7
  46.7 0.6 collective-permute-start.8
  47.3 0.0 collective-permute-done.17.refs_3_
  47.3 1.9 %collective-permute-start.3 = (bf16[1,130,512]{2,1,0:T(8,128)(2,1)S(1)}, bf16[1,130,512]{2,1,0:T(8,128)(2,1)S(1)}, u32[]{:S(2)}, u32[]{:S(2)}) collective-permute-start(bf16[1,130,512]{2,1,0:T(8,128)(2,1)S(1)} %pad_maximum_fusion.7), channel_id=1, source_target_pairs={{0,4},{4,8},{8,12},{12,16},{16,20},{20,24},{24,28},{1,5},{5,9},{9,... | collective-permute-start | bytes 399368 | tf_op jit(solution)/shard_map/ppermute | solution.py:18
  49.3 6.3 %collective-permute-done.11 = bf16[2,3,288,128]{3,2,1,0:T(8,128)(2,1)S(1)} collective-permute-done((bf16[2,3,288,128]{3,2,1,0:T(8,128)(2,1)S(1)}, bf16[2,3,288,128]{3,2,1,0:T(8,128)(2,1)S(1)}, u32[]{:S(2)}, u32[]{:S(2)}) %collective-permute-start.11) | collective-permute-done | bytes 442400 | tf_op jit(solution)/shard_map/ppermute | solution.py:11
  55.6 0.1 pad_maximum_fusion.1.refs_11_
  55.7 0.0 copy-start.2
  55.7 0.0 copy-start
  55.7 0.1 collective-permute-start.12
  55.8 2.7 %collective-permute-done.8 = bf16[2,3,288,128]{3,2,1,0:T(8,128)(2,1)S(1)} collective-permute-done((bf16[2,3,288,128]{3,2,1,0:T(8,128)(2,1)S(1)}, bf16[2,3,288,128]{3,2,1,0:T(8,128)(2,1)S(1)}, u32[]{:S(2)}, u32[]{:S(2)}) %collective-permute-start.8) | collective-permute-done | bytes 442400 | tf_op jit(solution)/shard_map/ppermute | solution.py:11
  58.5 0.1 pad_maximum_fusion.refs_9_
  58.6 0.1 collective-permute-start.9
  58.6 0.0 collective-permute-done.18.refs_4_
  58.7 2.4 %collective-permute-start.19 = (bf16[1,130,512]{2,1,0:T(8,128)(2,1)S(1)}, bf16[1,130,512]{2,1,0:T(8,128)(2,1)S(1)}, u32[]{:S(2)}, u32[]{:S(2)}) collective-permute-start(bf16[1,130,512]{2,1,0:T(8,128)(2,1)S(1)} %pad_maximum_fusion.9), channel_id=1, source_target_pairs={{0,4},{4,8},{8,12},{12,16},{16,20},{20,24},{24,28},{1,5},{5,9},{9,... | collective-permute-start | bytes 399368 | tf_op jit(solution)/shard_map/ppermute | solution.py:18
  61.2 3.2 %collective-permute-start.20 = (bf16[1,130,512]{2,1,0:T(8,128)(2,1)S(1)}, bf16[1,130,512]{2,1,0:T(8,128)(2,1)S(1)}, u32[]{:S(2)}, u32[]{:S(2)}) collective-permute-start(bf16[1,130,512]{2,1,0:T(8,128)(2,1)S(1)} %pad_maximum_fusion.10), channel_id=1, source_target_pairs={{4,0},{8,4},{12,8},{16,12},{20,16},{24,20},{28,24},{5,1},{9,5},{13... | collective-permute-start | bytes 399368 | tf_op jit(solution)/shard_map/ppermute | solution.py:18
  64.4 0.0 collective-permute-done.3.refs_5_
  64.4 4.2 %forward.1 = (bf16[512,128]{1,0:T(8,128)(2,1)S(1)}, bf16[512,128]{1,0:T(8,128)(2,1)S(1)}, bf16[512,128]{1,0:T(8,128)(2,1)S(1)}, bf16[512,128]{1,0:T(8,128)(2,1)S(1)}, bf16[4608,512]{1,0:T(8,128)(2,1)S(1)}) custom-call(s32[2]{0:T(128)S(1)} %pad_add_fusion.refs_0_, bf16[4,130,128]{2,1,0:T(8,128)(2,1)S(1)} %get-tuple-element.39.refs_1_, ...), custom_call_target="tpu_custom_call" | custom-call | flops 2415919104 | bytes 10485760 | tf_op jit(solution)/shard_map/forward/pallas_call | solution.py:200
  68.6 3.8 %backward.1 = (bf16[512,128]{1,0:T(8,128)(2,1)S(1)}, bf16[512,128]{1,0:T(8,128)(2,1)S(1)}, bf16[512,128]{1,0:T(8,128)(2,1)S(1)}, bf16[512,128]{1,0:T(8,128)(2,1)S(1)}) custom-call(s32[2]{0:T(128)S(1)} %pad_add_fusion.refs_0_, bf16[4,130,128]{2,1,0:T(8,128)(2,1)S(1)} %get-tuple-element.29.refs_1_, bf16[4,130,128]{2,1,0:T(8,128)(2,1)S(1)} %collective-permute-done.16.refs_2_, ...), custom_call_target="tpu_custom_call" | custom-call | flops 2415919104 | bytes 6291456 | tf_op jit(solution)/shard_map/backward/pallas_call | solution.py:226
  72.5 3.3 %collective-permute-start.21 = (bf16[512,128]{1,0:T(8,128)(2,1)S(1)}, bf16[512,128]{1,0:T(8,128)(2,1)S(1)}, u32[]{:S(2)}, u32[]{:S(2)}) collective-permute-start(bf16[512,128]{1,0:T(8,128)(2,1)S(1)} %get-tuple-element.17), channel_id=1, source_target_pairs={{0,1},{1,0},{2,3},{3,2},{4,5},{5,4},{6,7},{7,6},{8,9},{9,8},{10,11... | collective-permute-start | bytes 393224 | tf_op jit(solution)/shard_map/ppermute | solution.py:11
  75.8 2.2 %collective-permute-start.22 = (bf16[512,128]{1,0:T(8,128)(2,1)S(1)}, bf16[512,128]{1,0:T(8,128)(2,1)S(1)}, u32[]{:S(2)}, u32[]{:S(2)}) collective-permute-start(bf16[512,128]{1,0:T(8,128)(2,1)S(1)} %get-tuple-element.18), channel_id=1, source_target_pairs={{0,2},{1,3},{2,0},{3,1},{4,6},{5,7},{6,4},{7,5},{8,10},{9,11},{10,... | collective-permute-start | bytes 393224 | tf_op jit(solution)/shard_map/ppermute | solution.py:11
  78.0 0.5 collective-permute-start.23
  78.5 1.7 %collective-permute-start.13 = (bf16[512,128]{1,0:T(8,128)(2,1)S(1)}, bf16[512,128]{1,0:T(8,128)(2,1)S(1)}, u32[]{:S(2)}, u32[]{:S(2)}) collective-permute-start(bf16[512,128]{1,0:T(8,128)(2,1)S(1)} %get-tuple-element.12), channel_id=1, source_target_pairs={{0,1},{1,0},{2,3},{3,2},{4,5},{5,4},{6,7},{7,6},{8,9},{9,8},{10,11... | collective-permute-start | bytes 393224 | tf_op jit(solution)/shard_map/ppermute | solution.py:11
  80.1 2.1 %collective-permute-start.14 = (bf16[512,128]{1,0:T(8,128)(2,1)S(1)}, bf16[512,128]{1,0:T(8,128)(2,1)S(1)}, u32[]{:S(2)}, u32[]{:S(2)}) collective-permute-start(bf16[512,128]{1,0:T(8,128)(2,1)S(1)} %get-tuple-element.13), channel_id=1, source_target_pairs={{0,2},{1,3},{2,0},{3,1},{4,6},{5,7},{6,4},{7,5},{8,10},{9,11},{10,... | collective-permute-start | bytes 393224 | tf_op jit(solution)/shard_map/ppermute | solution.py:11
  82.3 0.7 collective-permute-start.15
  83.0 5.4 %collective-permute-done.22 = bf16[512,128]{1,0:T(8,128)(2,1)S(1)} collective-permute-done((bf16[512,128]{1,0:T(8,128)(2,1)S(1)}, bf16[512,128]{1,0:T(8,128)(2,1)S(1)}, u32[]{:S(2)}, u32[]{:S(2)}) %collective-permute-start.22) | collective-permute-done | bytes 131104 | tf_op jit(solution)/shard_map/ppermute | solution.py:11
  88.4 8.5 %collective-permute-done.23 = bf16[512,128]{1,0:T(8,128)(2,1)S(1)} collective-permute-done((bf16[512,128]{1,0:T(8,128)(2,1)S(1)}, bf16[512,128]{1,0:T(8,128)(2,1)S(1)}, u32[]{:S(2)}, u32[]{:S(2)}) %collective-permute-start.23) | collective-permute-done | bytes 131104 | tf_op jit(solution)/shard_map/ppermute | solution.py:11
  96.9 0.1 pad_maximum_fusion.3
  97.0 0.1 copy.12
  97.2 0.1 copy.13
  97.3 0.1 copy.14
  97.5 0.1 copy.15
  97.6 1.1 %collective-permute-done.14 = bf16[512,128]{1,0:T(8,128)(2,1)S(1)} collective-permute-done((bf16[512,128]{1,0:T(8,128)(2,1)S(1)}, bf16[512,128]{1,0:T(8,128)(2,1)S(1)}, u32[]{:S(2)}, u32[]{:S(2)}) %collective-permute-start.14) | collective-permute-done | bytes 131104 | tf_op jit(solution)/shard_map/ppermute | solution.py:11
  98.7 2.7 %collective-permute-done.15 = bf16[512,128]{1,0:T(8,128)(2,1)S(1)} collective-permute-done((bf16[512,128]{1,0:T(8,128)(2,1)S(1)}, bf16[512,128]{1,0:T(8,128)(2,1)S(1)}, u32[]{:S(2)}, u32[]{:S(2)}) %collective-permute-start.15) | collective-permute-done | bytes 131104 | tf_op jit(solution)/shard_map/ppermute | solution.py:11
  101.4 0.1 pad_maximum_fusion.2
  101.5 0.1 copy.7
  101.7 0.1 copy.8
  101.8 0.1 copy.9
  102.0 0.1 copy.10
  102.1 1.1 %maximum_bitcast_fusion.1 = bf16[128,4,512]{2,1,0:T(4,128)(2,1)} fusion(bf16[4,128,128]{1,0,2:T(4,128)(2,1)S(1)} %bitcast.48, bf16[4,128,128]{1,0,2:T(4,128)(2,1)S(1)} %bitcast.47, bf16[4,128,128]{1,0,2:T(4,128)(2,1)S(1)} %bitcast.46, bf16[4,128,128]{1,0,2:T(4,128)(2,1)S(1)} %bitcast.45), kind=kLoop, calls=%fused_computation.5 | loop fusion | flops 2097152 | bytes 1048576 | tf_op jit(solution)/shard_map/transpose | solution.py:267
  103.2 1.1 %maximum_bitcast_fusion = bf16[128,4,512]{2,1,0:T(4,128)(2,1)} fusion(bf16[4,128,128]{1,0,2:T(4,128)(2,1)S(1)} %bitcast.52, bf16[4,128,128]{1,0,2:T(4,128)(2,1)S(1)} %bitcast.51, bf16[4,128,128]{1,0,2:T(4,128)(2,1)S(1)} %bitcast.50, bf16[4,128,128]{1,0,2:T(4,128)(2,1)S(1)} %bitcast.49), kind=kLoop, calls=%fused_computation.3 | loop fusion | flops 2097152 | bytes 1048576 | tf_op jit(solution)/shard_map/transpose | solution.py:267
  (37 shorter events, 0.5 us)
Async XLA Ops:
  2.2 7.9 %copy-start.1 = (bf16[128,4,512]{2,1,0:T(4,128)(2,1)S(1)}, bf16[128,4,512]{2,1,0:T(4,128)(2,1)}, u32[]{:S(2)}) copy-start(bf16[128,4,512]{2,1,0:T(4,128)(2,1)} %param.7) | copy-start | bytes 1572868
  2.2 24.9 %collective-permute-start.5 = (bf16[1,592,128]{2,1,0:T(8,128)(2,1)S(1)}, bf16[1,592,128]{2,1,0:T(8,128)(2,1)S(1)}, u32[]{:S(2)}, u32[]{:S(2)}) collective-permute-start(bf16[1,592,128]{2,1,0:T(8,128)(2,1)S(1)} %maximum_bitcast_fusion.4), channel_id=1, source_target_pairs={{0,2},{1,3},{2,0},{3,1},{4,6},{5,7},{6,4},{7,5},{8,10},{9,11},{10,... | collective-permute-start | bytes 454664 | tf_op jit(solution)/shard_map/ppermute | solution.py:11
  6.6 7.3 %collective-permute-start = (bf16[4,130,128]{2,1,0:T(8,128)(2,1)S(1)}, bf16[4,130,128]{2,1,0:T(8,128)(2,1)S(1)}, u32[]{:S(2)}, u32[]{:S(2)}) collective-permute-start(bf16[4,130,128]{2,1,0:T(8,128)(2,1)S(1)} %get-tuple-element.37), channel_id=1, source_target_pairs={{0,1},{1,0},{2,3},{3,2},{4,5},{5,4},{6,7},{7,6},{8,9},{9,8},{10,11... | collective-permute-start | bytes 399368 | tf_op jit(solution)/shard_map/ppermute | solution.py:11
  7.1 14.4 %collective-permute-start.1 = (bf16[4,130,128]{2,1,0:T(8,128)(2,1)S(1)}, bf16[4,130,128]{2,1,0:T(8,128)(2,1)S(1)}, u32[]{:S(2)}, u32[]{:S(2)}) collective-permute-start(bf16[4,130,128]{2,1,0:T(8,128)(2,1)S(1)} %get-tuple-element.38), channel_id=1, source_target_pairs={{0,2},{1,3},{2,0},{3,1},{4,6},{5,7},{6,4},{7,5},{8,10},{9,11},{10,... | collective-permute-start | bytes 399368 | tf_op jit(solution)/shard_map/ppermute | solution.py:11
  7.4 19.7 %collective-permute-start.2 = (bf16[4,130,128]{2,1,0:T(8,128)(2,1)S(1)}, bf16[4,130,128]{2,1,0:T(8,128)(2,1)S(1)}, u32[]{:S(2)}, u32[]{:S(2)}) collective-permute-start(bf16[4,130,128]{2,1,0:T(8,128)(2,1)S(1)} %get-tuple-element.36), channel_id=1, source_target_pairs={{0,3},{1,2},{2,1},{3,0},{4,7},{5,6},{6,5},{7,4},{8,11},{9,10},{10,... | collective-permute-start | bytes 399368 | tf_op jit(solution)/shard_map/ppermute | solution.py:11
  10.7 28.2 %collective-permute-start.16 = (bf16[4,130,128]{2,1,0:T(8,128)(2,1)S(1)}, bf16[4,130,128]{2,1,0:T(8,128)(2,1)S(1)}, u32[]{:S(2)}, u32[]{:S(2)}) collective-permute-start(bf16[4,130,128]{2,1,0:T(8,128)(2,1)S(1)} %get-tuple-element.27), channel_id=1, source_target_pairs={{0,1},{1,0},{2,3},{3,2},{4,5},{5,4},{6,7},{7,6},{8,9},{9,8},{10,11... | collective-permute-start | bytes 399368 | tf_op jit(solution)/shard_map/ppermute | solution.py:11
  13.8 33.5 %collective-permute-start.17 = (bf16[4,130,128]{2,1,0:T(8,128)(2,1)S(1)}, bf16[4,130,128]{2,1,0:T(8,128)(2,1)S(1)}, u32[]{:S(2)}, u32[]{:S(2)}) collective-permute-start(bf16[4,130,128]{2,1,0:T(8,128)(2,1)S(1)} %get-tuple-element.28), channel_id=1, source_target_pairs={{0,2},{1,3},{2,0},{3,1},{4,6},{5,7},{6,4},{7,5},{8,10},{9,11},{10,... | collective-permute-start | bytes 399368 | tf_op jit(solution)/shard_map/ppermute | solution.py:11
  21.5 37.1 %collective-permute-start.18 = (bf16[4,130,128]{2,1,0:T(8,128)(2,1)S(1)}, bf16[4,130,128]{2,1,0:T(8,128)(2,1)S(1)}, u32[]{:S(2)}, u32[]{:S(2)}) collective-permute-start(bf16[4,130,128]{2,1,0:T(8,128)(2,1)S(1)} %get-tuple-element.26), channel_id=1, source_target_pairs={{0,3},{1,2},{2,1},{3,0},{4,7},{5,6},{6,5},{7,4},{8,11},{9,10},{10,... | collective-permute-start | bytes 399368 | tf_op jit(solution)/shard_map/ppermute | solution.py:11
  27.2 11.0 %collective-permute-start.6 = (bf16[2,592,128]{2,1,0:T(8,128)(2,1)S(1)}, bf16[2,592,128]{2,1,0:T(8,128)(2,1)S(1)}, u32[]{:S(2)}, u32[]{:S(2)}) collective-permute-start(bf16[2,592,128]{2,1,0:T(8,128)(2,1)S(1)} %pad_maximum_fusion.6), channel_id=1, source_target_pairs={{0,1},{1,0},{2,3},{3,2},{4,5},{5,4},{6,7},{7,6},{8,9},{9,8},{10,11... | collective-permute-start | bytes 909320 | tf_op jit(solution)/shard_map/ppermute | solution.py:11
  28.4 32.8 %collective-permute-start.4 = (bf16[1,130,512]{2,1,0:T(8,128)(2,1)S(1)}, bf16[1,130,512]{2,1,0:T(8,128)(2,1)S(1)}, u32[]{:S(2)}, u32[]{:S(2)}) collective-permute-start(bf16[1,130,512]{2,1,0:T(8,128)(2,1)S(1)} %pad_maximum_fusion.8), channel_id=1, source_target_pairs={{4,0},{8,4},{12,8},{16,12},{20,16},{24,20},{28,24},{5,1},{9,5},{13... | collective-permute-start | bytes 399368 | tf_op jit(solution)/shard_map/ppermute | solution.py:18
  38.3 6.7 %collective-permute-start.10 = (bf16[1,3,288,128]{3,2,1,0:T(8,128)(2,1)S(1)}, bf16[1,3,288,128]{3,2,1,0:T(8,128)(2,1)S(1)}, u32[]{:S(2)}, u32[]{:S(2)}) collective-permute-start(bf16[1,3,288,128]{3,2,1,0:T(8,128)(2,1)S(1)} %maximum_bitcast_fusion.3), channel_id=1, source_target_pairs={{0,8},{4,12},{8,0},{12,4},{16,24},{20,28},{24,16},{28,20},{1,9},{5... | collective-permute-start | bytes 663560 | tf_op jit(solution)/shard_map/ppermute | solution.py:11
  38.9 7.7 %collective-permute-start.7 = (bf16[1,3,288,128]{3,2,1,0:T(8,128)(2,1)S(1)}, bf16[1,3,288,128]{3,2,1,0:T(8,128)(2,1)S(1)}, u32[]{:S(2)}, u32[]{:S(2)}) collective-permute-start(bf16[1,3,288,128]{3,2,1,0:T(8,128)(2,1)S(1)} %maximum_bitcast_fusion.2), channel_id=1, source_target_pairs={{0,16},{4,20},{8,24},{12,28},{16,0},{20,4},{24,8},{28,12},{1,17},{... | collective-permute-start | bytes 663560 | tf_op jit(solution)/shard_map/ppermute | solution.py:11
  45.1 10.6 %collective-permute-start.11 = (bf16[2,3,288,128]{3,2,1,0:T(8,128)(2,1)S(1)}, bf16[2,3,288,128]{3,2,1,0:T(8,128)(2,1)S(1)}, u32[]{:S(2)}, u32[]{:S(2)}) collective-permute-start(bf16[2,3,288,128]{3,2,1,0:T(8,128)(2,1)S(1)} %pad_maximum_fusion.5), channel_id=1, source_target_pairs={{0,16},{4,20},{8,24},{12,28},{16,0},{20,4},{24,8},{28,12},{1,17},{... | collective-permute-start | bytes 1327112 | tf_op jit(solution)/shard_map/ppermute | solution.py:11
  46.7 11.8 %collective-permute-start.8 = (bf16[2,3,288,128]{3,2,1,0:T(8,128)(2,1)S(1)}, bf16[2,3,288,128]{3,2,1,0:T(8,128)(2,1)S(1)}, u32[]{:S(2)}, u32[]{:S(2)}) collective-permute-start(bf16[2,3,288,128]{3,2,1,0:T(8,128)(2,1)S(1)} %pad_maximum_fusion.4), channel_id=1, source_target_pairs={{0,8},{4,12},{8,0},{12,4},{16,24},{20,28},{24,16},{28,20},{1,9},{5... | collective-permute-start | bytes 1327112 | tf_op jit(solution)/shard_map/ppermute | solution.py:11
  47.3 17.0 %collective-permute-start.3 = (bf16[1,130,512]{2,1,0:T(8,128)(2,1)S(1)}, bf16[1,130,512]{2,1,0:T(8,128)(2,1)S(1)}, u32[]{:S(2)}, u32[]{:S(2)}) collective-permute-start(bf16[1,130,512]{2,1,0:T(8,128)(2,1)S(1)} %pad_maximum_fusion.7), channel_id=1, source_target_pairs={{0,4},{4,8},{8,12},{12,16},{16,20},{20,24},{24,28},{1,5},{5,9},{9,... | collective-permute-start | bytes 399368 | tf_op jit(solution)/shard_map/ppermute | solution.py:18
  55.7 5.4 %copy-start.2 = (bf16[128]{0:T(256)(128)(2,1)S(1)}, bf16[128]{0:T(256)(128)(2,1)}, u32[]{:S(2)}) copy-start(bf16[128]{0:T(256)(128)(2,1)} %param.6) | copy-start | bytes 772
  55.7 8.7 %copy-start = (bf16[9,512,128]{2,1,0:T(8,128)(2,1)S(1)}, bf16[9,512,128]{2,1,0:T(8,128)(2,1)}, u32[]{:S(2)}) copy-start(bf16[9,512,128]{2,1,0:T(8,128)(2,1)} %refs_7_.1) | copy-start | bytes 3538948
  55.7 8.6 %collective-permute-start.12 = (bf16[4,3,288,128]{3,2,1,0:T(8,128)(2,1)S(1)}, bf16[4,3,288,128]{3,2,1,0:T(8,128)(2,1)S(1)}, u32[]{:S(2)}, u32[]{:S(2)}) collective-permute-start(bf16[4,3,288,128]{3,2,1,0:T(8,128)(2,1)S(1)} %pad_maximum_fusion.1.refs_11_), channel_id=1, source_target_pairs={{0,4},{4,0},{8,12},{12,8},{16,20},{20,16},{24,28},{28,24},{1,5},{5... | collective-permute-start | bytes 2654216 | tf_op jit(solution)/shard_map/ppermute | solution.py:11
  58.6 5.8 %collective-permute-start.9 = (bf16[4,3,288,128]{3,2,1,0:T(8,128)(2,1)S(1)}, bf16[4,3,288,128]{3,2,1,0:T(8,128)(2,1)S(1)}, u32[]{:S(2)}, u32[]{:S(2)}) collective-permute-start(bf16[4,3,288,128]{3,2,1,0:T(8,128)(2,1)S(1)} %pad_maximum_fusion.refs_9_), channel_id=1, source_target_pairs={{0,4},{4,0},{8,12},{12,8},{16,20},{20,16},{24,28},{28,24},{1,5},{5... | collective-permute-start | bytes 2654216 | tf_op jit(solution)/shard_map/ppermute | solution.py:11
  58.7 9.9 %collective-permute-start.19 = (bf16[1,130,512]{2,1,0:T(8,128)(2,1)S(1)}, bf16[1,130,512]{2,1,0:T(8,128)(2,1)S(1)}, u32[]{:S(2)}, u32[]{:S(2)}) collective-permute-start(bf16[1,130,512]{2,1,0:T(8,128)(2,1)S(1)} %pad_maximum_fusion.9), channel_id=1, source_target_pairs={{0,4},{4,8},{8,12},{12,16},{16,20},{20,24},{24,28},{1,5},{5,9},{9,... | collective-permute-start | bytes 399368 | tf_op jit(solution)/shard_map/ppermute | solution.py:18
  61.2 7.4 %collective-permute-start.20 = (bf16[1,130,512]{2,1,0:T(8,128)(2,1)S(1)}, bf16[1,130,512]{2,1,0:T(8,128)(2,1)S(1)}, u32[]{:S(2)}, u32[]{:S(2)}) collective-permute-start(bf16[1,130,512]{2,1,0:T(8,128)(2,1)S(1)} %pad_maximum_fusion.10), channel_id=1, source_target_pairs={{4,0},{8,4},{12,8},{16,12},{20,16},{24,20},{28,24},{5,1},{9,5},{13... | collective-permute-start | bytes 399368 | tf_op jit(solution)/shard_map/ppermute | solution.py:18
  72.5 9.8 %collective-permute-start.21 = (bf16[512,128]{1,0:T(8,128)(2,1)S(1)}, bf16[512,128]{1,0:T(8,128)(2,1)S(1)}, u32[]{:S(2)}, u32[]{:S(2)}) collective-permute-start(bf16[512,128]{1,0:T(8,128)(2,1)S(1)} %get-tuple-element.17), channel_id=1, source_target_pairs={{0,1},{1,0},{2,3},{3,2},{4,5},{5,4},{6,7},{7,6},{8,9},{9,8},{10,11... | collective-permute-start | bytes 393224 | tf_op jit(solution)/shard_map/ppermute | solution.py:11
  75.8 12.6 %collective-permute-start.22 = (bf16[512,128]{1,0:T(8,128)(2,1)S(1)}, bf16[512,128]{1,0:T(8,128)(2,1)S(1)}, u32[]{:S(2)}, u32[]{:S(2)}) collective-permute-start(bf16[512,128]{1,0:T(8,128)(2,1)S(1)} %get-tuple-element.18), channel_id=1, source_target_pairs={{0,2},{1,3},{2,0},{3,1},{4,6},{5,7},{6,4},{7,5},{8,10},{9,11},{10,... | collective-permute-start | bytes 393224 | tf_op jit(solution)/shard_map/ppermute | solution.py:11
  78.0 18.9 %collective-permute-start.23 = (bf16[512,128]{1,0:T(8,128)(2,1)S(1)}, bf16[512,128]{1,0:T(8,128)(2,1)S(1)}, u32[]{:S(2)}, u32[]{:S(2)}) collective-permute-start(bf16[512,128]{1,0:T(8,128)(2,1)S(1)} %get-tuple-element.19), channel_id=1, source_target_pairs={{0,3},{1,2},{2,1},{3,0},{4,7},{5,6},{6,5},{7,4},{8,11},{9,10},{10,... | collective-permute-start | bytes 393224 | tf_op jit(solution)/shard_map/ppermute | solution.py:11
  78.5 19.2 %collective-permute-start.13 = (bf16[512,128]{1,0:T(8,128)(2,1)S(1)}, bf16[512,128]{1,0:T(8,128)(2,1)S(1)}, u32[]{:S(2)}, u32[]{:S(2)}) collective-permute-start(bf16[512,128]{1,0:T(8,128)(2,1)S(1)} %get-tuple-element.12), channel_id=1, source_target_pairs={{0,1},{1,0},{2,3},{3,2},{4,5},{5,4},{6,7},{7,6},{8,9},{9,8},{10,11... | collective-permute-start | bytes 393224 | tf_op jit(solution)/shard_map/ppermute | solution.py:11
  80.1 18.6 %collective-permute-start.14 = (bf16[512,128]{1,0:T(8,128)(2,1)S(1)}, bf16[512,128]{1,0:T(8,128)(2,1)S(1)}, u32[]{:S(2)}, u32[]{:S(2)}) collective-permute-start(bf16[512,128]{1,0:T(8,128)(2,1)S(1)} %get-tuple-element.13), channel_id=1, source_target_pairs={{0,2},{1,3},{2,0},{3,1},{4,6},{5,7},{6,4},{7,5},{8,10},{9,11},{10,... | collective-permute-start | bytes 393224 | tf_op jit(solution)/shard_map/ppermute | solution.py:11
  82.3 19.1 %collective-permute-start.15 = (bf16[512,128]{1,0:T(8,128)(2,1)S(1)}, bf16[512,128]{1,0:T(8,128)(2,1)S(1)}, u32[]{:S(2)}, u32[]{:S(2)}) collective-permute-start(bf16[512,128]{1,0:T(8,128)(2,1)S(1)} %get-tuple-element.14), channel_id=1, source_target_pairs={{0,3},{1,2},{2,1},{3,0},{4,7},{5,6},{6,5},{7,4},{8,11},{9,10},{10,... | collective-permute-start | bytes 393224 | tf_op jit(solution)/shard_map/ppermute | solution.py:11

commit v3 on v2

--- a/solution.py
+++ b/solution.py
@@ -127,13 +127,13 @@
 
 def forward_kernel(n, bands, halves, place, *refs):
     pieces, refs = refs[:n], refs[n:]
-    before, after, filters, bias = refs[:4]
-    shares, refs = refs[4 : 4 + 2 * len(halves)], refs[4 + 2 * len(halves) :]
+    before, after, filters = refs[:3]
+    shares, refs = refs[3 : 3 + 2 * len(halves)], refs[3 + 2 * len(halves) :]
     outs, (weights, source, total) = refs[:n], refs[n:]
     me, band = place[0], place[1]
     taps, channels, local = filters.shape
     rows, padded, _ = pieces[0].shape
-    width = padded - 2
+    width = padded - 3
     share = taps * channels // bands
     part = share // len(halves)
     for tap in range(taps):
@@ -159,7 +159,8 @@
     for j in range(n):
         total[j] = acc[:, j * local : (j + 1) * local]
     for k in range(n):
-        value = total[me ^ k] + bias[k : k + 1, :].astype(jnp.float32)
+        bias = pieces[k][0, padded - 1 : padded, :].astype(jnp.float32)
+        value = total[me ^ k] + bias
         outs[k][...] = value.astype(jnp.bfloat16)
 
 
@@ -169,7 +170,7 @@
     outs, (source,) = refs[3 : 3 + n], refs[3 + n :]
     me = place[0]
     rows, padded, local = pieces[0].shape
-    width = padded - 2
+    width = padded - 3
     channels = n * local
     fill_source(source, pieces, before, after, [me ^ k for k in range(n)], local, width)
     acc = None
@@ -190,12 +191,12 @@
 PARAMS = pltpu.CompilerParams(vmem_limit_bytes=40 * 2**20)
 
 
-def forward(place, pieces, before, after, filters, bias, shares, halves, bands):
+def forward(place, pieces, before, after, filters, shares, halves, bands):
     n = len(pieces)
     rows, padded, local = pieces[0].shape
-    width = padded - 2
+    width = padded - 3
     channels = filters.shape[1]
-    args = [*pieces, before, after, filters, bias, *shares]
+    args = [*pieces, before, after, filters, *shares]
     out = jax.ShapeDtypeStruct((rows * width, local), jnp.bfloat16)
     return pl.pallas_call(
         lambda *refs: forward_kernel(n, bands, halves, *refs),
@@ -220,7 +221,7 @@
 def backward(place, pieces, before, after, weights):
     n = len(pieces)
     rows, padded, local = pieces[0].shape
-    width = padded - 2
+    width = padded - 3
     args = [*pieces, before, after, weights]
     out = jax.ShapeDtypeStruct((rows * width, local), jnp.bfloat16)
     return pl.pallas_call(
@@ -239,6 +240,23 @@
     )(place, *args)
 
 
+def cut(value, bias, me, n):
+    width = value.shape[2] // n
+    padded = jnp.pad(jnp.transpose(value, (1, 2, 0)), ((0, 0), (1, 1), (0, 0)))
+    extra = jnp.broadcast_to(bias, (value.shape[1], 1, value.shape[0]))
+    return [
+        jnp.concatenate(
+            [lax.dynamic_slice_in_dim(padded, (me ^ k) * width, width + 2, axis=1), extra], axis=1
+        )
+        for k in range(n)
+    ]
+
+
+def exchange(pieces):
+    far = [swap(pieces[k], "chan", k) for k in range(len(pieces) - 1, 0, -1)]
+    return [pieces[0]] + far[::-1]
+
+
 def xor_gather(value, axis, steps):
     held, order = [value], [0]
     for step in steps:
@@ -280,28 +298,37 @@
     band = lax.axis_index("band")
     place = jnp.stack([me, band]).astype(jnp.int32)
 
-    part = lax.dynamic_slice_in_dim(filters.reshape(-1, local), band * share, share, axis=0)
-    part = jnp.concatenate([part, jnp.tile(bias[None], (16, 1))], axis=0)
-    held, order = xor_gather(part, "chan", halving(n))
-    held = [held[order.index(k)] for k in range(n)]
-    biases = jnp.concatenate([h[share : share + 1] for h in held], axis=0)
+    flat = filters.reshape(-1, local)
+    held = [lax.dynamic_slice_in_dim(flat, band * share, share, axis=0)]
+    x = cut(image, bias, me, n)
+    u = cut(upstream, bias, me, n)
+    order = [0]
+    for step in halving(n):
+        there = swap(jnp.stack(held), "chan", step)
+        there, x = lax.optimization_barrier((there, x))
+        held = held + [there[j] for j in range(len(held))]
+        order = order + [o ^ step for o in order]
+    held = [held[order.index(k)] for k in range(1, n)]
+    held, u = lax.optimization_barrier((held, u))
+    x = exchange(x)
 
     steps = halving(bands)[:-1]
     shares, halves = [], []
     for h, path in enumerate((steps, steps[::-1])):
-        half = jnp.stack([p[h * share // 2 : (h + 1) * share // 2] for p in held[1:]])
+        half = jnp.stack([p[h * share // 2 : (h + 1) * share // 2] for p in held])
         got, order = xor_gather(half, "band", path)
         got = jnp.stack(got)
         shares += [got, swap(got, "band", 1)]
         halves.append(order)
 
-    x = spread(jnp.transpose(image, (1, 2, 0)), me, width)
-    u = spread(jnp.transpose(upstream, (1, 2, 0)), me, width)
-
-    *sent, weights = forward(place, x, *rims(x), filters, biases, shares, halves, bands)
-    features = [swap(p, "chan", k) if k else p for k, p in enumerate(sent)]
+    u[0], x[1] = lax.optimization_barrier((u[0], x[1]))
+    u = exchange(u)
+
+    *sent, weights = forward(place, x, *rims(x), filters, shares, halves, bands)
+    features = exchange(sent)
     sent = backward(place, u, *rims(u), weights)
-    image_grad = [swap(p, "chan", k) if k else p for k, p in enumerate(sent)]
+    sent, features[1] = lax.optimization_barrier((sent, features[1]))
+    image_grad = exchange(sent)
     return home(features, me, rows, width), home(image_grad, me, rows, width)
 
 

time: 105 us -> 96.1 us (0.915)
  the two profiles are of different devices: /device:TPU:10 before, /device:TPU:0 now
where the time goes in v3:
time: 96.1 us; the launch traced here: 94.3 us
  starting transfers between devices  39.5 us (41%)
  waiting for transfers between devices  38.1 us (40%)
  Pallas kernels  7.98 us (8%)
  local copies, waits for them, and re-layouts  4.83 us (5%)
  other arithmetic  2.95 us (3%)
  between operations  1.04 us (1%)
    ppermute x20, waiting for transfers between devices, swap(): return lax.ppermute(value, axis, [(j, j ^ step) for j in range(size)])  38.1 us
    ppermute x20, starting transfers between devices, swap(): return lax.ppermute(value, axis, [(j, j ^ step) for j in range(size)])  32.6 us
    ppermute x4, starting transfers between devices, neighbours(): return (lax.ppermute(last, 'band', up), lax.ppermute(first, 'band', down))  6.91 us
    pallas_call x1, Pallas kernels, forward(): pl.pallas_call(lambda *refs: forward_kernel(n, bands, halves, *refs), out...  4.14 us
    pallas_call x1, Pallas kernels, backward(): pl.pallas_call(lambda *refs: backward_kernel(n, *refs), out_shape=[out] *...  3.84 us
    transpose x2, other arithmetic, home(): return jnp.transpose(whole, (2, 0, 1))  2.21 us
    unnamed x8, local copies, waits for them, and re-layouts  2.12 us
  transfers between devices with their start and end apart: 24, of which 7 were waited for; matrix products, arithmetic and copies ran while one was open for 5% of the time, Pallas kernels for 8%

profile of v3, /device:TPU:0, one launch (start us, length us, event | category | flops | bytes accessed | tf_op | source)
XLA Modules:
  0.0 94.3 jit_solution(1309146006958712630)
XLA Ops:
  0.6 1.0 %dynamic-slice_bitcast_fusion = bf16[1,576,128]{2,1,0:T(8,128)(2,1)S(1)} fusion(bf16[4608,128]{1,0:T(8,128)(2,1)} %bitcast.50, s32[]{:T(128)S(6)} %select_n.36), kind=kLoop, calls=%fused_computation.29 | loop fusion | bytes 294916 | tf_op jit(solution)/shard_map/stack | solution.py:307
  1.6 4.1 %collective-permute-start = (bf16[1,576,128]{2,1,0:T(8,128)(2,1)S(1)}, bf16[1,576,128]{2,1,0:T(8,128)(2,1)S(1)}, u32[]{:S(2)}, u32[]{:S(2)}) collective-permute-start(bf16[1,576,128]{2,1,0:T(8,128)(2,1)S(1)} %dynamic-slice_bitcast_fusion), channel_id=1, source_target_pairs={{0,2},{1,3},{2,0},{3,1},{4,6},{5,7},{6,4},{7,5},{8,10},{9,11},{10,... | collective-permute-start | bytes 442376 | tf_op jit(solution)/shard_map/ppermute | solution.py:11
  5.7 1.5 %copy.7 = bf16[128,4,512]{0,2,1:T(8,128)(2,1)S(1)} copy(bf16[128,4,512]{2,1,0:T(4,128)(2,1)} %param.7) | data formatting | bytes 1048576 | tf_op args[3]
  7.2 0.4 copy.6
  7.6 0.0 copy-start.2
  7.6 0.4 pad_dynamic-slice_fusion
  8.0 0.2 copy-done.2
  8.3 0.1 pad_maximum_fusion.4
  8.4 4.4 %collective-permute-done = bf16[1,576,128]{2,1,0:T(8,128)(2,1)S(1)} collective-permute-done((bf16[1,576,128]{2,1,0:T(8,128)(2,1)S(1)}, bf16[1,576,128]{2,1,0:T(8,128)(2,1)S(1)}, u32[]{:S(2)}, u32[]{:S(2)}) %collective-permute-start) | collective-permute-done | bytes 147488 | tf_op jit(solution)/shard_map/ppermute | solution.py:11
  12.8 0.8 collective-permute-start.1
  13.6 0.1 pad_add_fusion.refs_0_
  13.6 7.4 %collective-permute-done.1 = bf16[2,576,128]{2,1,0:T(8,128)(2,1)S(1)} collective-permute-done((bf16[2,576,128]{2,1,0:T(8,128)(2,1)S(1)}, bf16[2,576,128]{2,1,0:T(8,128)(2,1)S(1)}, u32[]{:S(2)}, u32[]{:S(2)}) %collective-permute-start.1) | collective-permute-done | bytes 294944 | tf_op jit(solution)/shard_map/ppermute | solution.py:11
  21.1 1.5 %collective-permute-start.2 = (bf16[4,131,128]{2,1,0:T(8,128)(2,1)S(1)}, bf16[4,131,128]{2,1,0:T(8,128)(2,1)S(1)}, u32[]{:S(2)}, u32[]{:S(2)}) collective-permute-start(bf16[4,131,128]{2,1,0:T(8,128)(2,1)S(1)} %get-tuple-element.43), channel_id=1, source_target_pairs={{0,1},{1,0},{2,3},{3,2},{4,5},{5,4},{6,7},{7,6},{8,9},{9,8},{10,11... | collective-permute-start | bytes 402440 | tf_op jit(solution)/shard_map/ppermute | solution.py:11
  22.6 3.4 %collective-permute-start.3 = (bf16[4,131,128]{2,1,0:T(8,128)(2,1)S(1)}, bf16[4,131,128]{2,1,0:T(8,128)(2,1)S(1)}, u32[]{:S(2)}, u32[]{:S(2)}) collective-permute-start(bf16[4,131,128]{2,1,0:T(8,128)(2,1)S(1)} %get-tuple-element.45), channel_id=1, source_target_pairs={{0,2},{1,3},{2,0},{3,1},{4,6},{5,7},{6,4},{7,5},{8,10},{9,11},{10,... | collective-permute-start | bytes 402440 | tf_op jit(solution)/shard_map/ppermute | solution.py:11
  26.0 0.0 collective-permute-start.4
  26.1 1.6 %collective-permute-start.7 = (bf16[1,3,288,128]{3,2,1,0:T(8,128)(2,1)S(1)}, bf16[1,3,288,128]{3,2,1,0:T(8,128)(2,1)S(1)}, u32[]{:S(2)}, u32[]{:S(2)}) collective-permute-start(bf16[1,3,288,128]{3,2,1,0:T(8,128)(2,1)S(1)} %maximum_bitcast_fusion.2), channel_id=1, source_target_pairs={{0,16},{4,20},{8,24},{12,28},{16,0},{20,4},{24,8},{28,12},{1,17},{... | collective-permute-start | bytes 663560 | tf_op jit(solution)/shard_map/ppermute | solution.py:11
  27.7 1.6 %collective-permute-start.10 = (bf16[1,3,288,128]{3,2,1,0:T(8,128)(2,1)S(1)}, bf16[1,3,288,128]{3,2,1,0:T(8,128)(2,1)S(1)}, u32[]{:S(2)}, u32[]{:S(2)}) collective-permute-start(bf16[1,3,288,128]{3,2,1,0:T(8,128)(2,1)S(1)} %maximum_bitcast_fusion.3), channel_id=1, source_target_pairs={{0,8},{4,12},{8,0},{12,4},{16,24},{20,28},{24,16},{28,20},{1,9},{5... | collective-permute-start | bytes 663560 | tf_op jit(solution)/shard_map/ppermute | solution.py:11
  29.2 0.0 collective-permute-done.2.refs_2_
  29.2 0.6 collective-permute-start.13
  29.9 6.4 %collective-permute-done.4.refs_4_ = bf16[4,131,128]{2,1,0:T(8,128)(2,1)S(1)} collective-permute-done((bf16[4,131,128]{2,1,0:T(8,128)(2,1)S(1)}, bf16[4,131,128]{2,1,0:T(8,128)(2,1)S(1)}, u32[]{:S(2)}, u32[]{:S(2)}) %collective-permute-start.4) | collective-permute-done | bytes 134176 | tf_op jit(solution)/shard_map/ppermute | solution.py:11
  36.2 3.8 %collective-permute-start.14 = (bf16[4,131,128]{2,1,0:T(8,128)(2,1)S(1)}, bf16[4,131,128]{2,1,0:T(8,128)(2,1)S(1)}, u32[]{:S(2)}, u32[]{:S(2)}) collective-permute-start(bf16[4,131,128]{2,1,0:T(8,128)(2,1)S(1)} %get-tuple-element.53), channel_id=1, source_target_pairs={{0,2},{1,3},{2,0},{3,1},{4,6},{5,7},{6,4},{7,5},{8,10},{9,11},{10,... | collective-permute-start | bytes 402440 | tf_op jit(solution)/shard_map/ppermute | solution.py:11
  40.0 0.0 collective-permute-done.3.refs_3_
  40.0 0.7 collective-permute-start.15
  40.7 0.0 collective-permute-done.7
  40.8 1.6 %collective-permute-start.8 = (bf16[2,3,288,128]{3,2,1,0:T(8,128)(2,1)S(1)}, bf16[2,3,288,128]{3,2,1,0:T(8,128)(2,1)S(1)}, u32[]{:S(2)}, u32[]{:S(2)}) collective-permute-start(bf16[2,3,288,128]{3,2,1,0:T(8,128)(2,1)S(1)} %pad_maximum_fusion.12), channel_id=1, source_target_pairs={{0,8},{4,12},{8,0},{12,4},{16,24},{20,28},{24,16},{28,20},{1,9},{5... | collective-permute-start | bytes 1327112 | tf_op jit(solution)/shard_map/ppermute | solution.py:11
  42.3 0.0 collective-permute-done.10
  42.4 1.6 %collective-permute-start.11 = (bf16[2,3,288,128]{3,2,1,0:T(8,128)(2,1)S(1)}, bf16[2,3,288,128]{3,2,1,0:T(8,128)(2,1)S(1)}, u32[]{:S(2)}, u32[]{:S(2)}) collective-permute-start(bf16[2,3,288,128]{3,2,1,0:T(8,128)(2,1)S(1)} %pad_maximum_fusion.13), channel_id=1, source_target_pairs={{0,16},{4,20},{8,24},{12,28},{16,0},{20,4},{24,8},{28,12},{1,17},{... | collective-permute-start | bytes 1327112 | tf_op jit(solution)/shard_map/ppermute | solution.py:11
  44.0 6.6 %collective-permute-done.8 = bf16[2,3,288,128]{3,2,1,0:T(8,128)(2,1)S(1)} collective-permute-done((bf16[2,3,288,128]{3,2,1,0:T(8,128)(2,1)S(1)}, bf16[2,3,288,128]{3,2,1,0:T(8,128)(2,1)S(1)}, u32[]{:S(2)}, u32[]{:S(2)}) %collective-permute-start.8) | collective-permute-done | bytes 442400 | tf_op jit(solution)/shard_map/ppermute | solution.py:11
  50.6 1.3 %collective-permute-start.5 = (bf16[1,131,512]{2,1,0:T(8,128)(2,1)S(1)}, bf16[1,131,512]{2,1,0:T(8,128)(2,1)S(1)}, u32[]{:S(2)}, u32[]{:S(2)}) collective-permute-start(bf16[1,131,512]{2,1,0:T(8,128)(2,1)S(1)} %pad_maximum_fusion.15), channel_id=1, source_target_pairs={{0,4},{4,8},{8,12},{12,16},{16,20},{20,24},{24,28},{1,5},{5,9},{9,... | collective-permute-start | bytes 402440 | tf_op jit(solution)/shard_map/ppermute | solution.py:18
  51.9 0.1 pad_maximum_fusion.refs_8_
  52.0 0.0 copy-start
  52.0 2.3 %collective-permute-start.9 = (bf16[4,3,288,128]{3,2,1,0:T(8,128)(2,1)S(1)}, bf16[4,3,288,128]{3,2,1,0:T(8,128)(2,1)S(1)}, u32[]{:S(2)}, u32[]{:S(2)}) collective-permute-start(bf16[4,3,288,128]{3,2,1,0:T(8,128)(2,1)S(1)} %pad_maximum_fusion.refs_8_), channel_id=1, source_target_pairs={{0,4},{4,0},{8,12},{12,8},{16,20},{20,16},{24,28},{28,24},{1,5},{5... | collective-permute-start | bytes 2654216 | tf_op jit(solution)/shard_map/ppermute | solution.py:11
  54.3 0.1 pad_maximum_fusion.1.refs_10_
  54.4 0.1 collective-permute-start.12
  54.5 0.0 collective-permute-done.14.refs_3_
  54.5 1.3 %collective-permute-start.6 = (bf16[1,131,512]{2,1,0:T(8,128)(2,1)S(1)}, bf16[1,131,512]{2,1,0:T(8,128)(2,1)S(1)}, u32[]{:S(2)}, u32[]{:S(2)}) collective-permute-start(bf16[1,131,512]{2,1,0:T(8,128)(2,1)S(1)} %pad_maximum_fusion.16), channel_id=1, source_target_pairs={{4,0},{8,4},{12,8},{16,12},{20,16},{24,20},{28,24},{5,1},{9,5},{13... | collective-permute-start | bytes 402440 | tf_op jit(solution)/shard_map/ppermute | solution.py:18
  55.9 3.0 %collective-permute-start.16 = (bf16[1,131,512]{2,1,0:T(8,128)(2,1)S(1)}, bf16[1,131,512]{2,1,0:T(8,128)(2,1)S(1)}, u32[]{:S(2)}, u32[]{:S(2)}) collective-permute-start(bf16[1,131,512]{2,1,0:T(8,128)(2,1)S(1)} %pad_maximum_fusion.17), channel_id=1, source_target_pairs={{0,4},{4,8},{8,12},{12,16},{16,20},{20,24},{24,28},{1,5},{5,9},{9,... | collective-permute-start | bytes 402440 | tf_op jit(solution)/shard_map/ppermute | solution.py:18
  59.0 1.3 %collective-permute-start.17 = (bf16[1,131,512]{2,1,0:T(8,128)(2,1)S(1)}, bf16[1,131,512]{2,1,0:T(8,128)(2,1)S(1)}, u32[]{:S(2)}, u32[]{:S(2)}) collective-permute-start(bf16[1,131,512]{2,1,0:T(8,128)(2,1)S(1)} %pad_maximum_fusion.18), channel_id=1, source_target_pairs={{4,0},{8,4},{12,8},{16,12},{20,16},{24,20},{28,24},{5,1},{9,5},{13... | collective-permute-start | bytes 402440 | tf_op jit(solution)/shard_map/ppermute | solution.py:18
  60.3 0.0 collective-permute-done.9.refs_9_
  60.3 4.1 %forward.1 = (bf16[512,128]{1,0:T(8,128)(2,1)S(1)}, bf16[512,128]{1,0:T(8,128)(2,1)S(1)}, bf16[512,128]{1,0:T(8,128)(2,1)S(1)}, bf16[512,128]{1,0:T(8,128)(2,1)S(1)}, bf16[4608,512]{1,0:T(8,128)(2,1)S(1)}) custom-call(s32[2]{0:T(128)S(1)} %pad_add_fusion.refs_0_, bf16[4,131,128]{2,1,0:T(8,128)(2,1)S(1)} %get-tuple-element.40.refs_1_, ...), custom_call_target="tpu_custom_call" | custom-call | flops 2415919104 | bytes 10485760 | tf_op jit(solution)/shard_map/forward/pallas_call | solution.py:201
  64.4 3.4 %collective-permute-start.20 = (bf16[512,128]{1,0:T(8,128)(2,1)S(1)}, bf16[512,128]{1,0:T(8,128)(2,1)S(1)}, u32[]{:S(2)}, u32[]{:S(2)}) collective-permute-start(bf16[512,128]{1,0:T(8,128)(2,1)S(1)} %get-tuple-element.63), channel_id=1, source_target_pairs={{0,3},{1,2},{2,1},{3,0},{4,7},{5,6},{6,5},{7,4},{8,11},{9,10},{10,... | collective-permute-start | bytes 393224 | tf_op jit(solution)/shard_map/ppermute | solution.py:11
  67.8 1.1 %collective-permute-start.18 = (bf16[512,128]{1,0:T(8,128)(2,1)S(1)}, bf16[512,128]{1,0:T(8,128)(2,1)S(1)}, u32[]{:S(2)}, u32[]{:S(2)}) collective-permute-start(bf16[512,128]{1,0:T(8,128)(2,1)S(1)} %get-tuple-element.60), channel_id=1, source_target_pairs={{0,1},{1,0},{2,3},{3,2},{4,5},{5,4},{6,7},{7,6},{8,9},{9,8},{10,11... | collective-permute-start | bytes 393224 | tf_op jit(solution)/shard_map/ppermute | solution.py:11
  68.9 3.8 %backward.1 = (bf16[512,128]{1,0:T(8,128)(2,1)S(1)}, bf16[512,128]{1,0:T(8,128)(2,1)S(1)}, bf16[512,128]{1,0:T(8,128)(2,1)S(1)}, bf16[512,128]{1,0:T(8,128)(2,1)S(1)}) custom-call(s32[2]{0:T(128)S(1)} %pad_add_fusion.refs_0_, bf16[4,131,128]{2,1,0:T(8,128)(2,1)S(1)} %get-tuple-element.51.refs_1_, bf16[4,131,128]{2,1,0:T(8,128)(2,1)S(1)} %collective-permute-done.13.refs_2_, ...), custom_call_target="tpu_custom_call" | custom-call | flops 2415919104 | bytes 6291456 | tf_op jit(solution)/shard_map/backward/pallas_call | solution.py:227
  72.7 3.2 %collective-permute-done.18 = bf16[512,128]{1,0:T(8,128)(2,1)S(1)} collective-permute-done((bf16[512,128]{1,0:T(8,128)(2,1)S(1)}, bf16[512,128]{1,0:T(8,128)(2,1)S(1)}, u32[]{:S(2)}, u32[]{:S(2)}) %collective-permute-start.18) | collective-permute-done | bytes 131104 | tf_op jit(solution)/shard_map/ppermute | solution.py:11
  76.0 4.0 %collective-permute-start.23 = (bf16[512,128]{1,0:T(8,128)(2,1)S(1)}, bf16[512,128]{1,0:T(8,128)(2,1)S(1)}, u32[]{:S(2)}, u32[]{:S(2)}) collective-permute-start(bf16[512,128]{1,0:T(8,128)(2,1)S(1)} %get-tuple-element.67), channel_id=1, source_target_pairs={{0,3},{1,2},{2,1},{3,0},{4,7},{5,6},{6,5},{7,4},{8,11},{9,10},{10,... | collective-permute-start | bytes 393224 | tf_op jit(solution)/shard_map/ppermute | solution.py:11
  80.0 0.0 collective-permute-start.22
  80.0 0.6 collective-permute-start.21
  80.6 0.0 collective-permute-done.20
  80.6 0.0 collective-permute-done.19
  80.6 0.1 pad_maximum_fusion.2
  80.7 0.1 copy.11
  80.9 0.1 copy.10
  81.0 0.1 copy.9
  81.2 0.1 copy.8
  81.3 1.1 %maximum_bitcast_fusion = bf16[128,4,512]{2,1,0:T(4,128)(2,1)} fusion(bf16[4,128,128]{1,0,2:T(4,128)(2,1)S(1)} %bitcast.54, bf16[4,128,128]{1,0,2:T(4,128)(2,1)S(1)} %bitcast.56, bf16[4,128,128]{1,0,2:T(4,128)(2,1)S(1)} %bitcast.58, bf16[4,128,128]{1,0,2:T(4,128)(2,1)S(1)} %bitcast.60), kind=kLoop, calls=%fused_computation.3 | loop fusion | flops 2097152 | bytes 1048576 | tf_op jit(solution)/shard_map/transpose | solution.py:285
  82.4 1.8 %collective-permute-done.23 = bf16[512,128]{1,0:T(8,128)(2,1)S(1)} collective-permute-done((bf16[512,128]{1,0:T(8,128)(2,1)S(1)}, bf16[512,128]{1,0:T(8,128)(2,1)S(1)}, u32[]{:S(2)}, u32[]{:S(2)}) %collective-permute-start.23) | collective-permute-done | bytes 131104 | tf_op jit(solution)/shard_map/ppermute | solution.py:11
  84.2 8.3 %collective-permute-done.22 = bf16[512,128]{1,0:T(8,128)(2,1)S(1)} collective-permute-done((bf16[512,128]{1,0:T(8,128)(2,1)S(1)}, bf16[512,128]{1,0:T(8,128)(2,1)S(1)}, u32[]{:S(2)}, u32[]{:S(2)}) %collective-permute-start.22) | collective-permute-done | bytes 131104 | tf_op jit(solution)/shard_map/ppermute | solution.py:11
  92.5 0.0 collective-permute-done.21
  92.5 0.1 pad_maximum_fusion.3
  92.6 0.1 copy.15
  92.8 0.1 copy.14
  92.9 0.1 copy.13
  93.1 0.1 copy.12
  93.2 1.1 %maximum_bitcast_fusion.1 = bf16[128,4,512]{2,1,0:T(4,128)(2,1)} fusion(bf16[4,128,128]{1,0,2:T(4,128)(2,1)S(1)} %bitcast.55, bf16[4,128,128]{1,0,2:T(4,128)(2,1)S(1)} %bitcast.57, bf16[4,128,128]{1,0,2:T(4,128)(2,1)S(1)} %bitcast.59, bf16[4,128,128]{1,0,2:T(4,128)(2,1)S(1)} %bitcast.61), kind=kLoop, calls=%fused_computation.5 | loop fusion | flops 2097152 | bytes 1048576 | tf_op jit(solution)/shard_map/transpose | solution.py:285
  (36 shorter events, 0.5 us)
Async XLA Ops:
  0.6 6.6 %copy-start.1 = (bf16[128,4,512]{2,1,0:T(4,128)(2,1)S(1)}, bf16[128,4,512]{2,1,0:T(4,128)(2,1)}, u32[]{:S(2)}) copy-start(bf16[128,4,512]{2,1,0:T(4,128)(2,1)} %param.4) | copy-start | bytes 1572868
  1.6 11.1 %collective-permute-start = (bf16[1,576,128]{2,1,0:T(8,128)(2,1)S(1)}, bf16[1,576,128]{2,1,0:T(8,128)(2,1)S(1)}, u32[]{:S(2)}, u32[]{:S(2)}) collective-permute-start(bf16[1,576,128]{2,1,0:T(8,128)(2,1)S(1)} %dynamic-slice_bitcast_fusion), channel_id=1, source_target_pairs={{0,2},{1,3},{2,0},{3,1},{4,6},{5,7},{6,4},{7,5},{8,10},{9,11},{10,... | collective-permute-start | bytes 442376 | tf_op jit(solution)/shard_map/ppermute | solution.py:11
  7.6 0.7 copy-start.2
  12.8 8.3 %collective-permute-start.1 = (bf16[2,576,128]{2,1,0:T(8,128)(2,1)S(1)}, bf16[2,576,128]{2,1,0:T(8,128)(2,1)S(1)}, u32[]{:S(2)}, u32[]{:S(2)}) collective-permute-start(bf16[2,576,128]{2,1,0:T(8,128)(2,1)S(1)} %pad_maximum_fusion.14), channel_id=1, source_target_pairs={{0,1},{1,0},{2,3},{3,2},{4,5},{5,4},{6,7},{7,6},{8,9},{9,8},{10,11... | collective-permute-start | bytes 884744 | tf_op jit(solution)/shard_map/ppermute | solution.py:11
  21.1 8.2 %collective-permute-start.2 = (bf16[4,131,128]{2,1,0:T(8,128)(2,1)S(1)}, bf16[4,131,128]{2,1,0:T(8,128)(2,1)S(1)}, u32[]{:S(2)}, u32[]{:S(2)}) collective-permute-start(bf16[4,131,128]{2,1,0:T(8,128)(2,1)S(1)} %get-tuple-element.43), channel_id=1, source_target_pairs={{0,1},{1,0},{2,3},{3,2},{4,5},{5,4},{6,7},{7,6},{8,9},{9,8},{10,11... | collective-permute-start | bytes 402440 | tf_op jit(solution)/shard_map/ppermute | solution.py:11
  22.6 17.4 %collective-permute-start.3 = (bf16[4,131,128]{2,1,0:T(8,128)(2,1)S(1)}, bf16[4,131,128]{2,1,0:T(8,128)(2,1)S(1)}, u32[]{:S(2)}, u32[]{:S(2)}) collective-permute-start(bf16[4,131,128]{2,1,0:T(8,128)(2,1)S(1)} %get-tuple-element.45), channel_id=1, source_target_pairs={{0,2},{1,3},{2,0},{3,1},{4,6},{5,7},{6,4},{7,5},{8,10},{9,11},{10,... | collective-permute-start | bytes 402440 | tf_op jit(solution)/shard_map/ppermute | solution.py:11
  26.0 10.3 %collective-permute-start.4 = (bf16[4,131,128]{2,1,0:T(8,128)(2,1)S(1)}, bf16[4,131,128]{2,1,0:T(8,128)(2,1)S(1)}, u32[]{:S(2)}, u32[]{:S(2)}) collective-permute-start(bf16[4,131,128]{2,1,0:T(8,128)(2,1)S(1)} %get-tuple-element.46), channel_id=1, source_target_pairs={{0,3},{1,2},{2,1},{3,0},{4,7},{5,6},{6,5},{7,4},{8,11},{9,10},{10,... | collective-permute-start | bytes 402440 | tf_op jit(solution)/shard_map/ppermute | solution.py:11
  26.1 14.6 %collective-permute-start.7 = (bf16[1,3,288,128]{3,2,1,0:T(8,128)(2,1)S(1)}, bf16[1,3,288,128]{3,2,1,0:T(8,128)(2,1)S(1)}, u32[]{:S(2)}, u32[]{:S(2)}) collective-permute-start(bf16[1,3,288,128]{3,2,1,0:T(8,128)(2,1)S(1)} %maximum_bitcast_fusion.2), channel_id=1, source_target_pairs={{0,16},{4,20},{8,24},{12,28},{16,0},{20,4},{24,8},{28,12},{1,17},{... | collective-permute-start | bytes 663560 | tf_op jit(solution)/shard_map/ppermute | solution.py:11
  27.7 14.6 %collective-permute-start.10 = (bf16[1,3,288,128]{3,2,1,0:T(8,128)(2,1)S(1)}, bf16[1,3,288,128]{3,2,1,0:T(8,128)(2,1)S(1)}, u32[]{:S(2)}, u32[]{:S(2)}) collective-permute-start(bf16[1,3,288,128]{3,2,1,0:T(8,128)(2,1)S(1)} %maximum_bitcast_fusion.3), channel_id=1, source_target_pairs={{0,8},{4,12},{8,0},{12,4},{16,24},{20,28},{24,16},{28,20},{1,9},{5... | collective-permute-start | bytes 663560 | tf_op jit(solution)/shard_map/ppermute | solution.py:11
  29.2 26.6 %collective-permute-start.13 = (bf16[4,131,128]{2,1,0:T(8,128)(2,1)S(1)}, bf16[4,131,128]{2,1,0:T(8,128)(2,1)S(1)}, u32[]{:S(2)}, u32[]{:S(2)}) collective-permute-start(bf16[4,131,128]{2,1,0:T(8,128)(2,1)S(1)} %get-tuple-element.52), channel_id=1, source_target_pairs={{0,1},{1,0},{2,3},{3,2},{4,5},{5,4},{6,7},{7,6},{8,9},{9,8},{10,11... | collective-permute-start | bytes 402440 | tf_op jit(solution)/shard_map/ppermute | solution.py:11
  36.2 18.3 %collective-permute-start.14 = (bf16[4,131,128]{2,1,0:T(8,128)(2,1)S(1)}, bf16[4,131,128]{2,1,0:T(8,128)(2,1)S(1)}, u32[]{:S(2)}, u32[]{:S(2)}) collective-permute-start(bf16[4,131,128]{2,1,0:T(8,128)(2,1)S(1)} %get-tuple-element.53), channel_id=1, source_target_pairs={{0,2},{1,3},{2,0},{3,1},{4,6},{5,7},{6,4},{7,5},{8,10},{9,11},{10,... | collective-permute-start | bytes 402440 | tf_op jit(solution)/shard_map/ppermute | solution.py:11
  40.0 14.4 %collective-permute-start.15 = (bf16[4,131,128]{2,1,0:T(8,128)(2,1)S(1)}, bf16[4,131,128]{2,1,0:T(8,128)(2,1)S(1)}, u32[]{:S(2)}, u32[]{:S(2)}) collective-permute-start(bf16[4,131,128]{2,1,0:T(8,128)(2,1)S(1)} %get-tuple-element.54), channel_id=1, source_target_pairs={{0,3},{1,2},{2,1},{3,0},{4,7},{5,6},{6,5},{7,4},{8,11},{9,10},{10,... | collective-permute-start | bytes 402440 | tf_op jit(solution)/shard_map/ppermute | solution.py:11
  40.8 9.8 %collective-permute-start.8 = (bf16[2,3,288,128]{3,2,1,0:T(8,128)(2,1)S(1)}, bf16[2,3,288,128]{3,2,1,0:T(8,128)(2,1)S(1)}, u32[]{:S(2)}, u32[]{:S(2)}) collective-permute-start(bf16[2,3,288,128]{3,2,1,0:T(8,128)(2,1)S(1)} %pad_maximum_fusion.12), channel_id=1, source_target_pairs={{0,8},{4,12},{8,0},{12,4},{16,24},{20,28},{24,16},{28,20},{1,9},{5... | collective-permute-start | bytes 1327112 | tf_op jit(solution)/shard_map/ppermute | solution.py:11
  42.4 9.6 %collective-permute-start.11 = (bf16[2,3,288,128]{3,2,1,0:T(8,128)(2,1)S(1)}, bf16[2,3,288,128]{3,2,1,0:T(8,128)(2,1)S(1)}, u32[]{:S(2)}, u32[]{:S(2)}) collective-permute-start(bf16[2,3,288,128]{3,2,1,0:T(8,128)(2,1)S(1)} %pad_maximum_fusion.13), channel_id=1, source_target_pairs={{0,16},{4,20},{8,24},{12,28},{16,0},{20,4},{24,8},{28,12},{1,17},{... | collective-permute-start | bytes 1327112 | tf_op jit(solution)/shard_map/ppermute | solution.py:11
  50.6 8.4 %collective-permute-start.5 = (bf16[1,131,512]{2,1,0:T(8,128)(2,1)S(1)}, bf16[1,131,512]{2,1,0:T(8,128)(2,1)S(1)}, u32[]{:S(2)}, u32[]{:S(2)}) collective-permute-start(bf16[1,131,512]{2,1,0:T(8,128)(2,1)S(1)} %pad_maximum_fusion.15), channel_id=1, source_target_pairs={{0,4},{4,8},{8,12},{12,16},{16,20},{20,24},{24,28},{1,5},{5,9},{9,... | collective-permute-start | bytes 402440 | tf_op jit(solution)/shard_map/ppermute | solution.py:18
  52.0 8.3 %copy-start = (bf16[9,512,128]{2,1,0:T(8,128)(2,1)S(1)}, bf16[9,512,128]{2,1,0:T(8,128)(2,1)}, u32[]{:S(2)}) copy-start(bf16[9,512,128]{2,1,0:T(8,128)(2,1)} %refs_7_.1) | copy-start | bytes 3538948
  52.0 8.3 %collective-permute-start.9 = (bf16[4,3,288,128]{3,2,1,0:T(8,128)(2,1)S(1)}, bf16[4,3,288,128]{3,2,1,0:T(8,128)(2,1)S(1)}, u32[]{:S(2)}, u32[]{:S(2)}) collective-permute-start(bf16[4,3,288,128]{3,2,1,0:T(8,128)(2,1)S(1)} %pad_maximum_fusion.refs_8_), channel_id=1, source_target_pairs={{0,4},{4,0},{8,12},{12,8},{16,20},{20,16},{24,28},{28,24},{1,5},{5... | collective-permute-start | bytes 2654216 | tf_op jit(solution)/shard_map/ppermute | solution.py:11
  54.4 5.9 %collective-permute-start.12 = (bf16[4,3,288,128]{3,2,1,0:T(8,128)(2,1)S(1)}, bf16[4,3,288,128]{3,2,1,0:T(8,128)(2,1)S(1)}, u32[]{:S(2)}, u32[]{:S(2)}) collective-permute-start(bf16[4,3,288,128]{3,2,1,0:T(8,128)(2,1)S(1)} %pad_maximum_fusion.1.refs_10_), channel_id=1, source_target_pairs={{0,4},{4,0},{8,12},{12,8},{16,20},{20,16},{24,28},{28,24},{1,5},{5... | collective-permute-start | bytes 2654216 | tf_op jit(solution)/shard_map/ppermute | solution.py:11
  54.5 5.8 %collective-permute-start.6 = (bf16[1,131,512]{2,1,0:T(8,128)(2,1)S(1)}, bf16[1,131,512]{2,1,0:T(8,128)(2,1)S(1)}, u32[]{:S(2)}, u32[]{:S(2)}) collective-permute-start(bf16[1,131,512]{2,1,0:T(8,128)(2,1)S(1)} %pad_maximum_fusion.16), channel_id=1, source_target_pairs={{4,0},{8,4},{12,8},{16,12},{20,16},{24,20},{28,24},{5,1},{9,5},{13... | collective-permute-start | bytes 402440 | tf_op jit(solution)/shard_map/ppermute | solution.py:18
  55.9 13.0 %collective-permute-start.16 = (bf16[1,131,512]{2,1,0:T(8,128)(2,1)S(1)}, bf16[1,131,512]{2,1,0:T(8,128)(2,1)S(1)}, u32[]{:S(2)}, u32[]{:S(2)}) collective-permute-start(bf16[1,131,512]{2,1,0:T(8,128)(2,1)S(1)} %pad_maximum_fusion.17), channel_id=1, source_target_pairs={{0,4},{4,8},{8,12},{12,16},{16,20},{20,24},{24,28},{1,5},{5,9},{9,... | collective-permute-start | bytes 402440 | tf_op jit(solution)/shard_map/ppermute | solution.py:18
  59.0 9.9 %collective-permute-start.17 = (bf16[1,131,512]{2,1,0:T(8,128)(2,1)S(1)}, bf16[1,131,512]{2,1,0:T(8,128)(2,1)S(1)}, u32[]{:S(2)}, u32[]{:S(2)}) collective-permute-start(bf16[1,131,512]{2,1,0:T(8,128)(2,1)S(1)} %pad_maximum_fusion.18), channel_id=1, source_target_pairs={{4,0},{8,4},{12,8},{16,12},{20,16},{24,20},{28,24},{5,1},{9,5},{13... | collective-permute-start | bytes 402440 | tf_op jit(solution)/shard_map/ppermute | solution.py:18
  64.4 16.1 %collective-permute-start.20 = (bf16[512,128]{1,0:T(8,128)(2,1)S(1)}, bf16[512,128]{1,0:T(8,128)(2,1)S(1)}, u32[]{:S(2)}, u32[]{:S(2)}) collective-permute-start(bf16[512,128]{1,0:T(8,128)(2,1)S(1)} %get-tuple-element.63), channel_id=1, source_target_pairs={{0,3},{1,2},{2,1},{3,0},{4,7},{5,6},{6,5},{7,4},{8,11},{9,10},{10,... | collective-permute-start | bytes 393224 | tf_op jit(solution)/shard_map/ppermute | solution.py:11
  67.8 12.8 %collective-permute-start.19 = (bf16[512,128]{1,0:T(8,128)(2,1)S(1)}, bf16[512,128]{1,0:T(8,128)(2,1)S(1)}, u32[]{:S(2)}, u32[]{:S(2)}) collective-permute-start(bf16[512,128]{1,0:T(8,128)(2,1)S(1)} %get-tuple-element.62), channel_id=1, source_target_pairs={{0,2},{1,3},{2,0},{3,1},{4,6},{5,7},{6,4},{7,5},{8,10},{9,11},{10,... | collective-permute-start | bytes 393224 | tf_op jit(solution)/shard_map/ppermute | solution.py:11
  67.8 8.2 %collective-permute-start.18 = (bf16[512,128]{1,0:T(8,128)(2,1)S(1)}, bf16[512,128]{1,0:T(8,128)(2,1)S(1)}, u32[]{:S(2)}, u32[]{:S(2)}) collective-permute-start(bf16[512,128]{1,0:T(8,128)(2,1)S(1)} %get-tuple-element.60), channel_id=1, source_target_pairs={{0,1},{1,0},{2,3},{3,2},{4,5},{5,4},{6,7},{7,6},{8,9},{9,8},{10,11... | collective-permute-start | bytes 393224 | tf_op jit(solution)/shard_map/ppermute | solution.py:11
  76.0 8.3 %collective-permute-start.23 = (bf16[512,128]{1,0:T(8,128)(2,1)S(1)}, bf16[512,128]{1,0:T(8,128)(2,1)S(1)}, u32[]{:S(2)}, u32[]{:S(2)}) collective-permute-start(bf16[512,128]{1,0:T(8,128)(2,1)S(1)} %get-tuple-element.67), channel_id=1, source_target_pairs={{0,3},{1,2},{2,1},{3,0},{4,7},{5,6},{6,5},{7,4},{8,11},{9,10},{10,... | collective-permute-start | bytes 393224 | tf_op jit(solution)/shard_map/ppermute | solution.py:11
  80.0 12.5 %collective-permute-start.22 = (bf16[512,128]{1,0:T(8,128)(2,1)S(1)}, bf16[512,128]{1,0:T(8,128)(2,1)S(1)}, u32[]{:S(2)}, u32[]{:S(2)}) collective-permute-start(bf16[512,128]{1,0:T(8,128)(2,1)S(1)} %get-tuple-element.66), channel_id=1, source_target_pairs={{0,2},{1,3},{2,0},{3,1},{4,6},{5,7},{6,4},{7,5},{8,10},{9,11},{10,... | collective-permute-start | bytes 393224 | tf_op jit(solution)/shard_map/ppermute | solution.py:11
  80.0 12.5 %collective-permute-start.21 = (bf16[512,128]{1,0:T(8,128)(2,1)S(1)}, bf16[512,128]{1,0:T(8,128)(2,1)S(1)}, u32[]{:S(2)}, u32[]{:S(2)}) collective-permute-start(bf16[512,128]{1,0:T(8,128)(2,1)S(1)} %get-tuple-element.65), channel_id=1, source_target_pairs={{0,1},{1,0},{2,3},{3,2},{4,5},{5,4},{6,7},{7,6},{8,9},{9,8},{10,11... | collective-permute-start | bytes 393224 | tf_op jit(solution)/shard_map/ppermute | solution.py:11

commit v4 on v1

--- a/solution.py
+++ b/solution.py
@@ -1,6 +1,8 @@
 import jax
 import jax.numpy as jnp
 from jax import lax
+from jax.experimental import pallas as pl
+from jax.experimental.pallas import tpu as pltpu
 from jax.sharding import PartitionSpec as P
 
 
@@ -49,7 +51,7 @@
     )[0]
 
 
-def per_device(image, filters, bias, upstream):
+def plain(image, filters, bias, upstream):
     n = lax.axis_size("chan")
     bands = lax.axis_size("band")
     me = lax.axis_index("chan")
@@ -107,6 +109,215 @@
     return jnp.transpose(whole, (2, 0, 1))
 
 
+def fill_rows(target, piece, row, lanes, width):
+    for shift in range(3):
+        target[shift, pl.ds(row * width, width), lanes] = piece[shift : shift + width, :]
+
+
+def fill_source(target, pieces, before, after, width):
+    rows, _, local = pieces[0].shape
+    for k, piece in enumerate(pieces):
+        lanes = slice(k * local, (k + 1) * local)
+        fill_rows(target, before[0, :, lanes], 0, lanes, width)
+        for row in range(rows):
+            fill_rows(target, piece[row], row + 1, lanes, width)
+        fill_rows(target, after[0, :, lanes], rows + 1, lanes, width)
+
+
+def backward_kernel(order, place, *refs):
+    pieces, (before, after, filters, near, far), refs = refs[:4], refs[4:9], refs[9:]
+    mine, other, weights, source = refs
+    me, band = place[0], place[1]
+    taps, channels, local = filters.shape
+    rows = pieces[0].shape[0]
+    width = pieces[0].shape[1] - 3
+    share = near.shape[2]
+    for tap in range(taps):
+        for j in range(4):
+            start = pl.multiple_of((me ^ j) * local, local)
+            weights[pl.ds(tap * channels + j * local, local), :local] = filters[
+                tap, pl.ds(start, local), :
+            ]
+    for bit, held in enumerate((near, far)):
+        for j, d in enumerate(order):
+            first = (band ^ (d | bit)) * share
+            block = lax.div(first, local)
+            start = (block ^ me) * local + first - block * local
+            for tap in range(taps):
+                place_row = pl.multiple_of(tap * channels + start, 16)
+                weights[pl.ds(place_row, share), local:] = held[j, tap]
+    fill_source(source, pieces, before, after, width)
+    acc = None
+    for a in range(3):
+        for b in range(3):
+            term = jnp.dot(
+                source[2 - b, pl.ds((2 - a) * width, rows * width), :],
+                weights[pl.ds((3 * a + b) * channels, channels), :],
+                preferred_element_type=jnp.float32,
+            )
+            acc = term if acc is None else acc + term
+    mine[...] = acc[:, :local].astype(jnp.bfloat16)
+    other[...] = acc[:, local:].astype(jnp.bfloat16)
+
+
+def forward_kernel(order, place, *refs):
+    pieces, (before, after, weights, near, far), refs = refs[:4], refs[4:9], refs[9:]
+    mine, other, extra, source = refs
+    me, band = place[0], place[1]
+    rows, padded, local = pieces[0].shape
+    width = padded - 3
+    taps = 9
+    channels = weights.shape[0] // taps
+    share = near.shape[3]
+    half = 2 * local
+    for bit, held in enumerate((near, far)):
+        for j, d in enumerate(order):
+            first = (band ^ (d | bit)) * share
+            block = lax.div(first, local)
+            start = (block ^ (me & 1)) * local + first - block * local
+            for tap in range(taps):
+                place_row = pl.multiple_of(tap * half + start, 16)
+                for k in range(2):
+                    extra[pl.ds(place_row, share), k * local : (k + 1) * local] = held[j, k, tap]
+    fill_source(source, pieces, before, after, width)
+    acc = None
+    for a in range(3):
+        for b in range(3):
+            tap = 3 * a + b
+            for part in range(2):
+                if part:
+                    filters = extra[pl.ds(tap * half, half), :]
+                else:
+                    filters = weights[pl.ds(tap * channels, half), :]
+                term = lax.dot_general(
+                    source[b, pl.ds(a * width, rows * width), part * half : (part + 1) * half],
+                    filters,
+                    (((1,), (1,)), ((), ())),
+                    preferred_element_type=jnp.float32,
+                )
+                acc = term if acc is None else acc + term
+    for k, out in enumerate((mine, other)):
+        bias = pieces[k][0, padded - 1 : padded, :].astype(jnp.float32)
+        out[...] = (acc[:, k * local : (k + 1) * local] + bias).astype(jnp.bfloat16)
+
+
+SMEM = pl.BlockSpec(memory_space=pltpu.SMEM)
+VMEM = pl.BlockSpec(memory_space=pltpu.VMEM)
+
+
+def kernel_call(body, order, place, args, outs, scratch, name):
+    rows, padded, local = args[0].shape
+    width = padded - 3
+    return pl.pallas_call(
+        lambda *refs: body(order, *refs),
+        out_shape=[jax.ShapeDtypeStruct((rows * width, local), jnp.bfloat16)] * 2 + outs,
+        in_specs=[SMEM] + [VMEM] * len(args),
+        out_specs=[VMEM] * (2 + len(outs)),
+        scratch_shapes=scratch
+        + [pltpu.VMEM((3, (rows + 2) * width, 4 * local), jnp.bfloat16)],
+        compiler_params=pltpu.CompilerParams(vmem_limit_bytes=40 * 2**20),
+        cost_estimate=pl.CostEstimate(
+            flops=18 * rows * width * 8 * local * local,
+            bytes_accessed=8 * 2**20,
+            transcendentals=0,
+        ),
+        name=name,
+    )(place, *args)
+
+
+def cut(value, bias, side):
+    rows, local = value.shape[1], value.shape[0]
+    width = value.shape[2] // 2
+    padded = jnp.pad(jnp.transpose(value, (1, 2, 0)), ((0, 0), (1, 1), (0, 0)))
+    extra = jnp.broadcast_to(bias, (rows, 1, local))
+    return [
+        jnp.concatenate(
+            [lax.dynamic_slice_in_dim(padded, (side ^ k) * width, width + 2, axis=1), extra], axis=1
+        )
+        for k in range(2)
+    ]
+
+
+def exchange(mine, other):
+    far = swap(other, "chan", 3)
+    middle = swap(mine, "chan", 2)
+    return [mine, swap(other, "chan", 1), middle, far]
+
+
+def rims(pieces):
+    first = jnp.concatenate([p[:1] for p in pieces], axis=2)
+    last = jnp.concatenate([p[-1:] for p in pieces], axis=2)
+    return neighbours(first, last)
+
+
+def after(value, *others):
+    return lax.optimization_barrier((value, others))[0]
+
+
+def gather(value):
+    bands = lax.axis_size("band")
+    order = list(range(0, bands, 2))
+    held = jnp.stack([swap(value, "band", d) if d else value for d in order])
+    return held, swap(held, "band", 1), order
+
+
+def home(mine, other, side, rows):
+    mine = mine.reshape(rows, -1, mine.shape[1])
+    other = other.reshape(mine.shape)
+    first = jnp.where(side == 0, mine, other)
+    second = jnp.where(side == 0, other, mine)
+    return jnp.transpose(jnp.concatenate([first, second], axis=1), (2, 0, 1))
+
+
+def per_device(image, filters, bias, upstream):
+    n = lax.axis_size("chan")
+    bands = lax.axis_size("band")
+    taps, outs, local = filters.shape
+    rows = image.shape[1]
+    if n != 4 or local % 128 or image.shape[2] % 256 or outs % (32 * bands) or bands < 4:
+        return plain(image, filters, bias, upstream)
+    me = lax.axis_index("chan")
+    band = lax.axis_index("band")
+    side, half = me & 1, me >> 1
+    place = jnp.stack([me, band]).astype(jnp.int32)
+
+    share = outs // bands
+    part = lax.dynamic_slice_in_dim(filters, band * share, share, axis=1)
+    start = (1 - half) * (outs // 2) + band * (share // 2)
+    part_across = lax.dynamic_slice_in_dim(filters, start, share // 2, axis=1)
+    near = swap(part, "chan", 1)
+    across = swap(part_across, "chan", 2)
+
+    u = exchange(*after(cut(upstream, bias, side), part, part_across))
+    held, there, order = gather(near)
+
+    mine, other, weights = kernel_call(
+        backward_kernel,
+        order,
+        place,
+        [*u, *rims(u), filters, held, there],
+        [jax.ShapeDtypeStruct((taps * outs, 2 * local), jnp.bfloat16)],
+        [],
+        "backward",
+    )
+    image_grad = home(mine, swap(other, "chan", 1), side, rows)
+
+    x = exchange(*after(cut(image, bias, side), u[1]))
+    across = after(jnp.stack([across, swap(across, "chan", 1)]), held)
+    held, there, order = gather(across)
+    x = after(x, mine)
+    mine, other = kernel_call(
+        forward_kernel,
+        order,
+        place,
+        [*x, *rims(x), weights, held, there],
+        [],
+        [pltpu.VMEM((taps * 2 * local, 2 * local), jnp.bfloat16)],
+        "forward",
+    )
+    return home(mine, swap(other, "chan", 1), side, rows), image_grad
+
+
 def solution(mesh):
     return jax.shard_map(
         per_device,

time: 137 us -> 109 us (0.80)
  the two profiles are of different devices: /device:TPU:0 before, /device:TPU:2 now
where the time goes in v4:
time: 109 us
  waiting for transfers between devices  57 us (52%)
  starting transfers between devices  28.7 us (26%)
  Pallas kernels  9.28 us (9%)
  local copies, waits for them, and re-layouts  8.27 us (8%)
  other arithmetic  4.97 us (5%)
    ppermute x19, waiting for transfers between devices, swap(): return lax.ppermute(value, axis, [(j, j ^ step) for j in range(size)])  51.5 us
    ppermute x19, starting transfers between devices, swap(): return lax.ppermute(value, axis, [(j, j ^ step) for j in range(size)])  20.4 us
    pallas_call x2, Pallas kernels, kernel_call(): pl.pallas_call(lambda *refs: body(order, *refs), out_shape=[jax.ShapeDtyp...  9.28 us
    ppermute x4, starting transfers between devices, neighbours(): return (lax.ppermute(last, 'band', up), lax.ppermute(first, 'band', down))  8.38 us
    unnamed x12, local copies, waits for them, and re-layouts  6.15 us
    ppermute x4, waiting for transfers between devices, neighbours(): return (lax.ppermute(last, 'band', up), lax.ppermute(first, 'band', down))  5.48 us
  transfers between devices with their start and end apart: 23, of which 10 were waited for; matrix products, arithmetic and copies ran while one was open for 6% of the time, Pallas kernels for 9%

profile of v4, /device:TPU:2, one launch (start us, length us, event | category | flops | bytes accessed | tf_op | source)
XLA Modules:
  0.0 109.1 jit_solution(15234165125972140547)
XLA Ops:
  0.6 1.0 constant_dynamic-slice_fusion
  1.6 2.6 %collective-permute-start.15 = (bf16[9,32,128]{2,1,0:T(8,128)(2,1)S(1)}, bf16[9,32,128]{2,1,0:T(8,128)(2,1)S(1)}, u32[]{:S(2)}, u32[]{:S(2)}) collective-permute-start(bf16[9,32,128]{2,1,0:T(8,128)(2,1)S(1)} %constant_dynamic-slice_fusion), channel_id=1, source_target_pairs={{0,2},{1,3},{2,0},{3,1},{4,6},{5,7},{6,4},{7,5},{8,10},{9,11},{10,... | collective-permute-start | bytes 221192 | tf_op jit(solution)/shard_map/ppermute | solution.py:11
  4.2 1.5 %copy.6 = bf16[128,4,512]{0,2,1:T(8,128)(2,1)S(1)} copy(bf16[128,4,512]{2,1,0:T(4,128)(2,1)} %param.4) | data formatting | bytes 1048576 | tf_op args[0]
  5.7 0.4 copy.7
  6.1 0.0 copy-start.4
  6.1 0.3 pad_dynamic-slice_fusion
  6.4 0.0 copy-start
  6.4 0.3 copy-done.4
  6.7 0.1 pad_maximum_fusion.2
  6.8 0.9 copy-done
  7.7 1.6 %collective-permute-start = (bf16[4,259,128]{2,1,0:T(8,128)(2,1)S(1)}, bf16[4,259,128]{2,1,0:T(8,128)(2,1)S(1)}, u32[]{:S(2)}, u32[]{:S(2)}) collective-permute-start(bf16[4,259,128]{2,1,0:T(8,128)(2,1)S(1)} %get-tuple-element.16), channel_id=1, source_target_pairs={{0,1},{1,0},{2,3},{3,2},{4,5},{5,4},{6,7},{7,6},{8,9},{9,8},{10,11... | collective-permute-start | bytes 795656 | tf_op jit(solution)/shard_map/ppermute | solution.py:11
  9.3 0.2 collective-permute-start.5
  9.6 0.7 collective-permute-start.8
  10.2 3.5 %collective-permute-start.4 = (bf16[4,259,128]{2,1,0:T(8,128)(2,1)S(1)}, bf16[4,259,128]{2,1,0:T(8,128)(2,1)S(1)}, u32[]{:S(2)}, u32[]{:S(2)}) collective-permute-start(bf16[4,259,128]{2,1,0:T(8,128)(2,1)S(1)} %get-tuple-element.19.refs_1_), channel_id=1, source_target_pairs={{0,2},{1,3},{2,0},{3,1},{4,6},{5,7},{6,4},{7,5},{8,10},{9,11},{10,... | collective-permute-start | bytes 795656 | tf_op jit(solution)/shard_map/ppermute | solution.py:11
  13.7 0.0 collective-permute-start.16
  13.7 17.4 %collective-permute-done.16 = bf16[9,32,128]{2,1,0:T(8,128)(2,1)S(1)} collective-permute-done((bf16[9,32,128]{2,1,0:T(8,128)(2,1)S(1)}, bf16[9,32,128]{2,1,0:T(8,128)(2,1)S(1)}, u32[]{:S(2)}, u32[]{:S(2)}) %collective-permute-start.16) | collective-permute-done | bytes 73760 | tf_op jit(solution)/shard_map/ppermute | solution.py:11
  31.2 0.6 collective-permute-start.9
  31.8 1.5 %collective-permute-start.10 = (bf16[9,64,128]{2,1,0:T(8,128)(2,1)S(1)}, bf16[9,64,128]{2,1,0:T(8,128)(2,1)S(1)}, u32[]{:S(2)}, u32[]{:S(2)}) collective-permute-start(bf16[9,64,128]{2,1,0:T(8,128)(2,1)S(1)} %collective-permute-done.8), channel_id=1, source_target_pairs={{0,16},{4,20},{8,24},{12,28},{16,0},{20,4},{24,8},{28,12},{1,17},{... | collective-permute-start | bytes 442376 | tf_op jit(solution)/shard_map/ppermute | solution.py:11
  33.3 0.0 collective-permute-done.refs_2_
  33.3 1.4 %collective-permute-start.11 = (bf16[9,64,128]{2,1,0:T(8,128)(2,1)S(1)}, bf16[9,64,128]{2,1,0:T(8,128)(2,1)S(1)}, u32[]{:S(2)}, u32[]{:S(2)}) collective-permute-start(bf16[9,64,128]{2,1,0:T(8,128)(2,1)S(1)} %collective-permute-done.8), channel_id=1, source_target_pairs={{0,24},{4,28},{8,16},{12,20},{16,8},{20,12},{24,0},{28,4},{1,25},{... | collective-permute-start | bytes 442376 | tf_op jit(solution)/shard_map/ppermute | solution.py:11
  34.8 0.0 collective-permute-done.4.refs_3_
  34.8 2.4 %collective-permute-done.9 = bf16[9,64,128]{2,1,0:T(8,128)(2,1)S(1)} collective-permute-done((bf16[9,64,128]{2,1,0:T(8,128)(2,1)S(1)}, bf16[9,64,128]{2,1,0:T(8,128)(2,1)S(1)}, u32[]{:S(2)}, u32[]{:S(2)}) %collective-permute-start.9) | collective-permute-done | bytes 147488 | tf_op jit(solution)/shard_map/ppermute | solution.py:11
  37.2 1.0 collective-permute-done.10
  38.2 1.6 %collective-permute-done.11 = bf16[9,64,128]{2,1,0:T(8,128)(2,1)S(1)} collective-permute-done((bf16[9,64,128]{2,1,0:T(8,128)(2,1)S(1)}, bf16[9,64,128]{2,1,0:T(8,128)(2,1)S(1)}, u32[]{:S(2)}, u32[]{:S(2)}) %collective-permute-start.11) | collective-permute-done | bytes 147488 | tf_op jit(solution)/shard_map/ppermute | solution.py:11
  39.8 0.1 pad_maximum_fusion.refs_8_
  39.9 0.1 collective-permute-start.12
  39.9 0.0 collective-permute-done.5.refs_4_
  40.0 1.7 %collective-permute-start.17 = (bf16[2,9,32,128]{3,2,1,0:T(8,128)(2,1)S(1)}, bf16[2,9,32,128]{3,2,1,0:T(8,128)(2,1)S(1)}, u32[]{:S(2)}, u32[]{:S(2)}) collective-permute-start(bf16[2,9,32,128]{3,2,1,0:T(8,128)(2,1)S(1)} %pad_maximum_fusion.10), channel_id=1, source_target_pairs={{0,8},{4,12},{8,0},{12,4},{16,24},{20,28},{24,16},{28,20},{1,9},{5... | collective-permute-start | bytes 442376 | tf_op jit(solution)/shard_map/ppermute | solution.py:11
  41.7 2.2 %collective-permute-start.7 = (bf16[1,259,512]{2,1,0:T(8,128)(2,1)S(1)}, bf16[1,259,512]{2,1,0:T(8,128)(2,1)S(1)}, u32[]{:S(2)}, u32[]{:S(2)}) collective-permute-start(bf16[1,259,512]{2,1,0:T(8,128)(2,1)S(1)} %pad_maximum_fusion.7), channel_id=1, source_target_pairs={{4,0},{8,4},{12,8},{16,12},{20,16},{24,20},{28,24},{5,1},{9,5},{13... | collective-permute-start | bytes 795656 | tf_op jit(solution)/shard_map/ppermute | solution.py:18
  43.8 0.9 collective-permute-start.18
  44.8 1.7 %collective-permute-start.19 = (bf16[2,9,32,128]{3,2,1,0:T(8,128)(2,1)S(1)}, bf16[2,9,32,128]{3,2,1,0:T(8,128)(2,1)S(1)}, u32[]{:S(2)}, u32[]{:S(2)}) collective-permute-start(bf16[2,9,32,128]{3,2,1,0:T(8,128)(2,1)S(1)} %pad_maximum_fusion.10), channel_id=1, source_target_pairs={{0,24},{4,28},{8,16},{12,20},{16,8},{20,12},{24,0},{28,4},{1,25},{... | collective-permute-start | bytes 442376 | tf_op jit(solution)/shard_map/ppermute | solution.py:11
  46.5 0.0 collective-permute-done.17
  46.5 1.9 %collective-permute-start.6 = (bf16[1,259,512]{2,1,0:T(8,128)(2,1)S(1)}, bf16[1,259,512]{2,1,0:T(8,128)(2,1)S(1)}, u32[]{:S(2)}, u32[]{:S(2)}) collective-permute-start(bf16[1,259,512]{2,1,0:T(8,128)(2,1)S(1)} %pad_maximum_fusion.6), channel_id=1, source_target_pairs={{0,4},{4,8},{8,12},{12,16},{16,20},{20,24},{24,28},{1,5},{5,9},{9,... | collective-permute-start | bytes 795656 | tf_op jit(solution)/shard_map/ppermute | solution.py:18
  48.4 0.1 pad_add_fusion.refs_0_
  48.5 7.5 %collective-permute-done.18 = bf16[2,9,32,128]{3,2,1,0:T(8,128)(2,1)S(1)} collective-permute-done((bf16[2,9,32,128]{3,2,1,0:T(8,128)(2,1)S(1)}, bf16[2,9,32,128]{3,2,1,0:T(8,128)(2,1)S(1)}, u32[]{:S(2)}, u32[]{:S(2)}) %collective-permute-start.18) | collective-permute-done | bytes 147488 | tf_op jit(solution)/shard_map/ppermute | solution.py:11
  56.0 2.2 %collective-permute-start.1 = (bf16[4,259,128]{2,1,0:T(8,128)(2,1)S(1)}, bf16[4,259,128]{2,1,0:T(8,128)(2,1)S(1)}, u32[]{:S(2)}, u32[]{:S(2)}) collective-permute-start(bf16[4,259,128]{2,1,0:T(8,128)(2,1)S(1)} %get-tuple-element.18), channel_id=1, source_target_pairs={{0,1},{1,0},{2,3},{3,2},{4,5},{5,4},{6,7},{7,6},{8,9},{9,8},{10,11... | collective-permute-start | bytes 795656 | tf_op jit(solution)/shard_map/ppermute | solution.py:11
  58.2 0.5 collective-permute-start.3
  58.7 1.0 collective-permute-start.2
  59.7 0.1 pad_maximum_fusion.1.refs_8_
  59.7 0.1 collective-permute-start.20
  59.8 0.0 collective-permute-done.12.refs_9_
  59.8 4.9 %backward.1 = (bf16[1024,128]{1,0:T(8,128)(2,1)S(1)}, bf16[1024,128]{1,0:T(8,128)(2,1)}, bf16[4608,256]{1,0:T(8,128)(2,1)S(1)}) custom-call(s32[2]{0:T(128)S(1)} %pad_add_fusion.refs_0_, bf16[4,259,128]{2,1,0:T(8,128)(2,1)S(1)} %get-tuple-element.19.refs_1_, bf16[4,259,128]{2,1,0:T(8,128)(2,1)S(1)} %collective-permute-done.refs_2_, ...), custom_call_target="tpu_custom_call" | custom-call | flops 2415919104 | bytes 8388608 | tf_op jit(solution)/shard_map/backward/pallas_call | solution.py:211
  64.7 1.4 %copy-done.1 = bf16[4608,256]{1,0:T(8,128)(2,1)} copy-done((bf16[4608,256]{1,0:T(8,128)(2,1)}, bf16[4608,256]{1,0:T(8,128)(2,1)S(1)}, u32[]{:S(2)}) %copy-start.1) | copy-done | bytes 2359320
  66.1 0.5 collective-permute-done.1.refs_2_
  66.6 16.3 %collective-permute-done.2.refs_3_ = bf16[4,259,128]{2,1,0:T(8,128)(2,1)S(1)} collective-permute-done((bf16[4,259,128]{2,1,0:T(8,128)(2,1)S(1)}, bf16[4,259,128]{2,1,0:T(8,128)(2,1)S(1)}, u32[]{:S(2)}, u32[]{:S(2)}) %collective-permute-start.2) | collective-permute-done | bytes 265248 | tf_op jit(solution)/shard_map/ppermute | solution.py:11
  82.9 0.0 collective-permute-done.3.refs_4_
  83.0 0.7 pad_maximum_fusion.9
  83.7 1.9 %collective-permute-start.14 = (bf16[1,259,512]{2,1,0:T(8,128)(2,1)}, bf16[1,259,512]{2,1,0:T(8,128)(2,1)S(1)}, u32[]{:S(2)}, u32[]{:S(2)}) collective-permute-start(bf16[1,259,512]{2,1,0:T(8,128)(2,1)} %pad_maximum_fusion.9), channel_id=1, source_target_pairs={{4,0},{8,4},{12,8},{16,12},{20,16},{24,20},{28,24},{5,1},{9,5},{13... | collective-permute-start | bytes 795656 | tf_op jit(solution)/shard_map/ppermute | solution.py:18
  85.6 0.7 pad_maximum_fusion.8
  86.4 2.4 %collective-permute-start.13 = (bf16[1,259,512]{2,1,0:T(8,128)(2,1)}, bf16[1,259,512]{2,1,0:T(8,128)(2,1)S(1)}, u32[]{:S(2)}, u32[]{:S(2)}) collective-permute-start(bf16[1,259,512]{2,1,0:T(8,128)(2,1)} %pad_maximum_fusion.8), channel_id=1, source_target_pairs={{0,4},{4,8},{8,12},{12,16},{16,20},{20,24},{24,28},{1,5},{5,9},{9,... | collective-permute-start | bytes 795656 | tf_op jit(solution)/shard_map/ppermute | solution.py:18
  88.8 0.1 collective-permute-start.22
  88.9 0.0 collective-permute-done.20.refs_9_
  88.9 1.0 collective-permute-done.14.refs_6_
  89.9 4.4 %collective-permute-done.13.refs_5_ = bf16[1,259,512]{2,1,0:T(8,128)(2,1)S(1)} collective-permute-done((bf16[1,259,512]{2,1,0:T(8,128)(2,1)}, bf16[1,259,512]{2,1,0:T(8,128)(2,1)S(1)}, u32[]{:S(2)}, u32[]{:S(2)}) %collective-permute-start.13) | collective-permute-done | bytes 265248 | tf_op jit(solution)/shard_map/ppermute | solution.py:18
  94.3 1.7 %copy-done.2 = bf16[4608,256]{1,0:T(8,128)(2,1)S(1)} copy-done((bf16[4608,256]{1,0:T(8,128)(2,1)S(1)}, bf16[4608,256]{1,0:T(8,128)(2,1)}, u32[]{:S(2)}) %copy-start.2) | copy-done | bytes 2359320
  96.0 4.4 %forward.1 = (bf16[1024,128]{1,0:T(8,128)(2,1)S(1)}, bf16[1024,128]{1,0:T(8,128)(2,1)}) custom-call(s32[2]{0:T(128)S(1)} %pad_add_fusion.refs_0_, bf16[4,259,128]{2,1,0:T(8,128)(2,1)S(1)} %get-tuple-element.21.refs_1_, bf16[4,259,128]{2,1,0:T(8,128)(2,1)S(1)} %collective-permute-done.1.refs_2_, bf16[4,259,128]{2,1,0:T(8,128)(2,1)S(1)} %collective-permute-done.2.refs_3_, ...), custom_call_target="tpu_custom_call" | custom-call | flops 2415919104 | bytes 8388608 | tf_op jit(solution)/shard_map/forward/pallas_call | solution.py:211
  100.4 1.0 broadcast_select_fusion.1
  101.4 0.2 copy.10
  101.6 0.2 copy.11
  101.8 1.0 maximum_bitcast_fusion.1
  102.8 4.8 %collective-permute-done.21 = bf16[1024,128]{1,0:T(8,128)(2,1)S(1)} collective-permute-done((bf16[1024,128]{1,0:T(8,128)(2,1)}, bf16[1024,128]{1,0:T(8,128)(2,1)S(1)}, u32[]{:S(2)}, u32[]{:S(2)}) %collective-permute-start.21) | collective-permute-done | bytes 262176 | tf_op jit(solution)/shard_map/ppermute | solution.py:11
  107.7 0.2 copy.8
  107.9 0.2 copy.9
  108.1 1.0 maximum_bitcast_fusion
  (25 shorter events, 0.2 us)
Async XLA Ops:
  0.6 5.0 %copy-start.3 = (bf16[128,4,512]{2,1,0:T(4,128)(2,1)S(1)}, bf16[128,4,512]{2,1,0:T(4,128)(2,1)}, u32[]{:S(2)}) copy-start(bf16[128,4,512]{2,1,0:T(4,128)(2,1)} %param.7) | copy-start | bytes 1572868
  1.6 12.1 %collective-permute-start.15 = (bf16[9,32,128]{2,1,0:T(8,128)(2,1)S(1)}, bf16[9,32,128]{2,1,0:T(8,128)(2,1)S(1)}, u32[]{:S(2)}, u32[]{:S(2)}) collective-permute-start(bf16[9,32,128]{2,1,0:T(8,128)(2,1)S(1)} %constant_dynamic-slice_fusion), channel_id=1, source_target_pairs={{0,2},{1,3},{2,0},{3,1},{4,6},{5,7},{6,4},{7,5},{8,10},{9,11},{10,... | collective-permute-start | bytes 221192 | tf_op jit(solution)/shard_map/ppermute | solution.py:11
  6.1 0.7 copy-start.4
  6.4 1.3 %copy-start = (bf16[9,512,128]{2,1,0:T(8,128)(2,1)S(1)}, bf16[9,512,128]{2,1,0:T(8,128)(2,1)}, u32[]{:S(2)}) copy-start(bf16[9,512,128]{2,1,0:T(8,128)(2,1)} %refs_7_.1) | copy-start | bytes 3538948
  7.7 25.6 %collective-permute-start = (bf16[4,259,128]{2,1,0:T(8,128)(2,1)S(1)}, bf16[4,259,128]{2,1,0:T(8,128)(2,1)S(1)}, u32[]{:S(2)}, u32[]{:S(2)}) collective-permute-start(bf16[4,259,128]{2,1,0:T(8,128)(2,1)S(1)} %get-tuple-element.16), channel_id=1, source_target_pairs={{0,1},{1,0},{2,3},{3,2},{4,5},{5,4},{6,7},{7,6},{8,9},{9,8},{10,11... | collective-permute-start | bytes 795656 | tf_op jit(solution)/shard_map/ppermute | solution.py:11
  9.3 30.6 %collective-permute-start.5 = (bf16[4,259,128]{2,1,0:T(8,128)(2,1)S(1)}, bf16[4,259,128]{2,1,0:T(8,128)(2,1)S(1)}, u32[]{:S(2)}, u32[]{:S(2)}) collective-permute-start(bf16[4,259,128]{2,1,0:T(8,128)(2,1)S(1)} %get-tuple-element.16), channel_id=1, source_target_pairs={{0,3},{1,2},{2,1},{3,0},{4,7},{5,6},{6,5},{7,4},{8,11},{9,10},{10,... | collective-permute-start | bytes 795656 | tf_op jit(solution)/shard_map/ppermute | solution.py:11
  9.6 21.6 %collective-permute-start.8 = (bf16[9,64,128]{2,1,0:T(8,128)(2,1)S(1)}, bf16[9,64,128]{2,1,0:T(8,128)(2,1)S(1)}, u32[]{:S(2)}, u32[]{:S(2)}) collective-permute-start(bf16[9,64,128]{2,1,0:T(8,128)(2,1)S(1)} %constant_dynamic-slice_fusion.1), channel_id=1, source_target_pairs={{0,1},{1,0},{2,3},{3,2},{4,5},{5,4},{6,7},{7,6},{8,9},{9,8},{10,11... | collective-permute-start | bytes 442376 | tf_op jit(solution)/shard_map/ppermute | solution.py:11
  10.2 24.5 %collective-permute-start.4 = (bf16[4,259,128]{2,1,0:T(8,128)(2,1)S(1)}, bf16[4,259,128]{2,1,0:T(8,128)(2,1)S(1)}, u32[]{:S(2)}, u32[]{:S(2)}) collective-permute-start(bf16[4,259,128]{2,1,0:T(8,128)(2,1)S(1)} %get-tuple-element.19.refs_1_), channel_id=1, source_target_pairs={{0,2},{1,3},{2,0},{3,1},{4,6},{5,7},{6,4},{7,5},{8,10},{9,11},{10,... | collective-permute-start | bytes 795656 | tf_op jit(solution)/shard_map/ppermute | solution.py:11
  13.7 17.4 %collective-permute-start.16 = (bf16[9,32,128]{2,1,0:T(8,128)(2,1)S(1)}, bf16[9,32,128]{2,1,0:T(8,128)(2,1)S(1)}, u32[]{:S(2)}, u32[]{:S(2)}) collective-permute-start(bf16[9,32,128]{2,1,0:T(8,128)(2,1)S(1)} %collective-permute-done.15), channel_id=1, source_target_pairs={{0,1},{1,0},{2,3},{3,2},{4,5},{5,4},{6,7},{7,6},{8,9},{9,8},{10,11... | collective-permute-start | bytes 221192 | tf_op jit(solution)/shard_map/ppermute | solution.py:11
  31.2 6.0 %collective-permute-start.9 = (bf16[9,64,128]{2,1,0:T(8,128)(2,1)S(1)}, bf16[9,64,128]{2,1,0:T(8,128)(2,1)S(1)}, u32[]{:S(2)}, u32[]{:S(2)}) collective-permute-start(bf16[9,64,128]{2,1,0:T(8,128)(2,1)S(1)} %collective-permute-done.8), channel_id=1, source_target_pairs={{0,8},{4,12},{8,0},{12,4},{16,24},{20,28},{24,16},{28,20},{1,9},{5... | collective-permute-start | bytes 442376 | tf_op jit(solution)/shard_map/ppermute | solution.py:11
  31.8 6.4 %collective-permute-start.10 = (bf16[9,64,128]{2,1,0:T(8,128)(2,1)S(1)}, bf16[9,64,128]{2,1,0:T(8,128)(2,1)S(1)}, u32[]{:S(2)}, u32[]{:S(2)}) collective-permute-start(bf16[9,64,128]{2,1,0:T(8,128)(2,1)S(1)} %collective-permute-done.8), channel_id=1, source_target_pairs={{0,16},{4,20},{8,24},{12,28},{16,0},{20,4},{24,8},{28,12},{1,17},{... | collective-permute-start | bytes 442376 | tf_op jit(solution)/shard_map/ppermute | solution.py:11
  33.3 6.5 %collective-permute-start.11 = (bf16[9,64,128]{2,1,0:T(8,128)(2,1)S(1)}, bf16[9,64,128]{2,1,0:T(8,128)(2,1)S(1)}, u32[]{:S(2)}, u32[]{:S(2)}) collective-permute-start(bf16[9,64,128]{2,1,0:T(8,128)(2,1)S(1)} %collective-permute-done.8), channel_id=1, source_target_pairs={{0,24},{4,28},{8,16},{12,20},{16,8},{20,12},{24,0},{28,4},{1,25},{... | collective-permute-start | bytes 442376 | tf_op jit(solution)/shard_map/ppermute | solution.py:11
  39.9 20.0 %collective-permute-start.12 = (bf16[4,9,64,128]{3,2,1,0:T(8,128)(2,1)S(1)}, bf16[4,9,64,128]{3,2,1,0:T(8,128)(2,1)S(1)}, u32[]{:S(2)}, u32[]{:S(2)}) collective-permute-start(bf16[4,9,64,128]{3,2,1,0:T(8,128)(2,1)S(1)} %pad_maximum_fusion.refs_8_), channel_id=1, source_target_pairs={{0,4},{4,0},{8,12},{12,8},{16,20},{20,16},{24,28},{28,24},{1,5},{5... | collective-permute-start | bytes 1769480 | tf_op jit(solution)/shard_map/ppermute | solution.py:11
  40.0 6.5 %collective-permute-start.17 = (bf16[2,9,32,128]{3,2,1,0:T(8,128)(2,1)S(1)}, bf16[2,9,32,128]{3,2,1,0:T(8,128)(2,1)S(1)}, u32[]{:S(2)}, u32[]{:S(2)}) collective-permute-start(bf16[2,9,32,128]{3,2,1,0:T(8,128)(2,1)S(1)} %pad_maximum_fusion.10), channel_id=1, source_target_pairs={{0,8},{4,12},{8,0},{12,4},{16,24},{20,28},{24,16},{28,20},{1,9},{5... | collective-permute-start | bytes 442376 | tf_op jit(solution)/shard_map/ppermute | solution.py:11
  41.7 17.0 %collective-permute-start.7 = (bf16[1,259,512]{2,1,0:T(8,128)(2,1)S(1)}, bf16[1,259,512]{2,1,0:T(8,128)(2,1)S(1)}, u32[]{:S(2)}, u32[]{:S(2)}) collective-permute-start(bf16[1,259,512]{2,1,0:T(8,128)(2,1)S(1)} %pad_maximum_fusion.7), channel_id=1, source_target_pairs={{4,0},{8,4},{12,8},{16,12},{20,16},{24,20},{28,24},{5,1},{9,5},{13... | collective-permute-start | bytes 795656 | tf_op jit(solution)/shard_map/ppermute | solution.py:18
  43.8 12.1 %collective-permute-start.18 = (bf16[2,9,32,128]{3,2,1,0:T(8,128)(2,1)S(1)}, bf16[2,9,32,128]{3,2,1,0:T(8,128)(2,1)S(1)}, u32[]{:S(2)}, u32[]{:S(2)}) collective-permute-start(bf16[2,9,32,128]{3,2,1,0:T(8,128)(2,1)S(1)} %pad_maximum_fusion.10), channel_id=1, source_target_pairs={{0,16},{4,20},{8,24},{12,28},{16,0},{20,4},{24,8},{28,12},{1,17},{... | collective-permute-start | bytes 442376 | tf_op jit(solution)/shard_map/ppermute | solution.py:11
  44.8 13.4 %collective-permute-start.19 = (bf16[2,9,32,128]{3,2,1,0:T(8,128)(2,1)S(1)}, bf16[2,9,32,128]{3,2,1,0:T(8,128)(2,1)S(1)}, u32[]{:S(2)}, u32[]{:S(2)}) collective-permute-start(bf16[2,9,32,128]{3,2,1,0:T(8,128)(2,1)S(1)} %pad_maximum_fusion.10), channel_id=1, source_target_pairs={{0,24},{4,28},{8,16},{12,20},{16,8},{20,12},{24,0},{28,4},{1,25},{... | collective-permute-start | bytes 442376 | tf_op jit(solution)/shard_map/ppermute | solution.py:11
  46.5 13.2 %collective-permute-start.6 = (bf16[1,259,512]{2,1,0:T(8,128)(2,1)S(1)}, bf16[1,259,512]{2,1,0:T(8,128)(2,1)S(1)}, u32[]{:S(2)}, u32[]{:S(2)}) collective-permute-start(bf16[1,259,512]{2,1,0:T(8,128)(2,1)S(1)} %pad_maximum_fusion.6), channel_id=1, source_target_pairs={{0,4},{4,8},{8,12},{12,16},{16,20},{20,24},{24,28},{1,5},{5,9},{9,... | collective-permute-start | bytes 795656 | tf_op jit(solution)/shard_map/ppermute | solution.py:18
  56.0 10.7 %collective-permute-start.1 = (bf16[4,259,128]{2,1,0:T(8,128)(2,1)S(1)}, bf16[4,259,128]{2,1,0:T(8,128)(2,1)S(1)}, u32[]{:S(2)}, u32[]{:S(2)}) collective-permute-start(bf16[4,259,128]{2,1,0:T(8,128)(2,1)S(1)} %get-tuple-element.18), channel_id=1, source_target_pairs={{0,1},{1,0},{2,3},{3,2},{4,5},{5,4},{6,7},{7,6},{8,9},{9,8},{10,11... | collective-permute-start | bytes 795656 | tf_op jit(solution)/shard_map/ppermute | solution.py:11
  58.2 24.7 %collective-permute-start.3 = (bf16[4,259,128]{2,1,0:T(8,128)(2,1)S(1)}, bf16[4,259,128]{2,1,0:T(8,128)(2,1)S(1)}, u32[]{:S(2)}, u32[]{:S(2)}) collective-permute-start(bf16[4,259,128]{2,1,0:T(8,128)(2,1)S(1)} %get-tuple-element.18), channel_id=1, source_target_pairs={{0,3},{1,2},{2,1},{3,0},{4,7},{5,6},{6,5},{7,4},{8,11},{9,10},{10,... | collective-permute-start | bytes 795656 | tf_op jit(solution)/shard_map/ppermute | solution.py:11
  58.7 24.2 %collective-permute-start.2 = (bf16[4,259,128]{2,1,0:T(8,128)(2,1)S(1)}, bf16[4,259,128]{2,1,0:T(8,128)(2,1)S(1)}, u32[]{:S(2)}, u32[]{:S(2)}) collective-permute-start(bf16[4,259,128]{2,1,0:T(8,128)(2,1)S(1)} %get-tuple-element.21.refs_1_), channel_id=1, source_target_pairs={{0,2},{1,3},{2,0},{3,1},{4,6},{5,7},{6,4},{7,5},{8,10},{9,11},{10,... | collective-permute-start | bytes 795656 | tf_op jit(solution)/shard_map/ppermute | solution.py:11
  59.7 29.1 %collective-permute-start.20 = (bf16[4,2,9,32,128]{4,3,2,1,0:T(8,128)(2,1)S(1)}, bf16[4,2,9,32,128]{4,3,2,1,0:T(8,128)(2,1)S(1)}, u32[]{:S(2)}, u32[]{:S(2)}) collective-permute-start(bf16[4,2,9,32,128]{4,3,2,1,0:T(8,128)(2,1)S(1)} %pad_maximum_fusion.1.refs_8_), channel_id=1, source_target_pairs={{0,4},{4,0},{8,12},{12,8},{16,20},{20,16},{24,28},{28,24},{1,5},{5... | collective-permute-start | bytes 1769480 | tf_op jit(solution)/shard_map/ppermute | solution.py:11
  64.7 1.4 %copy-start.1 = (bf16[4608,256]{1,0:T(8,128)(2,1)}, bf16[4608,256]{1,0:T(8,128)(2,1)S(1)}, u32[]{:S(2)}) copy-start(bf16[4608,256]{1,0:T(8,128)(2,1)S(1)} %get-tuple-element.25.refs_7_) | copy-start | bytes 7077892
  83.7 6.2 %collective-permute-start.14 = (bf16[1,259,512]{2,1,0:T(8,128)(2,1)}, bf16[1,259,512]{2,1,0:T(8,128)(2,1)S(1)}, u32[]{:S(2)}, u32[]{:S(2)}) collective-permute-start(bf16[1,259,512]{2,1,0:T(8,128)(2,1)} %pad_maximum_fusion.9), channel_id=1, source_target_pairs={{4,0},{8,4},{12,8},{16,12},{20,16},{24,20},{28,24},{5,1},{9,5},{13... | collective-permute-start | bytes 795656 | tf_op jit(solution)/shard_map/ppermute | solution.py:18
  86.4 8.0 %collective-permute-start.13 = (bf16[1,259,512]{2,1,0:T(8,128)(2,1)}, bf16[1,259,512]{2,1,0:T(8,128)(2,1)S(1)}, u32[]{:S(2)}, u32[]{:S(2)}) collective-permute-start(bf16[1,259,512]{2,1,0:T(8,128)(2,1)} %pad_maximum_fusion.8), channel_id=1, source_target_pairs={{0,4},{4,8},{8,12},{12,16},{16,20},{20,24},{24,28},{1,5},{5,9},{9,... | collective-permute-start | bytes 795656 | tf_op jit(solution)/shard_map/ppermute | solution.py:18
  88.8 11.7 %collective-permute-start.22 = (bf16[1024,128]{1,0:T(8,128)(2,1)}, bf16[1024,128]{1,0:T(8,128)(2,1)}, u32[]{:S(2)}, u32[]{:S(2)}) collective-permute-start(bf16[1024,128]{1,0:T(8,128)(2,1)} %get-tuple-element.29), channel_id=1, source_target_pairs={{0,1},{1,0},{2,3},{3,2},{4,5},{5,4},{6,7},{7,6},{8,9},{9,8},{10,11... | collective-permute-start | bytes 786440 | tf_op jit(solution)/shard_map/ppermute | solution.py:11
  94.3 1.7 %copy-start.2 = (bf16[4608,256]{1,0:T(8,128)(2,1)S(1)}, bf16[4608,256]{1,0:T(8,128)(2,1)}, u32[]{:S(2)}) copy-start(bf16[4608,256]{1,0:T(8,128)(2,1)} %copy-done.1) | copy-start | bytes 7077892
  100.4 7.3 %collective-permute-start.21 = (bf16[1024,128]{1,0:T(8,128)(2,1)}, bf16[1024,128]{1,0:T(8,128)(2,1)S(1)}, u32[]{:S(2)}, u32[]{:S(2)}) collective-permute-start(bf16[1024,128]{1,0:T(8,128)(2,1)} %get-tuple-element.28), channel_id=1, source_target_pairs={{0,1},{1,0},{2,3},{3,2},{4,5},{5,4},{6,7},{7,6},{8,9},{9,8},{10,11... | collective-permute-start | bytes 786440 | tf_op jit(solution)/shard_map/ppermute | solution.py:11

commit v5 on v1

--- a/solution.py
+++ b/solution.py
@@ -1,6 +1,8 @@
 import jax
 import jax.numpy as jnp
 from jax import lax
+from jax.experimental import pallas as pl
+from jax.experimental.pallas import tpu as pltpu
 from jax.sharding import PartitionSpec as P
 
 
@@ -49,7 +51,7 @@
     )[0]
 
 
-def per_device(image, filters, bias, upstream):
+def plain(image, filters, bias, upstream):
     n = lax.axis_size("chan")
     bands = lax.axis_size("band")
     me = lax.axis_index("chan")
@@ -107,6 +109,231 @@
     return jnp.transpose(whole, (2, 0, 1))
 
 
+def assemble_kernel(order, place, filters, near, far, weights, extra):
+    me, band = place[0], place[1]
+    taps, channels, local = filters.shape
+    share = near.shape[1] // (2 * taps)
+    half = share // 2
+    for tap in range(taps):
+        for j in range(4):
+            start = pl.multiple_of((me ^ j) * local, local)
+            weights[pl.ds(tap * channels + j * local, local), :local] = filters[
+                tap, pl.ds(start, local), :
+            ]
+    for bit, held in enumerate((near, far)):
+        for j, d in enumerate(order):
+            first = (band ^ (d | bit)) * share
+            block = lax.div(first, local)
+            start = (block ^ me) * local + first - block * local
+            for tap in range(taps):
+                row = pl.multiple_of(tap * channels + start, 16)
+                weights[pl.ds(row, share), local:] = held[j, tap * share : (tap + 1) * share]
+            first = (band ^ (d | bit)) * half
+            block = lax.div(first, local)
+            start = (block ^ (me & 1)) * local + first - block * local
+            for tap in range(taps):
+                row = pl.multiple_of(tap * 2 * local + start, 16)
+                for k in range(2):
+                    at = taps * share + (k * taps + tap) * half
+                    extra[pl.ds(row, half), k * local : (k + 1) * local] = held[j, at : at + half]
+
+
+def fill_rows(target, piece, start, row, lanes, width):
+    for shift in range(3):
+        target[shift, pl.ds(row * width, width), lanes] = piece[
+            start + shift : start + shift + width, :
+        ]
+
+
+def fill_source(target, pieces, before, after, which, rows, width):
+    pitch = width + 8
+    local = before.shape[1]
+    for k, piece in enumerate(pieces):
+        lanes = slice(k * local, (k + 1) * local)
+        rim = (2 * k + which) * pitch
+        fill_rows(target, before, rim, 0, lanes, width)
+        for row in range(rows):
+            fill_rows(target, piece, (which * rows + row) * pitch, row + 1, lanes, width)
+        fill_rows(target, after, rim, rows + 1, lanes, width)
+
+
+def conv_kernel(rows, width, *refs):
+    pieces, (before, after, weights, extra), refs = refs[:4], refs[4:8], refs[8:]
+    grad, feat, other, upstream, image = refs
+    size, local = grad.shape
+    channels, half = 4 * local, 2 * local
+    fill_source(upstream, pieces, before, after, 0, rows, width)
+    acc = None
+    for a in range(3):
+        for b in range(3):
+            term = jnp.dot(
+                upstream[2 - b, pl.ds((2 - a) * width, size), :],
+                weights[pl.ds((3 * a + b) * channels, channels), :],
+                preferred_element_type=jnp.float32,
+            )
+            acc = term if acc is None else acc + term
+    grad[...] = acc[:, :local].astype(jnp.bfloat16)
+    other[:size] = acc[:, local:].astype(jnp.bfloat16)
+    fill_source(image, pieces, before, after, 1, rows, width)
+    acc = None
+    for a in range(3):
+        for b in range(3):
+            tap = 3 * a + b
+            for part in range(2):
+                if part:
+                    filters = extra[pl.ds(tap * half, half), :]
+                else:
+                    filters = weights[pl.ds(tap * channels, half), :]
+                term = lax.dot_general(
+                    image[b, pl.ds(a * width, size), part * half : (part + 1) * half],
+                    filters,
+                    (((1,), (1,)), ((), ())),
+                    preferred_element_type=jnp.float32,
+                )
+                acc = term if acc is None else acc + term
+    bias = [p[rows * (width + 8) + width + 2 :][:1].astype(jnp.float32) for p in pieces[:2]]
+    feat[...] = (acc[:, :local] + bias[0]).astype(jnp.bfloat16)
+    other[size:] = (acc[:, local:] + bias[1]).astype(jnp.bfloat16)
+
+
+SMEM = pl.BlockSpec(memory_space=pltpu.SMEM)
+VMEM = pl.BlockSpec(memory_space=pltpu.VMEM)
+COST = pl.CostEstimate(flops=2**20, bytes_accessed=2**20, transcendentals=0)
+PARAMS = pltpu.CompilerParams(vmem_limit_bytes=32 * 2**20)
+
+
+def assemble(order, place, filters, near, far):
+    taps, channels, local = filters.shape
+    return pl.pallas_call(
+        lambda *refs: assemble_kernel(order, *refs),
+        out_shape=[
+            jax.ShapeDtypeStruct((taps * channels, 2 * local), jnp.bfloat16),
+            jax.ShapeDtypeStruct((taps * 2 * local, 2 * local), jnp.bfloat16),
+        ],
+        in_specs=[SMEM] + [VMEM] * 3,
+        out_specs=[VMEM] * 2,
+        compiler_params=PARAMS,
+        cost_estimate=COST,
+        name="assemble",
+    )(place, filters, near, far)
+
+
+def convolve(rows, width, pieces, before, after, weights, extra):
+    local = pieces[0].shape[1]
+    size = rows * width
+    args = [*pieces, before, after, weights, extra]
+    return pl.pallas_call(
+        lambda *refs: conv_kernel(rows, width, *refs),
+        out_shape=[
+            jax.ShapeDtypeStruct((n * size, local), jnp.bfloat16) for n in (1, 1, 2)
+        ],
+        in_specs=[VMEM] * len(args),
+        out_specs=[VMEM] * 3,
+        scratch_shapes=[pltpu.VMEM((3, (rows + 2) * width, 4 * local), jnp.bfloat16)] * 2,
+        compiler_params=PARAMS,
+        cost_estimate=COST,
+        name="conv",
+    )(*args)
+
+
+def channels_last(value):
+    return jnp.pad(jnp.transpose(value, (1, 2, 0)), ((0, 0), (1, 1), (0, 0)))
+
+
+def cut(value, bias, start, width):
+    rows, _, local = value.shape
+    extra = jnp.broadcast_to(bias, (rows, 6, local))
+    piece = lax.dynamic_slice_in_dim(value, start, width + 2, axis=1)
+    return jnp.concatenate([piece, extra], axis=1).reshape(-1, local)
+
+
+def exchange(mine, near, middle, far):
+    far = swap(far, "chan", 3)
+    middle = swap(middle, "chan", 2)
+    return [mine, swap(near, "chan", 1), middle, far]
+
+
+def rims(pieces, pitch):
+    rows = pieces[0].shape[0] // (2 * pitch)
+    row = lambda p, at: p[at * pitch : (at + 1) * pitch]
+    first = jnp.concatenate([row(p, i * rows) for p in pieces for i in range(2)])
+    last = jnp.concatenate([row(p, i * rows + rows - 1) for p in pieces for i in range(2)])
+    return neighbours(first, last)
+
+
+def after(value, *others):
+    return lax.optimization_barrier((value, others))[0]
+
+
+def gather(value):
+    bands = lax.axis_size("band")
+    order = list(range(0, bands, 2))
+    held = jnp.stack([swap(value, "band", d) if d else value for d in order])
+    return held, swap(held, "band", 1), order
+
+
+def home(mine, other, side, rows):
+    turn = lambda p: jnp.transpose(p.reshape(rows, -1, p.shape[1]), (2, 0, 1))
+    mine = jnp.concatenate([turn(p) for p in mine], axis=2)
+    other = jnp.concatenate([turn(p) for p in other], axis=2)
+    first = jnp.where(side == 0, mine, other)
+    second = jnp.where(side == 0, other, mine)
+    return jnp.concatenate([first, second], axis=2)
+
+
+CHUNKS = 2
+
+
+def per_device(image, filters, bias, upstream):
+    n = lax.axis_size("chan")
+    bands = lax.axis_size("band")
+    taps, outs, local = filters.shape
+    rows, cols = image.shape[1:]
+    if n != 4 or local % 128 or cols % (256 * CHUNKS) or outs % (32 * bands) or bands < 4:
+        return plain(image, filters, bias, upstream)
+    me = lax.axis_index("chan")
+    band = lax.axis_index("band")
+    side, half = me & 1, me >> 1
+    place = jnp.stack([me, band]).astype(jnp.int32)
+    width = cols // (2 * CHUNKS)
+    pitch = width + 8
+
+    share = outs // bands
+    near = lax.dynamic_slice_in_dim(filters, band * share, share, axis=1).reshape(-1, local)
+    start = (1 - half) * (outs // 2) + band * (share // 2)
+    across = lax.dynamic_slice_in_dim(filters, start, share // 2, axis=1).reshape(-1, local)
+    parts = [swap(near, "chan", 1), swap(across, "chan", 2), swap(across, "chan", 3)]
+
+    full = [channels_last(upstream), channels_last(image)]
+    payloads = []
+    for chunk in range(CHUNKS):
+        starts = [(side ^ k) * (cols // 2) + chunk * width for k in range(2)]
+        payloads.append(
+            [jnp.concatenate([cut(v, bias, at, width) for v in full]) for at in starts]
+        )
+    payloads[0] = after(payloads[0], near, across)
+    got = []
+    for mine, other in payloads:
+        if got:
+            mine, other = after((mine, other), got[-1][2])
+        got.append(exchange(mine, other, mine, other))
+
+    held, there, order = gather(jnp.concatenate(parts))
+    weights, extra = assemble(order, place, filters, held, there)
+
+    mine, other = [[], []], [[], []]
+    for pieces in got:
+        if mine[0]:
+            pieces = after(pieces, mine[0][-1])
+        grad, feat, sent = convolve(rows, width, pieces, *rims(pieces, pitch), weights, extra)
+        sent = swap(sent, "chan", 1)
+        size = grad.shape[0]
+        for i, (kept, come) in enumerate(((grad, sent[:size]), (feat, sent[size:]))):
+            mine[i].append(kept)
+            other[i].append(come)
+    return home(mine[1], other[1], side, rows), home(mine[0], other[0], side, rows)
+
+
 def solution(mesh):
     return jax.shard_map(
         per_device,

time: 137 us -> 99 us (0.72)
  the two profiles are of different devices: /device:TPU:0 before, /device:TPU:11 now
where the time goes in v5:
time: 99 us; the launch traced here: 98.8 us
  waiting for transfers between devices  49.5 us (50%)
  starting transfers between devices  27.2 us (27%)
  local copies, waits for them, and re-layouts  9.03 us (9%)
  Pallas kernels  7.54 us (8%)
  other arithmetic  4.47 us (5%)
  between operations  1.03 us (1%)
    ppermute x15, waiting for transfers between devices, swap(): return lax.ppermute(value, axis, [(j, j ^ step) for j in range(size)])  40.1 us
    ppermute x15, starting transfers between devices, swap(): return lax.ppermute(value, axis, [(j, j ^ step) for j in range(size)])  15 us
    ppermute x4, starting transfers between devices, neighbours(): return (lax.ppermute(last, 'band', up), lax.ppermute(first, 'band', down))  12.3 us
    ppermute x4, waiting for transfers between devices, neighbours(): return (lax.ppermute(last, 'band', up), lax.ppermute(first, 'band', down))  9.31 us
    pallas_call x2, Pallas kernels, convolve(): pl.pallas_call(lambda *refs: conv_kernel(rows, width, *refs), out_shape=[...  6.25 us
    dynamic_slice x2, local copies, waits for them, and re-layouts, cut(): piece = lax.dynamic_slice_in_dim(value, start, width + 2, axis=1)  3.67 us
    concatenate x2, other arithmetic, home(): return jnp.concatenate([first, second], axis=2)  2.06 us
  transfers between devices with their start and end apart: 19, of which 10 were waited for; matrix products, arithmetic and copies ran while one was open for 9% of the time, Pallas kernels for 8%

profile of v5, /device:TPU:11, one launch (start us, length us, event | category | flops | bytes accessed | tf_op | source)
XLA Modules:
  0.0 98.8 jit_solution(11426809370020436641)
XLA Ops:
  0.6 1.0 constant_dynamic-slice_fusion
  1.6 2.3 %collective-permute-start.6 = (bf16[288,128]{1,0:T(8,128)(2,1)S(1)}, bf16[288,128]{1,0:T(8,128)(2,1)S(1)}, u32[]{:S(2)}, u32[]{:S(2)}) collective-permute-start(bf16[288,128]{1,0:T(8,128)(2,1)S(1)} %bitcast.65), channel_id=1, source_target_pairs={{0,2},{1,3},{2,0},{3,1},{4,6},{5,7},{6,4},{7,5},{8,10},{9,11},{10,... | collective-permute-start | bytes 221192 | tf_op jit(solution)/shard_map/ppermute | solution.py:11
  3.9 0.0 collective-permute-start.7
  3.9 0.9 constant_dynamic-slice_fusion.1
  4.8 1.3 %collective-permute-start.5 = (bf16[576,128]{1,0:T(8,128)(2,1)S(1)}, bf16[576,128]{1,0:T(8,128)(2,1)S(1)}, u32[]{:S(2)}, u32[]{:S(2)}) collective-permute-start(bf16[576,128]{1,0:T(8,128)(2,1)S(1)} %bitcast.64), channel_id=1, source_target_pairs={{0,1},{1,0},{2,3},{3,2},{4,5},{5,4},{6,7},{7,6},{8,9},{9,8},{10,11... | collective-permute-start | bytes 442376 | tf_op jit(solution)/shard_map/ppermute | solution.py:11
  6.1 2.6 %pad_dynamic-slice_fusion.6 = (bf16[4,130,128]{1,0,2:T(4,128)(2,1)S(1)}, bf16[4,130,128]{1,0,2:T(4,128)(2,1)S(1)}, bf16[4,130,128]{1,0,2:T(4,128)(2,1)S(1)}, bf16[4,130,128]{1,0,2:T(4,128)(2,1)S(1)}) fusion(s32[]{:T(128)S(6)} %select_n.44, bf16[4,512,128]{1,0,2:T(4,128)(2,1)} %bitcast.55, s32[]{:T(128)S(6)} %select_n.47, s32[]{:T(128)S(6)} %select_n.48, ...), kind=kLoop, calls=%fused_computation.17 | loop fusion | bytes 1056784 | tf_op jit(solution)/shard_map/dynamic_slice | solution.py:246
  8.7 0.0 copy-start.2
  8.8 1.1 %pad_dynamic-slice_fusion.2 = (bf16[4,130,128]{1,0,2:T(4,128)(2,1)S(1)}, bf16[4,130,128]{1,0,2:T(4,128)(2,1)S(1)}, bf16[4,130,128]{1,0,2:T(4,128)(2,1)S(1)}, bf16[4,130,128]{1,0,2:T(4,128)(2,1)S(1)}) fusion(s32[]{:T(128)S(6)} %select_n.44, bf16[4,512,128]{1,0,2:T(4,128)(2,1)S(1)} %bitcast.56, s32[]{:T(128)S(6)} %select_n.47, s32[]{:T(128)S(6)} %select_n.48, ...), kind=kLoop, calls=%fused_computation.13 | loop fusion | bytes 1056784 | tf_op jit(solution)/shard_map/dynamic_slice | solution.py:246
  9.9 0.2 broadcast_in_dim.2
  10.1 1.4 %pad_maximum_fusion.6 = (bf16[4,136,128]{1,0,2:T(4,128)(2,1)S(1)}, bf16[4,136,128]{1,0,2:T(4,128)(2,1)S(1)}, bf16[4,136,128]{1,0,2:T(4,128)(2,1)S(1)}, bf16[4,13...) fusion(bf16[4,6,128]{1,0,2:T(4,128)(2,1)S(1)} %broadcast_in_dim, ...), kind=kLoop, calls=%fused_computation.6 | loop fusion | flops 1740800 | bytes 2185216 | tf_op jit(solution)/shard_map/concatenate | solution.py:247
  11.5 0.2 copy.8
  11.7 0.2 copy.9
  12.0 0.2 copy.6
  12.2 0.2 copy.7
  12.5 0.3 collective-permute-start
  12.8 2.2 %collective-permute-start.1 = (bf16[1088,128]{1,0:T(8,128)(2,1)S(1)}, bf16[1088,128]{1,0:T(8,128)(2,1)S(1)}, u32[]{:S(2)}, u32[]{:S(2)}) collective-permute-start(bf16[1088,128]{1,0:T(8,128)(2,1)S(1)} %pad_maximum_fusion.11.refs_0_), channel_id=1, source_target_pairs={{0,2},{1,3},{2,0},{3,1},{4,6},{5,7},{6,4},{7,5},{8,10},{9,11},{10,... | collective-permute-start | bytes 835592 | tf_op jit(solution)/shard_map/ppermute | solution.py:11
  15.0 0.2 copy.13
  15.2 0.2 copy.14
  15.5 0.2 copy.11
  15.7 0.2 copy.12
  16.0 0.0 collective-permute-done.5
  16.0 0.0 collective-permute-done.6
  16.1 0.3 collective-permute-start.8
  16.4 1.2 %collective-permute-start.9 = (bf16[1152,128]{1,0:T(8,128)(2,1)S(1)}, bf16[1152,128]{1,0:T(8,128)(2,1)S(1)}, u32[]{:S(2)}, u32[]{:S(2)}) collective-permute-start(bf16[1152,128]{1,0:T(8,128)(2,1)S(1)} %constant_dynamic-update-slice_fusion.16), channel_id=1, source_target_pairs={{0,16},{4,20},{8,24},{12,28},{16,0},{20,4},{24,8},{28,12},{1,17},{... | collective-permute-start | bytes 884744 | tf_op jit(solution)/shard_map/ppermute | solution.py:11
  17.6 1.2 %collective-permute-start.10 = (bf16[1152,128]{1,0:T(8,128)(2,1)S(1)}, bf16[1152,128]{1,0:T(8,128)(2,1)S(1)}, u32[]{:S(2)}, u32[]{:S(2)}) collective-permute-start(bf16[1152,128]{1,0:T(8,128)(2,1)S(1)} %constant_dynamic-update-slice_fusion.16), channel_id=1, source_target_pairs={{0,24},{4,28},{8,16},{12,20},{16,8},{20,12},{24,0},{28,4},{1,25},{... | collective-permute-start | bytes 884744 | tf_op jit(solution)/shard_map/ppermute | solution.py:11
  18.8 3.8 %collective-permute-done.8 = bf16[1152,128]{1,0:T(8,128)(2,1)S(1)} collective-permute-done((bf16[1152,128]{1,0:T(8,128)(2,1)S(1)}, bf16[1152,128]{1,0:T(8,128)(2,1)S(1)}, u32[]{:S(2)}, u32[]{:S(2)}) %collective-permute-start.8) | collective-permute-done | bytes 294944 | tf_op jit(solution)/shard_map/ppermute | solution.py:11
  22.6 0.2 collective-permute-start.2
  22.8 0.0 collective-permute-done.9
  22.8 7.1 %collective-permute-done.10 = bf16[1152,128]{1,0:T(8,128)(2,1)S(1)} collective-permute-done((bf16[1152,128]{1,0:T(8,128)(2,1)S(1)}, bf16[1152,128]{1,0:T(8,128)(2,1)S(1)}, u32[]{:S(2)}, u32[]{:S(2)}) %collective-permute-start.10) | collective-permute-done | bytes 294944 | tf_op jit(solution)/shard_map/ppermute | solution.py:11
  29.9 0.1 pad_maximum_fusion.refs_2_
  30.0 3.1 %collective-permute-start.11 = (bf16[4,1152,128]{2,1,0:T(8,128)(2,1)S(1)}, bf16[4,1152,128]{2,1,0:T(8,128)(2,1)S(1)}, u32[]{:S(2)}, u32[]{:S(2)}) collective-permute-start(bf16[4,1152,128]{2,1,0:T(8,128)(2,1)S(1)} %pad_maximum_fusion.refs_2_), channel_id=1, source_target_pairs={{0,4},{4,0},{8,12},{12,8},{16,20},{20,16},{24,28},{28,24},{1,5},{5... | collective-permute-start | bytes 3538952 | tf_op jit(solution)/shard_map/ppermute | solution.py:11
  33.1 0.0 collective-permute-done.refs_1_
  33.2 7.1 %collective-permute-done.2.refs_3_ = bf16[1088,128]{1,0:T(8,128)(2,1)S(1)} collective-permute-done((bf16[1088,128]{1,0:T(8,128)(2,1)S(1)}, bf16[1088,128]{1,0:T(8,128)(2,1)S(1)}, u32[]{:S(2)}, u32[]{:S(2)}) %collective-permute-start.2) | collective-permute-done | bytes 278560 | tf_op jit(solution)/shard_map/ppermute | solution.py:11
  40.3 3.5 %collective-permute-start.3 = (bf16[1088,128]{1,0:T(8,128)(2,1)S(1)}, bf16[1088,128]{1,0:T(8,128)(2,1)S(1)}, u32[]{:S(2)}, u32[]{:S(2)}) collective-permute-start(bf16[1088,128]{1,0:T(8,128)(2,1)S(1)} %get-tuple-element.63), channel_id=1, source_target_pairs={{0,4},{4,8},{8,12},{12,16},{16,20},{20,24},{24,28},{1,5},{5,9},{9,... | collective-permute-start | bytes 835592 | tf_op jit(solution)/shard_map/ppermute | solution.py:18
  43.8 1.9 %collective-permute-start.4 = (bf16[1088,128]{1,0:T(8,128)(2,1)S(1)}, bf16[1088,128]{1,0:T(8,128)(2,1)S(1)}, u32[]{:S(2)}, u32[]{:S(2)}) collective-permute-start(bf16[1088,128]{1,0:T(8,128)(2,1)S(1)} %get-tuple-element.62), channel_id=1, source_target_pairs={{4,0},{8,4},{12,8},{16,12},{20,16},{24,20},{28,24},{5,1},{9,5},{13... | collective-permute-start | bytes 835592 | tf_op jit(solution)/shard_map/ppermute | solution.py:18
  45.7 0.1 collective-permute-start.12
  45.8 2.5 %collective-permute-start.13 = (bf16[1088,128]{1,0:T(8,128)(2,1)S(1)}, bf16[1088,128]{1,0:T(8,128)(2,1)S(1)}, u32[]{:S(2)}, u32[]{:S(2)}) collective-permute-start(bf16[1088,128]{1,0:T(8,128)(2,1)S(1)} %pad_maximum_fusion.13.refs_0_), channel_id=1, source_target_pairs={{0,2},{1,3},{2,0},{3,1},{4,6},{5,7},{6,4},{7,5},{8,10},{9,11},{10,... | collective-permute-start | bytes 835592 | tf_op jit(solution)/shard_map/ppermute | solution.py:11
  48.3 0.2 collective-permute-start.14
  48.5 0.1 pad_add_fusion.refs_0_
  48.5 1.3 %assemble.1 = (bf16[4608,256]{1,0:T(8,128)(2,1)S(1)}, bf16[2304,256]{1,0:T(8,128)(2,1)S(1)}) custom-call(s32[2]{0:T(128)S(1)} %pad_add_fusion.refs_0_, bf16[9,512,128]{2,1,0:T(8,128)(2,1)S(1)} %copy-done, bf16[4,1152,128]{2,1,0:T(8,128)(2,1)S(1)} %pad_maximum_fusion.refs_2_, bf16[4,1152,128]{2,1,0:T(8,128)(2,1)S(1)} %collective-permute-done.11.refs_3_), custom_call_target="tpu_custom_call" | custom-call | flops 1048576 | bytes 1048576 | tf_op jit(solution)/shard_map/assemble/pallas_call | solution.py:207
  49.8 2.7 %collective-permute-done.4.refs_5_ = bf16[1088,128]{1,0:T(8,128)(2,1)S(1)} collective-permute-done((bf16[1088,128]{1,0:T(8,128)(2,1)S(1)}, bf16[1088,128]{1,0:T(8,128)(2,1)S(1)}, u32[]{:S(2)}, u32[]{:S(2)}) %collective-permute-start.4) | collective-permute-done | bytes 278560 | tf_op jit(solution)/shard_map/ppermute | solution.py:18
  52.6 3.1 %conv.2 = (bf16[512,128]{1,0:T(8,128)(2,1)S(1)}, bf16[512,128]{1,0:T(8,128)(2,1)S(1)}, bf16[1024,128]{1,0:T(8,128)(2,1)S(1)}) custom-call(bf16[1088,128]{1,0:T(8,128)(2,1)S(1)} %pad_maximum_fusion.11.refs_0_, bf16[1088,128]{1,0:T(8,128)(2,1)S(1)} %collective-permute-done.refs_1_, bf16[1088,128]{1,0:T(8,128)(2,1)S(1)} %collective-permute-done.1.refs_2_, ...), custom_call_target="tpu_custom_call" | custom-call | flops 1048576 | bytes 1048576 | tf_op jit(solution)/shard_map/conv/pallas_call | solution.py:225
  55.7 1.0 %collective-permute-done.12.refs_1_ = bf16[1088,128]{1,0:T(8,128)(2,1)S(1)} collective-permute-done((bf16[1088,128]{1,0:T(8,128)(2,1)S(1)}, bf16[1088,128]{1,0:T(8,128)(2,1)S(1)}, u32[]{:S(2)}, u32[]{:S(2)}) %collective-permute-start.12) | collective-permute-done | bytes 278560 | tf_op jit(solution)/shard_map/ppermute | solution.py:11
  56.7 3.7 %collective-permute-done.13.refs_2_ = bf16[1088,128]{1,0:T(8,128)(2,1)S(1)} collective-permute-done((bf16[1088,128]{1,0:T(8,128)(2,1)S(1)}, bf16[1088,128]{1,0:T(8,128)(2,1)S(1)}, u32[]{:S(2)}, u32[]{:S(2)}) %collective-permute-start.13) | collective-permute-done | bytes 278560 | tf_op jit(solution)/shard_map/ppermute | solution.py:11
  60.4 11.8 %collective-permute-done.14.refs_3_ = bf16[1088,128]{1,0:T(8,128)(2,1)S(1)} collective-permute-done((bf16[1088,128]{1,0:T(8,128)(2,1)S(1)}, bf16[1088,128]{1,0:T(8,128)(2,1)S(1)}, u32[]{:S(2)}, u32[]{:S(2)}) %collective-permute-start.14) | collective-permute-done | bytes 278560 | tf_op jit(solution)/shard_map/ppermute | solution.py:11
  72.4 4.8 %collective-permute-start.15 = (bf16[1088,128]{1,0:T(8,128)(2,1)S(1)}, bf16[1088,128]{1,0:T(8,128)(2,1)S(1)}, u32[]{:S(2)}, u32[]{:S(2)}) collective-permute-start(bf16[1088,128]{1,0:T(8,128)(2,1)S(1)} %get-tuple-element.47), channel_id=1, source_target_pairs={{0,4},{4,8},{8,12},{12,16},{16,20},{20,24},{24,28},{1,5},{5,9},{9,... | collective-permute-start | bytes 835592 | tf_op jit(solution)/shard_map/ppermute | solution.py:18
  77.2 2.1 %collective-permute-start.16 = (bf16[1088,128]{1,0:T(8,128)(2,1)S(1)}, bf16[1088,128]{1,0:T(8,128)(2,1)S(1)}, u32[]{:S(2)}, u32[]{:S(2)}) collective-permute-start(bf16[1088,128]{1,0:T(8,128)(2,1)S(1)} %get-tuple-element.46), channel_id=1, source_target_pairs={{4,0},{8,4},{12,8},{16,12},{20,16},{24,20},{28,24},{5,1},{9,5},{13... | collective-permute-start | bytes 835592 | tf_op jit(solution)/shard_map/ppermute | solution.py:18
  79.3 0.1 collective-permute-start.17
  79.4 1.3 %collective-permute-done.15.refs_4_ = bf16[1088,128]{1,0:T(8,128)(2,1)S(1)} collective-permute-done((bf16[1088,128]{1,0:T(8,128)(2,1)S(1)}, bf16[1088,128]{1,0:T(8,128)(2,1)S(1)}, u32[]{:S(2)}, u32[]{:S(2)}) %collective-permute-start.15) | collective-permute-done | bytes 278560 | tf_op jit(solution)/shard_map/ppermute | solution.py:18
  80.6 5.3 %collective-permute-done.16.refs_5_ = bf16[1088,128]{1,0:T(8,128)(2,1)S(1)} collective-permute-done((bf16[1088,128]{1,0:T(8,128)(2,1)S(1)}, bf16[1088,128]{1,0:T(8,128)(2,1)S(1)}, u32[]{:S(2)}, u32[]{:S(2)}) %collective-permute-start.16) | collective-permute-done | bytes 278560 | tf_op jit(solution)/shard_map/ppermute | solution.py:18
  85.9 3.1 %conv.3 = (bf16[512,128]{1,0:T(8,128)(2,1)S(1)}, bf16[512,128]{1,0:T(8,128)(2,1)S(1)}, bf16[1024,128]{1,0:T(8,128)(2,1)S(1)}) custom-call(bf16[1088,128]{1,0:T(8,128)(2,1)S(1)} %pad_maximum_fusion.13.refs_0_, bf16[1088,128]{1,0:T(8,128)(2,1)S(1)} %collective-permute-done.12.refs_1_, bf16[1088,128]{1,0:T(8,128)(2,1)S(1)} %collective-permute-done.13.refs_2_, ...), custom_call_target="tpu_custom_call" | custom-call | flops 1048576 | bytes 1048576 | tf_op jit(solution)/shard_map/conv/pallas_call | solution.py:225
  89.1 0.1 collective-permute-start.18
  89.2 0.1 copy.10
  89.3 0.1 copy.18
  89.5 0.1 copy.16
  89.6 0.1 copy.20
  89.8 0.1 copy.15
  89.9 0.1 copy.19
  90.1 5.6 %collective-permute-done.18 = bf16[1024,128]{1,0:T(8,128)(2,1)S(1)} collective-permute-done((bf16[1024,128]{1,0:T(8,128)(2,1)S(1)}, bf16[1024,128]{1,0:T(8,128)(2,1)S(1)}, u32[]{:S(2)}, u32[]{:S(2)}) %collective-permute-start.18) | collective-permute-done | bytes 262176 | tf_op jit(solution)/shard_map/ppermute | solution.py:11
  95.7 0.1 copy.17
  95.9 0.1 copy.21
  96.0 0.7 broadcast_select_fusion.1
  96.7 1.0 %pad_maximum_fusion.10 = bf16[128,4,512]{2,1,0:T(4,128)(2,1)} fusion(bf16[128,4,256]{2,1,0:T(4,128)(2,1)S(1)} %get-tuple-element.35, bf16[128,4,256]{2,1,0:T(4,128)(2,1)S(1)} %get-tuple-element.34), kind=kLoop, calls=%fused_computation.10 | loop fusion | flops 1048576 | bytes 1048576 | tf_op jit(solution)/shard_map/concatenate | solution.py:281
  97.7 1.0 %pad_maximum_fusion.9 = bf16[128,4,512]{2,1,0:T(4,128)(2,1)} fusion(bf16[128,4,256]{2,1,0:T(4,128)(2,1)S(1)} %get-tuple-element.90, bf16[128,4,256]{2,1,0:T(4,128)(2,1)S(1)} %get-tuple-element.91), kind=kLoop, calls=%fused_computation.9 | loop fusion | flops 1048576 | bytes 1048576 | tf_op jit(solution)/shard_map/concatenate | solution.py:281
  (35 shorter events, 0.4 us)
Async XLA Ops:
  0.6 8.1 %copy-start.1 = (bf16[128,4,512]{2,1,0:T(4,128)(2,1)S(1)}, bf16[128,4,512]{2,1,0:T(4,128)(2,1)}, u32[]{:S(2)}) copy-start(bf16[128,4,512]{2,1,0:T(4,128)(2,1)} %param.4) | copy-start | bytes 1572868
  1.6 14.4 %collective-permute-start.6 = (bf16[288,128]{1,0:T(8,128)(2,1)S(1)}, bf16[288,128]{1,0:T(8,128)(2,1)S(1)}, u32[]{:S(2)}, u32[]{:S(2)}) collective-permute-start(bf16[288,128]{1,0:T(8,128)(2,1)S(1)} %bitcast.65), channel_id=1, source_target_pairs={{0,2},{1,3},{2,0},{3,1},{4,6},{5,7},{6,4},{7,5},{8,10},{9,11},{10,... | collective-permute-start | bytes 221192 | tf_op jit(solution)/shard_map/ppermute | solution.py:11
  3.9 12.1 %collective-permute-start.7 = (bf16[288,128]{1,0:T(8,128)(2,1)S(1)}, bf16[288,128]{1,0:T(8,128)(2,1)S(1)}, u32[]{:S(2)}, u32[]{:S(2)}) collective-permute-start(bf16[288,128]{1,0:T(8,128)(2,1)S(1)} %bitcast.66), channel_id=1, source_target_pairs={{0,3},{1,2},{2,1},{3,0},{4,7},{5,6},{6,5},{7,4},{8,11},{9,10},{10,... | collective-permute-start | bytes 221192 | tf_op jit(solution)/shard_map/ppermute | solution.py:11
  4.8 11.2 %collective-permute-start.5 = (bf16[576,128]{1,0:T(8,128)(2,1)S(1)}, bf16[576,128]{1,0:T(8,128)(2,1)S(1)}, u32[]{:S(2)}, u32[]{:S(2)}) collective-permute-start(bf16[576,128]{1,0:T(8,128)(2,1)S(1)} %bitcast.64), channel_id=1, source_target_pairs={{0,1},{1,0},{2,3},{3,2},{4,5},{5,4},{6,7},{7,6},{8,9},{9,8},{10,11... | collective-permute-start | bytes 442376 | tf_op jit(solution)/shard_map/ppermute | solution.py:11
  8.7 1.1 %copy-start.2 = (bf16[128]{0:T(256)(128)(2,1)S(1)}, bf16[128]{0:T(256)(128)(2,1)}, u32[]{:S(2)}) copy-start(bf16[128]{0:T(256)(128)(2,1)} %param.6) | copy-start | bytes 772
  12.5 20.6 %collective-permute-start = (bf16[1088,128]{1,0:T(8,128)(2,1)S(1)}, bf16[1088,128]{1,0:T(8,128)(2,1)S(1)}, u32[]{:S(2)}, u32[]{:S(2)}) collective-permute-start(bf16[1088,128]{1,0:T(8,128)(2,1)S(1)} %pad_maximum_fusion.12), channel_id=1, source_target_pairs={{0,1},{1,0},{2,3},{3,2},{4,5},{5,4},{6,7},{7,6},{8,9},{9,8},{10,11... | collective-permute-start | bytes 835592 | tf_op jit(solution)/shard_map/ppermute | solution.py:11
  12.8 20.3 %collective-permute-start.1 = (bf16[1088,128]{1,0:T(8,128)(2,1)S(1)}, bf16[1088,128]{1,0:T(8,128)(2,1)S(1)}, u32[]{:S(2)}, u32[]{:S(2)}) collective-permute-start(bf16[1088,128]{1,0:T(8,128)(2,1)S(1)} %pad_maximum_fusion.11.refs_0_), channel_id=1, source_target_pairs={{0,2},{1,3},{2,0},{3,1},{4,6},{5,7},{6,4},{7,5},{8,10},{9,11},{10,... | collective-permute-start | bytes 835592 | tf_op jit(solution)/shard_map/ppermute | solution.py:11
  16.1 6.5 %collective-permute-start.8 = (bf16[1152,128]{1,0:T(8,128)(2,1)S(1)}, bf16[1152,128]{1,0:T(8,128)(2,1)S(1)}, u32[]{:S(2)}, u32[]{:S(2)}) collective-permute-start(bf16[1152,128]{1,0:T(8,128)(2,1)S(1)} %constant_dynamic-update-slice_fusion.16), channel_id=1, source_target_pairs={{0,8},{4,12},{8,0},{12,4},{16,24},{20,28},{24,16},{28,20},{1,9},{5... | collective-permute-start | bytes 884744 | tf_op jit(solution)/shard_map/ppermute | solution.py:11
  16.4 6.4 %collective-permute-start.9 = (bf16[1152,128]{1,0:T(8,128)(2,1)S(1)}, bf16[1152,128]{1,0:T(8,128)(2,1)S(1)}, u32[]{:S(2)}, u32[]{:S(2)}) collective-permute-start(bf16[1152,128]{1,0:T(8,128)(2,1)S(1)} %constant_dynamic-update-slice_fusion.16), channel_id=1, source_target_pairs={{0,16},{4,20},{8,24},{12,28},{16,0},{20,4},{24,8},{28,12},{1,17},{... | collective-permute-start | bytes 884744 | tf_op jit(solution)/shard_map/ppermute | solution.py:11
  17.6 12.2 %collective-permute-start.10 = (bf16[1152,128]{1,0:T(8,128)(2,1)S(1)}, bf16[1152,128]{1,0:T(8,128)(2,1)S(1)}, u32[]{:S(2)}, u32[]{:S(2)}) collective-permute-start(bf16[1152,128]{1,0:T(8,128)(2,1)S(1)} %constant_dynamic-update-slice_fusion.16), channel_id=1, source_target_pairs={{0,24},{4,28},{8,16},{12,20},{16,8},{20,12},{24,0},{28,4},{1,25},{... | collective-permute-start | bytes 884744 | tf_op jit(solution)/shard_map/ppermute | solution.py:11
  22.6 17.7 %collective-permute-start.2 = (bf16[1088,128]{1,0:T(8,128)(2,1)S(1)}, bf16[1088,128]{1,0:T(8,128)(2,1)S(1)}, u32[]{:S(2)}, u32[]{:S(2)}) collective-permute-start(bf16[1088,128]{1,0:T(8,128)(2,1)S(1)} %pad_maximum_fusion.12), channel_id=1, source_target_pairs={{0,3},{1,2},{2,1},{3,0},{4,7},{5,6},{6,5},{7,4},{8,11},{9,10},{10,... | collective-permute-start | bytes 835592 | tf_op jit(solution)/shard_map/ppermute | solution.py:11
  29.8 18.7 %copy-start = (bf16[9,512,128]{2,1,0:T(8,128)(2,1)S(1)}, bf16[9,512,128]{2,1,0:T(8,128)(2,1)}, u32[]{:S(2)}) copy-start(bf16[9,512,128]{2,1,0:T(8,128)(2,1)} %refs_1_.1) | copy-start | bytes 3538948
  30.0 18.3 %collective-permute-start.11 = (bf16[4,1152,128]{2,1,0:T(8,128)(2,1)S(1)}, bf16[4,1152,128]{2,1,0:T(8,128)(2,1)S(1)}, u32[]{:S(2)}, u32[]{:S(2)}) collective-permute-start(bf16[4,1152,128]{2,1,0:T(8,128)(2,1)S(1)} %pad_maximum_fusion.refs_2_), channel_id=1, source_target_pairs={{0,4},{4,0},{8,12},{12,8},{16,20},{20,16},{24,28},{28,24},{1,5},{5... | collective-permute-start | bytes 3538952 | tf_op jit(solution)/shard_map/ppermute | solution.py:11
  40.3 9.5 %collective-permute-start.3 = (bf16[1088,128]{1,0:T(8,128)(2,1)S(1)}, bf16[1088,128]{1,0:T(8,128)(2,1)S(1)}, u32[]{:S(2)}, u32[]{:S(2)}) collective-permute-start(bf16[1088,128]{1,0:T(8,128)(2,1)S(1)} %get-tuple-element.63), channel_id=1, source_target_pairs={{0,4},{4,8},{8,12},{12,16},{16,20},{20,24},{24,28},{1,5},{5,9},{9,... | collective-permute-start | bytes 835592 | tf_op jit(solution)/shard_map/ppermute | solution.py:18
  43.8 8.8 %collective-permute-start.4 = (bf16[1088,128]{1,0:T(8,128)(2,1)S(1)}, bf16[1088,128]{1,0:T(8,128)(2,1)S(1)}, u32[]{:S(2)}, u32[]{:S(2)}) collective-permute-start(bf16[1088,128]{1,0:T(8,128)(2,1)S(1)} %get-tuple-element.62), channel_id=1, source_target_pairs={{4,0},{8,4},{12,8},{16,12},{20,16},{24,20},{28,24},{5,1},{9,5},{13... | collective-permute-start | bytes 835592 | tf_op jit(solution)/shard_map/ppermute | solution.py:18
  45.7 11.0 %collective-permute-start.12 = (bf16[1088,128]{1,0:T(8,128)(2,1)S(1)}, bf16[1088,128]{1,0:T(8,128)(2,1)S(1)}, u32[]{:S(2)}, u32[]{:S(2)}) collective-permute-start(bf16[1088,128]{1,0:T(8,128)(2,1)S(1)} %pad_maximum_fusion.14), channel_id=1, source_target_pairs={{0,1},{1,0},{2,3},{3,2},{4,5},{5,4},{6,7},{7,6},{8,9},{9,8},{10,11... | collective-permute-start | bytes 835592 | tf_op jit(solution)/shard_map/ppermute | solution.py:11
  45.8 14.6 %collective-permute-start.13 = (bf16[1088,128]{1,0:T(8,128)(2,1)S(1)}, bf16[1088,128]{1,0:T(8,128)(2,1)S(1)}, u32[]{:S(2)}, u32[]{:S(2)}) collective-permute-start(bf16[1088,128]{1,0:T(8,128)(2,1)S(1)} %pad_maximum_fusion.13.refs_0_), channel_id=1, source_target_pairs={{0,2},{1,3},{2,0},{3,1},{4,6},{5,7},{6,4},{7,5},{8,10},{9,11},{10,... | collective-permute-start | bytes 835592 | tf_op jit(solution)/shard_map/ppermute | solution.py:11
  48.3 24.0 %collective-permute-start.14 = (bf16[1088,128]{1,0:T(8,128)(2,1)S(1)}, bf16[1088,128]{1,0:T(8,128)(2,1)S(1)}, u32[]{:S(2)}, u32[]{:S(2)}) collective-permute-start(bf16[1088,128]{1,0:T(8,128)(2,1)S(1)} %pad_maximum_fusion.14), channel_id=1, source_target_pairs={{0,3},{1,2},{2,1},{3,0},{4,7},{5,6},{6,5},{7,4},{8,11},{9,10},{10,... | collective-permute-start | bytes 835592 | tf_op jit(solution)/shard_map/ppermute | solution.py:11
  72.4 8.3 %collective-permute-start.15 = (bf16[1088,128]{1,0:T(8,128)(2,1)S(1)}, bf16[1088,128]{1,0:T(8,128)(2,1)S(1)}, u32[]{:S(2)}, u32[]{:S(2)}) collective-permute-start(bf16[1088,128]{1,0:T(8,128)(2,1)S(1)} %get-tuple-element.47), channel_id=1, source_target_pairs={{0,4},{4,8},{8,12},{12,16},{16,20},{20,24},{24,28},{1,5},{5,9},{9,... | collective-permute-start | bytes 835592 | tf_op jit(solution)/shard_map/ppermute | solution.py:18
  77.2 8.8 %collective-permute-start.16 = (bf16[1088,128]{1,0:T(8,128)(2,1)S(1)}, bf16[1088,128]{1,0:T(8,128)(2,1)S(1)}, u32[]{:S(2)}, u32[]{:S(2)}) collective-permute-start(bf16[1088,128]{1,0:T(8,128)(2,1)S(1)} %get-tuple-element.46), channel_id=1, source_target_pairs={{4,0},{8,4},{12,8},{16,12},{20,16},{24,20},{28,24},{5,1},{9,5},{13... | collective-permute-start | bytes 835592 | tf_op jit(solution)/shard_map/ppermute | solution.py:18
  79.3 10.2 %collective-permute-start.17 = (bf16[1024,128]{1,0:T(8,128)(2,1)S(1)}, bf16[1024,128]{1,0:T(8,128)(2,1)S(1)}, u32[]{:S(2)}, u32[]{:S(2)}) collective-permute-start(bf16[1024,128]{1,0:T(8,128)(2,1)S(1)} %get-tuple-element.31), channel_id=1, source_target_pairs={{0,1},{1,0},{2,3},{3,2},{4,5},{5,4},{6,7},{7,6},{8,9},{9,8},{10,11... | collective-permute-start | bytes 786440 | tf_op jit(solution)/shard_map/ppermute | solution.py:11
  89.1 6.6 %collective-permute-start.18 = (bf16[1024,128]{1,0:T(8,128)(2,1)S(1)}, bf16[1024,128]{1,0:T(8,128)(2,1)S(1)}, u32[]{:S(2)}, u32[]{:S(2)}) collective-permute-start(bf16[1024,128]{1,0:T(8,128)(2,1)S(1)} %get-tuple-element.32), channel_id=1, source_target_pairs={{0,1},{1,0},{2,3},{3,2},{4,5},{5,4},{6,7},{7,6},{8,9},{9,8},{10,11... | collective-permute-start | bytes 786440 | tf_op jit(solution)/shard_map/ppermute | solution.py:11

commit v6 on v1

--- a/solution.py
+++ b/solution.py
@@ -1,6 +1,8 @@
 import jax
 import jax.numpy as jnp
 from jax import lax
+from jax.experimental import pallas as pl
+from jax.experimental.pallas import tpu as pltpu
 from jax.sharding import PartitionSpec as P
 
 
@@ -49,7 +51,7 @@
     )[0]
 
 
-def per_device(image, filters, bias, upstream):
+def plain(image, filters, bias, upstream):
     n = lax.axis_size("chan")
     bands = lax.axis_size("band")
     me = lax.axis_index("chan")
@@ -107,6 +109,265 @@
     return jnp.transpose(whole, (2, 0, 1))
 
 
+def assemble_kernel(order, place, filters, near, far, weights, extra):
+    me, band = place[0], place[1]
+    taps, channels, local = filters.shape
+    share = near.shape[1] // (2 * taps)
+    half = share // 2
+    for tap in range(taps):
+        for j in range(4):
+            start = pl.multiple_of((me ^ j) * local, local)
+            weights[pl.ds(tap * channels + j * local, local), :local] = filters[
+                tap, pl.ds(start, local), :
+            ]
+    for bit, held in enumerate((near, far)):
+        for j, d in enumerate(order):
+            first = (band ^ (d | bit)) * share
+            block = lax.div(first, local)
+            start = (block ^ me) * local + first - block * local
+            for tap in range(taps):
+                row = pl.multiple_of(tap * channels + start, 16)
+                weights[pl.ds(row, share), local:] = held[j, tap * share : (tap + 1) * share]
+            first = (band ^ (d | bit)) * half
+            block = lax.div(first, local)
+            start = (block ^ (me & 1)) * local + first - block * local
+            for tap in range(taps):
+                row = pl.multiple_of(tap * 2 * local + start, 16)
+                for k in range(2):
+                    at = taps * share + (k * taps + tap) * half
+                    extra[pl.ds(row, half), k * local : (k + 1) * local] = held[j, at : at + half]
+
+
+def assemble_kernel(order, place, filters, near, far, weights, extra):
+    me, band = place[0], place[1]
+    taps, channels, local = filters.shape
+    share = near.shape[1] // (2 * taps)
+    half = share // 2
+    for tap in range(taps):
+        for j in range(4):
+            start = pl.multiple_of((me ^ j) * local, local)
+            weights[pl.ds(tap * channels + j * local, local), :local] = filters[
+                tap, pl.ds(start, local), :
+            ]
+    for bit, held in enumerate((near, far)):
+        for j, d in enumerate(order):
+            first = (band ^ (d | bit)) * share
+            block = lax.div(first, local)
+            start = (block ^ me) * local + first - block * local
+            for tap in range(taps):
+                row = pl.multiple_of(tap * channels + start, 16)
+                weights[pl.ds(row, share), local:] = held[j, tap * share : (tap + 1) * share]
+            first = (band ^ (d | bit)) * half
+            block = lax.div(first, local)
+            start = (block ^ (me & 1)) * local + first - block * local
+            for tap in range(taps):
+                row = pl.multiple_of(tap * 2 * local + start, 16)
+                for k in range(2):
+                    at = taps * share + (k * taps + tap) * half
+                    extra[pl.ds(row, half), k * local : (k + 1) * local] = held[j, at : at + half]
+
+
+def cut_kernel(upstream, image, bias, edge, first, second):
+    rows, cols, local = upstream.shape
+    width = cols // 2
+    line = bias[...].astype(jnp.float32)
+    zero = jnp.zeros((1, local), jnp.float32)
+    for out, parts in (
+        (edge, [(v, r) for v in (upstream, image) for r in (0, rows - 1)]),
+        (first, [(upstream, r) for r in range(1, rows - 1)]),
+        (second, [(image, r) for r in range(1, rows - 1)]),
+    ):
+        for t in range(2):
+            sides = []
+            for at, (v, r) in enumerate(parts):
+                piece = v[r, t * width : (t + 1) * width]
+                for p in range(t, 4, 2):
+                    out[p, at * width : (at + 1) * width] = piece
+                left = v[r, width - 16 : width].astype(jnp.float32)[15:]
+                right = v[r, width : width + 16].astype(jnp.float32)[:1]
+                sides += [left, zero] if t else [zero, right]
+            sides += [line] + [zero] * (15 - len(sides))
+            tail = jnp.concatenate(sides).astype(jnp.bfloat16)
+            for p in range(t, 4, 2):
+                out[p, len(parts) * width :] = tail
+
+
+def rim_kernel(width, edge, first, last):
+    base = 4 * width
+    for p in range(4):
+        ends = edge[p, base:].astype(jnp.float32)
+        for out, shift in ((first, 0), (last, 1)):
+            pairs = []
+            for i in range(2):
+                at = 2 * i + shift
+                out[p, i * width : (i + 1) * width] = edge[p, at * width : (at + 1) * width]
+                pairs.append(ends[2 * at : 2 * at + 2])
+            tail = jnp.concatenate(pairs + [jnp.zeros((12, ends.shape[1]), jnp.float32)])
+            out[p, 2 * width :] = tail.astype(jnp.bfloat16)
+
+
+def fill_source(target, me, which, width, edge, inner, before, after):
+    local = edge.shape[2]
+    count = inner.shape[1] // width
+    rows = [(before, which, 2)]
+    rows += [(edge, 2 * which, 4)]
+    rows += [(inner, r, count) for r in range(count)]
+    rows += [(edge, 2 * which + 1, 4), (after, which, 2)]
+    for k in range(4):
+        p = me ^ k
+        lanes = slice(k * local, (k + 1) * local)
+        for r, (ref, at, total) in enumerate(rows):
+            middle = ref[p, at * width : (at + 1) * width]
+            ends = ref[p, total * width : total * width + 16]
+            target[1, r * width : (r + 1) * width, lanes] = middle
+            target[0, r * width : (r + 1) * width, lanes] = jnp.concatenate(
+                [ends[2 * at : 2 * at + 1], middle[:-1]]
+            )
+            target[2, r * width : (r + 1) * width, lanes] = jnp.concatenate(
+                [middle[1:], ends[2 * at + 1 : 2 * at + 2]]
+            )
+
+
+def backward_kernel(place, edge, inner, before, after, weights, mine, other, source):
+    size, local = mine.shape
+    width = (before.shape[1] - 16) // 2
+    channels = 4 * local
+    fill_source(source, place[0], 0, width, edge, inner, before, after)
+    acc = None
+    for a in range(3):
+        for b in range(3):
+            term = jnp.dot(
+                source[2 - b, pl.ds((2 - a) * width, size), :],
+                weights[pl.ds((3 * a + b) * channels, channels), :],
+                preferred_element_type=jnp.float32,
+            )
+            acc = term if acc is None else acc + term
+    mine[...] = acc[:, :local].astype(jnp.bfloat16)
+    other[...] = acc[:, local:].astype(jnp.bfloat16)
+
+
+def forward_kernel(place, edge, inner, before, after, weights, extra, mine, other, source):
+    size, local = mine.shape
+    width = (before.shape[1] - 16) // 2
+    channels, half = 4 * local, 2 * local
+    me = place[0]
+    fill_source(source, me, 1, width, edge, inner, before, after)
+    acc = None
+    for a in range(3):
+        for b in range(3):
+            tap = 3 * a + b
+            for part in range(2):
+                if part:
+                    filters = extra[pl.ds(tap * half, half), :]
+                else:
+                    filters = weights[pl.ds(tap * channels, half), :]
+                term = lax.dot_general(
+                    source[b, pl.ds(a * width, size), part * half : (part + 1) * half],
+                    filters,
+                    (((1,), (1,)), ((), ())),
+                    preferred_element_type=jnp.float32,
+                )
+                acc = term if acc is None else acc + term
+    for k, out in enumerate((mine, other)):
+        bias = edge[me ^ k, 4 * width :].astype(jnp.float32)[8:9]
+        out[...] = (acc[:, k * local : (k + 1) * local] + bias).astype(jnp.bfloat16)
+
+
+SMEM = pl.BlockSpec(memory_space=pltpu.SMEM)
+VMEM = pl.BlockSpec(memory_space=pltpu.VMEM)
+
+
+def kernel(body, shapes, args, scratch, name, placed=True):
+    return pl.pallas_call(
+        body,
+        out_shape=[jax.ShapeDtypeStruct(s, jnp.bfloat16) for s in shapes],
+        in_specs=[SMEM] * placed + [VMEM] * (len(args) - placed),
+        out_specs=[VMEM] * len(shapes),
+        scratch_shapes=[pltpu.VMEM(s, jnp.bfloat16) for s in scratch],
+        compiler_params=pltpu.CompilerParams(vmem_limit_bytes=32 * 2**20),
+        cost_estimate=pl.CostEstimate(flops=2**20, bytes_accessed=2**20, transcendentals=0),
+        name=name,
+    )(*args)
+
+
+def exchange(payload):
+    return lax.all_to_all(payload, "chan", split_axis=0, concat_axis=0, tiled=True)
+
+
+def after(value, *others):
+    return lax.optimization_barrier((value, others))[0]
+
+
+def gather(value):
+    bands = lax.axis_size("band")
+    order = list(range(0, bands, 2))
+    held = jnp.stack([swap(value, "band", d) if d else value for d in order])
+    return held, swap(held, "band", 1), order
+
+
+def home(mine, other, side, rows):
+    turn = lambda p: jnp.transpose(p.reshape(rows, -1, p.shape[1]), (2, 0, 1))
+    mine, other = turn(mine), turn(other)
+    first = jnp.where(side == 0, mine, other)
+    second = jnp.where(side == 0, other, mine)
+    return jnp.concatenate([first, second], axis=2)
+
+
+def per_device(image, filters, bias, upstream):
+    n = lax.axis_size("chan")
+    bands = lax.axis_size("band")
+    taps, outs, local = filters.shape
+    rows, cols = image.shape[1:]
+    if n != 4 or local % 128 or cols % 256 or rows != 4 or outs % (32 * bands) or bands < 4:
+        return plain(image, filters, bias, upstream)
+    me = lax.axis_index("chan")
+    band = lax.axis_index("band")
+    side, half = me & 1, me >> 1
+    place = jnp.stack([me, band]).astype(jnp.int32)
+    width = cols // 2
+
+    share = outs // bands
+    near = lax.dynamic_slice_in_dim(filters, band * share, share, axis=1).reshape(-1, local)
+    start = (1 - half) * (outs // 2) + band * (share // 2)
+    across = lax.dynamic_slice_in_dim(filters, start, share // 2, axis=1).reshape(-1, local)
+    parts = [swap(near, "chan", 1), swap(across, "chan", 2), swap(across, "chan", 3)]
+
+    last = [jnp.transpose(v, (1, 2, 0)) for v in (upstream, image)]
+    inner = (4, (rows - 2) * width + 16, local)
+    rim = (4, 2 * width + 16, local)
+    edge, first, second = kernel(
+        cut_kernel,
+        [(4, 4 * width + 16, local), inner, inner],
+        [*last, bias[None]],
+        [],
+        "cut",
+        False,
+    )
+    edge = exchange(after(edge, near, across))
+    first = exchange(after(first, edge))
+    second = exchange(after(second, first))
+
+    held, there, order = gather(jnp.concatenate(parts))
+    weights, extra = kernel(
+        lambda *refs: assemble_kernel(order, *refs),
+        [(taps * outs, 2 * local), (taps * 2 * local, 2 * local)],
+        [place, filters, held, there],
+        [],
+        "assemble",
+    )
+    ends = kernel(lambda *refs: rim_kernel(width, *refs), [rim, rim], [edge], [], "rim", False)
+    rims = neighbours(*ends)
+
+    out = [(rows * width, local)] * 2
+    source = [(3, (rows + 2) * width, 4 * local)]
+    args = [place, edge, first, *rims, weights]
+    mine, other = kernel(backward_kernel, out, args, source, "backward")
+    image_grad = home(mine, swap(other, "chan", 1), side, rows)
+    args = [place, edge, after(second, mine), *rims, weights, extra]
+    mine, other = kernel(forward_kernel, out, args, source, "forward")
+    return home(mine, swap(other, "chan", 1), side, rows), image_grad
+
+
 def solution(mesh):
     return jax.shard_map(
         per_device,

time: 137 us -> 111 us (0.81)
  the two profiles are of different devices: /device:TPU:0 before, /device:TPU:3 now
where the time goes in v6:
time: 111 us
  waiting for transfers between devices  50 us (45%)
  starting transfers between devices  30.1 us (27%)
  local copies, waits for them, and re-layouts  12.9 us (12%)
  Pallas kernels  12.2 us (11%)
  other arithmetic  4.52 us (4%)
    ppermute x9, waiting for transfers between devices, swap(): return lax.ppermute(value, axis, [(j, j ^ step) for j in range(size)])  44 us
    all_to_all x3, starting transfers between devices, exchange(): lax.all_to_all(payload, 'chan', split_axis=0, concat_axis=0, tiled=True)  12.2 us
    pallas_call x5, Pallas kernels, kernel(): pl.pallas_call(body, out_shape=[jax.ShapeDtypeStruct(s, jnp.bfloat16) for...  12.2 us
    unnamed x34, local copies, waits for them, and re-layouts  10.3 us
    ppermute x9, starting transfers between devices, swap(): return lax.ppermute(value, axis, [(j, j ^ step) for j in range(size)])  9.26 us
    ppermute x2, starting transfers between devices, neighbours(): return (lax.ppermute(last, 'band', up), lax.ppermute(first, 'band', down))  8.69 us
    ppermute x2, waiting for transfers between devices, neighbours(): return (lax.ppermute(last, 'band', up), lax.ppermute(first, 'band', down))  6.02 us
  transfers between devices with their start and end apart: 14, of which 8 were waited for; matrix products, arithmetic and copies ran while one was open for 1% of the time, Pallas kernels for 10%

profile of v6, /device:TPU:3, one launch (start us, length us, event | category | flops | bytes accessed | tf_op | source)
XLA Modules:
  0.0 110.6 jit_solution(6359188891502880890)
XLA Ops:
  0.6 0.0 copy-start.14
  0.6 1.0 constant_dynamic-slice_fusion
  1.6 0.9 constant_dynamic-slice_fusion.1
  2.5 1.5 %copy.6 = bf16[128,4,512]{0,2,1:T(8,128)(2,1)S(1)} copy(bf16[128,4,512]{2,1,0:T(4,128)(2,1)} %param.7) | data formatting | bytes 1048576 | tf_op args[3]
  4.0 0.0 copy-done.14
  4.0 0.4 copy.7
  4.4 0.0 copy-done.13
  4.4 1.6 %cut.1 = (bf16[4,1040,128]{2,1,0:T(8,128)(2,1)}, bf16[4,528,128]{2,1,0:T(8,128)(2,1)}, bf16[4,528,128]{2,1,0:T(8,128)(2,1)}) custom-call(bf16[4,512,128]{2,1,0:T(8,128)(2,1)S(1)} %bitcast.19, bf16[4,512,128]{2,1,0:T(8,128)(2,1)S(1)} %bitcast.20, bf16[1,128]{1,0:T(2,128)(2,1)S(1)} %bitcast.21), custom_call_target="tpu_custom_call" | custom-call | flops 1048576 | bytes 1048576 | tf_op jit(solution)/shard_map/cut/pallas_call | solution.py:281
  6.0 4.6 %all-to-all-start = ((bf16[4,1040,128]{2,1,0:T(8,128)(2,1)}), bf16[4,1040,128]{2,1,0:T(8,128)(2,1)S(1)}, u32[]{:S(2)}, u32[]{:S(2)}) async-start(bf16[4,1040,128]{2,1,0:T(8,128)(2,1)} %get-tuple-element.18), calls=%async_computation | async-start | bytes 2129920 | tf_op jit(solution)/shard_map/all_to_all | solution.py:294
  10.6 1.5 %collective-permute-start.2 = (bf16[576,128]{1,0:T(8,128)(2,1)S(1)}, bf16[576,128]{1,0:T(8,128)(2,1)S(1)}, u32[]{:S(2)}, u32[]{:S(2)}) collective-permute-start(bf16[576,128]{1,0:T(8,128)(2,1)S(1)} %bitcast.32), channel_id=1, source_target_pairs={{0,1},{1,0},{2,3},{3,2},{4,5},{5,4},{6,7},{7,6},{8,9},{9,8},{10,11... | collective-permute-start | bytes 442376 | tf_op jit(solution)/shard_map/ppermute | solution.py:11
  12.1 2.1 %collective-permute-start.3 = (bf16[288,128]{1,0:T(8,128)(2,1)S(1)}, bf16[288,128]{1,0:T(8,128)(2,1)S(1)}, u32[]{:S(2)}, u32[]{:S(2)}) collective-permute-start(bf16[288,128]{1,0:T(8,128)(2,1)S(1)} %bitcast.33), channel_id=1, source_target_pairs={{0,2},{1,3},{2,0},{3,1},{4,6},{5,7},{6,4},{7,5},{8,10},{9,11},{10,... | collective-permute-start | bytes 221192 | tf_op jit(solution)/shard_map/ppermute | solution.py:11
  14.2 0.0 collective-permute-start.4
  14.2 16.3 %collective-permute-done.2 = bf16[576,128]{1,0:T(8,128)(2,1)S(1)} collective-permute-done((bf16[576,128]{1,0:T(8,128)(2,1)S(1)}, bf16[576,128]{1,0:T(8,128)(2,1)S(1)}, u32[]{:S(2)}, u32[]{:S(2)}) %collective-permute-start.2) | collective-permute-done | bytes 147488 | tf_op jit(solution)/shard_map/ppermute | solution.py:11
  30.5 10.4 %collective-permute-done.3 = bf16[288,128]{1,0:T(8,128)(2,1)S(1)} collective-permute-done((bf16[288,128]{1,0:T(8,128)(2,1)S(1)}, bf16[288,128]{1,0:T(8,128)(2,1)S(1)}, u32[]{:S(2)}, u32[]{:S(2)}) %collective-permute-start.3) | collective-permute-done | bytes 73760 | tf_op jit(solution)/shard_map/ppermute | solution.py:11
  41.0 0.0 collective-permute-done.4
  41.0 1.3 %collective-permute-start.7 = (bf16[1152,128]{1,0:T(8,128)(2,1)S(1)}, bf16[1152,128]{1,0:T(8,128)(2,1)S(1)}, u32[]{:S(2)}, u32[]{:S(2)}) collective-permute-start(bf16[1152,128]{1,0:T(8,128)(2,1)S(1)} %constant_dynamic-update-slice_fusion), channel_id=1, source_target_pairs={{0,24},{4,28},{8,16},{12,20},{16,8},{20,12},{24,0},{28,4},{1,25},{... | collective-permute-start | bytes 884744 | tf_op jit(solution)/shard_map/ppermute | solution.py:11
  42.3 1.2 %collective-permute-start.5 = (bf16[1152,128]{1,0:T(8,128)(2,1)S(1)}, bf16[1152,128]{1,0:T(8,128)(2,1)}, u32[]{:S(2)}, u32[]{:S(2)}) collective-permute-start(bf16[1152,128]{1,0:T(8,128)(2,1)S(1)} %constant_dynamic-update-slice_fusion), channel_id=1, source_target_pairs={{0,8},{4,12},{8,0},{12,4},{16,24},{20,28},{24,16},{28,20},{1,9},{5... | collective-permute-start | bytes 884744 | tf_op jit(solution)/shard_map/ppermute | solution.py:11
  43.5 0.2 collective-permute-start.6
  43.7 0.0 all-to-all-done.refs_0_.edge
  43.7 3.5 %all-to-all-start.1 = ((bf16[4,528,128]{2,1,0:T(8,128)(2,1)}), bf16[4,528,128]{2,1,0:T(8,128)(2,1)S(1)}, u32[]{:S(2)}, u32[]{:S(2)}) async-start(bf16[4,528,128]{2,1,0:T(8,128)(2,1)} %get-tuple-element.21), calls=%async_computation.1 | async-start | bytes 1081344 | tf_op jit(solution)/shard_map/all_to_all | solution.py:294
  47.2 1.1 collective-permute-done.7
  48.3 6.5 %collective-permute-done.5 = bf16[1152,128]{1,0:T(8,128)(2,1)} collective-permute-done((bf16[1152,128]{1,0:T(8,128)(2,1)S(1)}, bf16[1152,128]{1,0:T(8,128)(2,1)}, u32[]{:S(2)}, u32[]{:S(2)}) %collective-permute-start.5) | collective-permute-done | bytes 294944 | tf_op jit(solution)/shard_map/ppermute | solution.py:11
  54.8 1.9 %collective-permute-done.6 = bf16[1152,128]{1,0:T(8,128)(2,1)} collective-permute-done((bf16[1152,128]{1,0:T(8,128)(2,1)S(1)}, bf16[1152,128]{1,0:T(8,128)(2,1)}, u32[]{:S(2)}, u32[]{:S(2)}) %collective-permute-start.6) | collective-permute-done | bytes 294944 | tf_op jit(solution)/shard_map/ppermute | solution.py:11
  56.7 1.2 %pad_maximum_fusion.refs_2_ = bf16[4,1152,128]{2,1,0:T(8,128)(2,1)S(1)} fusion(bf16[1,1152,128]{2,1,0:T(8,128)(2,1)S(1)} %bitcast.31, bf16[1,1152,128]{2,1,0:T(8,128)(2,1)} %bitcast.9, bf16[1,1152,128]{2,1,0:T(8,128)(2,1)} %bitcast.8, bf16[1,1152,128]{2,1,0:T(8,128)(2,1)S(1)} %bitcast.30), kind=kLoop, calls=%fused_computation | loop fusion | flops 1769472 | bytes 2359296 | tf_op jit(solution)/shard_map/stack | solution.py:304
  57.9 0.0 copy-start
  57.9 1.3 %collective-permute-start.8 = (bf16[4,1152,128]{2,1,0:T(8,128)(2,1)S(1)}, bf16[4,1152,128]{2,1,0:T(8,128)(2,1)}, u32[]{:S(2)}, u32[]{:S(2)}) collective-permute-start(bf16[4,1152,128]{2,1,0:T(8,128)(2,1)S(1)} %pad_maximum_fusion.refs_2_), channel_id=1, source_target_pairs={{0,4},{4,0},{8,12},{12,8},{16,20},{20,16},{24,28},{28,24},{1,5},{5... | collective-permute-start | bytes 3538952 | tf_op jit(solution)/shard_map/ppermute | solution.py:11
  59.2 0.0 all-to-all-done.1.inner
  59.2 4.1 %all-to-all-start.2 = ((bf16[4,528,128]{2,1,0:T(8,128)(2,1)}), bf16[4,528,128]{2,1,0:T(8,128)(2,1)}, u32[]{:S(2)}, u32[]{:S(2)}) async-start(bf16[4,528,128]{2,1,0:T(8,128)(2,1)} %get-tuple-element.22), calls=%async_computation.2 | async-start | bytes 1081344 | tf_op jit(solution)/shard_map/all_to_all | solution.py:294
  63.4 0.1 rim.1
  63.4 6.8 %collective-permute-start = (bf16[4,528,128]{2,1,0:T(8,128)(2,1)S(1)}, bf16[4,528,128]{2,1,0:T(8,128)(2,1)S(1)}, u32[]{:S(2)}, u32[]{:S(2)}) collective-permute-start(bf16[4,528,128]{2,1,0:T(8,128)(2,1)S(1)} %get-tuple-element.23), channel_id=1, source_target_pairs={{0,4},{4,8},{8,12},{12,16},{16,20},{20,24},{24,28},{1,5},{5,9},{9,... | collective-permute-start | bytes 1622024 | tf_op jit(solution)/shard_map/ppermute | solution.py:18
  70.2 1.9 %collective-permute-start.1 = (bf16[4,528,128]{2,1,0:T(8,128)(2,1)S(1)}, bf16[4,528,128]{2,1,0:T(8,128)(2,1)S(1)}, u32[]{:S(2)}, u32[]{:S(2)}) collective-permute-start(bf16[4,528,128]{2,1,0:T(8,128)(2,1)S(1)} %get-tuple-element.24), channel_id=1, source_target_pairs={{4,0},{8,4},{12,8},{16,12},{20,16},{24,20},{28,24},{5,1},{9,5},{13... | collective-permute-start | bytes 1622024 | tf_op jit(solution)/shard_map/ppermute | solution.py:18
  72.1 0.1 pad_add_fusion.refs_0_.place
  72.2 0.0 copy-done
  72.2 0.0 copy-done.6
  72.2 0.0 collective-permute-done.8.refs_3_
  72.2 0.0 copy-start.1
  72.2 1.3 %copy-done.1 = bf16[4,1152,128]{2,1,0:T(8,128)(2,1)S(1)} copy-done((bf16[4,1152,128]{2,1,0:T(8,128)(2,1)S(1)}, bf16[4,1152,128]{2,1,0:T(8,128)(2,1)}, u32[]{:S(2)}) %copy-start.1) | copy-done | bytes 1179672
  73.5 1.3 %copy-done.8 = bf16[9,512,128]{2,1,0:T(8,128)(2,1)S(1)} copy-done((bf16[9,512,128]{2,1,0:T(8,128)(2,1)S(1)}, bf16[9,512,128]{2,1,0:T(8,128)(2,1)}, u32[]{:S(2)}) %copy-start.8) | copy-done | bytes 1179672
  74.8 2.1 %assemble.1 = (bf16[4608,256]{1,0:T(8,128)(2,1)S(1)}, bf16[2304,256]{1,0:T(8,128)(2,1)S(1)}) custom-call(s32[2]{0:T(128)S(1)} %pad_add_fusion.refs_0_.place, bf16[9,512,128]{2,1,0:T(8,128)(2,1)S(1)} %copy-done.8, bf16[4,1152,128]{2,1,0:T(8,128)(2,1)S(1)} %copy-done.1, bf16[4,1152,128]{2,1,0:T(8,128)(2,1)} %collective-permute-done.8.refs_3_), custom_call_target="tpu_custom_call" | custom-call | flops 1048576 | bytes 1048576 | tf_op jit(solution)/shard_map/assemble/pallas_call | solution.py:281
  76.9 0.0 copy-start.9
  76.9 1.0 copy-done.9
  77.9 1.6 %collective-permute-done.before = bf16[4,528,128]{2,1,0:T(8,128)(2,1)S(1)} collective-permute-done((bf16[4,528,128]{2,1,0:T(8,128)(2,1)S(1)}, bf16[4,528,128]{2,1,0:T(8,128)(2,1)S(1)}, u32[]{:S(2)}, u32[]{:S(2)}) %collective-permute-start) | collective-permute-done | bytes 540704 | tf_op jit(solution)/shard_map/ppermute | solution.py:18
  79.5 4.5 %collective-permute-done.1.after = bf16[4,528,128]{2,1,0:T(8,128)(2,1)S(1)} collective-permute-done((bf16[4,528,128]{2,1,0:T(8,128)(2,1)S(1)}, bf16[4,528,128]{2,1,0:T(8,128)(2,1)S(1)}, u32[]{:S(2)}, u32[]{:S(2)}) %collective-permute-start.1) | collective-permute-done | bytes 540704 | tf_op jit(solution)/shard_map/ppermute | solution.py:18
  83.9 0.0 copy-done.7
  83.9 3.9 %backward.1 = (bf16[1024,128]{1,0:T(8,128)(2,1)S(1)}, bf16[1024,128]{1,0:T(8,128)(2,1)}) custom-call(s32[2]{0:T(128)S(1)} %pad_add_fusion.refs_0_.place, bf16[4,1040,128]{2,1,0:T(8,128)(2,1)S(1)} %all-to-all-done.refs_0_.edge, bf16[4,528,128]{2,1,0:T(8,128)(2,1)S(1)} %copy-done.7, bf16[4,528,128]{2,1,0:T(8,128)(2,1)S(1)} %collective-permute-done.before, ...), custom_call_target="tpu_custom_call" | custom-call | flops 1048576 | bytes 1048576 | tf_op jit(solution)/shard_map/backward/pallas_call | solution.py:281
  87.9 0.0 copy-done.2
  87.9 0.7 copy-done.11
  88.6 1.7 %collective-permute-start.10 = (bf16[1024,128]{1,0:T(8,128)(2,1)}, bf16[1024,128]{1,0:T(8,128)(2,1)}, u32[]{:S(2)}, u32[]{:S(2)}) collective-permute-start(bf16[1024,128]{1,0:T(8,128)(2,1)} %get-tuple-element.31), channel_id=1, source_target_pairs={{0,1},{1,0},{2,3},{3,2},{4,5},{5,4},{6,7},{7,6},{8,9},{9,8},{10,11... | collective-permute-start | bytes 786440 | tf_op jit(solution)/shard_map/ppermute | solution.py:11
  90.3 0.0 all-to-all-done.2.inner
  90.3 1.0 copy-done.3
  91.3 1.0 copy-done.5
  92.4 1.3 %copy-done.10 = bf16[2304,256]{1,0:T(8,128)(2,1)S(1)} copy-done((bf16[2304,256]{1,0:T(8,128)(2,1)S(1)}, bf16[2304,256]{1,0:T(8,128)(2,1)}, u32[]{:S(2)}) %copy-start.10) | copy-done | bytes 1179672
  93.6 4.5 %forward.1 = (bf16[1024,128]{1,0:T(8,128)(2,1)S(1)}, bf16[1024,128]{1,0:T(8,128)(2,1)}) custom-call(s32[2]{0:T(128)S(1)} %pad_add_fusion.refs_0_.place, bf16[4,1040,128]{2,1,0:T(8,128)(2,1)S(1)} %all-to-all-done.refs_0_.edge, bf16[4,528,128]{2,1,0:T(8,128)(2,1)} %all-to-all-done.2.inner, bf16[4,528,128]{2,1,0:T(8,128)(2,1)S(1)} %copy-done.3, ...), custom_call_target="tpu_custom_call" | custom-call | flops 1048576 | bytes 1048576 | tf_op jit(solution)/shard_map/forward/pallas_call | solution.py:281
  98.1 0.7 copy-done.12
  98.8 0.0 collective-permute-start.9
  98.8 0.0 collective-permute-done.10
  98.8 7.7 %collective-permute-done.9 = bf16[1024,128]{1,0:T(8,128)(2,1)S(1)} collective-permute-done((bf16[1024,128]{1,0:T(8,128)(2,1)}, bf16[1024,128]{1,0:T(8,128)(2,1)S(1)}, u32[]{:S(2)}, u32[]{:S(2)}) %collective-permute-start.9) | collective-permute-done | bytes 262176 | tf_op jit(solution)/shard_map/ppermute | solution.py:11
  106.6 1.2 %broadcast_select_fusion.1 = (bf16[1024,128]{1,0:T(8,128)(2,1)S(1)}, bf16[1024,128]{1,0:T(8,128)(2,1)S(1)}, bf16[1024,128]{1,0:T(8,128)(2,1)S(1)}, bf16[1024,128]{1,0:T(8,128)(2,1)S(1)}) fusion(bf16[1024,128]{1,0:T(8,128)(2,1)} %copy-done.11, bf16[1024,128]{1,0:T(8,128)(2,1)} %collective-permute-done.10, pred[]{:T(512)S(6)} %eq.2, ...), kind=kLoop, calls=%fused_computation.4 | loop fusion | flops 524288 | bytes 2097153 | tf_op jit(solution)/shard_map/jit(_where)/select_n | solution.py:311
  107.7 0.2 copy.10
  107.9 0.2 copy.11
  108.1 0.2 copy.8
  108.3 0.2 copy.9
  108.5 1.0 pad_maximum_fusion.2
  109.6 1.0 pad_maximum_fusion.1
  (15 shorter events, 0.1 us)
Async XLA Ops:
  0.6 3.4 %copy-start.14 = (bf16[128,4,512]{2,1,0:T(4,128)(2,1)S(1)}, bf16[128,4,512]{2,1,0:T(4,128)(2,1)}, u32[]{:S(2)}) copy-start(bf16[128,4,512]{2,1,0:T(4,128)(2,1)} %param.4) | copy-start | bytes 1572868
  1.6 2.8 %copy-start.13 = (bf16[128]{0:T(256)(128)(2,1)S(1)}, bf16[128]{0:T(256)(128)(2,1)}, u32[]{:S(2)}) copy-start(bf16[128]{0:T(256)(128)(2,1)} %param.6) | copy-start | bytes 772
  6.0 37.7 %all-to-all-start = ((bf16[4,1040,128]{2,1,0:T(8,128)(2,1)}), bf16[4,1040,128]{2,1,0:T(8,128)(2,1)S(1)}, u32[]{:S(2)}, u32[]{:S(2)}) async-start(bf16[4,1040,128]{2,1,0:T(8,128)(2,1)} %get-tuple-element.18), calls=%async_computation | async-start | bytes 2129920 | tf_op jit(solution)/shard_map/all_to_all | solution.py:294
  10.6 19.9 %collective-permute-start.2 = (bf16[576,128]{1,0:T(8,128)(2,1)S(1)}, bf16[576,128]{1,0:T(8,128)(2,1)S(1)}, u32[]{:S(2)}, u32[]{:S(2)}) collective-permute-start(bf16[576,128]{1,0:T(8,128)(2,1)S(1)} %bitcast.32), channel_id=1, source_target_pairs={{0,1},{1,0},{2,3},{3,2},{4,5},{5,4},{6,7},{7,6},{8,9},{9,8},{10,11... | collective-permute-start | bytes 442376 | tf_op jit(solution)/shard_map/ppermute | solution.py:11
  12.1 28.9 %collective-permute-start.3 = (bf16[288,128]{1,0:T(8,128)(2,1)S(1)}, bf16[288,128]{1,0:T(8,128)(2,1)S(1)}, u32[]{:S(2)}, u32[]{:S(2)}) collective-permute-start(bf16[288,128]{1,0:T(8,128)(2,1)S(1)} %bitcast.33), channel_id=1, source_target_pairs={{0,2},{1,3},{2,0},{3,1},{4,6},{5,7},{6,4},{7,5},{8,10},{9,11},{10,... | collective-permute-start | bytes 221192 | tf_op jit(solution)/shard_map/ppermute | solution.py:11
  14.2 26.8 %collective-permute-start.4 = (bf16[288,128]{1,0:T(8,128)(2,1)S(1)}, bf16[288,128]{1,0:T(8,128)(2,1)S(1)}, u32[]{:S(2)}, u32[]{:S(2)}) collective-permute-start(bf16[288,128]{1,0:T(8,128)(2,1)S(1)} %bitcast.34), channel_id=1, source_target_pairs={{0,3},{1,2},{2,1},{3,0},{4,7},{5,6},{6,5},{7,4},{8,11},{9,10},{10,... | collective-permute-start | bytes 221192 | tf_op jit(solution)/shard_map/ppermute | solution.py:11
  41.0 7.3 %collective-permute-start.7 = (bf16[1152,128]{1,0:T(8,128)(2,1)S(1)}, bf16[1152,128]{1,0:T(8,128)(2,1)S(1)}, u32[]{:S(2)}, u32[]{:S(2)}) collective-permute-start(bf16[1152,128]{1,0:T(8,128)(2,1)S(1)} %constant_dynamic-update-slice_fusion), channel_id=1, source_target_pairs={{0,24},{4,28},{8,16},{12,20},{16,8},{20,12},{24,0},{28,4},{1,25},{... | collective-permute-start | bytes 884744 | tf_op jit(solution)/shard_map/ppermute | solution.py:11
  42.3 12.5 %collective-permute-start.5 = (bf16[1152,128]{1,0:T(8,128)(2,1)S(1)}, bf16[1152,128]{1,0:T(8,128)(2,1)}, u32[]{:S(2)}, u32[]{:S(2)}) collective-permute-start(bf16[1152,128]{1,0:T(8,128)(2,1)S(1)} %constant_dynamic-update-slice_fusion), channel_id=1, source_target_pairs={{0,8},{4,12},{8,0},{12,4},{16,24},{20,28},{24,16},{28,20},{1,9},{5... | collective-permute-start | bytes 884744 | tf_op jit(solution)/shard_map/ppermute | solution.py:11
  43.5 13.2 %collective-permute-start.6 = (bf16[1152,128]{1,0:T(8,128)(2,1)S(1)}, bf16[1152,128]{1,0:T(8,128)(2,1)}, u32[]{:S(2)}, u32[]{:S(2)}) collective-permute-start(bf16[1152,128]{1,0:T(8,128)(2,1)S(1)} %constant_dynamic-update-slice_fusion), channel_id=1, source_target_pairs={{0,16},{4,20},{8,24},{12,28},{16,0},{20,4},{24,8},{28,12},{1,17},{... | collective-permute-start | bytes 884744 | tf_op jit(solution)/shard_map/ppermute | solution.py:11
  43.7 15.5 %all-to-all-start.1 = ((bf16[4,528,128]{2,1,0:T(8,128)(2,1)}), bf16[4,528,128]{2,1,0:T(8,128)(2,1)S(1)}, u32[]{:S(2)}, u32[]{:S(2)}) async-start(bf16[4,528,128]{2,1,0:T(8,128)(2,1)} %get-tuple-element.21), calls=%async_computation.1 | async-start | bytes 1081344 | tf_op jit(solution)/shard_map/all_to_all | solution.py:294
  57.9 14.3 %copy-start = (bf16[4,1152,128]{2,1,0:T(8,128)(2,1)}, bf16[4,1152,128]{2,1,0:T(8,128)(2,1)S(1)}, u32[]{:S(2)}) copy-start(bf16[4,1152,128]{2,1,0:T(8,128)(2,1)S(1)} %pad_maximum_fusion.refs_2_) | copy-start | bytes 3538948
  57.9 14.3 %collective-permute-start.8 = (bf16[4,1152,128]{2,1,0:T(8,128)(2,1)S(1)}, bf16[4,1152,128]{2,1,0:T(8,128)(2,1)}, u32[]{:S(2)}, u32[]{:S(2)}) collective-permute-start(bf16[4,1152,128]{2,1,0:T(8,128)(2,1)S(1)} %pad_maximum_fusion.refs_2_), channel_id=1, source_target_pairs={{0,4},{4,0},{8,12},{12,8},{16,20},{20,16},{24,28},{28,24},{1,5},{5... | collective-permute-start | bytes 3538952 | tf_op jit(solution)/shard_map/ppermute | solution.py:11
  59.2 13.0 %copy-start.6 = (bf16[4,528,128]{2,1,0:T(8,128)(2,1)}, bf16[4,528,128]{2,1,0:T(8,128)(2,1)S(1)}, u32[]{:S(2)}) copy-start(bf16[4,528,128]{2,1,0:T(8,128)(2,1)S(1)} %all-to-all-done.1.inner) | copy-start | bytes 1622020
  59.2 31.1 %all-to-all-start.2 = ((bf16[4,528,128]{2,1,0:T(8,128)(2,1)}), bf16[4,528,128]{2,1,0:T(8,128)(2,1)}, u32[]{:S(2)}, u32[]{:S(2)}) async-start(bf16[4,528,128]{2,1,0:T(8,128)(2,1)} %get-tuple-element.22), calls=%async_computation.2 | async-start | bytes 1081344 | tf_op jit(solution)/shard_map/all_to_all | solution.py:294
  63.4 16.0 %collective-permute-start = (bf16[4,528,128]{2,1,0:T(8,128)(2,1)S(1)}, bf16[4,528,128]{2,1,0:T(8,128)(2,1)S(1)}, u32[]{:S(2)}, u32[]{:S(2)}) collective-permute-start(bf16[4,528,128]{2,1,0:T(8,128)(2,1)S(1)} %get-tuple-element.23), channel_id=1, source_target_pairs={{0,4},{4,8},{8,12},{12,16},{16,20},{20,24},{24,28},{1,5},{5,9},{9,... | collective-permute-start | bytes 1622024 | tf_op jit(solution)/shard_map/ppermute | solution.py:18
  70.2 13.7 %collective-permute-start.1 = (bf16[4,528,128]{2,1,0:T(8,128)(2,1)S(1)}, bf16[4,528,128]{2,1,0:T(8,128)(2,1)S(1)}, u32[]{:S(2)}, u32[]{:S(2)}) collective-permute-start(bf16[4,528,128]{2,1,0:T(8,128)(2,1)S(1)} %get-tuple-element.24), channel_id=1, source_target_pairs={{4,0},{8,4},{12,8},{16,12},{20,16},{24,20},{28,24},{5,1},{9,5},{13... | collective-permute-start | bytes 1622024 | tf_op jit(solution)/shard_map/ppermute | solution.py:18
  72.2 1.3 %copy-start.1 = (bf16[4,1152,128]{2,1,0:T(8,128)(2,1)S(1)}, bf16[4,1152,128]{2,1,0:T(8,128)(2,1)}, u32[]{:S(2)}) copy-start(bf16[4,1152,128]{2,1,0:T(8,128)(2,1)} %copy-done) | copy-start | bytes 3538948
  73.5 1.3 %copy-start.8 = (bf16[9,512,128]{2,1,0:T(8,128)(2,1)S(1)}, bf16[9,512,128]{2,1,0:T(8,128)(2,1)}, u32[]{:S(2)}) copy-start(bf16[9,512,128]{2,1,0:T(8,128)(2,1)} %refs_1_.1) | copy-start | bytes 3538948
  74.8 9.2 %copy-start.7 = (bf16[4,528,128]{2,1,0:T(8,128)(2,1)S(1)}, bf16[4,528,128]{2,1,0:T(8,128)(2,1)}, u32[]{:S(2)}) copy-start(bf16[4,528,128]{2,1,0:T(8,128)(2,1)} %copy-done.6) | copy-start | bytes 1622020
  76.9 1.0 copy-start.9
  79.5 8.4 %copy-start.2 = (bf16[4,528,128]{2,1,0:T(8,128)(2,1)}, bf16[4,528,128]{2,1,0:T(8,128)(2,1)S(1)}, u32[]{:S(2)}) copy-start(bf16[4,528,128]{2,1,0:T(8,128)(2,1)S(1)} %collective-permute-done.before) | copy-start | bytes 1622020
  83.9 3.9 %copy-start.4 = (bf16[4,528,128]{2,1,0:T(8,128)(2,1)}, bf16[4,528,128]{2,1,0:T(8,128)(2,1)S(1)}, u32[]{:S(2)}) copy-start(bf16[4,528,128]{2,1,0:T(8,128)(2,1)S(1)} %collective-permute-done.1.after) | copy-start | bytes 1622020
  87.9 0.7 copy-start.11
  88.6 10.3 %collective-permute-start.10 = (bf16[1024,128]{1,0:T(8,128)(2,1)}, bf16[1024,128]{1,0:T(8,128)(2,1)}, u32[]{:S(2)}, u32[]{:S(2)}) collective-permute-start(bf16[1024,128]{1,0:T(8,128)(2,1)} %get-tuple-element.31), channel_id=1, source_target_pairs={{0,1},{1,0},{2,3},{3,2},{4,5},{5,4},{6,7},{7,6},{8,9},{9,8},{10,11... | collective-permute-start | bytes 786440 | tf_op jit(solution)/shard_map/ppermute | solution.py:11
  90.3 1.0 copy-start.3
  91.3 1.0 copy-start.5
  92.4 1.3 %copy-start.10 = (bf16[2304,256]{1,0:T(8,128)(2,1)S(1)}, bf16[2304,256]{1,0:T(8,128)(2,1)}, u32[]{:S(2)}) copy-start(bf16[2304,256]{1,0:T(8,128)(2,1)} %copy-done.9) | copy-start | bytes 3538948
  98.1 0.7 copy-start.12
  98.8 7.7 %collective-permute-start.9 = (bf16[1024,128]{1,0:T(8,128)(2,1)}, bf16[1024,128]{1,0:T(8,128)(2,1)S(1)}, u32[]{:S(2)}, u32[]{:S(2)}) collective-permute-start(bf16[1024,128]{1,0:T(8,128)(2,1)} %get-tuple-element.30), channel_id=1, source_target_pairs={{0,1},{1,0},{2,3},{3,2},{4,5},{5,4},{6,7},{7,6},{8,9},{9,8},{10,11... | collective-permute-start | bytes 786440 | tf_op jit(solution)/shard_map/ppermute | solution.py:11

commit v7 on v6

--- a/solution.py
+++ b/solution.py
@@ -167,72 +167,75 @@
                     extra[pl.ds(row, half), k * local : (k + 1) * local] = held[j, at : at + half]
 
 
-def cut_kernel(upstream, image, bias, edge, first, second):
-    rows, cols, local = upstream.shape
-    width = cols // 2
+def cut_kernel(rows, place, *refs):
+    sources, (bias, mine, other) = refs[:-3], refs[-3:]
+    side = place[0] & 1
+    local = bias.shape[1]
+    width = sources[0].shape[1] // 2
+    pitch = width + 8
     line = bias[...].astype(jnp.float32)
     zero = jnp.zeros((1, local), jnp.float32)
-    for out, parts in (
-        (edge, [(v, r) for v in (upstream, image) for r in (0, rows - 1)]),
-        (first, [(upstream, r) for r in range(1, rows - 1)]),
-        (second, [(image, r) for r in range(1, rows - 1)]),
-    ):
-        for t in range(2):
-            sides = []
-            for at, (v, r) in enumerate(parts):
-                piece = v[r, t * width : (t + 1) * width]
-                for p in range(t, 4, 2):
-                    out[p, at * width : (at + 1) * width] = piece
-                left = v[r, width - 16 : width].astype(jnp.float32)[15:]
-                right = v[r, width : width + 16].astype(jnp.float32)[:1]
-                sides += [left, zero] if t else [zero, right]
-            sides += [line] + [zero] * (15 - len(sides))
-            tail = jnp.concatenate(sides).astype(jnp.bfloat16)
-            for p in range(t, 4, 2):
-                out[p, len(parts) * width :] = tail
-
-
-def rim_kernel(width, edge, first, last):
-    base = 4 * width
-    for p in range(4):
-        ends = edge[p, base:].astype(jnp.float32)
-        for out, shift in ((first, 0), (last, 1)):
-            pairs = []
-            for i in range(2):
-                at = 2 * i + shift
-                out[p, i * width : (i + 1) * width] = edge[p, at * width : (at + 1) * width]
-                pairs.append(ends[2 * at : 2 * at + 2])
-            tail = jnp.concatenate(pairs + [jnp.zeros((12, ends.shape[1]), jnp.float32)])
-            out[p, 2 * width :] = tail.astype(jnp.bfloat16)
-
-
-def fill_source(target, me, which, width, edge, inner, before, after):
-    local = edge.shape[2]
-    count = inner.shape[1] // width
-    rows = [(before, which, 2)]
-    rows += [(edge, 2 * which, 4)]
-    rows += [(inner, r, count) for r in range(count)]
-    rows += [(edge, 2 * which + 1, 4), (after, which, 2)]
+    rest = jnp.concatenate([line, zero, zero, zero, zero, zero])
+    at = 0
+    for source in sources:
+        for r in rows:
+            left = source[r, width - 16 : width].astype(jnp.float32)[15:]
+            right = source[r, width : width + 16].astype(jnp.float32)[:1]
+            ends = (zero, right), (left, zero)
+            pieces = []
+            for t, (before, behind) in enumerate(ends):
+                tail = jnp.concatenate([behind, line, rest]).astype(jnp.bfloat16)
+                pieces.append(
+                    jnp.concatenate(
+                        [
+                            before.astype(jnp.bfloat16),
+                            source[r, t * width : (t + 1) * width],
+                            tail[:7],
+                        ]
+                    )
+                )
+            first = side == 0
+            mine[at : at + pitch] = jnp.where(first, pieces[0], pieces[1])
+            other[at : at + pitch] = jnp.where(first, pieces[1], pieces[0])
+            at += pitch
+
+
+def rim_kernel(width, *refs):
+    pieces, (first, last) = refs[:4], refs[4:]
+    pitch = width + 8
+    for k, piece in enumerate(pieces):
+        for i in range(2):
+            for out, end in ((first, 0), (last, 1)):
+                at = (2 * i + end) * pitch
+                out[(2 * k + i) * pitch : (2 * k + i + 1) * pitch] = piece[at : at + pitch]
+
+
+def fill_rows(target, piece, start, row, lanes, width):
+    for shift in range(3):
+        target[shift, row * width : (row + 1) * width, lanes] = piece[
+            start + shift : start + shift + width
+        ]
+
+
+def fill_source(target, which, width, edges, inners, before, after):
+    local = before.shape[1]
+    pitch = width + 8
+    count = inners[0].shape[0] // pitch
     for k in range(4):
-        p = me ^ k
         lanes = slice(k * local, (k + 1) * local)
-        for r, (ref, at, total) in enumerate(rows):
-            middle = ref[p, at * width : (at + 1) * width]
-            ends = ref[p, total * width : total * width + 16]
-            target[1, r * width : (r + 1) * width, lanes] = middle
-            target[0, r * width : (r + 1) * width, lanes] = jnp.concatenate(
-                [ends[2 * at : 2 * at + 1], middle[:-1]]
-            )
-            target[2, r * width : (r + 1) * width, lanes] = jnp.concatenate(
-                [middle[1:], ends[2 * at + 1 : 2 * at + 2]]
-            )
-
-
-def backward_kernel(place, edge, inner, before, after, weights, mine, other, source):
+        rows = [(before, 2 * k + which), (edges[k], 2 * which)]
+        rows += [(inners[k], r) for r in range(count)]
+        rows += [(edges[k], 2 * which + 1), (after, 2 * k + which)]
+        for r, (ref, at) in enumerate(rows):
+            fill_rows(target, ref, at * pitch, r, lanes, width)
+
+
+def backward_kernel(*refs):
+    edges, inners, (before, after, weights, mine, other, source) = refs[:4], refs[4:8], refs[8:]
     size, local = mine.shape
-    width = (before.shape[1] - 16) // 2
+    width = before.shape[0] // 8 - 8
     channels = 4 * local
-    fill_source(source, place[0], 0, width, edge, inner, before, after)
+    fill_source(source, 0, width, edges, inners, before, after)
     acc = None
     for a in range(3):
         for b in range(3):
@@ -246,12 +249,13 @@
     other[...] = acc[:, local:].astype(jnp.bfloat16)
 
 
-def forward_kernel(place, edge, inner, before, after, weights, extra, mine, other, source):
+def forward_kernel(*refs):
+    edges, inners, refs = refs[:4], refs[4:8], refs[8:]
+    before, after, weights, extra, mine, other, source = refs
     size, local = mine.shape
-    width = (before.shape[1] - 16) // 2
+    width = before.shape[0] // 8 - 8
     channels, half = 4 * local, 2 * local
-    me = place[0]
-    fill_source(source, me, 1, width, edge, inner, before, after)
+    fill_source(source, 1, width, edges, inners, before, after)
     acc = None
     for a in range(3):
         for b in range(3):
@@ -269,7 +273,7 @@
                 )
                 acc = term if acc is None else acc + term
     for k, out in enumerate((mine, other)):
-        bias = edge[me ^ k, 4 * width :].astype(jnp.float32)[8:9]
+        bias = edges[k][width : width + 8, :].astype(jnp.float32)[2:3]
         out[...] = (acc[:, k * local : (k + 1) * local] + bias).astype(jnp.bfloat16)
 
 
@@ -277,7 +281,7 @@
 VMEM = pl.BlockSpec(memory_space=pltpu.VMEM)
 
 
-def kernel(body, shapes, args, scratch, name, placed=True):
+def kernel(body, shapes, args, scratch, name, placed=False, flops=2**20):
     return pl.pallas_call(
         body,
         out_shape=[jax.ShapeDtypeStruct(s, jnp.bfloat16) for s in shapes],
@@ -285,13 +289,22 @@
         out_specs=[VMEM] * len(shapes),
         scratch_shapes=[pltpu.VMEM(s, jnp.bfloat16) for s in scratch],
         compiler_params=pltpu.CompilerParams(vmem_limit_bytes=32 * 2**20),
-        cost_estimate=pl.CostEstimate(flops=2**20, bytes_accessed=2**20, transcendentals=0),
+        cost_estimate=pl.CostEstimate(flops=flops, bytes_accessed=2**20, transcendentals=0),
         name=name,
     )(*args)
 
 
-def exchange(payload):
-    return lax.all_to_all(payload, "chan", split_axis=0, concat_axis=0, tiled=True)
+def cut(place, sources, bias, rows, name, flops):
+    local = bias.shape[1]
+    shape = (len(sources) * len(rows) * (sources[0].shape[1] // 2 + 8), local)
+    body = lambda *refs: cut_kernel(rows, *refs)
+    return kernel(body, [shape] * 2, [place, *sources, bias], [], name, True, flops)
+
+
+def exchange(mine, other):
+    far = swap(other, "chan", 3)
+    middle = swap(mine, "chan", 2)
+    return [mine, swap(other, "chan", 1), middle, far]
 
 
 def after(value, *others):
@@ -311,6 +324,9 @@
     first = jnp.where(side == 0, mine, other)
     second = jnp.where(side == 0, other, mine)
     return jnp.concatenate([first, second], axis=2)
+
+
+MICROSECOND = 10**9
 
 
 def per_device(image, filters, bias, upstream):
@@ -332,20 +348,19 @@
     across = lax.dynamic_slice_in_dim(filters, start, share // 2, axis=1).reshape(-1, local)
     parts = [swap(near, "chan", 1), swap(across, "chan", 2), swap(across, "chan", 3)]
 
-    last = [jnp.transpose(v, (1, 2, 0)) for v in (upstream, image)]
-    inner = (4, (rows - 2) * width + 16, local)
-    rim = (4, 2 * width + 16, local)
-    edge, first, second = kernel(
-        cut_kernel,
-        [(4, 4 * width + 16, local), inner, inner],
-        [*last, bias[None]],
-        [],
-        "cut",
-        False,
-    )
-    edge = exchange(after(edge, near, across))
-    first = exchange(after(first, edge))
-    second = exchange(after(second, first))
+    upstream, image = [jnp.transpose(v, (1, 2, 0)) for v in (upstream, image)]
+    line = bias[None]
+    edge = cut(place, [upstream, image], line, (0, rows - 1), "cut_edge", 2**20)
+    edge = exchange(*after(edge, near, across))
+    middle = range(1, rows - 1)
+    upstream = after(upstream, edge[1])
+    early = cut(place, [upstream], line, middle, "cut_first", 5 * MICROSECOND)
+    edge = after(edge, early)
+    first = exchange(*early)
+    image = after(image, first[1:])
+    late = cut(place, [image], line, middle, "cut_second", 18 * MICROSECOND)
+    first = after(first, late)
+    second = exchange(*late)
 
     held, there, order = gather(jnp.concatenate(parts))
     weights, extra = kernel(
@@ -354,18 +369,21 @@
         [place, filters, held, there],
         [],
         "assemble",
+        True,
     )
-    ends = kernel(lambda *refs: rim_kernel(width, *refs), [rim, rim], [edge], [], "rim", False)
-    rims = neighbours(*ends)
+    rim = (8 * (width + 8), local)
+    rims = neighbours(*kernel(lambda *refs: rim_kernel(width, *refs), [rim] * 2, edge, [], "rim", False, 16 * MICROSECOND))
 
     out = [(rows * width, local)] * 2
     source = [(3, (rows + 2) * width, 4 * local)]
-    args = [place, edge, first, *rims, weights]
-    mine, other = kernel(backward_kernel, out, args, source, "backward")
-    image_grad = home(mine, swap(other, "chan", 1), side, rows)
-    args = [place, edge, after(second, mine), *rims, weights, extra]
-    mine, other = kernel(forward_kernel, out, args, source, "forward")
-    return home(mine, swap(other, "chan", 1), side, rows), image_grad
+    args = [*edge, *first, *rims, weights]
+    mine, other = kernel(backward_kernel, out, args, source, "backward", False, 10 * MICROSECOND)
+    other = swap(other, "chan", 1)
+    image_grad = home(mine, other, side, rows)
+    args = [*edge, *after(second, mine), *rims, weights, extra]
+    mine, sent = kernel(forward_kernel, out, args, source, "forward", False, 5 * MICROSECOND)
+    other = swap(after(sent, other), "chan", 1)
+    return home(mine, other, side, rows), image_grad
 
 
 def solution(mesh):

time: 111 us -> 92.2 us (0.83)
  the two profiles are of different devices: /device:TPU:3 before, /device:TPU:0 now
where the time goes in v7:
time: 92.2 us; the launch traced here: 92 us
  starting transfers between devices  42 us (46%)
  waiting for transfers between devices  32.6 us (35%)
  Pallas kernels  9.51 us (10%)
  local copies, waits for them, and re-layouts  4.58 us (5%)
  other arithmetic  2.36 us (3%)
    ppermute x18, starting transfers between devices, swap(): return lax.ppermute(value, axis, [(j, j ^ step) for j in range(size)])  37.7 us
    ppermute x18, waiting for transfers between devices, swap(): return lax.ppermute(value, axis, [(j, j ^ step) for j in range(size)])  32.6 us
    pallas_call x7, Pallas kernels, kernel(): pl.pallas_call(body, out_shape=[jax.ShapeDtypeStruct(s, jnp.bfloat16) for...  9.51 us
    ppermute x2, starting transfers between devices, neighbours(): return (lax.ppermute(last, 'band', up), lax.ppermute(first, 'band', down))  4.34 us
    concatenate x2, other arithmetic, home(): return jnp.concatenate([first, second], axis=2)  2.06 us
    unnamed x10, local copies, waits for them, and re-layouts  1.92 us
  transfers between devices with their start and end apart: 20, of which 6 were waited for; matrix products, arithmetic and copies ran while one was open for 0% of the time, Pallas kernels for 10%

profile of v7, /device:TPU:0, one launch (start us, length us, event | category | flops | bytes accessed | tf_op | source)
XLA Modules:
  0.0 92.0 jit_solution(6039961776830146209)
XLA Ops:
  0.6 0.0 copy-start.2
  0.6 1.0 %constant_dynamic-slice_fusion = bf16[9,32,128]{2,1,0:T(8,128)(2,1)S(1)} fusion(bf16[9,512,128]{2,1,0:T(8,128)(2,1)} %refs_1_.1, s32[]{:T(128)S(6)} %select_n.52), kind=kLoop, calls=%fused_computation.11 | loop fusion | bytes 147460 | tf_op jit(solution)/shard_map/dynamic_slice | solution.py:348
  1.6 0.9 %constant_dynamic-slice_fusion.1 = bf16[9,64,128]{2,1,0:T(8,128)(2,1)S(1)} fusion(bf16[9,512,128]{2,1,0:T(8,128)(2,1)} %refs_1_.1, s32[]{:T(128)S(6)} %select_n.51), kind=kLoop, calls=%fused_computation.12 | loop fusion | bytes 294916 | tf_op jit(solution)/shard_map/dynamic_slice | solution.py:346
  2.5 1.5 %copy.6 = bf16[128,4,512]{0,2,1:T(8,128)(2,1)S(1)} copy(bf16[128,4,512]{2,1,0:T(4,128)(2,1)} %param.7) | data formatting | bytes 1048576 | tf_op args[3]
  4.0 0.0 copy-done.2
  4.0 0.4 copy.7
  4.4 0.1 pad_add_fusion.refs_0_
  4.5 0.0 copy-done.1
  4.5 0.7 cut_edge.1
  5.2 3.1 %collective-permute-start = (bf16[1056,128]{1,0:T(8,128)(2,1)S(1)}, bf16[1056,128]{1,0:T(8,128)(2,1)S(1)}, u32[]{:S(2)}, u32[]{:S(2)}) collective-permute-start(bf16[1056,128]{1,0:T(8,128)(2,1)S(1)} %get-tuple-element.36), channel_id=1, source_target_pairs={{0,1},{1,0},{2,3},{3,2},{4,5},{5,4},{6,7},{7,6},{8,9},{9,8},{10,11... | collective-permute-start | bytes 811016 | tf_op jit(solution)/shard_map/ppermute | solution.py:11
  8.3 0.1 collective-permute-start.11
  8.4 3.0 %collective-permute-start.12 = (bf16[288,128]{1,0:T(8,128)(2,1)S(1)}, bf16[288,128]{1,0:T(8,128)(2,1)S(1)}, u32[]{:S(2)}, u32[]{:S(2)}) collective-permute-start(bf16[288,128]{1,0:T(8,128)(2,1)S(1)} %bitcast.39), channel_id=1, source_target_pairs={{0,2},{1,3},{2,0},{3,1},{4,6},{5,7},{6,4},{7,5},{8,10},{9,11},{10,... | collective-permute-start | bytes 221192 | tf_op jit(solution)/shard_map/ppermute | solution.py:11
  11.3 1.3 %collective-permute-start.13 = (bf16[288,128]{1,0:T(8,128)(2,1)S(1)}, bf16[288,128]{1,0:T(8,128)(2,1)S(1)}, u32[]{:S(2)}, u32[]{:S(2)}) collective-permute-start(bf16[288,128]{1,0:T(8,128)(2,1)S(1)} %bitcast.40), channel_id=1, source_target_pairs={{0,3},{1,2},{2,1},{3,0},{4,7},{5,6},{6,5},{7,4},{8,11},{9,10},{10,... | collective-permute-start | bytes 221192 | tf_op jit(solution)/shard_map/ppermute | solution.py:11
  12.7 2.5 %collective-permute-start.2 = (bf16[1056,128]{1,0:T(8,128)(2,1)S(1)}, bf16[1056,128]{1,0:T(8,128)(2,1)S(1)}, u32[]{:S(2)}, u32[]{:S(2)}) collective-permute-start(bf16[1056,128]{1,0:T(8,128)(2,1)S(1)} %get-tuple-element.36), channel_id=1, source_target_pairs={{0,3},{1,2},{2,1},{3,0},{4,7},{5,6},{6,5},{7,4},{8,11},{9,10},{10,... | collective-permute-start | bytes 811016 | tf_op jit(solution)/shard_map/ppermute | solution.py:11
  15.2 4.4 %collective-permute-done.11 = bf16[576,128]{1,0:T(8,128)(2,1)S(1)} collective-permute-done((bf16[576,128]{1,0:T(8,128)(2,1)S(1)}, bf16[576,128]{1,0:T(8,128)(2,1)S(1)}, u32[]{:S(2)}, u32[]{:S(2)}) %collective-permute-start.11) | collective-permute-done | bytes 147488 | tf_op jit(solution)/shard_map/ppermute | solution.py:11
  19.5 3.0 %collective-permute-start.1 = (bf16[1056,128]{1,0:T(8,128)(2,1)S(1)}, bf16[1056,128]{1,0:T(8,128)(2,1)S(1)}, u32[]{:S(2)}, u32[]{:S(2)}) collective-permute-start(bf16[1056,128]{1,0:T(8,128)(2,1)S(1)} %get-tuple-element.40.refs_0_), channel_id=1, source_target_pairs={{0,2},{1,3},{2,0},{3,1},{4,6},{5,7},{6,4},{7,5},{8,10},{9,11},{10,... | collective-permute-start | bytes 811016 | tf_op jit(solution)/shard_map/ppermute | solution.py:11
  22.5 0.0 collective-permute-done.refs_1_
  22.5 0.6 cut_first.1
  23.2 7.7 %collective-permute-start.3 = (bf16[528,128]{1,0:T(8,128)(2,1)S(1)}, bf16[528,128]{1,0:T(8,128)(2,1)S(1)}, u32[]{:S(2)}, u32[]{:S(2)}) collective-permute-start(bf16[528,128]{1,0:T(8,128)(2,1)S(1)} %get-tuple-element.39), channel_id=1, source_target_pairs={{0,1},{1,0},{2,3},{3,2},{4,5},{5,4},{6,7},{7,6},{8,9},{9,8},{10,11... | collective-permute-start | bytes 405512 | tf_op jit(solution)/shard_map/ppermute | solution.py:11
  30.9 0.0 collective-permute-done.12
  30.9 0.0 collective-permute-done.13
  30.9 2.5 %collective-permute-start.16 = (bf16[1152,128]{1,0:T(8,128)(2,1)S(1)}, bf16[1152,128]{1,0:T(8,128)(2,1)S(1)}, u32[]{:S(2)}, u32[]{:S(2)}) collective-permute-start(bf16[1152,128]{1,0:T(8,128)(2,1)S(1)} %constant_dynamic-update-slice_fusion), channel_id=1, source_target_pairs={{0,24},{4,28},{8,16},{12,20},{16,8},{20,12},{24,0},{28,4},{1,25},{... | collective-permute-start | bytes 884744 | tf_op jit(solution)/shard_map/ppermute | solution.py:11
  33.4 0.5 collective-permute-start.14
  34.0 7.9 %collective-permute-done.1.refs_2_ = bf16[1056,128]{1,0:T(8,128)(2,1)S(1)} collective-permute-done((bf16[1056,128]{1,0:T(8,128)(2,1)S(1)}, bf16[1056,128]{1,0:T(8,128)(2,1)S(1)}, u32[]{:S(2)}, u32[]{:S(2)}) %collective-permute-start.1) | collective-permute-done | bytes 270368 | tf_op jit(solution)/shard_map/ppermute | solution.py:11
  41.9 1.6 %collective-permute-start.15 = (bf16[1152,128]{1,0:T(8,128)(2,1)S(1)}, bf16[1152,128]{1,0:T(8,128)(2,1)S(1)}, u32[]{:S(2)}, u32[]{:S(2)}) collective-permute-start(bf16[1152,128]{1,0:T(8,128)(2,1)S(1)} %constant_dynamic-update-slice_fusion), channel_id=1, source_target_pairs={{0,16},{4,20},{8,24},{12,28},{16,0},{20,4},{24,8},{28,12},{1,17},{... | collective-permute-start | bytes 884744 | tf_op jit(solution)/shard_map/ppermute | solution.py:11
  43.4 0.0 collective-permute-done.2.refs_3_
  43.4 0.0 collective-permute-start.4
  43.5 0.0 collective-permute-done.3.refs_5_
  43.5 2.8 %collective-permute-start.5 = (bf16[528,128]{1,0:T(8,128)(2,1)S(1)}, bf16[528,128]{1,0:T(8,128)(2,1)S(1)}, u32[]{:S(2)}, u32[]{:S(2)}) collective-permute-start(bf16[528,128]{1,0:T(8,128)(2,1)S(1)} %get-tuple-element.39), channel_id=1, source_target_pairs={{0,3},{1,2},{2,1},{3,0},{4,7},{5,6},{6,5},{7,4},{8,11},{9,10},{10,... | collective-permute-start | bytes 405512 | tf_op jit(solution)/shard_map/ppermute | solution.py:11
  46.2 0.1 rim.1
  46.3 7.6 %collective-permute-done.4.refs_6_ = bf16[528,128]{1,0:T(8,128)(2,1)S(1)} collective-permute-done((bf16[528,128]{1,0:T(8,128)(2,1)S(1)}, bf16[528,128]{1,0:T(8,128)(2,1)S(1)}, u32[]{:S(2)}, u32[]{:S(2)}) %collective-permute-start.4) | collective-permute-done | bytes 135200 | tf_op jit(solution)/shard_map/ppermute | solution.py:11
  53.9 1.3 %collective-permute-start.10 = (bf16[2112,128]{1,0:T(8,128)(2,1)S(1)}, bf16[2112,128]{1,0:T(8,128)(2,1)S(1)}, u32[]{:S(2)}, u32[]{:S(2)}) collective-permute-start(bf16[2112,128]{1,0:T(8,128)(2,1)S(1)} %get-tuple-element.52), channel_id=1, source_target_pairs={{4,0},{8,4},{12,8},{16,12},{20,16},{24,20},{28,24},{5,1},{9,5},{13... | collective-permute-start | bytes 1622024 | tf_op jit(solution)/shard_map/ppermute | solution.py:18
  55.2 0.0 collective-permute-done.5.refs_7_
  55.2 3.1 %collective-permute-start.9 = (bf16[2112,128]{1,0:T(8,128)(2,1)S(1)}, bf16[2112,128]{1,0:T(8,128)(2,1)S(1)}, u32[]{:S(2)}, u32[]{:S(2)}) collective-permute-start(bf16[2112,128]{1,0:T(8,128)(2,1)S(1)} %get-tuple-element.51), channel_id=1, source_target_pairs={{0,4},{4,8},{8,12},{12,16},{16,20},{20,24},{24,28},{1,5},{5,9},{9,... | collective-permute-start | bytes 1622024 | tf_op jit(solution)/shard_map/ppermute | solution.py:18
  58.3 0.0 collective-permute-done.16
  58.3 0.0 collective-permute-done.14
  58.3 0.0 collective-permute-done.15
  58.3 0.2 pad_maximum_fusion.refs_2_
  58.5 0.0 copy-start
  58.5 1.1 %collective-permute-start.17 = (bf16[4,1152,128]{2,1,0:T(8,128)(2,1)S(1)}, bf16[4,1152,128]{2,1,0:T(8,128)(2,1)S(1)}, u32[]{:S(2)}, u32[]{:S(2)}) collective-permute-start(bf16[4,1152,128]{2,1,0:T(8,128)(2,1)S(1)} %pad_maximum_fusion.refs_2_), channel_id=1, source_target_pairs={{0,4},{4,0},{8,12},{12,8},{16,20},{20,16},{24,28},{28,24},{1,5},{5... | collective-permute-start | bytes 3538952 | tf_op jit(solution)/shard_map/ppermute | solution.py:11
  59.6 0.6 cut_second.1
  60.2 1.4 %collective-permute-start.6 = (bf16[528,128]{1,0:T(8,128)(2,1)S(1)}, bf16[528,128]{1,0:T(8,128)(2,1)S(1)}, u32[]{:S(2)}, u32[]{:S(2)}) collective-permute-start(bf16[528,128]{1,0:T(8,128)(2,1)S(1)} %get-tuple-element.46), channel_id=1, source_target_pairs={{0,1},{1,0},{2,3},{3,2},{4,5},{5,4},{6,7},{7,6},{8,9},{9,8},{10,11... | collective-permute-start | bytes 405512 | tf_op jit(solution)/shard_map/ppermute | solution.py:11
  61.7 1.3 %collective-permute-start.7 = (bf16[528,128]{1,0:T(8,128)(2,1)S(1)}, bf16[528,128]{1,0:T(8,128)(2,1)S(1)}, u32[]{:S(2)}, u32[]{:S(2)}) collective-permute-start(bf16[528,128]{1,0:T(8,128)(2,1)S(1)} %get-tuple-element.55.refs_4_), channel_id=1, source_target_pairs={{0,2},{1,3},{2,0},{3,1},{4,6},{5,7},{6,4},{7,5},{8,10},{9,11},{10,... | collective-permute-start | bytes 405512 | tf_op jit(solution)/shard_map/ppermute | solution.py:11
  63.0 0.0 collective-permute-done.17.refs_3_
  63.0 1.7 %collective-permute-start.8 = (bf16[528,128]{1,0:T(8,128)(2,1)S(1)}, bf16[528,128]{1,0:T(8,128)(2,1)S(1)}, u32[]{:S(2)}, u32[]{:S(2)}) collective-permute-start(bf16[528,128]{1,0:T(8,128)(2,1)S(1)} %get-tuple-element.46), channel_id=1, source_target_pairs={{0,3},{1,2},{2,1},{3,0},{4,7},{5,6},{6,5},{7,4},{8,11},{9,10},{10,... | collective-permute-start | bytes 405512 | tf_op jit(solution)/shard_map/ppermute | solution.py:11
  64.7 1.3 %assemble.1 = (bf16[4608,256]{1,0:T(8,128)(2,1)S(1)}, bf16[2304,256]{1,0:T(8,128)(2,1)S(1)}) custom-call(s32[2]{0:T(128)S(1)} %pad_add_fusion.refs_0_, bf16[9,512,128]{2,1,0:T(8,128)(2,1)S(1)} %copy-done, bf16[4,1152,128]{2,1,0:T(8,128)(2,1)S(1)} %pad_maximum_fusion.refs_2_, bf16[4,1152,128]{2,1,0:T(8,128)(2,1)S(1)} %collective-permute-done.17.refs_3_), custom_call_target="tpu_custom_call" | custom-call | flops 1048576 | bytes 1048576 | tf_op jit(solution)/shard_map/assemble/pallas_call | solution.py:285
  66.0 0.0 collective-permute-done.10.refs_9_
  66.0 0.0 collective-permute-done.9.refs_8_
  66.0 3.2 %backward.1 = (bf16[1024,128]{1,0:T(8,128)(2,1)S(1)}, bf16[1024,128]{1,0:T(8,128)(2,1)S(1)}) custom-call(bf16[1056,128]{1,0:T(8,128)(2,1)S(1)} %get-tuple-element.40.refs_0_, bf16[1056,128]{1,0:T(8,128)(2,1)S(1)} %collective-permute-done.refs_1_, bf16[1056,128]{1,0:T(8,128)(2,1)S(1)} %collective-permute-done.1.refs_2_, ...), custom_call_target="tpu_custom_call" | custom-call | flops 10000000000 | bytes 1048576 | tf_op jit(solution)/shard_map/backward/pallas_call | solution.py:285
  69.2 0.0 collective-permute-done.6.refs_5_
  69.2 5.6 %collective-permute-done.7.refs_6_ = bf16[528,128]{1,0:T(8,128)(2,1)S(1)} collective-permute-done((bf16[528,128]{1,0:T(8,128)(2,1)S(1)}, bf16[528,128]{1,0:T(8,128)(2,1)S(1)}, u32[]{:S(2)}, u32[]{:S(2)}) %collective-permute-start.7) | collective-permute-done | bytes 135200 | tf_op jit(solution)/shard_map/ppermute | solution.py:11
  74.8 0.0 collective-permute-done.8.refs_7_
  74.8 2.3 %collective-permute-start.18 = (bf16[1024,128]{1,0:T(8,128)(2,1)S(1)}, bf16[1024,128]{1,0:T(8,128)(2,1)S(1)}, u32[]{:S(2)}, u32[]{:S(2)}) collective-permute-start(bf16[1024,128]{1,0:T(8,128)(2,1)S(1)} %get-tuple-element.62), channel_id=1, source_target_pairs={{0,1},{1,0},{2,3},{3,2},{4,5},{5,4},{6,7},{7,6},{8,9},{9,8},{10,11... | collective-permute-start | bytes 786440 | tf_op jit(solution)/shard_map/ppermute | solution.py:11
  77.1 3.0 %forward.1 = (bf16[1024,128]{1,0:T(8,128)(2,1)S(1)}, bf16[1024,128]{1,0:T(8,128)(2,1)S(1)}) custom-call(bf16[1056,128]{1,0:T(8,128)(2,1)S(1)} %get-tuple-element.40.refs_0_, bf16[1056,128]{1,0:T(8,128)(2,1)S(1)} %collective-permute-done.refs_1_, bf16[1056,128]{1,0:T(8,128)(2,1)S(1)} %collective-permute-done.1.refs_2_, ...), custom_call_target="tpu_custom_call" | custom-call | flops 5000000000 | bytes 1048576 | tf_op jit(solution)/shard_map/forward/pallas_call | solution.py:285
  80.2 2.4 %collective-permute-done.18 = bf16[1024,128]{1,0:T(8,128)(2,1)S(1)} collective-permute-done((bf16[1024,128]{1,0:T(8,128)(2,1)S(1)}, bf16[1024,128]{1,0:T(8,128)(2,1)S(1)}, u32[]{:S(2)}, u32[]{:S(2)}) %collective-permute-start.18) | collective-permute-done | bytes 262176 | tf_op jit(solution)/shard_map/ppermute | solution.py:11
  82.5 1.7 %collective-permute-start.19 = (bf16[1024,128]{1,0:T(8,128)(2,1)S(1)}, bf16[1024,128]{1,0:T(8,128)(2,1)S(1)}, u32[]{:S(2)}, u32[]{:S(2)}) collective-permute-start(bf16[1024,128]{1,0:T(8,128)(2,1)S(1)} %get-tuple-element.63), channel_id=1, source_target_pairs={{0,1},{1,0},{2,3},{3,2},{4,5},{5,4},{6,7},{7,6},{8,9},{9,8},{10,11... | collective-permute-start | bytes 786440 | tf_op jit(solution)/shard_map/ppermute | solution.py:11
  84.3 4.8 %collective-permute-done.19 = bf16[1024,128]{1,0:T(8,128)(2,1)S(1)} collective-permute-done((bf16[1024,128]{1,0:T(8,128)(2,1)S(1)}, bf16[1024,128]{1,0:T(8,128)(2,1)S(1)}, u32[]{:S(2)}, u32[]{:S(2)}) %collective-permute-start.19) | collective-permute-done | bytes 262176 | tf_op jit(solution)/shard_map/ppermute | solution.py:11
  89.1 0.1 broadcast_select_fusion.1
  89.1 0.2 copy.10
  89.3 0.2 copy.11
  89.5 0.2 copy.8
  89.7 0.2 copy.9
  89.9 1.0 %pad_maximum_fusion.2 = bf16[128,4,512]{2,1,0:T(4,128)(2,1)} fusion(bf16[128,4,256]{2,1,0:T(4,128)(2,1)S(1)} %bitcast.31, bf16[128,4,256]{2,1,0:T(4,128)(2,1)S(1)} %bitcast.30), kind=kLoop, calls=%fused_computation.2 | loop fusion | flops 1048576 | bytes 1048576 | tf_op jit(solution)/shard_map/concatenate | solution.py:326
  90.9 1.0 %pad_maximum_fusion.1 = bf16[128,4,512]{2,1,0:T(4,128)(2,1)} fusion(bf16[128,4,256]{2,1,0:T(4,128)(2,1)S(1)} %bitcast.33, bf16[128,4,256]{2,1,0:T(4,128)(2,1)S(1)} %bitcast.32), kind=kLoop, calls=%fused_computation.1 | loop fusion | flops 1048576 | bytes 1048576 | tf_op jit(solution)/shard_map/concatenate | solution.py:326
  (5 shorter events, 0.0 us)
Async XLA Ops:
  0.6 3.4 %copy-start.2 = (bf16[128,4,512]{2,1,0:T(4,128)(2,1)S(1)}, bf16[128,4,512]{2,1,0:T(4,128)(2,1)}, u32[]{:S(2)}) copy-start(bf16[128,4,512]{2,1,0:T(4,128)(2,1)} %param.4) | copy-start | bytes 1572868
  1.6 2.9 %copy-start.1 = (bf16[128]{0:T(256)(128)(2,1)S(1)}, bf16[128]{0:T(256)(128)(2,1)}, u32[]{:S(2)}) copy-start(bf16[128]{0:T(256)(128)(2,1)} %param.6) | copy-start | bytes 772
  5.2 17.3 %collective-permute-start = (bf16[1056,128]{1,0:T(8,128)(2,1)S(1)}, bf16[1056,128]{1,0:T(8,128)(2,1)S(1)}, u32[]{:S(2)}, u32[]{:S(2)}) collective-permute-start(bf16[1056,128]{1,0:T(8,128)(2,1)S(1)} %get-tuple-element.36), channel_id=1, source_target_pairs={{0,1},{1,0},{2,3},{3,2},{4,5},{5,4},{6,7},{7,6},{8,9},{9,8},{10,11... | collective-permute-start | bytes 811016 | tf_op jit(solution)/shard_map/ppermute | solution.py:11
  8.3 11.2 %collective-permute-start.11 = (bf16[576,128]{1,0:T(8,128)(2,1)S(1)}, bf16[576,128]{1,0:T(8,128)(2,1)S(1)}, u32[]{:S(2)}, u32[]{:S(2)}) collective-permute-start(bf16[576,128]{1,0:T(8,128)(2,1)S(1)} %bitcast.38), channel_id=1, source_target_pairs={{0,1},{1,0},{2,3},{3,2},{4,5},{5,4},{6,7},{7,6},{8,9},{9,8},{10,11... | collective-permute-start | bytes 442376 | tf_op jit(solution)/shard_map/ppermute | solution.py:11
  8.4 22.5 %collective-permute-start.12 = (bf16[288,128]{1,0:T(8,128)(2,1)S(1)}, bf16[288,128]{1,0:T(8,128)(2,1)S(1)}, u32[]{:S(2)}, u32[]{:S(2)}) collective-permute-start(bf16[288,128]{1,0:T(8,128)(2,1)S(1)} %bitcast.39), channel_id=1, source_target_pairs={{0,2},{1,3},{2,0},{3,1},{4,6},{5,7},{6,4},{7,5},{8,10},{9,11},{10,... | collective-permute-start | bytes 221192 | tf_op jit(solution)/shard_map/ppermute | solution.py:11
  11.3 19.5 %collective-permute-start.13 = (bf16[288,128]{1,0:T(8,128)(2,1)S(1)}, bf16[288,128]{1,0:T(8,128)(2,1)S(1)}, u32[]{:S(2)}, u32[]{:S(2)}) collective-permute-start(bf16[288,128]{1,0:T(8,128)(2,1)S(1)} %bitcast.40), channel_id=1, source_target_pairs={{0,3},{1,2},{2,1},{3,0},{4,7},{5,6},{6,5},{7,4},{8,11},{9,10},{10,... | collective-permute-start | bytes 221192 | tf_op jit(solution)/shard_map/ppermute | solution.py:11
  12.7 30.8 %collective-permute-start.2 = (bf16[1056,128]{1,0:T(8,128)(2,1)S(1)}, bf16[1056,128]{1,0:T(8,128)(2,1)S(1)}, u32[]{:S(2)}, u32[]{:S(2)}) collective-permute-start(bf16[1056,128]{1,0:T(8,128)(2,1)S(1)} %get-tuple-element.36), channel_id=1, source_target_pairs={{0,3},{1,2},{2,1},{3,0},{4,7},{5,6},{6,5},{7,4},{8,11},{9,10},{10,... | collective-permute-start | bytes 811016 | tf_op jit(solution)/shard_map/ppermute | solution.py:11
  19.5 22.3 %collective-permute-start.1 = (bf16[1056,128]{1,0:T(8,128)(2,1)S(1)}, bf16[1056,128]{1,0:T(8,128)(2,1)S(1)}, u32[]{:S(2)}, u32[]{:S(2)}) collective-permute-start(bf16[1056,128]{1,0:T(8,128)(2,1)S(1)} %get-tuple-element.40.refs_0_), channel_id=1, source_target_pairs={{0,2},{1,3},{2,0},{3,1},{4,6},{5,7},{6,4},{7,5},{8,10},{9,11},{10,... | collective-permute-start | bytes 811016 | tf_op jit(solution)/shard_map/ppermute | solution.py:11
  23.2 20.3 %collective-permute-start.3 = (bf16[528,128]{1,0:T(8,128)(2,1)S(1)}, bf16[528,128]{1,0:T(8,128)(2,1)S(1)}, u32[]{:S(2)}, u32[]{:S(2)}) collective-permute-start(bf16[528,128]{1,0:T(8,128)(2,1)S(1)} %get-tuple-element.39), channel_id=1, source_target_pairs={{0,1},{1,0},{2,3},{3,2},{4,5},{5,4},{6,7},{7,6},{8,9},{9,8},{10,11... | collective-permute-start | bytes 405512 | tf_op jit(solution)/shard_map/ppermute | solution.py:11
  30.9 27.4 %collective-permute-start.16 = (bf16[1152,128]{1,0:T(8,128)(2,1)S(1)}, bf16[1152,128]{1,0:T(8,128)(2,1)S(1)}, u32[]{:S(2)}, u32[]{:S(2)}) collective-permute-start(bf16[1152,128]{1,0:T(8,128)(2,1)S(1)} %constant_dynamic-update-slice_fusion), channel_id=1, source_target_pairs={{0,24},{4,28},{8,16},{12,20},{16,8},{20,12},{24,0},{28,4},{1,25},{... | collective-permute-start | bytes 884744 | tf_op jit(solution)/shard_map/ppermute | solution.py:11
  33.4 24.9 %collective-permute-start.14 = (bf16[1152,128]{1,0:T(8,128)(2,1)S(1)}, bf16[1152,128]{1,0:T(8,128)(2,1)S(1)}, u32[]{:S(2)}, u32[]{:S(2)}) collective-permute-start(bf16[1152,128]{1,0:T(8,128)(2,1)S(1)} %constant_dynamic-update-slice_fusion), channel_id=1, source_target_pairs={{0,8},{4,12},{8,0},{12,4},{16,24},{20,28},{24,16},{28,20},{1,9},{5... | collective-permute-start | bytes 884744 | tf_op jit(solution)/shard_map/ppermute | solution.py:11
  41.9 16.4 %collective-permute-start.15 = (bf16[1152,128]{1,0:T(8,128)(2,1)S(1)}, bf16[1152,128]{1,0:T(8,128)(2,1)S(1)}, u32[]{:S(2)}, u32[]{:S(2)}) collective-permute-start(bf16[1152,128]{1,0:T(8,128)(2,1)S(1)} %constant_dynamic-update-slice_fusion), channel_id=1, source_target_pairs={{0,16},{4,20},{8,24},{12,28},{16,0},{20,4},{24,8},{28,12},{1,17},{... | collective-permute-start | bytes 884744 | tf_op jit(solution)/shard_map/ppermute | solution.py:11
  43.4 10.5 %collective-permute-start.4 = (bf16[528,128]{1,0:T(8,128)(2,1)S(1)}, bf16[528,128]{1,0:T(8,128)(2,1)S(1)}, u32[]{:S(2)}, u32[]{:S(2)}) collective-permute-start(bf16[528,128]{1,0:T(8,128)(2,1)S(1)} %get-tuple-element.47.refs_4_), channel_id=1, source_target_pairs={{0,2},{1,3},{2,0},{3,1},{4,6},{5,7},{6,4},{7,5},{8,10},{9,11},{10,... | collective-permute-start | bytes 405512 | tf_op jit(solution)/shard_map/ppermute | solution.py:11
  43.5 11.7 %collective-permute-start.5 = (bf16[528,128]{1,0:T(8,128)(2,1)S(1)}, bf16[528,128]{1,0:T(8,128)(2,1)S(1)}, u32[]{:S(2)}, u32[]{:S(2)}) collective-permute-start(bf16[528,128]{1,0:T(8,128)(2,1)S(1)} %get-tuple-element.39), channel_id=1, source_target_pairs={{0,3},{1,2},{2,1},{3,0},{4,7},{5,6},{6,5},{7,4},{8,11},{9,10},{10,... | collective-permute-start | bytes 405512 | tf_op jit(solution)/shard_map/ppermute | solution.py:11
  53.9 12.1 %collective-permute-start.10 = (bf16[2112,128]{1,0:T(8,128)(2,1)S(1)}, bf16[2112,128]{1,0:T(8,128)(2,1)S(1)}, u32[]{:S(2)}, u32[]{:S(2)}) collective-permute-start(bf16[2112,128]{1,0:T(8,128)(2,1)S(1)} %get-tuple-element.52), channel_id=1, source_target_pairs={{4,0},{8,4},{12,8},{16,12},{20,16},{24,20},{28,24},{5,1},{9,5},{13... | collective-permute-start | bytes 1622024 | tf_op jit(solution)/shard_map/ppermute | solution.py:18
  55.2 10.8 %collective-permute-start.9 = (bf16[2112,128]{1,0:T(8,128)(2,1)S(1)}, bf16[2112,128]{1,0:T(8,128)(2,1)S(1)}, u32[]{:S(2)}, u32[]{:S(2)}) collective-permute-start(bf16[2112,128]{1,0:T(8,128)(2,1)S(1)} %get-tuple-element.51), channel_id=1, source_target_pairs={{0,4},{4,8},{8,12},{12,16},{16,20},{20,24},{24,28},{1,5},{5,9},{9,... | collective-permute-start | bytes 1622024 | tf_op jit(solution)/shard_map/ppermute | solution.py:18
  58.5 6.2 %copy-start = (bf16[9,512,128]{2,1,0:T(8,128)(2,1)S(1)}, bf16[9,512,128]{2,1,0:T(8,128)(2,1)}, u32[]{:S(2)}) copy-start(bf16[9,512,128]{2,1,0:T(8,128)(2,1)} %refs_1_.1) | copy-start | bytes 3538948
  58.5 4.5 %collective-permute-start.17 = (bf16[4,1152,128]{2,1,0:T(8,128)(2,1)S(1)}, bf16[4,1152,128]{2,1,0:T(8,128)(2,1)S(1)}, u32[]{:S(2)}, u32[]{:S(2)}) collective-permute-start(bf16[4,1152,128]{2,1,0:T(8,128)(2,1)S(1)} %pad_maximum_fusion.refs_2_), channel_id=1, source_target_pairs={{0,4},{4,0},{8,12},{12,8},{16,20},{20,16},{24,28},{28,24},{1,5},{5... | collective-permute-start | bytes 3538952 | tf_op jit(solution)/shard_map/ppermute | solution.py:11
  60.2 9.0 %collective-permute-start.6 = (bf16[528,128]{1,0:T(8,128)(2,1)S(1)}, bf16[528,128]{1,0:T(8,128)(2,1)S(1)}, u32[]{:S(2)}, u32[]{:S(2)}) collective-permute-start(bf16[528,128]{1,0:T(8,128)(2,1)S(1)} %get-tuple-element.46), channel_id=1, source_target_pairs={{0,1},{1,0},{2,3},{3,2},{4,5},{5,4},{6,7},{7,6},{8,9},{9,8},{10,11... | collective-permute-start | bytes 405512 | tf_op jit(solution)/shard_map/ppermute | solution.py:11
  61.7 13.1 %collective-permute-start.7 = (bf16[528,128]{1,0:T(8,128)(2,1)S(1)}, bf16[528,128]{1,0:T(8,128)(2,1)S(1)}, u32[]{:S(2)}, u32[]{:S(2)}) collective-permute-start(bf16[528,128]{1,0:T(8,128)(2,1)S(1)} %get-tuple-element.55.refs_4_), channel_id=1, source_target_pairs={{0,2},{1,3},{2,0},{3,1},{4,6},{5,7},{6,4},{7,5},{8,10},{9,11},{10,... | collective-permute-start | bytes 405512 | tf_op jit(solution)/shard_map/ppermute | solution.py:11
  63.0 11.9 %collective-permute-start.8 = (bf16[528,128]{1,0:T(8,128)(2,1)S(1)}, bf16[528,128]{1,0:T(8,128)(2,1)S(1)}, u32[]{:S(2)}, u32[]{:S(2)}) collective-permute-start(bf16[528,128]{1,0:T(8,128)(2,1)S(1)} %get-tuple-element.46), channel_id=1, source_target_pairs={{0,3},{1,2},{2,1},{3,0},{4,7},{5,6},{6,5},{7,4},{8,11},{9,10},{10,... | collective-permute-start | bytes 405512 | tf_op jit(solution)/shard_map/ppermute | solution.py:11
  74.8 7.7 %collective-permute-start.18 = (bf16[1024,128]{1,0:T(8,128)(2,1)S(1)}, bf16[1024,128]{1,0:T(8,128)(2,1)S(1)}, u32[]{:S(2)}, u32[]{:S(2)}) collective-permute-start(bf16[1024,128]{1,0:T(8,128)(2,1)S(1)} %get-tuple-element.62), channel_id=1, source_target_pairs={{0,1},{1,0},{2,3},{3,2},{4,5},{5,4},{6,7},{7,6},{8,9},{9,8},{10,11... | collective-permute-start | bytes 786440 | tf_op jit(solution)/shard_map/ppermute | solution.py:11
  82.5 6.5 %collective-permute-start.19 = (bf16[1024,128]{1,0:T(8,128)(2,1)S(1)}, bf16[1024,128]{1,0:T(8,128)(2,1)S(1)}, u32[]{:S(2)}, u32[]{:S(2)}) collective-permute-start(bf16[1024,128]{1,0:T(8,128)(2,1)S(1)} %get-tuple-element.63), channel_id=1, source_target_pairs={{0,1},{1,0},{2,3},{3,2},{4,5},{5,4},{6,7},{7,6},{8,9},{9,8},{10,11... | collective-permute-start | bytes 786440 | tf_op jit(solution)/shard_map/ppermute | solution.py:11

commit v8 on v7

--- a/solution.py
+++ b/solution.py
@@ -109,10 +109,10 @@
     return jnp.transpose(whole, (2, 0, 1))
 
 
-def assemble_kernel(order, place, filters, near, far, weights, extra):
+def assemble_kernel(orders, place, filters, near, near_far, across, across_far, weights, extra):
     me, band = place[0], place[1]
     taps, channels, local = filters.shape
-    share = near.shape[1] // (2 * taps)
+    share = near.shape[1] // taps
     half = share // 2
     for tap in range(taps):
         for j in range(4):
@@ -120,54 +120,27 @@
             weights[pl.ds(tap * channels + j * local, local), :local] = filters[
                 tap, pl.ds(start, local), :
             ]
-    for bit, held in enumerate((near, far)):
-        for j, d in enumerate(order):
+    for bit, held in enumerate((near, near_far)):
+        for j, d in enumerate(orders[0]):
             first = (band ^ (d | bit)) * share
             block = lax.div(first, local)
             start = (block ^ me) * local + first - block * local
             for tap in range(taps):
                 row = pl.multiple_of(tap * channels + start, 16)
                 weights[pl.ds(row, share), local:] = held[j, tap * share : (tap + 1) * share]
+    for bit, held in enumerate((across, across_far)):
+        for j, d in enumerate(orders[1]):
             first = (band ^ (d | bit)) * half
             block = lax.div(first, local)
             start = (block ^ (me & 1)) * local + first - block * local
             for tap in range(taps):
                 row = pl.multiple_of(tap * 2 * local + start, 16)
                 for k in range(2):
-                    at = taps * share + (k * taps + tap) * half
+                    at = (k * taps + tap) * half
                     extra[pl.ds(row, half), k * local : (k + 1) * local] = held[j, at : at + half]
 
 
-def assemble_kernel(order, place, filters, near, far, weights, extra):
-    me, band = place[0], place[1]
-    taps, channels, local = filters.shape
-    share = near.shape[1] // (2 * taps)
-    half = share // 2
-    for tap in range(taps):
-        for j in range(4):
-            start = pl.multiple_of((me ^ j) * local, local)
-            weights[pl.ds(tap * channels + j * local, local), :local] = filters[
-                tap, pl.ds(start, local), :
-            ]
-    for bit, held in enumerate((near, far)):
-        for j, d in enumerate(order):
-            first = (band ^ (d | bit)) * share
-            block = lax.div(first, local)
-            start = (block ^ me) * local + first - block * local
-            for tap in range(taps):
-                row = pl.multiple_of(tap * channels + start, 16)
-                weights[pl.ds(row, share), local:] = held[j, tap * share : (tap + 1) * share]
-            first = (band ^ (d | bit)) * half
-            block = lax.div(first, local)
-            start = (block ^ (me & 1)) * local + first - block * local
-            for tap in range(taps):
-                row = pl.multiple_of(tap * 2 * local + start, 16)
-                for k in range(2):
-                    at = taps * share + (k * taps + tap) * half
-                    extra[pl.ds(row, half), k * local : (k + 1) * local] = held[j, at : at + half]
-
-
-def cut_kernel(rows, place, *refs):
+def cut_kernel(parts, place, *refs):
     sources, (bias, mine, other) = refs[:-3], refs[-3:]
     side = place[0] & 1
     local = bias.shape[1]
@@ -176,37 +149,27 @@
     line = bias[...].astype(jnp.float32)
     zero = jnp.zeros((1, local), jnp.float32)
     rest = jnp.concatenate([line, zero, zero, zero, zero, zero])
-    at = 0
-    for source in sources:
-        for r in rows:
-            left = source[r, width - 16 : width].astype(jnp.float32)[15:]
-            right = source[r, width : width + 16].astype(jnp.float32)[:1]
-            ends = (zero, right), (left, zero)
-            pieces = []
-            for t, (before, behind) in enumerate(ends):
-                tail = jnp.concatenate([behind, line, rest]).astype(jnp.bfloat16)
-                pieces.append(
-                    jnp.concatenate(
-                        [
-                            before.astype(jnp.bfloat16),
-                            source[r, t * width : (t + 1) * width],
-                            tail[:7],
-                        ]
-                    )
-                )
-            first = side == 0
-            mine[at : at + pitch] = jnp.where(first, pieces[0], pieces[1])
-            other[at : at + pitch] = jnp.where(first, pieces[1], pieces[0])
-            at += pitch
-
-
-def rim_kernel(width, *refs):
+    for n, (i, r) in enumerate(parts):
+        source = sources[i]
+        left = source[r, width - 16 : width].astype(jnp.float32)[15:]
+        right = source[r, width : width + 16].astype(jnp.float32)[:1]
+        pieces = []
+        for t, (before, behind) in enumerate(((zero, right), (left, zero))):
+            tail = jnp.concatenate([behind, line, rest]).astype(jnp.bfloat16)
+            middle = source[r, t * width : (t + 1) * width]
+            pieces.append(jnp.concatenate([before.astype(jnp.bfloat16), middle, tail[:7]]))
+        at = n * pitch
+        mine[at : at + pitch] = jnp.where(side == 0, pieces[0], pieces[1])
+        other[at : at + pitch] = jnp.where(side == 0, pieces[1], pieces[0])
+
+
+def rim_kernel(width, rows, *refs):
     pieces, (first, last) = refs[:4], refs[4:]
     pitch = width + 8
     for k, piece in enumerate(pieces):
         for i in range(2):
             for out, end in ((first, 0), (last, 1)):
-                at = (2 * i + end) * pitch
+                at = (i * rows + end * (1 if i else rows - 1)) * pitch
                 out[(2 * k + i) * pitch : (2 * k + i + 1) * pitch] = piece[at : at + pitch]
 
 
@@ -217,25 +180,23 @@
         ]
 
 
-def fill_source(target, which, width, edges, inners, before, after):
+def fill_source(target, which, width, rows, before, after):
     local = before.shape[1]
     pitch = width + 8
-    count = inners[0].shape[0] // pitch
-    for k in range(4):
+    for k, held in enumerate(rows):
         lanes = slice(k * local, (k + 1) * local)
-        rows = [(before, 2 * k + which), (edges[k], 2 * which)]
-        rows += [(inners[k], r) for r in range(count)]
-        rows += [(edges[k], 2 * which + 1), (after, 2 * k + which)]
-        for r, (ref, at) in enumerate(rows):
+        held = [(before, 2 * k + which), *held, (after, 2 * k + which)]
+        for r, (ref, at) in enumerate(held):
             fill_rows(target, ref, at * pitch, r, lanes, width)
 
 
 def backward_kernel(*refs):
-    edges, inners, (before, after, weights, mine, other, source) = refs[:4], refs[4:8], refs[8:]
+    edges, (before, after, weights, mine, other, source) = refs[:4], refs[4:]
     size, local = mine.shape
     width = before.shape[0] // 8 - 8
     channels = 4 * local
-    fill_source(source, 0, width, edges, inners, before, after)
+    rows = [[(p, r) for r in range(size // width)] for p in edges]
+    fill_source(source, 0, width, rows, before, after)
     acc = None
     for a in range(3):
         for b in range(3):
@@ -255,7 +216,12 @@
     size, local = mine.shape
     width = before.shape[0] // 8 - 8
     channels, half = 4 * local, 2 * local
-    fill_source(source, 1, width, edges, inners, before, after)
+    count = size // width
+    rows = [
+        [(p, count), *((q, r) for r in range(count - 2)), (p, count + 1)]
+        for p, q in zip(edges, inners)
+    ]
+    fill_source(source, 1, width, rows, before, after)
     acc = None
     for a in range(3):
         for b in range(3):
@@ -279,6 +245,7 @@
 
 SMEM = pl.BlockSpec(memory_space=pltpu.SMEM)
 VMEM = pl.BlockSpec(memory_space=pltpu.VMEM)
+ANY = pl.BlockSpec(memory_space=pl.ANY)
 
 
 def kernel(body, shapes, args, scratch, name, placed=False, flops=2**20):
@@ -294,10 +261,10 @@
     )(*args)
 
 
-def cut(place, sources, bias, rows, name, flops):
+def cut(place, sources, bias, parts, name, flops):
     local = bias.shape[1]
-    shape = (len(sources) * len(rows) * (sources[0].shape[1] // 2 + 8), local)
-    body = lambda *refs: cut_kernel(rows, *refs)
+    shape = (len(parts) * (sources[0].shape[1] // 2 + 8), local)
+    body = lambda *refs: cut_kernel(parts, *refs)
     return kernel(body, [shape] * 2, [place, *sources, bias], [], name, True, flops)
 
 
@@ -311,19 +278,48 @@
     return lax.optimization_barrier((value, others))[0]
 
 
-def gather(value):
-    bands = lax.axis_size("band")
-    order = list(range(0, bands, 2))
-    held = jnp.stack([swap(value, "band", d) if d else value for d in order])
-    return held, swap(held, "band", 1), order
-
-
-def home(mine, other, side, rows):
+def gather(value, steps):
+    held, order = value[None], [0]
+    for step in steps:
+        held = jnp.concatenate([held, swap(held, "band", step)])
+        order = order + [o ^ step for o in order]
+    return held, order
+
+
+def halving(size):
+    steps = []
+    while size > 1:
+        size //= 2
+        steps.append(size)
+    return steps
+
+
+def home_kernel(place, mine, other, out, sems):
+    width = mine.shape[2]
+    side = place[0] & 1
+    copies = []
+    for i, ref in enumerate((mine, other)):
+        start = pl.multiple_of((side ^ i) * width, width)
+        copies.append(pltpu.make_async_copy(ref, out.at[:, :, pl.ds(start, width)], sems.at[i]))
+    for copy in copies:
+        copy.start()
+    for copy in copies:
+        copy.wait()
+
+
+def home(place, mine, other, rows):
     turn = lambda p: jnp.transpose(p.reshape(rows, -1, p.shape[1]), (2, 0, 1))
     mine, other = turn(mine), turn(other)
-    first = jnp.where(side == 0, mine, other)
-    second = jnp.where(side == 0, other, mine)
-    return jnp.concatenate([first, second], axis=2)
+    channels, rows, width = mine.shape
+    return pl.pallas_call(
+        home_kernel,
+        out_shape=jax.ShapeDtypeStruct((channels, rows, 2 * width), jnp.bfloat16),
+        in_specs=[SMEM, ANY, ANY],
+        out_specs=ANY,
+        scratch_shapes=[pltpu.SemaphoreType.DMA((2,))],
+        cost_estimate=pl.CostEstimate(flops=2**20, bytes_accessed=2**20, transcendentals=0),
+        name="home",
+    )(place, mine, other)
 
 
 MICROSECOND = 10**9
@@ -334,11 +330,11 @@
     bands = lax.axis_size("band")
     taps, outs, local = filters.shape
     rows, cols = image.shape[1:]
-    if n != 4 or local % 128 or cols % 256 or rows != 4 or outs % (32 * bands) or bands < 4:
+    if n != 4 or local % 128 or cols % 256 or rows < 3 or outs % (32 * bands) or bands < 4:
         return plain(image, filters, bias, upstream)
     me = lax.axis_index("chan")
     band = lax.axis_index("band")
-    side, half = me & 1, me >> 1
+    half = me >> 1
     place = jnp.stack([me, band]).astype(jnp.int32)
     width = cols // 2
 
@@ -346,44 +342,46 @@
     near = lax.dynamic_slice_in_dim(filters, band * share, share, axis=1).reshape(-1, local)
     start = (1 - half) * (outs // 2) + band * (share // 2)
     across = lax.dynamic_slice_in_dim(filters, start, share // 2, axis=1).reshape(-1, local)
-    parts = [swap(near, "chan", 1), swap(across, "chan", 2), swap(across, "chan", 3)]
+    near = swap(near, "chan", 1)
+    across = jnp.concatenate([swap(across, "chan", k) for k in (2, 3)])
 
     upstream, image = [jnp.transpose(v, (1, 2, 0)) for v in (upstream, image)]
-    line = bias[None]
-    edge = cut(place, [upstream, image], line, (0, rows - 1), "cut_edge", 2**20)
-    edge = exchange(*after(edge, near, across))
-    middle = range(1, rows - 1)
-    upstream = after(upstream, edge[1])
-    early = cut(place, [upstream], line, middle, "cut_first", 5 * MICROSECOND)
-    edge = after(edge, early)
-    first = exchange(*early)
-    image = after(image, first[1:])
-    late = cut(place, [image], line, middle, "cut_second", 18 * MICROSECOND)
-    first = after(first, late)
+    parts = [(0, r) for r in range(rows)] + [(1, 0), (1, rows - 1)]
+    edge = cut(place, [upstream, image], bias[None], parts, "cut_first", 2**20)
+    near, across = after((near, across), edge)
+    edge = exchange(*edge)
+    parts = [(0, r) for r in range(1, rows - 1)]
+    late = cut(place, [after(image, edge[1])], bias[None], parts, "cut_second", 2**20)
+    edge = after(edge, late)
     second = exchange(*late)
 
-    held, there, order = gather(jnp.concatenate(parts))
+    steps = halving(bands)[:-1]
+    near, near_order = gather(near, steps)
+    across, across_order = gather(across, steps[::-1])
+    held = [near, swap(near, "band", 1), across, swap(across, "band", 1)]
     weights, extra = kernel(
-        lambda *refs: assemble_kernel(order, *refs),
+        lambda *refs: assemble_kernel((near_order, across_order), *refs),
         [(taps * outs, 2 * local), (taps * 2 * local, 2 * local)],
-        [place, filters, held, there],
+        [place, filters, *held],
         [],
         "assemble",
         True,
+        2 * MICROSECOND,
     )
     rim = (8 * (width + 8), local)
-    rims = neighbours(*kernel(lambda *refs: rim_kernel(width, *refs), [rim] * 2, edge, [], "rim", False, 16 * MICROSECOND))
+    body = lambda *refs: rim_kernel(width, rows, *refs)
+    rims = neighbours(*kernel(body, [rim] * 2, edge, [], "rim", False, 4 * MICROSECOND))
 
     out = [(rows * width, local)] * 2
     source = [(3, (rows + 2) * width, 4 * local)]
-    args = [*edge, *first, *rims, weights]
+    args = [*edge, *rims, weights]
     mine, other = kernel(backward_kernel, out, args, source, "backward", False, 10 * MICROSECOND)
     other = swap(other, "chan", 1)
-    image_grad = home(mine, other, side, rows)
+    image_grad = home(place, mine, other, rows)
     args = [*edge, *after(second, mine), *rims, weights, extra]
     mine, sent = kernel(forward_kernel, out, args, source, "forward", False, 5 * MICROSECOND)
     other = swap(after(sent, other), "chan", 1)
-    return home(mine, other, side, rows), image_grad
+    return home(place, mine, other, rows), image_grad
 
 
 def solution(mesh):

time: 92.2 us -> 121 us (1.31); the launches traced: 92 us -> 119 us
  Pallas kernels: 9.51 us -> 44.3 us
  starting transfers between devices: 42 us -> 31.9 us
  local copies, waits for them, and re-layouts: 4.58 us -> 7.3 us
  other arithmetic: 2.36 us -> 0.26 us
  waiting for transfers between devices: 32.6 us -> 33.9 us
    pallas_call x0 -> x2, Pallas kernels: none -> 35.3 us  [home(): pl.pallas_call(home_kernel, out_shape=jax.ShapeDtypeStruct((channels, row...]
    ppermute x18 -> x17, starting transfers between devices: 37.7 us -> 28.5 us  [swap(): return lax.ppermute(value, axis, [(j, j ^ step) for j in range(size)])]
    reshape x0 -> x4, local copies, waits for them, and re-layouts: none -> 3.52 us  [home(): turn = lambda p: jnp.transpose(p.reshape(rows, -1, p.shape[1]), (2, 0, 1))]
    concatenate x2 -> x5, other arithmetic: 2.06 us -> 0.19 us  [the longest x4 0.18 us: gather(): held = jnp.concatenate([held, swap(held, 'band', step)])]
    ppermute x18 -> x17, waiting for transfers between devices: 32.6 us -> 33.9 us  [swap(): return lax.ppermute(value, axis, [(j, j ^ step) for j in range(size)])]
    pallas_call x7 -> x6, Pallas kernels: 9.51 us -> 8.95 us  [kernel(): pl.pallas_call(body, out_shape=[jax.ShapeDtypeStruct(s, jnp.bfloat16) for...]
  transfers between devices with their start and end apart: 20 -> 19, of which waited for: 6 -> 5; matrix products, arithmetic and copies ran while one was open for 0% -> 5% of each run, Pallas kernels for 10% -> 22%
where the time goes in v8:
time: 121 us; the launch traced here: 119 us
  Pallas kernels  44.3 us (37%)
  waiting for transfers between devices  33.9 us (28%)
  starting transfers between devices  31.9 us (26%)
  local copies, waits for them, and re-layouts  7.3 us (6%)
    pallas_call x2, Pallas kernels, home(): pl.pallas_call(home_kernel, out_shape=jax.ShapeDtypeStruct((channels, row...  35.3 us
    ppermute x17, waiting for transfers between devices, swap(): return lax.ppermute(value, axis, [(j, j ^ step) for j in range(size)])  33.9 us
    ppermute x17, starting transfers between devices, swap(): return lax.ppermute(value, axis, [(j, j ^ step) for j in range(size)])  28.5 us
    pallas_call x6, Pallas kernels, kernel(): pl.pallas_call(body, out_shape=[jax.ShapeDtypeStruct(s, jnp.bfloat16) for...  8.95 us
    reshape x4, local copies, waits for them, and re-layouts, home(): turn = lambda p: jnp.transpose(p.reshape(rows, -1, p.shape[1]), (2, 0, 1))  3.52 us
    ppermute x2, starting transfers between devices, neighbours(): return (lax.ppermute(last, 'band', up), lax.ppermute(first, 'band', down))  3.39 us
  transfers between devices with their start and end apart: 19, of which 5 were waited for; matrix products, arithmetic and copies ran while one was open for 5% of the time, Pallas kernels for 22%

profile of v8, /device:TPU:0, one launch (start us, length us, event | category | flops | bytes accessed | tf_op | source)
XLA Modules:
  0.0 118.5 jit_solution(2887229342569476749)
XLA Ops:
  0.6 0.0 copy-start.3
  0.7 1.0 constant_dynamic-slice_fusion
  1.6 5.0 %collective-permute-start.10 = (bf16[288,128]{1,0:T(8,128)(2,1)S(1)}, bf16[288,128]{1,0:T(8,128)(2,1)S(1)}, u32[]{:S(2)}, u32[]{:S(2)}) collective-permute-start(bf16[288,128]{1,0:T(8,128)(2,1)S(1)} %bitcast.37), channel_id=1, source_target_pairs={{0,3},{1,2},{2,1},{3,0},{4,7},{5,6},{6,5},{7,4},{8,11},{9,10},{10,... | collective-permute-start | bytes 221192 | tf_op jit(solution)/shard_map/ppermute | solution.py:11
  6.7 0.0 collective-permute-start.9
  6.7 0.0 copy-start.2
  6.7 0.9 constant_dynamic-slice_fusion.1
  7.6 0.7 collective-permute-start.8
  8.3 0.1 pad_add_fusion.refs_0_.place
  8.4 1.5 %copy.7 = bf16[128,4,512]{0,2,1:T(8,128)(2,1)S(1)} copy(bf16[128,4,512]{2,1,0:T(4,128)(2,1)} %param.4) | data formatting | bytes 1048576 | tf_op args[0]
  9.8 0.0 copy-done.3
  9.8 0.4 copy.6
  10.2 0.0 copy-done.2
  10.3 0.8 cut_first.1
  11.0 0.0 collective-permute-done.10
  11.1 1.9 %collective-permute-done.9 = bf16[288,128]{1,0:T(8,128)(2,1)S(1)} collective-permute-done((bf16[288,128]{1,0:T(8,128)(2,1)S(1)}, bf16[288,128]{1,0:T(8,128)(2,1)S(1)}, u32[]{:S(2)}, u32[]{:S(2)}) %collective-permute-start.9) | collective-permute-done | bytes 73760 | tf_op jit(solution)/shard_map/ppermute | solution.py:11
  13.0 1.6 %collective-permute-done.8 = bf16[576,128]{1,0:T(8,128)(2,1)S(1)} collective-permute-done((bf16[576,128]{1,0:T(8,128)(2,1)S(1)}, bf16[576,128]{1,0:T(8,128)(2,1)S(1)}, u32[]{:S(2)}, u32[]{:S(2)}) %collective-permute-start.8) | collective-permute-done | bytes 147488 | tf_op jit(solution)/shard_map/ppermute | solution.py:11
  14.5 1.5 %collective-permute-start.14 = (bf16[1,576,128]{2,1,0:T(8,128)(2,1)S(1)}, bf16[1,576,128]{2,1,0:T(8,128)(2,1)S(1)}, u32[]{:S(2)}, u32[]{:S(2)}) collective-permute-start(bf16[1,576,128]{2,1,0:T(8,128)(2,1)S(1)} %bitcast.24), channel_id=1, source_target_pairs={{0,8},{4,12},{8,0},{12,4},{16,24},{20,28},{24,16},{28,20},{1,9},{5... | collective-permute-start | bytes 442376 | tf_op jit(solution)/shard_map/ppermute | solution.py:11
  16.0 1.5 %collective-permute-start.11 = (bf16[1,576,128]{2,1,0:T(8,128)(2,1)S(1)}, bf16[1,576,128]{2,1,0:T(8,128)(2,1)S(1)}, u32[]{:S(2)}, u32[]{:S(2)}) collective-permute-start(bf16[1,576,128]{2,1,0:T(8,128)(2,1)S(1)} %bitcast.31), channel_id=1, source_target_pairs={{0,16},{4,20},{8,24},{12,28},{16,0},{20,4},{24,8},{28,12},{1,17},{... | collective-permute-start | bytes 442376 | tf_op jit(solution)/shard_map/ppermute | solution.py:11
  17.6 0.9 collective-permute-start
  18.5 2.3 %collective-permute-start.1 = (bf16[1584,128]{1,0:T(8,128)(2,1)S(1)}, bf16[1584,128]{1,0:T(8,128)(2,1)S(1)}, u32[]{:S(2)}, u32[]{:S(2)}) collective-permute-start(bf16[1584,128]{1,0:T(8,128)(2,1)S(1)} %get-tuple-element.31.refs_0_), channel_id=1, source_target_pairs={{0,2},{1,3},{2,0},{3,1},{4,6},{5,7},{6,4},{7,5},{8,10},{9,11},{10,... | collective-permute-start | bytes 1216520 | tf_op jit(solution)/shard_map/ppermute | solution.py:11
  20.7 1.2 %collective-permute-start.2 = (bf16[1584,128]{1,0:T(8,128)(2,1)S(1)}, bf16[1584,128]{1,0:T(8,128)(2,1)S(1)}, u32[]{:S(2)}, u32[]{:S(2)}) collective-permute-start(bf16[1584,128]{1,0:T(8,128)(2,1)S(1)} %get-tuple-element.27), channel_id=1, source_target_pairs={{0,3},{1,2},{2,1},{3,0},{4,7},{5,6},{6,5},{7,4},{8,11},{9,10},{10,... | collective-permute-start | bytes 1216520 | tf_op jit(solution)/shard_map/ppermute | solution.py:11
  21.9 0.0 collective-permute-done.14
  22.0 0.6 collective-permute-start.15
  22.6 0.0 collective-permute-done.11
  22.6 0.6 collective-permute-start.12
  23.2 11.2 %collective-permute-done.refs_1_ = bf16[1584,128]{1,0:T(8,128)(2,1)S(1)} collective-permute-done((bf16[1584,128]{1,0:T(8,128)(2,1)S(1)}, bf16[1584,128]{1,0:T(8,128)(2,1)S(1)}, u32[]{:S(2)}, u32[]{:S(2)}) %collective-permute-start) | collective-permute-done | bytes 405536 | tf_op jit(solution)/shard_map/ppermute | solution.py:11
  34.4 0.6 cut_second.1
  35.0 14.1 %collective-permute-done.1.refs_2_ = bf16[1584,128]{1,0:T(8,128)(2,1)S(1)} collective-permute-done((bf16[1584,128]{1,0:T(8,128)(2,1)S(1)}, bf16[1584,128]{1,0:T(8,128)(2,1)S(1)}, u32[]{:S(2)}, u32[]{:S(2)}) %collective-permute-start.1) | collective-permute-done | bytes 405536 | tf_op jit(solution)/shard_map/ppermute | solution.py:11
  49.1 0.0 collective-permute-done.2.refs_3_
  49.1 0.0 collective-permute-done.15
  49.1 0.1 pad_maximum_fusion.1.refs_4_
  49.1 0.1 collective-permute-start.16
  49.2 0.0 collective-permute-done.12
  49.2 0.1 pad_maximum_fusion.refs_2_
  49.3 0.0 copy-start
  49.3 0.6 collective-permute-start.13
  49.8 0.1 rim.1
  49.9 2.1 %collective-permute-start.6 = (bf16[2112,128]{1,0:T(8,128)(2,1)S(1)}, bf16[2112,128]{1,0:T(8,128)(2,1)S(1)}, u32[]{:S(2)}, u32[]{:S(2)}) collective-permute-start(bf16[2112,128]{1,0:T(8,128)(2,1)S(1)} %get-tuple-element.35), channel_id=1, source_target_pairs={{0,4},{4,8},{8,12},{12,16},{16,20},{20,24},{24,28},{1,5},{5,9},{9,... | collective-permute-start | bytes 1622024 | tf_op jit(solution)/shard_map/ppermute | solution.py:18
  52.0 1.3 %collective-permute-start.7 = (bf16[2112,128]{1,0:T(8,128)(2,1)S(1)}, bf16[2112,128]{1,0:T(8,128)(2,1)S(1)}, u32[]{:S(2)}, u32[]{:S(2)}) collective-permute-start(bf16[2112,128]{1,0:T(8,128)(2,1)S(1)} %get-tuple-element.36), channel_id=1, source_target_pairs={{4,0},{8,4},{12,8},{16,12},{20,16},{24,20},{28,24},{5,1},{9,5},{13... | collective-permute-start | bytes 1622024 | tf_op jit(solution)/shard_map/ppermute | solution.py:18
  53.3 6.6 %collective-permute-start.3 = (bf16[528,128]{1,0:T(8,128)(2,1)S(1)}, bf16[528,128]{1,0:T(8,128)(2,1)S(1)}, u32[]{:S(2)}, u32[]{:S(2)}) collective-permute-start(bf16[528,128]{1,0:T(8,128)(2,1)S(1)} %get-tuple-element.30), channel_id=1, source_target_pairs={{0,1},{1,0},{2,3},{3,2},{4,5},{5,4},{6,7},{7,6},{8,9},{9,8},{10,11... | collective-permute-start | bytes 405512 | tf_op jit(solution)/shard_map/ppermute | solution.py:11
  59.9 0.0 collective-permute-done.16.refs_5_
  59.9 1.0 collective-permute-start.4
  60.9 0.0 collective-permute-done.13.refs_3_
  60.9 1.5 %collective-permute-start.5 = (bf16[528,128]{1,0:T(8,128)(2,1)S(1)}, bf16[528,128]{1,0:T(8,128)(2,1)S(1)}, u32[]{:S(2)}, u32[]{:S(2)}) collective-permute-start(bf16[528,128]{1,0:T(8,128)(2,1)S(1)} %get-tuple-element.30), channel_id=1, source_target_pairs={{0,3},{1,2},{2,1},{3,0},{4,7},{5,6},{6,5},{7,4},{8,11},{9,10},{10,... | collective-permute-start | bytes 405512 | tf_op jit(solution)/shard_map/ppermute | solution.py:11
  62.4 0.0 copy-done.1
  62.4 0.0 copy-done
  62.4 1.3 %assemble.1 = (bf16[4608,256]{1,0:T(8,128)(2,1)S(1)}, bf16[2304,256]{1,0:T(8,128)(2,1)S(1)}) custom-call(s32[2]{0:T(128)S(1)} %pad_add_fusion.refs_0_.place, bf16[9,512,128]{2,1,0:T(8,128)(2,1)S(1)} %copy-done, bf16[4,576,128]{2,1,0:T(8,128)(2,1)S(1)} %pad_maximum_fusion.refs_2_, bf16[4,576,128]{2,1,0:T(8,128)(2,1)S(1)} %collective-permute-done.13.refs_3_, ...), custom_call_target="tpu_custom_call" | custom-call | flops 2000000000 | bytes 1048576 | tf_op jit(solution)/shard_map/assemble/pallas_call | solution.py:252
  63.7 0.0 collective-permute-done.6.refs_4_.refs_8_
  63.7 0.0 collective-permute-done.7.refs_5_.refs_9_
  63.7 3.2 %backward.1 = (bf16[1024,128]{1,0:T(8,128)(2,1)S(1)}, bf16[1024,128]{1,0:T(8,128)(2,1)S(1)}) custom-call(bf16[1584,128]{1,0:T(8,128)(2,1)S(1)} %get-tuple-element.31.refs_0_, bf16[1584,128]{1,0:T(8,128)(2,1)S(1)} %collective-permute-done.refs_1_, bf16[1584,128]{1,0:T(8,128)(2,1)S(1)} %collective-permute-done.1.refs_2_, ...), custom_call_target="tpu_custom_call" | custom-call | flops 10000000000 | bytes 1048576 | tf_op jit(solution)/shard_map/backward/pallas_call | solution.py:252
  66.9 1.1 collective-permute-start.17
  68.0 0.0 collective-permute-done.3.refs_5_
  68.0 5.2 %collective-permute-done.4.refs_6_ = bf16[528,128]{1,0:T(8,128)(2,1)S(1)} collective-permute-done((bf16[528,128]{1,0:T(8,128)(2,1)S(1)}, bf16[528,128]{1,0:T(8,128)(2,1)S(1)}, u32[]{:S(2)}, u32[]{:S(2)}) %collective-permute-start.4) | collective-permute-done | bytes 135200 | tf_op jit(solution)/shard_map/ppermute | solution.py:11
  73.2 0.0 collective-permute-done.5.refs_7_
  73.2 3.0 %forward.1 = (bf16[1024,128]{1,0:T(8,128)(2,1)S(1)}, bf16[1024,128]{1,0:T(8,128)(2,1)S(1)}) custom-call(bf16[1584,128]{1,0:T(8,128)(2,1)S(1)} %get-tuple-element.31.refs_0_, bf16[1584,128]{1,0:T(8,128)(2,1)S(1)} %collective-permute-done.refs_1_, bf16[1584,128]{1,0:T(8,128)(2,1)S(1)} %collective-permute-done.1.refs_2_, ...), custom_call_target="tpu_custom_call" | custom-call | flops 5000000000 | bytes 1048576 | tf_op jit(solution)/shard_map/forward/pallas_call | solution.py:252
  76.2 0.0 collective-permute-done.17
  76.2 3.4 %collective-permute-start.18 = (bf16[1024,128]{1,0:T(8,128)(2,1)S(1)}, bf16[1024,128]{1,0:T(8,128)(2,1)S(1)}, u32[]{:S(2)}, u32[]{:S(2)}) collective-permute-start(bf16[1024,128]{1,0:T(8,128)(2,1)S(1)} %get-tuple-element.49), channel_id=1, source_target_pairs={{0,1},{1,0},{2,3},{3,2},{4,5},{5,4},{6,7},{7,6},{8,9},{9,8},{10,11... | collective-permute-start | bytes 786440 | tf_op jit(solution)/shard_map/ppermute | solution.py:11
  79.6 0.9 copy.14
  80.5 0.9 copy.12
  81.4 0.9 copy.15
  82.3 17.7 %home.3 = bf16[128,4,512]{2,1,0:T(4,128)(2,1)} custom-call(s32[2]{0:T(128)} %copy-done.1, bf16[128,4,256]{2,1,0:T(4,128)(2,1)} %bitcast.28, bf16[128,4,256]{2,1,0:T(4,128)(2,1)} %bitcast.30), custom_call_target="tpu_custom_call" | custom-call | flops 1048576 | bytes 1048576 | tf_op jit(solution)/shard_map/home/pallas_call | solution.py:314
  100.0 0.0 collective-permute-done.18
  100.0 0.9 copy.13
  100.8 17.7 %home.2 = bf16[128,4,512]{2,1,0:T(4,128)(2,1)} custom-call(s32[2]{0:T(128)} %copy-done.1, bf16[128,4,256]{2,1,0:T(4,128)(2,1)} %bitcast.27, bf16[128,4,256]{2,1,0:T(4,128)(2,1)} %bitcast.29), custom_call_target="tpu_custom_call" | custom-call | flops 1048576 | bytes 1048576 | tf_op jit(solution)/shard_map/home/pallas_call | solution.py:314
  (4 shorter events, 0.1 us)
Async XLA Ops:
  0.6 9.2 %copy-start.3 = (bf16[128,4,512]{2,1,0:T(4,128)(2,1)S(1)}, bf16[128,4,512]{2,1,0:T(4,128)(2,1)}, u32[]{:S(2)}) copy-start(bf16[128,4,512]{2,1,0:T(4,128)(2,1)} %param.7) | copy-start | bytes 1572868
  1.6 9.4 %collective-permute-start.10 = (bf16[288,128]{1,0:T(8,128)(2,1)S(1)}, bf16[288,128]{1,0:T(8,128)(2,1)S(1)}, u32[]{:S(2)}, u32[]{:S(2)}) collective-permute-start(bf16[288,128]{1,0:T(8,128)(2,1)S(1)} %bitcast.37), channel_id=1, source_target_pairs={{0,3},{1,2},{2,1},{3,0},{4,7},{5,6},{6,5},{7,4},{8,11},{9,10},{10,... | collective-permute-start | bytes 221192 | tf_op jit(solution)/shard_map/ppermute | solution.py:11
  6.7 6.3 %collective-permute-start.9 = (bf16[288,128]{1,0:T(8,128)(2,1)S(1)}, bf16[288,128]{1,0:T(8,128)(2,1)S(1)}, u32[]{:S(2)}, u32[]{:S(2)}) collective-permute-start(bf16[288,128]{1,0:T(8,128)(2,1)S(1)} %bitcast.38), channel_id=1, source_target_pairs={{0,2},{1,3},{2,0},{3,1},{4,6},{5,7},{6,4},{7,5},{8,10},{9,11},{10,... | collective-permute-start | bytes 221192 | tf_op jit(solution)/shard_map/ppermute | solution.py:11
  6.7 3.6 %copy-start.2 = (bf16[128]{0:T(256)(128)(2,1)S(1)}, bf16[128]{0:T(256)(128)(2,1)}, u32[]{:S(2)}) copy-start(bf16[128]{0:T(256)(128)(2,1)} %param.6) | copy-start | bytes 772
  7.6 7.0 %collective-permute-start.8 = (bf16[576,128]{1,0:T(8,128)(2,1)S(1)}, bf16[576,128]{1,0:T(8,128)(2,1)S(1)}, u32[]{:S(2)}, u32[]{:S(2)}) collective-permute-start(bf16[576,128]{1,0:T(8,128)(2,1)S(1)} %bitcast.36), channel_id=1, source_target_pairs={{0,1},{1,0},{2,3},{3,2},{4,5},{5,4},{6,7},{7,6},{8,9},{9,8},{10,11... | collective-permute-start | bytes 442376 | tf_op jit(solution)/shard_map/ppermute | solution.py:11
  8.4 54.0 %copy-start.1 = (s32[2]{0:T(128)}, s32[2]{0:T(128)S(1)}, u32[]{:S(2)}) copy-start(s32[2]{0:T(128)S(1)} %pad_add_fusion.refs_0_.place) | copy-start | bytes 28
  14.5 7.4 %collective-permute-start.14 = (bf16[1,576,128]{2,1,0:T(8,128)(2,1)S(1)}, bf16[1,576,128]{2,1,0:T(8,128)(2,1)S(1)}, u32[]{:S(2)}, u32[]{:S(2)}) collective-permute-start(bf16[1,576,128]{2,1,0:T(8,128)(2,1)S(1)} %bitcast.24), channel_id=1, source_target_pairs={{0,8},{4,12},{8,0},{12,4},{16,24},{20,28},{24,16},{28,20},{1,9},{5... | collective-permute-start | bytes 442376 | tf_op jit(solution)/shard_map/ppermute | solution.py:11
  16.0 6.5 %collective-permute-start.11 = (bf16[1,576,128]{2,1,0:T(8,128)(2,1)S(1)}, bf16[1,576,128]{2,1,0:T(8,128)(2,1)S(1)}, u32[]{:S(2)}, u32[]{:S(2)}) collective-permute-start(bf16[1,576,128]{2,1,0:T(8,128)(2,1)S(1)} %bitcast.31), channel_id=1, source_target_pairs={{0,16},{4,20},{8,24},{12,28},{16,0},{20,4},{24,8},{28,12},{1,17},{... | collective-permute-start | bytes 442376 | tf_op jit(solution)/shard_map/ppermute | solution.py:11
  17.6 16.8 %collective-permute-start = (bf16[1584,128]{1,0:T(8,128)(2,1)S(1)}, bf16[1584,128]{1,0:T(8,128)(2,1)S(1)}, u32[]{:S(2)}, u32[]{:S(2)}) collective-permute-start(bf16[1584,128]{1,0:T(8,128)(2,1)S(1)} %get-tuple-element.27), channel_id=1, source_target_pairs={{0,1},{1,0},{2,3},{3,2},{4,5},{5,4},{6,7},{7,6},{8,9},{9,8},{10,11... | collective-permute-start | bytes 1216520 | tf_op jit(solution)/shard_map/ppermute | solution.py:11
  18.5 30.6 %collective-permute-start.1 = (bf16[1584,128]{1,0:T(8,128)(2,1)S(1)}, bf16[1584,128]{1,0:T(8,128)(2,1)S(1)}, u32[]{:S(2)}, u32[]{:S(2)}) collective-permute-start(bf16[1584,128]{1,0:T(8,128)(2,1)S(1)} %get-tuple-element.31.refs_0_), channel_id=1, source_target_pairs={{0,2},{1,3},{2,0},{3,1},{4,6},{5,7},{6,4},{7,5},{8,10},{9,11},{10,... | collective-permute-start | bytes 1216520 | tf_op jit(solution)/shard_map/ppermute | solution.py:11
  20.7 28.3 %collective-permute-start.2 = (bf16[1584,128]{1,0:T(8,128)(2,1)S(1)}, bf16[1584,128]{1,0:T(8,128)(2,1)S(1)}, u32[]{:S(2)}, u32[]{:S(2)}) collective-permute-start(bf16[1584,128]{1,0:T(8,128)(2,1)S(1)} %get-tuple-element.27), channel_id=1, source_target_pairs={{0,3},{1,2},{2,1},{3,0},{4,7},{5,6},{6,5},{7,4},{8,11},{9,10},{10,... | collective-permute-start | bytes 1216520 | tf_op jit(solution)/shard_map/ppermute | solution.py:11
  22.0 27.1 %collective-permute-start.15 = (bf16[2,576,128]{2,1,0:T(8,128)(2,1)S(1)}, bf16[2,576,128]{2,1,0:T(8,128)(2,1)S(1)}, u32[]{:S(2)}, u32[]{:S(2)}) collective-permute-start(bf16[2,576,128]{2,1,0:T(8,128)(2,1)S(1)} %pad_maximum_fusion.3), channel_id=1, source_target_pairs={{0,16},{4,20},{8,24},{12,28},{16,0},{20,4},{24,8},{28,12},{1,17},{... | collective-permute-start | bytes 884744 | tf_op jit(solution)/shard_map/ppermute | solution.py:11
  22.6 26.6 %collective-permute-start.12 = (bf16[2,576,128]{2,1,0:T(8,128)(2,1)S(1)}, bf16[2,576,128]{2,1,0:T(8,128)(2,1)S(1)}, u32[]{:S(2)}, u32[]{:S(2)}) collective-permute-start(bf16[2,576,128]{2,1,0:T(8,128)(2,1)S(1)} %pad_maximum_fusion.2), channel_id=1, source_target_pairs={{0,8},{4,12},{8,0},{12,4},{16,24},{20,28},{24,16},{28,20},{1,9},{5... | collective-permute-start | bytes 884744 | tf_op jit(solution)/shard_map/ppermute | solution.py:11
  49.1 10.8 %collective-permute-start.16 = (bf16[4,576,128]{2,1,0:T(8,128)(2,1)S(1)}, bf16[4,576,128]{2,1,0:T(8,128)(2,1)S(1)}, u32[]{:S(2)}, u32[]{:S(2)}) collective-permute-start(bf16[4,576,128]{2,1,0:T(8,128)(2,1)S(1)} %pad_maximum_fusion.1.refs_4_), channel_id=1, source_target_pairs={{0,4},{4,0},{8,12},{12,8},{16,20},{20,16},{24,28},{28,24},{1,5},{5... | collective-permute-start | bytes 1769480 | tf_op jit(solution)/shard_map/ppermute | solution.py:11
  49.3 13.1 %copy-start = (bf16[9,512,128]{2,1,0:T(8,128)(2,1)S(1)}, bf16[9,512,128]{2,1,0:T(8,128)(2,1)}, u32[]{:S(2)}) copy-start(bf16[9,512,128]{2,1,0:T(8,128)(2,1)} %refs_1_.1) | copy-start | bytes 3538948
  49.3 11.6 %collective-permute-start.13 = (bf16[4,576,128]{2,1,0:T(8,128)(2,1)S(1)}, bf16[4,576,128]{2,1,0:T(8,128)(2,1)S(1)}, u32[]{:S(2)}, u32[]{:S(2)}) collective-permute-start(bf16[4,576,128]{2,1,0:T(8,128)(2,1)S(1)} %pad_maximum_fusion.refs_2_), channel_id=1, source_target_pairs={{0,4},{4,0},{8,12},{12,8},{16,20},{20,16},{24,28},{28,24},{1,5},{5... | collective-permute-start | bytes 1769480 | tf_op jit(solution)/shard_map/ppermute | solution.py:11
  49.9 13.8 %collective-permute-start.6 = (bf16[2112,128]{1,0:T(8,128)(2,1)S(1)}, bf16[2112,128]{1,0:T(8,128)(2,1)S(1)}, u32[]{:S(2)}, u32[]{:S(2)}) collective-permute-start(bf16[2112,128]{1,0:T(8,128)(2,1)S(1)} %get-tuple-element.35), channel_id=1, source_target_pairs={{0,4},{4,8},{8,12},{12,16},{16,20},{20,24},{24,28},{1,5},{5,9},{9,... | collective-permute-start | bytes 1622024 | tf_op jit(solution)/shard_map/ppermute | solution.py:18
  52.0 11.7 %collective-permute-start.7 = (bf16[2112,128]{1,0:T(8,128)(2,1)S(1)}, bf16[2112,128]{1,0:T(8,128)(2,1)S(1)}, u32[]{:S(2)}, u32[]{:S(2)}) collective-permute-start(bf16[2112,128]{1,0:T(8,128)(2,1)S(1)} %get-tuple-element.36), channel_id=1, source_target_pairs={{4,0},{8,4},{12,8},{16,12},{20,16},{24,20},{28,24},{5,1},{9,5},{13... | collective-permute-start | bytes 1622024 | tf_op jit(solution)/shard_map/ppermute | solution.py:18
  53.3 14.7 %collective-permute-start.3 = (bf16[528,128]{1,0:T(8,128)(2,1)S(1)}, bf16[528,128]{1,0:T(8,128)(2,1)S(1)}, u32[]{:S(2)}, u32[]{:S(2)}) collective-permute-start(bf16[528,128]{1,0:T(8,128)(2,1)S(1)} %get-tuple-element.30), channel_id=1, source_target_pairs={{0,1},{1,0},{2,3},{3,2},{4,5},{5,4},{6,7},{7,6},{8,9},{9,8},{10,11... | collective-permute-start | bytes 405512 | tf_op jit(solution)/shard_map/ppermute | solution.py:11
  59.9 13.2 %collective-permute-start.4 = (bf16[528,128]{1,0:T(8,128)(2,1)S(1)}, bf16[528,128]{1,0:T(8,128)(2,1)S(1)}, u32[]{:S(2)}, u32[]{:S(2)}) collective-permute-start(bf16[528,128]{1,0:T(8,128)(2,1)S(1)} %get-tuple-element.41.refs_4_), channel_id=1, source_target_pairs={{0,2},{1,3},{2,0},{3,1},{4,6},{5,7},{6,4},{7,5},{8,10},{9,11},{10,... | collective-permute-start | bytes 405512 | tf_op jit(solution)/shard_map/ppermute | solution.py:11
  60.9 12.2 %collective-permute-start.5 = (bf16[528,128]{1,0:T(8,128)(2,1)S(1)}, bf16[528,128]{1,0:T(8,128)(2,1)S(1)}, u32[]{:S(2)}, u32[]{:S(2)}) collective-permute-start(bf16[528,128]{1,0:T(8,128)(2,1)S(1)} %get-tuple-element.30), channel_id=1, source_target_pairs={{0,3},{1,2},{2,1},{3,0},{4,7},{5,6},{6,5},{7,4},{8,11},{9,10},{10,... | collective-permute-start | bytes 405512 | tf_op jit(solution)/shard_map/ppermute | solution.py:11
  66.9 9.3 %collective-permute-start.17 = (bf16[1024,128]{1,0:T(8,128)(2,1)S(1)}, bf16[1024,128]{1,0:T(8,128)(2,1)S(1)}, u32[]{:S(2)}, u32[]{:S(2)}) collective-permute-start(bf16[1024,128]{1,0:T(8,128)(2,1)S(1)} %get-tuple-element.48), channel_id=1, source_target_pairs={{0,1},{1,0},{2,3},{3,2},{4,5},{5,4},{6,7},{7,6},{8,9},{9,8},{10,11... | collective-permute-start | bytes 786440 | tf_op jit(solution)/shard_map/ppermute | solution.py:11
  76.2 23.7 %collective-permute-start.18 = (bf16[1024,128]{1,0:T(8,128)(2,1)S(1)}, bf16[1024,128]{1,0:T(8,128)(2,1)S(1)}, u32[]{:S(2)}, u32[]{:S(2)}) collective-permute-start(bf16[1024,128]{1,0:T(8,128)(2,1)S(1)} %get-tuple-element.49), channel_id=1, source_target_pairs={{0,1},{1,0},{2,3},{3,2},{4,5},{5,4},{6,7},{7,6},{8,9},{9,8},{10,11... | collective-permute-start | bytes 786440 | tf_op jit(solution)/shard_map/ppermute | solution.py:11

commit v9 on v8

--- a/solution.py
+++ b/solution.py
@@ -163,13 +163,13 @@
         other[at : at + pitch] = jnp.where(side == 0, pieces[1], pieces[0])
 
 
-def rim_kernel(width, rows, *refs):
+def rim_kernel(width, *refs):
     pieces, (first, last) = refs[:4], refs[4:]
     pitch = width + 8
     for k, piece in enumerate(pieces):
         for i in range(2):
             for out, end in ((first, 0), (last, 1)):
-                at = (i * rows + end * (1 if i else rows - 1)) * pitch
+                at = (2 * i + end) * pitch
                 out[(2 * k + i) * pitch : (2 * k + i + 1) * pitch] = piece[at : at + pitch]
 
 
@@ -190,13 +190,19 @@
             fill_rows(target, ref, at * pitch, r, lanes, width)
 
 
+def inside(edges, inners, which, count):
+    return [
+        [(p, 2 * which), *((q, r) for r in range(count - 2)), (p, 2 * which + 1)]
+        for p, q in zip(edges, inners)
+    ]
+
+
 def backward_kernel(*refs):
-    edges, (before, after, weights, mine, other, source) = refs[:4], refs[4:]
+    edges, inners, (before, after, weights, _, mine, other, source) = refs[:4], refs[4:8], refs[8:]
     size, local = mine.shape
     width = before.shape[0] // 8 - 8
     channels = 4 * local
-    rows = [[(p, r) for r in range(size // width)] for p in edges]
-    fill_source(source, 0, width, rows, before, after)
+    fill_source(source, 0, width, inside(edges, inners, 0, size // width), before, after)
     acc = None
     for a in range(3):
         for b in range(3):
@@ -216,12 +222,7 @@
     size, local = mine.shape
     width = before.shape[0] // 8 - 8
     channels, half = 4 * local, 2 * local
-    count = size // width
-    rows = [
-        [(p, count), *((q, r) for r in range(count - 2)), (p, count + 1)]
-        for p, q in zip(edges, inners)
-    ]
-    fill_source(source, 1, width, rows, before, after)
+    fill_source(source, 1, width, inside(edges, inners, 1, size // width), before, after)
     acc = None
     for a in range(3):
         for b in range(3):
@@ -248,7 +249,12 @@
 ANY = pl.BlockSpec(memory_space=pl.ANY)
 
 
-def kernel(body, shapes, args, scratch, name, placed=False, flops=2**20):
+def cost(microseconds):
+    work = 2**20 + 10**9 * microseconds
+    return pl.CostEstimate(flops=work, bytes_accessed=2**20, transcendentals=0)
+
+
+def kernel(body, shapes, args, scratch, name, placed=False, micros=0):
     return pl.pallas_call(
         body,
         out_shape=[jax.ShapeDtypeStruct(s, jnp.bfloat16) for s in shapes],
@@ -256,16 +262,16 @@
         out_specs=[VMEM] * len(shapes),
         scratch_shapes=[pltpu.VMEM(s, jnp.bfloat16) for s in scratch],
         compiler_params=pltpu.CompilerParams(vmem_limit_bytes=32 * 2**20),
-        cost_estimate=pl.CostEstimate(flops=flops, bytes_accessed=2**20, transcendentals=0),
+        cost_estimate=cost(micros),
         name=name,
     )(*args)
 
 
-def cut(place, sources, bias, parts, name, flops):
+def cut(place, sources, bias, parts, name, micros):
     local = bias.shape[1]
     shape = (len(parts) * (sources[0].shape[1] // 2 + 8), local)
     body = lambda *refs: cut_kernel(parts, *refs)
-    return kernel(body, [shape] * 2, [place, *sources, bias], [], name, True, flops)
+    return kernel(body, [shape] * 2, [place, *sources, bias], [], name, True, micros)
 
 
 def exchange(mine, other):
@@ -294,35 +300,38 @@
     return steps
 
 
-def home_kernel(place, mine, other, out, sems):
+def home_kernel(place, mine, other, out):
     width = mine.shape[2]
     side = place[0] & 1
-    copies = []
-    for i, ref in enumerate((mine, other)):
-        start = pl.multiple_of((side ^ i) * width, width)
-        copies.append(pltpu.make_async_copy(ref, out.at[:, :, pl.ds(start, width)], sems.at[i]))
-    for copy in copies:
-        copy.start()
-    for copy in copies:
-        copy.wait()
+    for t in range(2):
+
+        @pl.when(side == t)
+        def _():
+            out[:, :, t * width : (t + 1) * width] = mine[...]
+            out[:, :, (1 - t) * width : (2 - t) * width] = other[...]
 
 
 def home(place, mine, other, rows):
     turn = lambda p: jnp.transpose(p.reshape(rows, -1, p.shape[1]), (2, 0, 1))
     mine, other = turn(mine), turn(other)
     channels, rows, width = mine.shape
+    shape = (channels, rows, 2 * width)
+    return kernel(home_kernel, [shape], [place, mine, other], [], "home", True)[0]
+
+
+def token_kernel(*refs):
+    refs[-1][...] = jnp.zeros_like(refs[-1])
+
+
+def token(pieces, micros):
     return pl.pallas_call(
-        home_kernel,
-        out_shape=jax.ShapeDtypeStruct((channels, rows, 2 * width), jnp.bfloat16),
-        in_specs=[SMEM, ANY, ANY],
-        out_specs=ANY,
-        scratch_shapes=[pltpu.SemaphoreType.DMA((2,))],
-        cost_estimate=pl.CostEstimate(flops=2**20, bytes_accessed=2**20, transcendentals=0),
-        name="home",
-    )(place, mine, other)
-
-
-MICROSECOND = 10**9
+        token_kernel,
+        out_shape=jax.ShapeDtypeStruct((16, 128), jnp.bfloat16),
+        in_specs=[ANY] * len(pieces),
+        out_specs=VMEM,
+        cost_estimate=cost(micros),
+        name="token",
+    )(*pieces)
 
 
 def per_device(image, filters, bias, upstream):
@@ -346,14 +355,14 @@
     across = jnp.concatenate([swap(across, "chan", k) for k in (2, 3)])
 
     upstream, image = [jnp.transpose(v, (1, 2, 0)) for v in (upstream, image)]
-    parts = [(0, r) for r in range(rows)] + [(1, 0), (1, rows - 1)]
-    edge = cut(place, [upstream, image], bias[None], parts, "cut_first", 2**20)
+    parts = [(i, r) for i in range(2) for r in (0, rows - 1)]
+    edge = cut(place, [upstream, image], bias[None], parts, "cut_edge", 0)
     near, across = after((near, across), edge)
     edge = exchange(*edge)
     parts = [(0, r) for r in range(1, rows - 1)]
-    late = cut(place, [after(image, edge[1])], bias[None], parts, "cut_second", 2**20)
-    edge = after(edge, late)
-    second = exchange(*late)
+    first = exchange(*cut(place, [upstream], bias[None], parts, "cut_first", 0))
+    second = exchange(*cut(place, [image], bias[None], parts, "cut_second", 0))
+    mark = token(first, 18)
 
     steps = halving(bands)[:-1]
     near, near_order = gather(near, steps)
@@ -366,20 +375,20 @@
         [],
         "assemble",
         True,
-        2 * MICROSECOND,
+        2,
     )
     rim = (8 * (width + 8), local)
-    body = lambda *refs: rim_kernel(width, rows, *refs)
-    rims = neighbours(*kernel(body, [rim] * 2, edge, [], "rim", False, 4 * MICROSECOND))
+    body = lambda *refs: rim_kernel(width, *refs)
+    rims = neighbours(*kernel(body, [rim] * 2, edge, [], "rim", False, 16))
 
     out = [(rows * width, local)] * 2
     source = [(3, (rows + 2) * width, 4 * local)]
-    args = [*edge, *rims, weights]
-    mine, other = kernel(backward_kernel, out, args, source, "backward", False, 10 * MICROSECOND)
+    args = [*edge, *first, *rims, weights, mark]
+    mine, other = kernel(backward_kernel, out, args, source, "backward", False, 10)
     other = swap(other, "chan", 1)
     image_grad = home(place, mine, other, rows)
     args = [*edge, *after(second, mine), *rims, weights, extra]
-    mine, sent = kernel(forward_kernel, out, args, source, "forward", False, 5 * MICROSECOND)
+    mine, sent = kernel(forward_kernel, out, args, source, "forward", False, 5)
     other = swap(after(sent, other), "chan", 1)
     return home(place, mine, other, rows), image_grad
 

time: 121 us -> 91.3 us (0.75); the launches traced: 119 us -> 90.6 us
  Pallas kernels: 44.3 us -> 17.1 us
  starting transfers between devices: 31.9 us -> 39.7 us
  waiting for transfers between devices: 33.9 us -> 27 us
  local copies, waits for them, and re-layouts: 7.3 us -> 5.55 us
    pallas_call x2 -> x1, Pallas kernels: 35.3 us -> 0.59 us  [token(): pl.pallas_call(token_kernel, out_shape=jax.ShapeDtypeStruct((16, 128), jn...]
    pallas_call x6 -> x9, Pallas kernels: 8.95 us -> 16.5 us  [kernel(): pl.pallas_call(body, out_shape=[jax.ShapeDtypeStruct(s, jnp.bfloat16) for...]
    ppermute x17 -> x20, starting transfers between devices: 28.5 us -> 35.6 us  [swap(): return lax.ppermute(value, axis, [(j, j ^ step) for j in range(size)])]
    ppermute x17 -> x20, waiting for transfers between devices: 33.9 us -> 27 us  [swap(): return lax.ppermute(value, axis, [(j, j ^ step) for j in range(size)])]
    reshape x4, local copies, waits for them, and re-layouts: 3.52 us -> 0.78 us  [home(): turn = lambda p: jnp.transpose(p.reshape(rows, -1, p.shape[1]), (2, 0, 1))]
    unnamed x10 -> x46, local copies, waits for them, and re-layouts: 1.89 us -> 2.89 us
  transfers between devices with their start and end apart: 19 -> 22, of which waited for: 5 -> 10; matrix products, arithmetic and copies ran while one was open for 5% -> 4% of each run, Pallas kernels for 22% -> 17%
where the time goes in v9:
time: 91.3 us; the launch traced here: 90.6 us
  starting transfers between devices  39.7 us (43%)
  waiting for transfers between devices  27 us (30%)
  Pallas kernels  17.1 us (19%)
  local copies, waits for them, and re-layouts  5.55 us (6%)
  between operations  1.01 us (1%)
    ppermute x20, starting transfers between devices, swap(): return lax.ppermute(value, axis, [(j, j ^ step) for j in range(size)])  35.6 us
    ppermute x20, waiting for transfers between devices, swap(): return lax.ppermute(value, axis, [(j, j ^ step) for j in range(size)])  27 us
    pallas_call x9, Pallas kernels, kernel(): pl.pallas_call(body, out_shape=[jax.ShapeDtypeStruct(s, jnp.bfloat16) for...  16.5 us
    ppermute x2, starting transfers between devices, neighbours(): return (lax.ppermute(last, 'band', up), lax.ppermute(first, 'band', down))  4.07 us
    unnamed x46, local copies, waits for them, and re-layouts  2.89 us
  transfers between devices with their start and end apart: 22, of which 10 were waited for; matrix products, arithmetic and copies ran while one was open for 4% of the time, Pallas kernels for 17%

profile of v9, /device:TPU:0, one launch (start us, length us, event | category | flops | bytes accessed | tf_op | source)
XLA Modules:
  0.0 90.6 jit_solution(15031580097390062166)
XLA Ops:
  0.6 1.0 %constant_dynamic-slice_fusion = bf16[9,32,128]{2,1,0:T(8,128)(2,1)S(1)} fusion(bf16[9,512,128]{2,1,0:T(8,128)(2,1)} %refs_1_.1, s32[]{:T(128)S(6)} %select_n.7), kind=kLoop, calls=%fused_computation.6 | loop fusion | bytes 147460 | tf_op jit(solution)/shard_map/dynamic_slice | solution.py:353
  1.6 4.0 %collective-permute-start.12 = (bf16[288,128]{1,0:T(8,128)(2,1)S(1)}, bf16[288,128]{1,0:T(8,128)(2,1)S(1)}, u32[]{:S(2)}, u32[]{:S(2)}) collective-permute-start(bf16[288,128]{1,0:T(8,128)(2,1)S(1)} %bitcast.39), channel_id=1, source_target_pairs={{0,2},{1,3},{2,0},{3,1},{4,6},{5,7},{6,4},{7,5},{8,10},{9,11},{10,... | collective-permute-start | bytes 221192 | tf_op jit(solution)/shard_map/ppermute | solution.py:11
  5.6 1.3 %collective-permute-start.13 = (bf16[288,128]{1,0:T(8,128)(2,1)S(1)}, bf16[288,128]{1,0:T(8,128)(2,1)S(1)}, u32[]{:S(2)}, u32[]{:S(2)}) collective-permute-start(bf16[288,128]{1,0:T(8,128)(2,1)S(1)} %bitcast.40), channel_id=1, source_target_pairs={{0,3},{1,2},{2,1},{3,0},{4,7},{5,6},{6,5},{7,4},{8,11},{9,10},{10,... | collective-permute-start | bytes 221192 | tf_op jit(solution)/shard_map/ppermute | solution.py:11
  7.0 0.9 %constant_dynamic-slice_fusion.1 = bf16[9,64,128]{2,1,0:T(8,128)(2,1)S(1)} fusion(bf16[9,512,128]{2,1,0:T(8,128)(2,1)} %refs_1_.1, s32[]{:T(128)S(6)} %select_n.6), kind=kLoop, calls=%fused_computation.7 | loop fusion | bytes 294916 | tf_op jit(solution)/shard_map/dynamic_slice | solution.py:351
  7.9 0.3 collective-permute-start.11
  8.2 0.1 pad_add_fusion.refs_0_.place
  8.3 1.5 %copy.6 = bf16[128,4,512]{0,2,1:T(8,128)(2,1)S(1)} copy(bf16[128,4,512]{2,1,0:T(4,128)(2,1)} %param.7) | data formatting | bytes 1048576 | tf_op args[3]
  9.8 0.4 copy.7
  10.2 0.7 cut_edge.1
  10.9 0.0 copy-start.2
  10.9 0.0 collective-permute-done.12
  10.9 1.6 %collective-permute-done.13 = bf16[288,128]{1,0:T(8,128)(2,1)S(1)} collective-permute-done((bf16[288,128]{1,0:T(8,128)(2,1)S(1)}, bf16[288,128]{1,0:T(8,128)(2,1)S(1)}, u32[]{:S(2)}, u32[]{:S(2)}) %collective-permute-start.13) | collective-permute-done | bytes 73760 | tf_op jit(solution)/shard_map/ppermute | solution.py:11
  12.6 1.8 %collective-permute-done.11 = bf16[576,128]{1,0:T(8,128)(2,1)S(1)} collective-permute-done((bf16[576,128]{1,0:T(8,128)(2,1)S(1)}, bf16[576,128]{1,0:T(8,128)(2,1)S(1)}, u32[]{:S(2)}, u32[]{:S(2)}) %collective-permute-start.11) | collective-permute-done | bytes 147488 | tf_op jit(solution)/shard_map/ppermute | solution.py:11
  14.4 1.7 %collective-permute-start.17 = (bf16[1,576,128]{2,1,0:T(8,128)(2,1)S(1)}, bf16[1,576,128]{2,1,0:T(8,128)(2,1)S(1)}, u32[]{:S(2)}, u32[]{:S(2)}) collective-permute-start(bf16[1,576,128]{2,1,0:T(8,128)(2,1)S(1)} %bitcast.30), channel_id=1, source_target_pairs={{0,8},{4,12},{8,0},{12,4},{16,24},{20,28},{24,16},{28,20},{1,9},{5... | collective-permute-start | bytes 442376 | tf_op jit(solution)/shard_map/ppermute | solution.py:11
  16.1 1.1 %collective-permute-start.1 = (bf16[1056,128]{1,0:T(8,128)(2,1)S(1)}, bf16[1056,128]{1,0:T(8,128)(2,1)S(1)}, u32[]{:S(2)}, u32[]{:S(2)}) collective-permute-start(bf16[1056,128]{1,0:T(8,128)(2,1)S(1)} %get-tuple-element.23.refs_0_), channel_id=1, source_target_pairs={{0,2},{1,3},{2,0},{3,1},{4,6},{5,7},{6,4},{7,5},{8,10},{9,11},{10,... | collective-permute-start | bytes 811016 | tf_op jit(solution)/shard_map/ppermute | solution.py:11
  17.2 2.5 %collective-permute-start = (bf16[1056,128]{1,0:T(8,128)(2,1)S(1)}, bf16[1056,128]{1,0:T(8,128)(2,1)S(1)}, u32[]{:S(2)}, u32[]{:S(2)}) collective-permute-start(bf16[1056,128]{1,0:T(8,128)(2,1)S(1)} %get-tuple-element.24), channel_id=1, source_target_pairs={{0,1},{1,0},{2,3},{3,2},{4,5},{5,4},{6,7},{7,6},{8,9},{9,8},{10,11... | collective-permute-start | bytes 811016 | tf_op jit(solution)/shard_map/ppermute | solution.py:11
  19.7 0.8 collective-permute-start.2
  20.5 1.5 %collective-permute-start.14 = (bf16[1,576,128]{2,1,0:T(8,128)(2,1)S(1)}, bf16[1,576,128]{2,1,0:T(8,128)(2,1)S(1)}, u32[]{:S(2)}, u32[]{:S(2)}) collective-permute-start(bf16[1,576,128]{2,1,0:T(8,128)(2,1)S(1)} %bitcast.33), channel_id=1, source_target_pairs={{0,16},{4,20},{8,24},{12,28},{16,0},{20,4},{24,8},{28,12},{1,17},{... | collective-permute-start | bytes 442376 | tf_op jit(solution)/shard_map/ppermute | solution.py:11
  22.0 0.6 cut_first.1
  22.7 1.3 %cut_second.1 = (bf16[528,128]{1,0:T(8,128)(2,1)S(1)}, bf16[528,128]{1,0:T(8,128)(2,1)}) custom-call(s32[2]{0:T(128)S(1)} %pad_add_fusion.refs_0_.place, bf16[4,512,128]{2,1,0:T(8,128)(2,1)S(1)} %bitcast.18, bf16[1,128]{1,0:T(2,128)(2,1)S(1)} %bitcast.29), custom_call_target="tpu_custom_call" | custom-call | flops 1048576 | bytes 1048576 | tf_op jit(solution)/shard_map/cut_second/pallas_call | solution.py:258
  23.9 0.0 collective-permute-done.17
  23.9 0.0 collective-permute-start.6
  24.0 1.7 %collective-permute-done.14 = bf16[1,576,128]{2,1,0:T(8,128)(2,1)S(1)} collective-permute-done((bf16[1,576,128]{2,1,0:T(8,128)(2,1)S(1)}, bf16[1,576,128]{2,1,0:T(8,128)(2,1)S(1)}, u32[]{:S(2)}, u32[]{:S(2)}) %collective-permute-start.14) | collective-permute-done | bytes 147488 | tf_op jit(solution)/shard_map/ppermute | solution.py:11
  25.7 3.0 %collective-permute-start.8 = (bf16[528,128]{1,0:T(8,128)(2,1)S(1)}, bf16[528,128]{1,0:T(8,128)(2,1)S(1)}, u32[]{:S(2)}, u32[]{:S(2)}) collective-permute-start(bf16[528,128]{1,0:T(8,128)(2,1)S(1)} %get-tuple-element.28), channel_id=1, source_target_pairs={{0,3},{1,2},{2,1},{3,0},{4,7},{5,6},{6,5},{7,4},{8,11},{9,10},{10,... | collective-permute-start | bytes 405512 | tf_op jit(solution)/shard_map/ppermute | solution.py:11
  28.7 7.6 %collective-permute-done.1.refs_2_ = bf16[1056,128]{1,0:T(8,128)(2,1)S(1)} collective-permute-done((bf16[1056,128]{1,0:T(8,128)(2,1)S(1)}, bf16[1056,128]{1,0:T(8,128)(2,1)S(1)}, u32[]{:S(2)}, u32[]{:S(2)}) %collective-permute-start.1) | collective-permute-done | bytes 270368 | tf_op jit(solution)/shard_map/ppermute | solution.py:11
  36.3 0.0 collective-permute-start.7
  36.3 0.4 collective-permute-done.refs_1_
  36.7 2.2 %collective-permute-start.18 = (bf16[2,576,128]{2,1,0:T(8,128)(2,1)S(1)}, bf16[2,576,128]{2,1,0:T(8,128)(2,1)S(1)}, u32[]{:S(2)}, u32[]{:S(2)}) collective-permute-start(bf16[2,576,128]{2,1,0:T(8,128)(2,1)S(1)} %pad_maximum_fusion.3), channel_id=1, source_target_pairs={{0,16},{4,20},{8,24},{12,28},{16,0},{20,4},{24,8},{28,12},{1,17},{... | collective-permute-start | bytes 884744 | tf_op jit(solution)/shard_map/ppermute | solution.py:11
  38.9 0.0 collective-permute-done.2.refs_3_
  38.9 0.6 collective-permute-start.15
  39.5 1.1 %rim.1 = (bf16[2112,128]{1,0:T(8,128)(2,1)}, bf16[2112,128]{1,0:T(8,128)(2,1)}) custom-call(bf16[1056,128]{1,0:T(8,128)(2,1)S(1)} %get-tuple-element.23.refs_0_, bf16[1056,128]{1,0:T(8,128)(2,1)S(1)} %collective-permute-done.refs_1_, bf16[1056,128]{1,0:T(8,128)(2,1)S(1)} %collective-permute-done.1.refs_2_, bf16[1056,128]{1,0:T(8,128)(2,1)S(1)} %collective-permute-done.2.refs_3_), custom_call_target="tpu_custom_call" | custom-call | flops 16001048576 | bytes 1048576 | tf_op jit(solution)/shard_map/rim/pallas_call | solution.py:258
  40.6 3.0 %collective-permute-done.18 = bf16[2,576,128]{2,1,0:T(8,128)(2,1)S(1)} collective-permute-done((bf16[2,576,128]{2,1,0:T(8,128)(2,1)S(1)}, bf16[2,576,128]{2,1,0:T(8,128)(2,1)S(1)}, u32[]{:S(2)}, u32[]{:S(2)}) %collective-permute-start.18) | collective-permute-done | bytes 294944 | tf_op jit(solution)/shard_map/ppermute | solution.py:11
  43.6 7.4 %collective-permute-start.3 = (bf16[528,128]{1,0:T(8,128)(2,1)}, bf16[528,128]{1,0:T(8,128)(2,1)}, u32[]{:S(2)}, u32[]{:S(2)}) collective-permute-start(bf16[528,128]{1,0:T(8,128)(2,1)} %get-tuple-element.26), channel_id=1, source_target_pairs={{0,1},{1,0},{2,3},{3,2},{4,5},{5,4},{6,7},{7,6},{8,9},{9,8},{10,11... | collective-permute-start | bytes 405512 | tf_op jit(solution)/shard_map/ppermute | solution.py:11
  51.0 0.1 pad_maximum_fusion.1.refs_4_
  51.1 0.0 collective-permute-done.15
  51.1 1.3 %collective-permute-start.10 = (bf16[2112,128]{1,0:T(8,128)(2,1)}, bf16[2112,128]{1,0:T(8,128)(2,1)}, u32[]{:S(2)}, u32[]{:S(2)}) collective-permute-start(bf16[2112,128]{1,0:T(8,128)(2,1)} %get-tuple-element.30), channel_id=1, source_target_pairs={{4,0},{8,4},{12,8},{16,12},{20,16},{24,20},{28,24},{5,1},{9,5},{13... | collective-permute-start | bytes 1622024 | tf_op jit(solution)/shard_map/ppermute | solution.py:18
  52.4 0.1 pad_maximum_fusion.refs_2_
  52.5 1.2 %collective-permute-done.7.refs_2_.refs_6_ = bf16[528,128]{1,0:T(8,128)(2,1)S(1)} collective-permute-done((bf16[528,128]{1,0:T(8,128)(2,1)S(1)}, bf16[528,128]{1,0:T(8,128)(2,1)S(1)}, u32[]{:S(2)}, u32[]{:S(2)}) %collective-permute-start.7) | collective-permute-done | bytes 135200 | tf_op jit(solution)/shard_map/ppermute | solution.py:11
  53.7 2.8 %collective-permute-start.9 = (bf16[2112,128]{1,0:T(8,128)(2,1)}, bf16[2112,128]{1,0:T(8,128)(2,1)}, u32[]{:S(2)}, u32[]{:S(2)}) collective-permute-start(bf16[2112,128]{1,0:T(8,128)(2,1)} %get-tuple-element.29), channel_id=1, source_target_pairs={{0,4},{4,8},{8,12},{12,16},{16,20},{20,24},{24,28},{1,5},{5,9},{9,... | collective-permute-start | bytes 1622024 | tf_op jit(solution)/shard_map/ppermute | solution.py:18
  56.5 0.0 collective-permute-done.6.refs_1_.refs_5_
  56.5 0.4 collective-permute-start.19
  56.9 0.3 copy-done.14
  57.1 0.0 collective-permute-done.8.refs_3_.refs_7_
  57.1 0.7 copy-done.16
  57.8 0.3 collective-permute-start.16
  58.1 0.6 token_.1.refs_11_
  58.7 0.0 collective-permute-done.19.refs_5_
  58.7 2.3 %collective-permute-start.5 = (bf16[528,128]{1,0:T(8,128)(2,1)}, bf16[528,128]{1,0:T(8,128)(2,1)S(1)}, u32[]{:S(2)}, u32[]{:S(2)}) collective-permute-start(bf16[528,128]{1,0:T(8,128)(2,1)} %get-tuple-element.26), channel_id=1, source_target_pairs={{0,3},{1,2},{2,1},{3,0},{4,7},{5,6},{6,5},{7,4},{8,11},{9,10},{10,... | collective-permute-start | bytes 405512 | tf_op jit(solution)/shard_map/ppermute | solution.py:11
  61.0 0.0 collective-permute-done.16.refs_3_
  61.0 6.1 %collective-permute-start.4 = (bf16[528,128]{1,0:T(8,128)(2,1)}, bf16[528,128]{1,0:T(8,128)(2,1)S(1)}, u32[]{:S(2)}, u32[]{:S(2)}) collective-permute-start(bf16[528,128]{1,0:T(8,128)(2,1)} %copy-done.10), channel_id=1, source_target_pairs={{0,2},{1,3},{2,0},{3,1},{4,6},{5,7},{6,4},{7,5},{8,10},{9,11},{10,... | collective-permute-start | bytes 405512 | tf_op jit(solution)/shard_map/ppermute | solution.py:11
  67.1 1.3 %assemble.1 = (bf16[4608,256]{1,0:T(8,128)(2,1)S(1)}, bf16[2304,256]{1,0:T(8,128)(2,1)S(1)}) custom-call(s32[2]{0:T(128)S(1)} %pad_add_fusion.refs_0_.place, bf16[9,512,128]{2,1,0:T(8,128)(2,1)S(1)} %copy-done, bf16[4,576,128]{2,1,0:T(8,128)(2,1)S(1)} %pad_maximum_fusion.refs_2_, bf16[4,576,128]{2,1,0:T(8,128)(2,1)S(1)} %collective-permute-done.16.refs_3_, ...), custom_call_target="tpu_custom_call" | custom-call | flops 2001048576 | bytes 1048576 | tf_op jit(solution)/shard_map/assemble/pallas_call | solution.py:258
  68.5 4.4 %backward.1 = (bf16[1024,128]{1,0:T(8,128)(2,1)S(1)}, bf16[1024,128]{1,0:T(8,128)(2,1)S(1)}) custom-call(bf16[1056,128]{1,0:T(8,128)(2,1)S(1)} %copy-done.3, bf16[1056,128]{1,0:T(8,128)(2,1)S(1)} %copy-done.7, bf16[1056,128]{1,0:T(8,128)(2,1)S(1)} %copy-done.5, bf16[1056,128]{1,0:T(8,128)(2,1)S(1)} %copy-done.9, bf16[528,128]{1,0:T(8,128)(2,1)S(1)} %copy-done.13, ...), custom_call_target="tpu_custom_call" | custom-call | flops 10001048576 | bytes 1048576 | tf_op jit(solution)/shard_map/backward/pallas_call | solution.py:258
  72.9 0.1 collective-permute-start.20
  73.0 2.8 %collective-permute-done.4.refs_6_ = bf16[528,128]{1,0:T(8,128)(2,1)S(1)} collective-permute-done((bf16[528,128]{1,0:T(8,128)(2,1)}, bf16[528,128]{1,0:T(8,128)(2,1)S(1)}, u32[]{:S(2)}, u32[]{:S(2)}) %collective-permute-start.4) | collective-permute-done | bytes 135200 | tf_op jit(solution)/shard_map/ppermute | solution.py:11
  75.9 4.3 %forward.1 = (bf16[1024,128]{1,0:T(8,128)(2,1)S(1)}, bf16[1024,128]{1,0:T(8,128)(2,1)S(1)}) custom-call(bf16[1056,128]{1,0:T(8,128)(2,1)S(1)} %copy-done.3, bf16[1056,128]{1,0:T(8,128)(2,1)S(1)} %copy-done.7, bf16[1056,128]{1,0:T(8,128)(2,1)S(1)} %copy-done.5, bf16[1056,128]{1,0:T(8,128)(2,1)S(1)} %copy-done.9, bf16[528,128]{1,0:T(8,128)(2,1)S(1)} %copy-done.11, ...), custom_call_target="tpu_custom_call" | custom-call | flops 5001048576 | bytes 1048576 | tf_op jit(solution)/shard_map/forward/pallas_call | solution.py:258
  80.1 1.3 %collective-permute-done.20 = bf16[1024,128]{1,0:T(8,128)(2,1)S(1)} collective-permute-done((bf16[1024,128]{1,0:T(8,128)(2,1)S(1)}, bf16[1024,128]{1,0:T(8,128)(2,1)S(1)}, u32[]{:S(2)}, u32[]{:S(2)}) %collective-permute-start.20) | collective-permute-done | bytes 262176 | tf_op jit(solution)/shard_map/ppermute | solution.py:11
  81.4 0.0 collective-permute-start.21
  81.4 0.2 copy.14
  81.6 0.2 copy.12
  81.8 0.2 copy.15
  82.0 1.4 %home.3 = bf16[128,4,512]{2,1,0:T(4,128)(2,1)} custom-call(s32[2]{0:T(128)S(1)} %pad_add_fusion.refs_0_.place, bf16[128,4,256]{2,1,0:T(4,128)(2,1)S(1)} %bitcast.22, bf16[128,4,256]{2,1,0:T(4,128)(2,1)S(1)} %bitcast.24), custom_call_target="tpu_custom_call" | custom-call | flops 1048576 | bytes 1048576 | tf_op jit(solution)/shard_map/home/pallas_call | solution.py:258
  83.5 5.5 %collective-permute-done.21 = bf16[1024,128]{1,0:T(8,128)(2,1)S(1)} collective-permute-done((bf16[1024,128]{1,0:T(8,128)(2,1)S(1)}, bf16[1024,128]{1,0:T(8,128)(2,1)S(1)}, u32[]{:S(2)}, u32[]{:S(2)}) %collective-permute-start.21) | collective-permute-done | bytes 262176 | tf_op jit(solution)/shard_map/ppermute | solution.py:11
  89.0 0.2 copy.13
  89.2 1.4 %home.2 = bf16[128,4,512]{2,1,0:T(4,128)(2,1)} custom-call(s32[2]{0:T(128)S(1)} %pad_add_fusion.refs_0_.place, bf16[128,4,256]{2,1,0:T(4,128)(2,1)S(1)} %bitcast.21, bf16[128,4,256]{2,1,0:T(4,128)(2,1)S(1)} %bitcast.23), custom_call_target="tpu_custom_call" | custom-call | flops 1048576 | bytes 1048576 | tf_op jit(solution)/shard_map/home/pallas_call | solution.py:258
  (48 shorter events, 0.2 us)
Async XLA Ops:
  0.6 9.1 %copy-start.21 = (bf16[128,4,512]{2,1,0:T(4,128)(2,1)S(1)}, bf16[128,4,512]{2,1,0:T(4,128)(2,1)}, u32[]{:S(2)}) copy-start(bf16[128,4,512]{2,1,0:T(4,128)(2,1)} %param.4) | copy-start | bytes 1572868
  1.6 9.3 %collective-permute-start.12 = (bf16[288,128]{1,0:T(8,128)(2,1)S(1)}, bf16[288,128]{1,0:T(8,128)(2,1)S(1)}, u32[]{:S(2)}, u32[]{:S(2)}) collective-permute-start(bf16[288,128]{1,0:T(8,128)(2,1)S(1)} %bitcast.39), channel_id=1, source_target_pairs={{0,2},{1,3},{2,0},{3,1},{4,6},{5,7},{6,4},{7,5},{8,10},{9,11},{10,... | collective-permute-start | bytes 221192 | tf_op jit(solution)/shard_map/ppermute | solution.py:11
  5.6 6.9 %collective-permute-start.13 = (bf16[288,128]{1,0:T(8,128)(2,1)S(1)}, bf16[288,128]{1,0:T(8,128)(2,1)S(1)}, u32[]{:S(2)}, u32[]{:S(2)}) collective-permute-start(bf16[288,128]{1,0:T(8,128)(2,1)S(1)} %bitcast.40), channel_id=1, source_target_pairs={{0,3},{1,2},{2,1},{3,0},{4,7},{5,6},{6,5},{7,4},{8,11},{9,10},{10,... | collective-permute-start | bytes 221192 | tf_op jit(solution)/shard_map/ppermute | solution.py:11
  7.0 3.2 %copy-start.1 = (bf16[128]{0:T(256)(128)(2,1)S(1)}, bf16[128]{0:T(256)(128)(2,1)}, u32[]{:S(2)}) copy-start(bf16[128]{0:T(256)(128)(2,1)} %param.6) | copy-start | bytes 772
  7.9 6.5 %collective-permute-start.11 = (bf16[576,128]{1,0:T(8,128)(2,1)S(1)}, bf16[576,128]{1,0:T(8,128)(2,1)S(1)}, u32[]{:S(2)}, u32[]{:S(2)}) collective-permute-start(bf16[576,128]{1,0:T(8,128)(2,1)S(1)} %bitcast.38), channel_id=1, source_target_pairs={{0,1},{1,0},{2,3},{3,2},{4,5},{5,4},{6,7},{7,6},{8,9},{9,8},{10,11... | collective-permute-start | bytes 442376 | tf_op jit(solution)/shard_map/ppermute | solution.py:11
  10.9 28.6 %copy-start.2 = (bf16[1056,128]{1,0:T(8,128)(2,1)}, bf16[1056,128]{1,0:T(8,128)(2,1)S(1)}, u32[]{:S(2)}) copy-start(bf16[1056,128]{1,0:T(8,128)(2,1)S(1)} %get-tuple-element.23.refs_0_) | copy-start | bytes 811012
  14.4 9.6 %collective-permute-start.17 = (bf16[1,576,128]{2,1,0:T(8,128)(2,1)S(1)}, bf16[1,576,128]{2,1,0:T(8,128)(2,1)S(1)}, u32[]{:S(2)}, u32[]{:S(2)}) collective-permute-start(bf16[1,576,128]{2,1,0:T(8,128)(2,1)S(1)} %bitcast.30), channel_id=1, source_target_pairs={{0,8},{4,12},{8,0},{12,4},{16,24},{20,28},{24,16},{28,20},{1,9},{5... | collective-permute-start | bytes 442376 | tf_op jit(solution)/shard_map/ppermute | solution.py:11
  16.1 20.2 %collective-permute-start.1 = (bf16[1056,128]{1,0:T(8,128)(2,1)S(1)}, bf16[1056,128]{1,0:T(8,128)(2,1)S(1)}, u32[]{:S(2)}, u32[]{:S(2)}) collective-permute-start(bf16[1056,128]{1,0:T(8,128)(2,1)S(1)} %get-tuple-element.23.refs_0_), channel_id=1, source_target_pairs={{0,2},{1,3},{2,0},{3,1},{4,6},{5,7},{6,4},{7,5},{8,10},{9,11},{10,... | collective-permute-start | bytes 811016 | tf_op jit(solution)/shard_map/ppermute | solution.py:11
  17.2 19.5 %collective-permute-start = (bf16[1056,128]{1,0:T(8,128)(2,1)S(1)}, bf16[1056,128]{1,0:T(8,128)(2,1)S(1)}, u32[]{:S(2)}, u32[]{:S(2)}) collective-permute-start(bf16[1056,128]{1,0:T(8,128)(2,1)S(1)} %get-tuple-element.24), channel_id=1, source_target_pairs={{0,1},{1,0},{2,3},{3,2},{4,5},{5,4},{6,7},{7,6},{8,9},{9,8},{10,11... | collective-permute-start | bytes 811016 | tf_op jit(solution)/shard_map/ppermute | solution.py:11
  19.7 19.2 %collective-permute-start.2 = (bf16[1056,128]{1,0:T(8,128)(2,1)S(1)}, bf16[1056,128]{1,0:T(8,128)(2,1)S(1)}, u32[]{:S(2)}, u32[]{:S(2)}) collective-permute-start(bf16[1056,128]{1,0:T(8,128)(2,1)S(1)} %get-tuple-element.24), channel_id=1, source_target_pairs={{0,3},{1,2},{2,1},{3,0},{4,7},{5,6},{6,5},{7,4},{8,11},{9,10},{10,... | collective-permute-start | bytes 811016 | tf_op jit(solution)/shard_map/ppermute | solution.py:11
  20.5 5.1 %collective-permute-start.14 = (bf16[1,576,128]{2,1,0:T(8,128)(2,1)S(1)}, bf16[1,576,128]{2,1,0:T(8,128)(2,1)S(1)}, u32[]{:S(2)}, u32[]{:S(2)}) collective-permute-start(bf16[1,576,128]{2,1,0:T(8,128)(2,1)S(1)} %bitcast.33), channel_id=1, source_target_pairs={{0,16},{4,20},{8,24},{12,28},{16,0},{20,4},{24,8},{28,12},{1,17},{... | collective-permute-start | bytes 442376 | tf_op jit(solution)/shard_map/ppermute | solution.py:11
  22.7 17.9 %copy-start.12 = (bf16[528,128]{1,0:T(8,128)(2,1)}, bf16[528,128]{1,0:T(8,128)(2,1)S(1)}, u32[]{:S(2)}) copy-start(bf16[528,128]{1,0:T(8,128)(2,1)S(1)} %get-tuple-element.27.refs_0_.refs_4_) | copy-start | bytes 405508
  23.9 15.0 %copy-start.10 = (bf16[528,128]{1,0:T(8,128)(2,1)}, bf16[528,128]{1,0:T(8,128)(2,1)S(1)}, u32[]{:S(2)}) copy-start(bf16[528,128]{1,0:T(8,128)(2,1)S(1)} %get-tuple-element.35.refs_4_) | copy-start | bytes 405508
  23.9 32.6 %collective-permute-start.6 = (bf16[528,128]{1,0:T(8,128)(2,1)S(1)}, bf16[528,128]{1,0:T(8,128)(2,1)S(1)}, u32[]{:S(2)}, u32[]{:S(2)}) collective-permute-start(bf16[528,128]{1,0:T(8,128)(2,1)S(1)} %get-tuple-element.28), channel_id=1, source_target_pairs={{0,1},{1,0},{2,3},{3,2},{4,5},{5,4},{6,7},{7,6},{8,9},{9,8},{10,11... | collective-permute-start | bytes 405512 | tf_op jit(solution)/shard_map/ppermute | solution.py:11
  25.7 31.5 %collective-permute-start.8 = (bf16[528,128]{1,0:T(8,128)(2,1)S(1)}, bf16[528,128]{1,0:T(8,128)(2,1)S(1)}, u32[]{:S(2)}, u32[]{:S(2)}) collective-permute-start(bf16[528,128]{1,0:T(8,128)(2,1)S(1)} %get-tuple-element.28), channel_id=1, source_target_pairs={{0,3},{1,2},{2,1},{3,0},{4,7},{5,6},{6,5},{7,4},{8,11},{9,10},{10,... | collective-permute-start | bytes 405512 | tf_op jit(solution)/shard_map/ppermute | solution.py:11
  36.3 4.3 %copy-start.4 = (bf16[1056,128]{1,0:T(8,128)(2,1)}, bf16[1056,128]{1,0:T(8,128)(2,1)S(1)}, u32[]{:S(2)}) copy-start(bf16[1056,128]{1,0:T(8,128)(2,1)S(1)} %collective-permute-done.1.refs_2_) | copy-start | bytes 811012
  36.3 17.4 %collective-permute-start.7 = (bf16[528,128]{1,0:T(8,128)(2,1)S(1)}, bf16[528,128]{1,0:T(8,128)(2,1)S(1)}, u32[]{:S(2)}, u32[]{:S(2)}) collective-permute-start(bf16[528,128]{1,0:T(8,128)(2,1)S(1)} %get-tuple-element.27.refs_0_.refs_4_), channel_id=1, source_target_pairs={{0,2},{1,3},{2,0},{3,1},{4,6},{5,7},{6,4},{7,5},{8,10},{9,11},{10,... | collective-permute-start | bytes 405512 | tf_op jit(solution)/shard_map/ppermute | solution.py:11
  36.7 3.9 %copy-start.6 = (bf16[1056,128]{1,0:T(8,128)(2,1)}, bf16[1056,128]{1,0:T(8,128)(2,1)S(1)}, u32[]{:S(2)}) copy-start(bf16[1056,128]{1,0:T(8,128)(2,1)S(1)} %collective-permute-done.refs_1_) | copy-start | bytes 811012
  36.7 6.9 %collective-permute-start.18 = (bf16[2,576,128]{2,1,0:T(8,128)(2,1)S(1)}, bf16[2,576,128]{2,1,0:T(8,128)(2,1)S(1)}, u32[]{:S(2)}, u32[]{:S(2)}) collective-permute-start(bf16[2,576,128]{2,1,0:T(8,128)(2,1)S(1)} %pad_maximum_fusion.3), channel_id=1, source_target_pairs={{0,16},{4,20},{8,24},{12,28},{16,0},{20,4},{24,8},{28,12},{1,17},{... | collective-permute-start | bytes 884744 | tf_op jit(solution)/shard_map/ppermute | solution.py:11
  38.9 1.7 %copy-start.8 = (bf16[1056,128]{1,0:T(8,128)(2,1)}, bf16[1056,128]{1,0:T(8,128)(2,1)S(1)}, u32[]{:S(2)}) copy-start(bf16[1056,128]{1,0:T(8,128)(2,1)S(1)} %collective-permute-done.2.refs_3_) | copy-start | bytes 811012
  38.9 12.2 %collective-permute-start.15 = (bf16[2,576,128]{2,1,0:T(8,128)(2,1)S(1)}, bf16[2,576,128]{2,1,0:T(8,128)(2,1)S(1)}, u32[]{:S(2)}, u32[]{:S(2)}) collective-permute-start(bf16[2,576,128]{2,1,0:T(8,128)(2,1)S(1)} %pad_maximum_fusion.2), channel_id=1, source_target_pairs={{0,8},{4,12},{8,0},{12,4},{16,24},{20,28},{24,16},{28,20},{1,9},{5... | collective-permute-start | bytes 884744 | tf_op jit(solution)/shard_map/ppermute | solution.py:11
  43.6 29.4 %collective-permute-start.3 = (bf16[528,128]{1,0:T(8,128)(2,1)}, bf16[528,128]{1,0:T(8,128)(2,1)}, u32[]{:S(2)}, u32[]{:S(2)}) collective-permute-start(bf16[528,128]{1,0:T(8,128)(2,1)} %get-tuple-element.26), channel_id=1, source_target_pairs={{0,1},{1,0},{2,3},{3,2},{4,5},{5,4},{6,7},{7,6},{8,9},{9,8},{10,11... | collective-permute-start | bytes 405512 | tf_op jit(solution)/shard_map/ppermute | solution.py:11
  51.1 17.3 %collective-permute-start.10 = (bf16[2112,128]{1,0:T(8,128)(2,1)}, bf16[2112,128]{1,0:T(8,128)(2,1)}, u32[]{:S(2)}, u32[]{:S(2)}) collective-permute-start(bf16[2112,128]{1,0:T(8,128)(2,1)} %get-tuple-element.30), channel_id=1, source_target_pairs={{4,0},{8,4},{12,8},{16,12},{20,16},{24,20},{28,24},{5,1},{9,5},{13... | collective-permute-start | bytes 1622024 | tf_op jit(solution)/shard_map/ppermute | solution.py:18
  53.7 3.4 %copy-start.18 = (bf16[528,128]{1,0:T(8,128)(2,1)}, bf16[528,128]{1,0:T(8,128)(2,1)S(1)}, u32[]{:S(2)}) copy-start(bf16[528,128]{1,0:T(8,128)(2,1)S(1)} %collective-permute-done.7.refs_2_.refs_6_) | copy-start | bytes 405508
  53.7 13.4 %copy-start = (bf16[9,512,128]{2,1,0:T(8,128)(2,1)S(1)}, bf16[9,512,128]{2,1,0:T(8,128)(2,1)}, u32[]{:S(2)}) copy-start(bf16[9,512,128]{2,1,0:T(8,128)(2,1)} %refs_1_.1) | copy-start | bytes 3538948
  53.7 14.7 %collective-permute-start.9 = (bf16[2112,128]{1,0:T(8,128)(2,1)}, bf16[2112,128]{1,0:T(8,128)(2,1)}, u32[]{:S(2)}, u32[]{:S(2)}) collective-permute-start(bf16[2112,128]{1,0:T(8,128)(2,1)} %get-tuple-element.29), channel_id=1, source_target_pairs={{0,4},{4,8},{8,12},{12,16},{16,20},{20,24},{24,28},{1,5},{5,9},{9,... | collective-permute-start | bytes 1622024 | tf_op jit(solution)/shard_map/ppermute | solution.py:18
  56.5 0.6 copy-start.14
  56.5 2.2 %collective-permute-start.19 = (bf16[4,576,128]{2,1,0:T(8,128)(2,1)S(1)}, bf16[4,576,128]{2,1,0:T(8,128)(2,1)S(1)}, u32[]{:S(2)}, u32[]{:S(2)}) collective-permute-start(bf16[4,576,128]{2,1,0:T(8,128)(2,1)S(1)} %pad_maximum_fusion.1.refs_4_), channel_id=1, source_target_pairs={{0,4},{4,0},{8,12},{12,8},{16,20},{20,16},{24,28},{28,24},{1,5},{5... | collective-permute-start | bytes 1769480 | tf_op jit(solution)/shard_map/ppermute | solution.py:11
  57.1 0.7 copy-start.16
  57.8 3.1 %collective-permute-start.16 = (bf16[4,576,128]{2,1,0:T(8,128)(2,1)S(1)}, bf16[4,576,128]{2,1,0:T(8,128)(2,1)S(1)}, u32[]{:S(2)}, u32[]{:S(2)}) collective-permute-start(bf16[4,576,128]{2,1,0:T(8,128)(2,1)S(1)} %pad_maximum_fusion.refs_2_), channel_id=1, source_target_pairs={{0,4},{4,0},{8,12},{12,8},{16,20},{20,16},{24,28},{28,24},{1,5},{5... | collective-permute-start | bytes 1769480 | tf_op jit(solution)/shard_map/ppermute | solution.py:11
  58.7 17.2 %collective-permute-start.5 = (bf16[528,128]{1,0:T(8,128)(2,1)}, bf16[528,128]{1,0:T(8,128)(2,1)S(1)}, u32[]{:S(2)}, u32[]{:S(2)}) collective-permute-start(bf16[528,128]{1,0:T(8,128)(2,1)} %get-tuple-element.26), channel_id=1, source_target_pairs={{0,3},{1,2},{2,1},{3,0},{4,7},{5,6},{6,5},{7,4},{8,11},{9,10},{10,... | collective-permute-start | bytes 405512 | tf_op jit(solution)/shard_map/ppermute | solution.py:11
  61.0 7.4 %copy-start.3 = (bf16[1056,128]{1,0:T(8,128)(2,1)S(1)}, bf16[1056,128]{1,0:T(8,128)(2,1)}, u32[]{:S(2)}) copy-start(bf16[1056,128]{1,0:T(8,128)(2,1)} %copy-done.2) | copy-start | bytes 811012
  61.0 7.5 %copy-start.5 = (bf16[1056,128]{1,0:T(8,128)(2,1)S(1)}, bf16[1056,128]{1,0:T(8,128)(2,1)}, u32[]{:S(2)}) copy-start(bf16[1056,128]{1,0:T(8,128)(2,1)} %copy-done.4) | copy-start | bytes 811012
  61.0 7.5 %copy-start.7 = (bf16[1056,128]{1,0:T(8,128)(2,1)S(1)}, bf16[1056,128]{1,0:T(8,128)(2,1)}, u32[]{:S(2)}) copy-start(bf16[1056,128]{1,0:T(8,128)(2,1)} %copy-done.6) | copy-start | bytes 811012
  61.0 7.5 %copy-start.9 = (bf16[1056,128]{1,0:T(8,128)(2,1)S(1)}, bf16[1056,128]{1,0:T(8,128)(2,1)}, u32[]{:S(2)}) copy-start(bf16[1056,128]{1,0:T(8,128)(2,1)} %copy-done.8) | copy-start | bytes 811012
  61.0 7.5 %copy-start.13 = (bf16[528,128]{1,0:T(8,128)(2,1)S(1)}, bf16[528,128]{1,0:T(8,128)(2,1)}, u32[]{:S(2)}) copy-start(bf16[528,128]{1,0:T(8,128)(2,1)} %copy-done.12) | copy-start | bytes 405508
  61.0 7.5 %copy-start.15 = (bf16[528,128]{1,0:T(8,128)(2,1)S(1)}, bf16[528,128]{1,0:T(8,128)(2,1)}, u32[]{:S(2)}) copy-start(bf16[528,128]{1,0:T(8,128)(2,1)} %copy-done.14) | copy-start | bytes 405508
  61.0 7.5 %copy-start.17 = (bf16[528,128]{1,0:T(8,128)(2,1)S(1)}, bf16[528,128]{1,0:T(8,128)(2,1)}, u32[]{:S(2)}) copy-start(bf16[528,128]{1,0:T(8,128)(2,1)} %copy-done.16) | copy-start | bytes 405508
  61.0 7.5 %copy-start.19 = (bf16[528,128]{1,0:T(8,128)(2,1)S(1)}, bf16[528,128]{1,0:T(8,128)(2,1)}, u32[]{:S(2)}) copy-start(bf16[528,128]{1,0:T(8,128)(2,1)} %copy-done.18) | copy-start | bytes 405508
  61.0 7.5 %copy-start.20 = (bf16[16,128]{1,0:T(8,128)(2,1)S(1)}, bf16[16,128]{1,0:T(8,128)(2,1)}, u32[]{:S(2)}) copy-start(bf16[16,128]{1,0:T(8,128)(2,1)} %token_.1.refs_11_) | copy-start | bytes 12292
  61.0 14.8 %collective-permute-start.4 = (bf16[528,128]{1,0:T(8,128)(2,1)}, bf16[528,128]{1,0:T(8,128)(2,1)S(1)}, u32[]{:S(2)}, u32[]{:S(2)}) collective-permute-start(bf16[528,128]{1,0:T(8,128)(2,1)} %copy-done.10), channel_id=1, source_target_pairs={{0,2},{1,3},{2,0},{3,1},{4,6},{5,7},{6,4},{7,5},{8,10},{9,11},{10,... | collective-permute-start | bytes 405512 | tf_op jit(solution)/shard_map/ppermute | solution.py:11
  68.5 7.4 %copy-start.11 = (bf16[528,128]{1,0:T(8,128)(2,1)S(1)}, bf16[528,128]{1,0:T(8,128)(2,1)}, u32[]{:S(2)}) copy-start(bf16[528,128]{1,0:T(8,128)(2,1)} %copy-done.10) | copy-start | bytes 405508
  72.9 8.5 %collective-permute-start.20 = (bf16[1024,128]{1,0:T(8,128)(2,1)S(1)}, bf16[1024,128]{1,0:T(8,128)(2,1)S(1)}, u32[]{:S(2)}, u32[]{:S(2)}) collective-permute-start(bf16[1024,128]{1,0:T(8,128)(2,1)S(1)} %get-tuple-element.42), channel_id=1, source_target_pairs={{0,1},{1,0},{2,3},{3,2},{4,5},{5,4},{6,7},{7,6},{8,9},{9,8},{10,11... | collective-permute-start | bytes 786440 | tf_op jit(solution)/shard_map/ppermute | solution.py:11
  81.4 7.6 %collective-permute-start.21 = (bf16[1024,128]{1,0:T(8,128)(2,1)S(1)}, bf16[1024,128]{1,0:T(8,128)(2,1)S(1)}, u32[]{:S(2)}, u32[]{:S(2)}) collective-permute-start(bf16[1024,128]{1,0:T(8,128)(2,1)S(1)} %get-tuple-element.43), channel_id=1, source_target_pairs={{0,1},{1,0},{2,3},{3,2},{4,5},{5,4},{6,7},{7,6},{8,9},{9,8},{10,11... | collective-permute-start | bytes 786440 | tf_op jit(solution)/shard_map/ppermute | solution.py:11

commit v10 on v9

--- a/solution.py
+++ b/solution.py
@@ -163,14 +163,15 @@
         other[at : at + pitch] = jnp.where(side == 0, pieces[1], pieces[0])
 
 
-def rim_kernel(width, *refs):
-    pieces, (first, last) = refs[:4], refs[4:]
+def rim_kernel(width, where, *refs):
+    groups, (first, last) = [refs[at : at + 4] for at in range(0, len(refs) - 2, 4)], refs[-2:]
     pitch = width + 8
-    for k, piece in enumerate(pieces):
+    for k in range(4):
         for i in range(2):
-            for out, end in ((first, 0), (last, 1)):
-                at = (2 * i + end) * pitch
-                out[(2 * k + i) * pitch : (2 * k + i + 1) * pitch] = piece[at : at + pitch]
+            for out, end in ((first, 0), (last, -1)):
+                group, at = where[i][end]
+                piece = groups[group][k][at * pitch : (at + 1) * pitch]
+                out[(2 * k + i) * pitch : (2 * k + i + 1) * pitch] = piece
 
 
 def fill_rows(target, piece, start, row, lanes, width):
@@ -190,19 +191,18 @@
             fill_rows(target, ref, at * pitch, r, lanes, width)
 
 
-def inside(edges, inners, which, count):
-    return [
-        [(p, 2 * which), *((q, r) for r in range(count - 2)), (p, 2 * which + 1)]
-        for p, q in zip(edges, inners)
-    ]
-
-
-def backward_kernel(*refs):
-    edges, inners, (before, after, weights, _, mine, other, source) = refs[:4], refs[4:8], refs[8:]
+def fill(source, which, where, refs, before, after, size):
+    rows = [[(refs[4 * group + k], at) for group, at in where[which]] for k in range(4)]
+    fill_source(source, which, size // len(where[which]), rows, before, after)
+
+
+def backward_kernel(where, marks, *refs):
+    mine, other, source = refs[-3:]
+    before, after, weights = refs[-6 - marks : -3 - marks]
     size, local = mine.shape
-    width = before.shape[0] // 8 - 8
     channels = 4 * local
-    fill_source(source, 0, width, inside(edges, inners, 0, size // width), before, after)
+    fill(source, 0, where, refs, before, after, size)
+    width = size // len(where[0])
     acc = None
     for a in range(3):
         for b in range(3):
@@ -216,13 +216,13 @@
     other[...] = acc[:, local:].astype(jnp.bfloat16)
 
 
-def forward_kernel(*refs):
-    edges, inners, refs = refs[:4], refs[4:8], refs[8:]
-    before, after, weights, extra, mine, other, source = refs
+def forward_kernel(where, marks, *refs):
+    mine, other, source = refs[-3:]
+    before, after, weights, extra = refs[-7 - marks : -3 - marks]
     size, local = mine.shape
-    width = before.shape[0] // 8 - 8
     channels, half = 4 * local, 2 * local
-    fill_source(source, 1, width, inside(edges, inners, 1, size // width), before, after)
+    fill(source, 1, where, refs, before, after, size)
+    width = size // len(where[1])
     acc = None
     for a in range(3):
         for b in range(3):
@@ -239,8 +239,10 @@
                     preferred_element_type=jnp.float32,
                 )
                 acc = term if acc is None else acc + term
+    group, at = where[1][0]
+    at = at * (width + 8) + width
     for k, out in enumerate((mine, other)):
-        bias = edges[k][width : width + 8, :].astype(jnp.float32)[2:3]
+        bias = refs[4 * group + k][at : at + 8, :].astype(jnp.float32)[2:3]
         out[...] = (acc[:, k * local : (k + 1) * local] + bias).astype(jnp.bfloat16)
 
 
@@ -261,7 +263,7 @@
         in_specs=[SMEM] * placed + [VMEM] * (len(args) - placed),
         out_specs=[VMEM] * len(shapes),
         scratch_shapes=[pltpu.VMEM(s, jnp.bfloat16) for s in scratch],
-        compiler_params=pltpu.CompilerParams(vmem_limit_bytes=32 * 2**20),
+        compiler_params=pltpu.CompilerParams(vmem_limit_bytes=20 * 2**20),
         cost_estimate=cost(micros),
         name=name,
     )(*args)
@@ -275,9 +277,8 @@
 
 
 def exchange(mine, other):
-    far = swap(other, "chan", 3)
-    middle = swap(mine, "chan", 2)
-    return [mine, swap(other, "chan", 1), middle, far]
+    held = {k: swap(other if k & 1 else mine, "chan", k) for k in (2, 3, 1)}
+    return [mine, held[1], held[2], held[3]]
 
 
 def after(value, *others):
@@ -324,14 +325,7 @@
 
 
 def token(pieces, micros):
-    return pl.pallas_call(
-        token_kernel,
-        out_shape=jax.ShapeDtypeStruct((16, 128), jnp.bfloat16),
-        in_specs=[ANY] * len(pieces),
-        out_specs=VMEM,
-        cost_estimate=cost(micros),
-        name="token",
-    )(*pieces)
+    return kernel(token_kernel, [(16, 128)], pieces, [], "token", False, micros)[0]
 
 
 def per_device(image, filters, bias, upstream):
@@ -355,19 +349,30 @@
     across = jnp.concatenate([swap(across, "chan", k) for k in (2, 3)])
 
     upstream, image = [jnp.transpose(v, (1, 2, 0)) for v in (upstream, image)]
-    parts = [(i, r) for i in range(2) for r in (0, rows - 1)]
-    edge = cut(place, [upstream, image], bias[None], parts, "cut_edge", 0)
-    near, across = after((near, across), edge)
-    edge = exchange(*edge)
-    parts = [(0, r) for r in range(1, rows - 1)]
-    first = exchange(*cut(place, [upstream], bias[None], parts, "cut_first", 0))
-    second = exchange(*cut(place, [image], bias[None], parts, "cut_second", 0))
-    mark = token(first, 18)
+    edges = [(i, r) for i in range(2) for r in (0, rows - 1)]
+    groups = [edges, [(i, r) for i in range(2) for r in range(1, rows - 1)]]
+    spot = {part: (g, at) for g, parts in enumerate(groups) for at, part in enumerate(parts)}
+    where = [[spot[i, r] for r in range(rows)] for i in range(2)]
+    needed = [sorted({g for g, _ in rows_of}) for rows_of in where]
+    where = [[(need.index(g), at) for g, at in rows_of] for need, rows_of in zip(needed, where)]
+    ends = [[rows_of[0], rows_of[-1]] for rows_of in where]
+
+    sent = cut(place, [upstream, image], bias[None], groups[0], "cut", 0)
+    got = [exchange(*sent)]
+    sent = cut(place, after([upstream, image], got[-1][3]), bias[None], groups[1], "cut", 40)
+    got[0] = after(got[0], sent)
+    got.append(exchange(*sent))
+    marks = [[], []]
+    marks[0].append(token(got[1], 13))
 
     steps = halving(bands)[:-1]
     near, near_order = gather(near, steps)
     across, across_order = gather(across, steps[::-1])
-    held = [near, swap(near, "band", 1), across, swap(across, "band", 1)]
+    near, across = after((near, across), got[0][1:])
+    held = jnp.concatenate([near, across], axis=1)
+    there = swap(held, "band", 1)
+    cutoff = near.shape[1]
+    held = [near, there[:, :cutoff], across, there[:, cutoff:]]
     weights, extra = kernel(
         lambda *refs: assemble_kernel((near_order, across_order), *refs),
         [(taps * outs, 2 * local), (taps * 2 * local, 2 * local)],
@@ -375,21 +380,24 @@
         [],
         "assemble",
         True,
-        2,
+        0,
     )
     rim = (8 * (width + 8), local)
-    body = lambda *refs: rim_kernel(width, *refs)
-    rims = neighbours(*kernel(body, [rim] * 2, edge, [], "rim", False, 16))
+    pieces = [p for p in after(got[0], held)]
+    body = lambda *refs: rim_kernel(width, ends, *refs)
+    rims = neighbours(*kernel(body, [rim] * 2, pieces, [], "rim", False, 0))
 
     out = [(rows * width, local)] * 2
     source = [(3, (rows + 2) * width, 4 * local)]
-    args = [*edge, *first, *rims, weights, mark]
-    mine, other = kernel(backward_kernel, out, args, source, "backward", False, 10)
+    args = [p for g in needed[0] for p in got[g]] + [*rims, weights, *marks[0]]
+    body = lambda *refs: backward_kernel(where, len(marks[0]), *refs)
+    mine, other = kernel(body, out, args, source, "backward", False, 4)
     other = swap(other, "chan", 1)
     image_grad = home(place, mine, other, rows)
-    args = [*edge, *after(second, mine), *rims, weights, extra]
-    mine, sent = kernel(forward_kernel, out, args, source, "forward", False, 5)
-    other = swap(after(sent, other), "chan", 1)
+    args = [p for g in needed[1] for p in got[g]] + [*rims, weights, extra, *marks[1]]
+    body = lambda *refs: forward_kernel(where, len(marks[1]), *refs)
+    mine, sent = kernel(body, out, args, source, "forward", False, 2)
+    other = swap(sent, "chan", 1)
     return home(place, mine, other, rows), image_grad
 
 

time: 91.3 us -> 86.4 us (0.946)
  waiting for transfers between devices: 27 us -> 38.9 us
  starting transfers between devices: 39.7 us -> 30.6 us
  Pallas kernels: 17.1 us -> 11.8 us
  local copies, waits for them, and re-layouts: 5.55 us -> 3.68 us
    ppermute x20 -> x16, waiting for transfers between devices: 27 us -> 38.9 us  [swap(): return lax.ppermute(value, axis, [(j, j ^ step) for j in range(size)])]
    ppermute x20 -> x16, starting transfers between devices: 35.6 us -> 27.7 us  [swap(): return lax.ppermute(value, axis, [(j, j ^ step) for j in range(size)])]
    pallas_call x9, Pallas kernels: 16.5 us -> 11.8 us  [kernel(): pl.pallas_call(body, out_shape=[jax.ShapeDtypeStruct(s, jnp.bfloat16) for...]
    ppermute x2, starting transfers between devices: 4.07 us -> 2.84 us  [neighbours(): return (lax.ppermute(last, 'band', up), lax.ppermute(first, 'band', down))]
    unnamed x46 -> x8, local copies, waits for them, and re-layouts: 2.89 us -> 1.89 us
    dynamic_slice x1, local copies, waits for them, and re-layouts: 0.93 us -> 0.01 us  [per_device(): lax.dynamic_slice_in_dim(filters, band * share, share, axis=1)]
  transfers between devices with their start and end apart: 22 -> 18, of which waited for: 10 -> 9; matrix products, arithmetic and copies ran while one was open for 4% -> 3% of each run, Pallas kernels for 17% -> 7%
where the time goes in v10:
time: 86.4 us; the launch traced here: 86.2 us
  waiting for transfers between devices  38.9 us (45%)
  starting transfers between devices  30.6 us (35%)
  Pallas kernels  11.8 us (14%)
  local copies, waits for them, and re-layouts  3.68 us (4%)
    ppermute x16, waiting for transfers between devices, swap(): return lax.ppermute(value, axis, [(j, j ^ step) for j in range(size)])  38.9 us
    ppermute x16, starting transfers between devices, swap(): return lax.ppermute(value, axis, [(j, j ^ step) for j in range(size)])  27.7 us
    pallas_call x9, Pallas kernels, kernel(): pl.pallas_call(body, out_shape=[jax.ShapeDtypeStruct(s, jnp.bfloat16) for...  11.8 us
    ppermute x2, starting transfers between devices, neighbours(): return (lax.ppermute(last, 'band', up), lax.ppermute(first, 'band', down))  2.84 us
    unnamed x8, local copies, waits for them, and re-layouts  1.89 us
  transfers between devices with their start and end apart: 18, of which 9 were waited for; matrix products, arithmetic and copies ran while one was open for 3% of the time, Pallas kernels for 7%

profile of v10, /device:TPU:0, one launch (start us, length us, event | category | flops | bytes accessed | tf_op | source)
XLA Modules:
  0.0 86.2 jit_solution(8178717586949516145)
XLA Ops:
  0.6 0.0 copy-start.2
  0.6 0.0 copy-start.1
  0.7 1.0 %constant_dynamic-slice_fusion = bf16[9,32,128]{2,1,0:T(8,128)(2,1)S(1)} fusion(bf16[9,512,128]{2,1,0:T(8,128)(2,1)} %refs_1_.1, s32[]{:T(128)S(6)} %select_n.7), kind=kLoop, calls=%fused_computation.7 | loop fusion | bytes 147460 | tf_op jit(solution)/shard_map/dynamic_slice | solution.py:347
  1.6 5.0 %collective-permute-start.10 = (bf16[288,128]{1,0:T(8,128)(2,1)S(1)}, bf16[288,128]{1,0:T(8,128)(2,1)S(1)}, u32[]{:S(2)}, u32[]{:S(2)}) collective-permute-start(bf16[288,128]{1,0:T(8,128)(2,1)S(1)} %bitcast.36), channel_id=1, source_target_pairs={{0,3},{1,2},{2,1},{3,0},{4,7},{5,6},{6,5},{7,4},{8,11},{9,10},{10,... | collective-permute-start | bytes 221192 | tf_op jit(solution)/shard_map/ppermute | solution.py:11
  6.7 0.0 collective-permute-start.9
  6.7 1.5 %copy.6 = bf16[128,4,512]{0,2,1:T(8,128)(2,1)S(1)} copy(bf16[128,4,512]{2,1,0:T(4,128)(2,1)} %param.7) | data formatting | bytes 1048576 | tf_op args[3]
  8.1 0.0 copy-done.2
  8.1 0.0 copy-start
  8.1 0.4 copy.7
  8.6 0.1 pad_add_fusion.refs_0_.place
  8.6 0.0 copy-done.1
  8.6 0.7 cut.2
  9.3 2.0 %collective-permute-start.2 = (bf16[1056,128]{1,0:T(8,128)(2,1)S(1)}, bf16[1056,128]{1,0:T(8,128)(2,1)S(1)}, u32[]{:S(2)}, u32[]{:S(2)}) collective-permute-start(bf16[1056,128]{1,0:T(8,128)(2,1)S(1)} %get-tuple-element.27), channel_id=1, source_target_pairs={{0,3},{1,2},{2,1},{3,0},{4,7},{5,6},{6,5},{7,4},{8,11},{9,10},{10,... | collective-permute-start | bytes 811016 | tf_op jit(solution)/shard_map/ppermute | solution.py:11
  11.3 0.0 copy-done
  11.3 1.6 %collective-permute-start.6 = (bf16[576,128]{1,0:T(8,128)(2,1)S(1)}, bf16[576,128]{1,0:T(8,128)(2,1)S(1)}, u32[]{:S(2)}, u32[]{:S(2)}) collective-permute-start(bf16[576,128]{1,0:T(8,128)(2,1)S(1)} %bitcast.35), channel_id=1, source_target_pairs={{0,1},{1,0},{2,3},{3,2},{4,5},{5,4},{6,7},{7,6},{8,9},{9,8},{10,11... | collective-permute-start | bytes 442376 | tf_op jit(solution)/shard_map/ppermute | solution.py:11
  13.0 0.0 collective-permute-done.10
  13.0 0.2 collective-permute-done.9
  13.2 1.6 %collective-permute-start.11 = (bf16[1,576,128]{2,1,0:T(8,128)(2,1)S(1)}, bf16[1,576,128]{2,1,0:T(8,128)(2,1)S(1)}, u32[]{:S(2)}, u32[]{:S(2)}) collective-permute-start(bf16[1,576,128]{2,1,0:T(8,128)(2,1)S(1)} %maximum_bitcast_fusion), channel_id=1, source_target_pairs={{0,8},{4,12},{8,0},{12,4},{16,24},{20,28},{24,16},{28,20},{1,9},{5... | collective-permute-start | bytes 442376 | tf_op jit(solution)/shard_map/ppermute | solution.py:11
  14.8 7.3 %collective-permute-done.6 = bf16[576,128]{1,0:T(8,128)(2,1)S(1)} collective-permute-done((bf16[576,128]{1,0:T(8,128)(2,1)S(1)}, bf16[576,128]{1,0:T(8,128)(2,1)S(1)}, u32[]{:S(2)}, u32[]{:S(2)}) %collective-permute-start.6) | collective-permute-done | bytes 147488 | tf_op jit(solution)/shard_map/ppermute | solution.py:11
  22.1 1.5 %collective-permute-start.7 = (bf16[1,576,128]{2,1,0:T(8,128)(2,1)S(1)}, bf16[1,576,128]{2,1,0:T(8,128)(2,1)S(1)}, u32[]{:S(2)}, u32[]{:S(2)}) collective-permute-start(bf16[1,576,128]{2,1,0:T(8,128)(2,1)S(1)} %bitcast.30), channel_id=1, source_target_pairs={{0,16},{4,20},{8,24},{12,28},{16,0},{20,4},{24,8},{28,12},{1,17},{... | collective-permute-start | bytes 442376 | tf_op jit(solution)/shard_map/ppermute | solution.py:11
  23.6 0.2 collective-permute-start
  23.7 2.9 %collective-permute-start.1 = (bf16[1056,128]{1,0:T(8,128)(2,1)S(1)}, bf16[1056,128]{1,0:T(8,128)(2,1)S(1)}, u32[]{:S(2)}, u32[]{:S(2)}) collective-permute-start(bf16[1056,128]{1,0:T(8,128)(2,1)S(1)} %get-tuple-element.38.refs_0_), channel_id=1, source_target_pairs={{0,2},{1,3},{2,0},{3,1},{4,6},{5,7},{6,4},{7,5},{8,10},{9,11},{10,... | collective-permute-start | bytes 811016 | tf_op jit(solution)/shard_map/ppermute | solution.py:11
  26.6 0.0 collective-permute-done.11
  26.7 0.6 collective-permute-start.12
  27.2 0.0 collective-permute-done.2.refs_3_
  27.2 0.2 collective-permute-done.7
  27.5 1.6 %collective-permute-start.8 = (bf16[2,576,128]{2,1,0:T(8,128)(2,1)S(1)}, bf16[2,576,128]{2,1,0:T(8,128)(2,1)S(1)}, u32[]{:S(2)}, u32[]{:S(2)}) collective-permute-start(bf16[2,576,128]{2,1,0:T(8,128)(2,1)S(1)} %pad_maximum_fusion.3), channel_id=1, source_target_pairs={{0,8},{4,12},{8,0},{12,4},{16,24},{20,28},{24,16},{28,20},{1,9},{5... | collective-permute-start | bytes 884744 | tf_op jit(solution)/shard_map/ppermute | solution.py:11
  29.0 0.7 cut.3
  29.8 7.1 %collective-permute-done.refs_1_ = bf16[1056,128]{1,0:T(8,128)(2,1)S(1)} collective-permute-done((bf16[1056,128]{1,0:T(8,128)(2,1)S(1)}, bf16[1056,128]{1,0:T(8,128)(2,1)S(1)}, u32[]{:S(2)}, u32[]{:S(2)}) %collective-permute-start) | collective-permute-done | bytes 270368 | tf_op jit(solution)/shard_map/ppermute | solution.py:11
  36.9 1.7 %collective-permute-done.1.refs_2_ = bf16[1056,128]{1,0:T(8,128)(2,1)S(1)} collective-permute-done((bf16[1056,128]{1,0:T(8,128)(2,1)S(1)}, bf16[1056,128]{1,0:T(8,128)(2,1)S(1)}, u32[]{:S(2)}, u32[]{:S(2)}) %collective-permute-start.1) | collective-permute-done | bytes 270368 | tf_op jit(solution)/shard_map/ppermute | solution.py:11
  38.6 0.0 collective-permute-done.12
  38.6 0.1 pad_maximum_fusion.2.refs_4_
  38.6 0.0 collective-permute-done.8
  38.6 0.1 pad_maximum_fusion.1.refs_2_
  38.7 0.1 pad_maximum_fusion
  38.8 0.1 collective-permute-start.13
  38.9 0.1 collective-permute-start.4
  38.9 2.9 %collective-permute-start.3 = (bf16[1056,128]{1,0:T(8,128)(2,1)S(1)}, bf16[1056,128]{1,0:T(8,128)(2,1)S(1)}, u32[]{:S(2)}, u32[]{:S(2)}) collective-permute-start(bf16[1056,128]{1,0:T(8,128)(2,1)S(1)} %get-tuple-element.31), channel_id=1, source_target_pairs={{0,1},{1,0},{2,3},{3,2},{4,5},{5,4},{6,7},{7,6},{8,9},{9,8},{10,11... | collective-permute-start | bytes 811016 | tf_op jit(solution)/shard_map/ppermute | solution.py:11
  41.9 1.5 %collective-permute-start.5 = (bf16[1056,128]{1,0:T(8,128)(2,1)S(1)}, bf16[1056,128]{1,0:T(8,128)(2,1)S(1)}, u32[]{:S(2)}, u32[]{:S(2)}) collective-permute-start(bf16[1056,128]{1,0:T(8,128)(2,1)S(1)} %get-tuple-element.31), channel_id=1, source_target_pairs={{0,3},{1,2},{2,1},{3,0},{4,7},{5,6},{6,5},{7,4},{8,11},{9,10},{10,... | collective-permute-start | bytes 811016 | tf_op jit(solution)/shard_map/ppermute | solution.py:11
  43.3 0.0 collective-permute-done.13
  43.3 0.1 fusion
  43.4 0.1 rim.1
  43.5 1.5 %collective-permute-start.14 = (bf16[2112,128]{1,0:T(8,128)(2,1)S(1)}, bf16[2112,128]{1,0:T(8,128)(2,1)S(1)}, u32[]{:S(2)}, u32[]{:S(2)}) collective-permute-start(bf16[2112,128]{1,0:T(8,128)(2,1)S(1)} %get-tuple-element.42), channel_id=1, source_target_pairs={{0,4},{4,8},{8,12},{12,16},{16,20},{20,24},{24,28},{1,5},{5,9},{9,... | collective-permute-start | bytes 1622024 | tf_op jit(solution)/shard_map/ppermute | solution.py:18
  45.0 1.3 %collective-permute-start.15 = (bf16[2112,128]{1,0:T(8,128)(2,1)S(1)}, bf16[2112,128]{1,0:T(8,128)(2,1)S(1)}, u32[]{:S(2)}, u32[]{:S(2)}) collective-permute-start(bf16[2112,128]{1,0:T(8,128)(2,1)S(1)} %get-tuple-element.43), channel_id=1, source_target_pairs={{4,0},{8,4},{12,8},{16,12},{20,16},{24,20},{28,24},{5,1},{9,5},{13... | collective-permute-start | bytes 1622024 | tf_op jit(solution)/shard_map/ppermute | solution.py:18
  46.3 8.5 %collective-permute-done.4.refs_6_.refs_2_ = bf16[1056,128]{1,0:T(8,128)(2,1)S(1)} collective-permute-done((bf16[1056,128]{1,0:T(8,128)(2,1)S(1)}, bf16[1056,128]{1,0:T(8,128)(2,1)S(1)}, u32[]{:S(2)}, u32[]{:S(2)}) %collective-permute-start.4) | collective-permute-done | bytes 270368 | tf_op jit(solution)/shard_map/ppermute | solution.py:11
  54.8 5.5 %collective-permute-done.3.refs_5_.refs_1_ = bf16[1056,128]{1,0:T(8,128)(2,1)S(1)} collective-permute-done((bf16[1056,128]{1,0:T(8,128)(2,1)S(1)}, bf16[1056,128]{1,0:T(8,128)(2,1)S(1)}, u32[]{:S(2)}, u32[]{:S(2)}) %collective-permute-start.3) | collective-permute-done | bytes 270368 | tf_op jit(solution)/shard_map/ppermute | solution.py:11
  60.3 0.0 collective-permute-done.5.refs_7_.refs_3_
  60.3 1.3 %assemble.1 = (bf16[4608,256]{1,0:T(8,128)(2,1)S(1)}, bf16[2304,256]{1,0:T(8,128)(2,1)S(1)}) custom-call(s32[2]{0:T(128)S(1)} %pad_add_fusion.refs_0_.place, bf16[9,512,128]{2,1,0:T(8,128)(2,1)S(1)} %copy-done, bf16[4,576,128]{2,1,0:T(8,128)(2,1)S(1)} %pad_maximum_fusion.1.refs_2_, bf16[4,576,128]{2,1,0:T(8,128)(2,1)S(1)} %get-tuple-element.51.refs_3_, ...), custom_call_target="tpu_custom_call" | custom-call | flops 1048576 | bytes 1048576 | tf_op jit(solution)/shard_map/assemble/pallas_call | solution.py:260
  61.6 0.0 collective-permute-done.14.refs_8_
  61.6 0.0 collective-permute-done.15.refs_9_
  61.6 3.2 %backward.1 = (bf16[1024,128]{1,0:T(8,128)(2,1)S(1)}, bf16[1024,128]{1,0:T(8,128)(2,1)S(1)}) custom-call(bf16[1056,128]{1,0:T(8,128)(2,1)S(1)} %get-tuple-element.38.refs_0_, bf16[1056,128]{1,0:T(8,128)(2,1)S(1)} %collective-permute-done.refs_1_, bf16[1056,128]{1,0:T(8,128)(2,1)S(1)} %collective-permute-done.1.refs_2_, ...), custom_call_target="tpu_custom_call" | custom-call | flops 4001048576 | bytes 1048576 | tf_op jit(solution)/shard_map/backward/pallas_call | solution.py:260
  64.7 6.2 %collective-permute-start.17 = (bf16[1024,128]{1,0:T(8,128)(2,1)S(1)}, bf16[1024,128]{1,0:T(8,128)(2,1)S(1)}, u32[]{:S(2)}, u32[]{:S(2)}) collective-permute-start(bf16[1024,128]{1,0:T(8,128)(2,1)S(1)} %get-tuple-element.49), channel_id=1, source_target_pairs={{0,1},{1,0},{2,3},{3,2},{4,5},{5,4},{6,7},{7,6},{8,9},{9,8},{10,11... | collective-permute-start | bytes 786440 | tf_op jit(solution)/shard_map/ppermute | solution.py:11
  71.0 3.0 %forward.1 = (bf16[1024,128]{1,0:T(8,128)(2,1)S(1)}, bf16[1024,128]{1,0:T(8,128)(2,1)S(1)}) custom-call(bf16[1056,128]{1,0:T(8,128)(2,1)S(1)} %get-tuple-element.38.refs_0_, bf16[1056,128]{1,0:T(8,128)(2,1)S(1)} %collective-permute-done.refs_1_, bf16[1056,128]{1,0:T(8,128)(2,1)S(1)} %collective-permute-done.1.refs_2_, ...), custom_call_target="tpu_custom_call" | custom-call | flops 2001048576 | bytes 1048576 | tf_op jit(solution)/shard_map/forward/pallas_call | solution.py:260
  74.0 0.1 collective-permute-start.16
  74.1 0.2 copy.14
  74.3 0.2 copy.12
  74.5 3.6 %collective-permute-done.17 = bf16[1024,128]{1,0:T(8,128)(2,1)S(1)} collective-permute-done((bf16[1024,128]{1,0:T(8,128)(2,1)S(1)}, bf16[1024,128]{1,0:T(8,128)(2,1)S(1)}, u32[]{:S(2)}, u32[]{:S(2)}) %collective-permute-start.17) | collective-permute-done | bytes 262176 | tf_op jit(solution)/shard_map/ppermute | solution.py:11
  78.1 0.2 copy.15
  78.3 4.9 %collective-permute-done.16 = bf16[1024,128]{1,0:T(8,128)(2,1)S(1)} collective-permute-done((bf16[1024,128]{1,0:T(8,128)(2,1)S(1)}, bf16[1024,128]{1,0:T(8,128)(2,1)S(1)}, u32[]{:S(2)}, u32[]{:S(2)}) %collective-permute-start.16) | collective-permute-done | bytes 262176 | tf_op jit(solution)/shard_map/ppermute | solution.py:11
  83.1 0.2 copy.13
  83.3 1.4 %home.3 = bf16[128,4,512]{2,1,0:T(4,128)(2,1)} custom-call(s32[2]{0:T(128)S(1)} %pad_add_fusion.refs_0_.place, bf16[128,4,256]{2,1,0:T(4,128)(2,1)S(1)} %bitcast.23, bf16[128,4,256]{2,1,0:T(4,128)(2,1)S(1)} %bitcast.24), custom_call_target="tpu_custom_call" | custom-call | flops 1048576 | bytes 1048576 | tf_op jit(solution)/shard_map/home/pallas_call | solution.py:260
  84.8 1.4 %home.2 = bf16[128,4,512]{2,1,0:T(4,128)(2,1)} custom-call(s32[2]{0:T(128)S(1)} %pad_add_fusion.refs_0_.place, bf16[128,4,256]{2,1,0:T(4,128)(2,1)S(1)} %bitcast.22, bf16[128,4,256]{2,1,0:T(4,128)(2,1)S(1)} %bitcast.25), custom_call_target="tpu_custom_call" | custom-call | flops 1048576 | bytes 1048576 | tf_op jit(solution)/shard_map/home/pallas_call | solution.py:260
  (5 shorter events, 0.1 us)
Async XLA Ops:
  0.6 7.5 %copy-start.2 = (bf16[128,4,512]{2,1,0:T(4,128)(2,1)S(1)}, bf16[128,4,512]{2,1,0:T(4,128)(2,1)}, u32[]{:S(2)}) copy-start(bf16[128,4,512]{2,1,0:T(4,128)(2,1)} %param.4) | copy-start | bytes 1572868
  0.6 8.0 %copy-start.1 = (bf16[128]{0:T(256)(128)(2,1)S(1)}, bf16[128]{0:T(256)(128)(2,1)}, u32[]{:S(2)}) copy-start(bf16[128]{0:T(256)(128)(2,1)} %param.6) | copy-start | bytes 772
  1.6 11.4 %collective-permute-start.10 = (bf16[288,128]{1,0:T(8,128)(2,1)S(1)}, bf16[288,128]{1,0:T(8,128)(2,1)S(1)}, u32[]{:S(2)}, u32[]{:S(2)}) collective-permute-start(bf16[288,128]{1,0:T(8,128)(2,1)S(1)} %bitcast.36), channel_id=1, source_target_pairs={{0,3},{1,2},{2,1},{3,0},{4,7},{5,6},{6,5},{7,4},{8,11},{9,10},{10,... | collective-permute-start | bytes 221192 | tf_op jit(solution)/shard_map/ppermute | solution.py:11
  6.7 6.6 %collective-permute-start.9 = (bf16[288,128]{1,0:T(8,128)(2,1)S(1)}, bf16[288,128]{1,0:T(8,128)(2,1)S(1)}, u32[]{:S(2)}, u32[]{:S(2)}) collective-permute-start(bf16[288,128]{1,0:T(8,128)(2,1)S(1)} %bitcast.37), channel_id=1, source_target_pairs={{0,2},{1,3},{2,0},{3,1},{4,6},{5,7},{6,4},{7,5},{8,10},{9,11},{10,... | collective-permute-start | bytes 221192 | tf_op jit(solution)/shard_map/ppermute | solution.py:11
  8.1 3.2 %copy-start = (bf16[9,512,128]{2,1,0:T(8,128)(2,1)S(1)}, bf16[9,512,128]{2,1,0:T(8,128)(2,1)}, u32[]{:S(2)}) copy-start(bf16[9,512,128]{2,1,0:T(8,128)(2,1)} %refs_1_.1) | copy-start | bytes 3538948
  9.3 17.9 %collective-permute-start.2 = (bf16[1056,128]{1,0:T(8,128)(2,1)S(1)}, bf16[1056,128]{1,0:T(8,128)(2,1)S(1)}, u32[]{:S(2)}, u32[]{:S(2)}) collective-permute-start(bf16[1056,128]{1,0:T(8,128)(2,1)S(1)} %get-tuple-element.27), channel_id=1, source_target_pairs={{0,3},{1,2},{2,1},{3,0},{4,7},{5,6},{6,5},{7,4},{8,11},{9,10},{10,... | collective-permute-start | bytes 811016 | tf_op jit(solution)/shard_map/ppermute | solution.py:11
  11.3 10.7 %collective-permute-start.6 = (bf16[576,128]{1,0:T(8,128)(2,1)S(1)}, bf16[576,128]{1,0:T(8,128)(2,1)S(1)}, u32[]{:S(2)}, u32[]{:S(2)}) collective-permute-start(bf16[576,128]{1,0:T(8,128)(2,1)S(1)} %bitcast.35), channel_id=1, source_target_pairs={{0,1},{1,0},{2,3},{3,2},{4,5},{5,4},{6,7},{7,6},{8,9},{9,8},{10,11... | collective-permute-start | bytes 442376 | tf_op jit(solution)/shard_map/ppermute | solution.py:11
  13.2 13.4 %collective-permute-start.11 = (bf16[1,576,128]{2,1,0:T(8,128)(2,1)S(1)}, bf16[1,576,128]{2,1,0:T(8,128)(2,1)S(1)}, u32[]{:S(2)}, u32[]{:S(2)}) collective-permute-start(bf16[1,576,128]{2,1,0:T(8,128)(2,1)S(1)} %maximum_bitcast_fusion), channel_id=1, source_target_pairs={{0,8},{4,12},{8,0},{12,4},{16,24},{20,28},{24,16},{28,20},{1,9},{5... | collective-permute-start | bytes 442376 | tf_op jit(solution)/shard_map/ppermute | solution.py:11
  22.1 5.4 %collective-permute-start.7 = (bf16[1,576,128]{2,1,0:T(8,128)(2,1)S(1)}, bf16[1,576,128]{2,1,0:T(8,128)(2,1)S(1)}, u32[]{:S(2)}, u32[]{:S(2)}) collective-permute-start(bf16[1,576,128]{2,1,0:T(8,128)(2,1)S(1)} %bitcast.30), channel_id=1, source_target_pairs={{0,16},{4,20},{8,24},{12,28},{16,0},{20,4},{24,8},{28,12},{1,17},{... | collective-permute-start | bytes 442376 | tf_op jit(solution)/shard_map/ppermute | solution.py:11
  23.6 13.3 %collective-permute-start = (bf16[1056,128]{1,0:T(8,128)(2,1)S(1)}, bf16[1056,128]{1,0:T(8,128)(2,1)S(1)}, u32[]{:S(2)}, u32[]{:S(2)}) collective-permute-start(bf16[1056,128]{1,0:T(8,128)(2,1)S(1)} %get-tuple-element.27), channel_id=1, source_target_pairs={{0,1},{1,0},{2,3},{3,2},{4,5},{5,4},{6,7},{7,6},{8,9},{9,8},{10,11... | collective-permute-start | bytes 811016 | tf_op jit(solution)/shard_map/ppermute | solution.py:11
  23.7 14.8 %collective-permute-start.1 = (bf16[1056,128]{1,0:T(8,128)(2,1)S(1)}, bf16[1056,128]{1,0:T(8,128)(2,1)S(1)}, u32[]{:S(2)}, u32[]{:S(2)}) collective-permute-start(bf16[1056,128]{1,0:T(8,128)(2,1)S(1)} %get-tuple-element.38.refs_0_), channel_id=1, source_target_pairs={{0,2},{1,3},{2,0},{3,1},{4,6},{5,7},{6,4},{7,5},{8,10},{9,11},{10,... | collective-permute-start | bytes 811016 | tf_op jit(solution)/shard_map/ppermute | solution.py:11
  26.7 11.9 %collective-permute-start.12 = (bf16[2,576,128]{2,1,0:T(8,128)(2,1)S(1)}, bf16[2,576,128]{2,1,0:T(8,128)(2,1)S(1)}, u32[]{:S(2)}, u32[]{:S(2)}) collective-permute-start(bf16[2,576,128]{2,1,0:T(8,128)(2,1)S(1)} %pad_maximum_fusion.4), channel_id=1, source_target_pairs={{0,16},{4,20},{8,24},{12,28},{16,0},{20,4},{24,8},{28,12},{1,17},{... | collective-permute-start | bytes 884744 | tf_op jit(solution)/shard_map/ppermute | solution.py:11
  27.5 11.1 %collective-permute-start.8 = (bf16[2,576,128]{2,1,0:T(8,128)(2,1)S(1)}, bf16[2,576,128]{2,1,0:T(8,128)(2,1)S(1)}, u32[]{:S(2)}, u32[]{:S(2)}) collective-permute-start(bf16[2,576,128]{2,1,0:T(8,128)(2,1)S(1)} %pad_maximum_fusion.3), channel_id=1, source_target_pairs={{0,8},{4,12},{8,0},{12,4},{16,24},{20,28},{24,16},{28,20},{1,9},{5... | collective-permute-start | bytes 884744 | tf_op jit(solution)/shard_map/ppermute | solution.py:11
  38.8 4.5 %collective-permute-start.13 = (bf16[4,1152,128]{2,1,0:T(8,128)(2,1)S(1)}, bf16[4,1152,128]{2,1,0:T(8,128)(2,1)S(1)}, u32[]{:S(2)}, u32[]{:S(2)}) collective-permute-start(bf16[4,1152,128]{2,1,0:T(8,128)(2,1)S(1)} %pad_maximum_fusion), channel_id=1, source_target_pairs={{0,4},{4,0},{8,12},{12,8},{16,20},{20,16},{24,28},{28,24},{1,5},{5... | collective-permute-start | bytes 3538952 | tf_op jit(solution)/shard_map/ppermute | solution.py:11
  38.9 15.9 %collective-permute-start.4 = (bf16[1056,128]{1,0:T(8,128)(2,1)S(1)}, bf16[1056,128]{1,0:T(8,128)(2,1)S(1)}, u32[]{:S(2)}, u32[]{:S(2)}) collective-permute-start(bf16[1056,128]{1,0:T(8,128)(2,1)S(1)} %get-tuple-element.30.refs_4_.refs_0_), channel_id=1, source_target_pairs={{0,2},{1,3},{2,0},{3,1},{4,6},{5,7},{6,4},{7,5},{8,10},{9,11},{10,... | collective-permute-start | bytes 811016 | tf_op jit(solution)/shard_map/ppermute | solution.py:11
  38.9 21.3 %collective-permute-start.3 = (bf16[1056,128]{1,0:T(8,128)(2,1)S(1)}, bf16[1056,128]{1,0:T(8,128)(2,1)S(1)}, u32[]{:S(2)}, u32[]{:S(2)}) collective-permute-start(bf16[1056,128]{1,0:T(8,128)(2,1)S(1)} %get-tuple-element.31), channel_id=1, source_target_pairs={{0,1},{1,0},{2,3},{3,2},{4,5},{5,4},{6,7},{7,6},{8,9},{9,8},{10,11... | collective-permute-start | bytes 811016 | tf_op jit(solution)/shard_map/ppermute | solution.py:11
  41.9 18.4 %collective-permute-start.5 = (bf16[1056,128]{1,0:T(8,128)(2,1)S(1)}, bf16[1056,128]{1,0:T(8,128)(2,1)S(1)}, u32[]{:S(2)}, u32[]{:S(2)}) collective-permute-start(bf16[1056,128]{1,0:T(8,128)(2,1)S(1)} %get-tuple-element.31), channel_id=1, source_target_pairs={{0,3},{1,2},{2,1},{3,0},{4,7},{5,6},{6,5},{7,4},{8,11},{9,10},{10,... | collective-permute-start | bytes 811016 | tf_op jit(solution)/shard_map/ppermute | solution.py:11
  43.5 18.1 %collective-permute-start.14 = (bf16[2112,128]{1,0:T(8,128)(2,1)S(1)}, bf16[2112,128]{1,0:T(8,128)(2,1)S(1)}, u32[]{:S(2)}, u32[]{:S(2)}) collective-permute-start(bf16[2112,128]{1,0:T(8,128)(2,1)S(1)} %get-tuple-element.42), channel_id=1, source_target_pairs={{0,4},{4,8},{8,12},{12,16},{16,20},{20,24},{24,28},{1,5},{5,9},{9,... | collective-permute-start | bytes 1622024 | tf_op jit(solution)/shard_map/ppermute | solution.py:18
  45.0 16.5 %collective-permute-start.15 = (bf16[2112,128]{1,0:T(8,128)(2,1)S(1)}, bf16[2112,128]{1,0:T(8,128)(2,1)S(1)}, u32[]{:S(2)}, u32[]{:S(2)}) collective-permute-start(bf16[2112,128]{1,0:T(8,128)(2,1)S(1)} %get-tuple-element.43), channel_id=1, source_target_pairs={{4,0},{8,4},{12,8},{16,12},{20,16},{24,20},{28,24},{5,1},{9,5},{13... | collective-permute-start | bytes 1622024 | tf_op jit(solution)/shard_map/ppermute | solution.py:18
  64.7 13.3 %collective-permute-start.17 = (bf16[1024,128]{1,0:T(8,128)(2,1)S(1)}, bf16[1024,128]{1,0:T(8,128)(2,1)S(1)}, u32[]{:S(2)}, u32[]{:S(2)}) collective-permute-start(bf16[1024,128]{1,0:T(8,128)(2,1)S(1)} %get-tuple-element.49), channel_id=1, source_target_pairs={{0,1},{1,0},{2,3},{3,2},{4,5},{5,4},{6,7},{7,6},{8,9},{9,8},{10,11... | collective-permute-start | bytes 786440 | tf_op jit(solution)/shard_map/ppermute | solution.py:11
  74.0 9.1 %collective-permute-start.16 = (bf16[1024,128]{1,0:T(8,128)(2,1)S(1)}, bf16[1024,128]{1,0:T(8,128)(2,1)S(1)}, u32[]{:S(2)}, u32[]{:S(2)}) collective-permute-start(bf16[1024,128]{1,0:T(8,128)(2,1)S(1)} %get-tuple-element.47), channel_id=1, source_target_pairs={{0,1},{1,0},{2,3},{3,2},{4,5},{5,4},{6,7},{7,6},{8,9},{9,8},{10,11... | collective-permute-start | bytes 786440 | tf_op jit(solution)/shard_map/ppermute | solution.py:11

commit v11 on v9

--- a/solution.py
+++ b/solution.py
@@ -163,9 +163,8 @@
         other[at : at + pitch] = jnp.where(side == 0, pieces[1], pieces[0])
 
 
-def rim_kernel(width, *refs):
+def rim_kernel(pitch, *refs):
     pieces, (first, last) = refs[:4], refs[4:]
-    pitch = width + 8
     for k, piece in enumerate(pieces):
         for i in range(2):
             for out, end in ((first, 0), (last, 1)):
@@ -173,75 +172,94 @@
                 out[(2 * k + i) * pitch : (2 * k + i + 1) * pitch] = piece[at : at + pitch]
 
 
-def fill_rows(target, piece, start, row, lanes, width):
-    for shift in range(3):
-        target[shift, row * width : (row + 1) * width, lanes] = piece[
-            start + shift : start + shift + width
+def fill(target, rows):
+    width = target.shape[1] // len(rows)
+    for r, row in enumerate(rows):
+        for k, (ref, start) in enumerate(row):
+            local = ref.shape[1]
+            for shift in range(3):
+                target[
+                    shift, r * width : (r + 1) * width, k * local : (k + 1) * local
+                ] = ref[start + shift : start + shift + width]
+
+
+def product(which, source, at, size, weights, extra, down, across):
+    half = weights.shape[1]
+    if which == 0:
+        tap = 3 * (2 - down) + across
+        filters = weights[pl.ds(tap * 2 * half, 2 * half), :]
+        return jnp.dot(
+            source[2 - across, at : at + size], filters, preferred_element_type=jnp.float32
+        )
+    tap = 3 * down + across
+    total = None
+    for block in range(2):
+        if block:
+            filters = extra[pl.ds(tap * half, half), :]
+        else:
+            filters = weights[pl.ds(tap * 2 * half, half), :]
+        term = lax.dot_general(
+            source[across, at : at + size, block * half : (block + 1) * half],
+            filters,
+            (((1,), (1,)), ((), ())),
+            preferred_element_type=jnp.float32,
+        )
+        total = term if total is None else total + term
+    return total
+
+
+def outer_kernel(*refs):
+    pieces, (before, after, weights, extra), (*totals, upstream, image) = (
+        refs[:4],
+        refs[4:8],
+        refs[8:],
+    )
+    pitch = before.shape[0] // 8
+    for which, (total, source) in enumerate(zip(totals, (upstream, image))):
+        rims = [[(rim, (2 * k + which) * pitch) for k in range(4)] for rim in (before, after)]
+        edges = [[(p, (2 * which + end) * pitch) for p in pieces] for end in range(2)]
+        fill(source, [rims[0], *edges, rims[1]])
+        size = total.shape[0] // 2
+        row = size // 2
+        top = middle = bottom = None
+        for across in range(3):
+            terms = [
+                product(which, source, at, size, weights, extra, down, across)
+                for down, at in ((0, 0), (1, row), (2, size))
+            ]
+            if across:
+                terms = [old + term for old, term in zip((top, middle, bottom), terms)]
+            top, middle, bottom = terms
+        total[:row] = top[:row] + middle[:row]
+        total[row:size] = top[row:]
+        total[size : size + row] = bottom[:row]
+        total[size + row :] = bottom[row:] + middle[row:]
+
+
+def inner_kernel(which, *refs):
+    inners, (total, weights, extra, lines) = refs[:4], refs[4:8]
+    mine, other, source = refs[-3:]
+    size = total.shape[0] // 2
+    row = size // 2
+    local = mine.shape[1]
+    pitch = row + 8
+    fill(source, [[(p, (2 * which + r) * pitch) for p in inners] for r in range(2)])
+    top = middle = bottom = None
+    for across in range(3):
+        terms = [
+            product(which, source, 0, size, weights, extra, down, across) for down in (2, 1, 0)
         ]
-
-
-def fill_source(target, which, width, rows, before, after):
-    local = before.shape[1]
-    pitch = width + 8
-    for k, held in enumerate(rows):
-        lanes = slice(k * local, (k + 1) * local)
-        held = [(before, 2 * k + which), *held, (after, 2 * k + which)]
-        for r, (ref, at) in enumerate(held):
-            fill_rows(target, ref, at * pitch, r, lanes, width)
-
-
-def inside(edges, inners, which, count):
-    return [
-        [(p, 2 * which), *((q, r) for r in range(count - 2)), (p, 2 * which + 1)]
-        for p, q in zip(edges, inners)
-    ]
-
-
-def backward_kernel(*refs):
-    edges, inners, (before, after, weights, _, mine, other, source) = refs[:4], refs[4:8], refs[8:]
-    size, local = mine.shape
-    width = before.shape[0] // 8 - 8
-    channels = 4 * local
-    fill_source(source, 0, width, inside(edges, inners, 0, size // width), before, after)
-    acc = None
-    for a in range(3):
-        for b in range(3):
-            term = jnp.dot(
-                source[2 - b, pl.ds((2 - a) * width, size), :],
-                weights[pl.ds((3 * a + b) * channels, channels), :],
-                preferred_element_type=jnp.float32,
-            )
-            acc = term if acc is None else acc + term
-    mine[...] = acc[:, :local].astype(jnp.bfloat16)
-    other[...] = acc[:, local:].astype(jnp.bfloat16)
-
-
-def forward_kernel(*refs):
-    edges, inners, refs = refs[:4], refs[4:8], refs[8:]
-    before, after, weights, extra, mine, other, source = refs
-    size, local = mine.shape
-    width = before.shape[0] // 8 - 8
-    channels, half = 4 * local, 2 * local
-    fill_source(source, 1, width, inside(edges, inners, 1, size // width), before, after)
-    acc = None
-    for a in range(3):
-        for b in range(3):
-            tap = 3 * a + b
-            for part in range(2):
-                if part:
-                    filters = extra[pl.ds(tap * half, half), :]
-                else:
-                    filters = weights[pl.ds(tap * channels, half), :]
-                term = lax.dot_general(
-                    source[b, pl.ds(a * width, size), part * half : (part + 1) * half],
-                    filters,
-                    (((1,), (1,)), ((), ())),
-                    preferred_element_type=jnp.float32,
-                )
-                acc = term if acc is None else acc + term
-    for k, out in enumerate((mine, other)):
-        bias = edges[k][width : width + 8, :].astype(jnp.float32)[2:3]
-        out[...] = (acc[:, k * local : (k + 1) * local] + bias).astype(jnp.bfloat16)
+        if across:
+            terms = [old + term for old, term in zip((top, middle, bottom), terms)]
+        top, middle, bottom = terms
+    parts = [top[:row], top[row:] + middle[:row], middle[row:] + bottom[:row], bottom[row:]]
+    for r, part in enumerate(parts):
+        value = total[r * row : (r + 1) * row] + part
+        for k, out in enumerate((mine, other)):
+            block = value[:, k * local : (k + 1) * local]
+            if which:
+                block = block + lines[k : k + 1, :]
+            out[r * row : (r + 1) * row] = block.astype(jnp.bfloat16)
 
 
 SMEM = pl.BlockSpec(memory_space=pltpu.SMEM)
@@ -254,30 +272,30 @@
     return pl.CostEstimate(flops=work, bytes_accessed=2**20, transcendentals=0)
 
 
-def kernel(body, shapes, args, scratch, name, placed=False, micros=0):
+def kernel(body, shapes, args, scratch, name, placed=False, micros=0, kind=jnp.bfloat16):
     return pl.pallas_call(
         body,
-        out_shape=[jax.ShapeDtypeStruct(s, jnp.bfloat16) for s in shapes],
+        out_shape=[jax.ShapeDtypeStruct(s, kind) for s in shapes],
         in_specs=[SMEM] * placed + [VMEM] * (len(args) - placed),
         out_specs=[VMEM] * len(shapes),
         scratch_shapes=[pltpu.VMEM(s, jnp.bfloat16) for s in scratch],
-        compiler_params=pltpu.CompilerParams(vmem_limit_bytes=32 * 2**20),
+        compiler_params=pltpu.CompilerParams(vmem_limit_bytes=20 * 2**20),
         cost_estimate=cost(micros),
         name=name,
     )(*args)
 
 
-def cut(place, sources, bias, parts, name, micros):
+def cut(place, sources, bias, parts, micros):
     local = bias.shape[1]
     shape = (len(parts) * (sources[0].shape[1] // 2 + 8), local)
     body = lambda *refs: cut_kernel(parts, *refs)
-    return kernel(body, [shape] * 2, [place, *sources, bias], [], name, True, micros)
-
-
-def exchange(mine, other):
-    far = swap(other, "chan", 3)
-    middle = swap(mine, "chan", 2)
-    return [mine, swap(other, "chan", 1), middle, far]
+    return kernel(body, [shape] * 2, [place, *sources, bias], [], "cut", True, micros)
+
+
+def exchange(mine, other, near=None):
+    sent = {1: other if near is None else near, 2: mine, 3: other}
+    held = {k: swap(sent[k], "chan", k) for k in (2, 3, 1)}
+    return [mine, held[1], held[2], held[3]]
 
 
 def after(value, *others):
@@ -324,14 +342,7 @@
 
 
 def token(pieces, micros):
-    return pl.pallas_call(
-        token_kernel,
-        out_shape=jax.ShapeDtypeStruct((16, 128), jnp.bfloat16),
-        in_specs=[ANY] * len(pieces),
-        out_specs=VMEM,
-        cost_estimate=cost(micros),
-        name="token",
-    )(*pieces)
+    return kernel(token_kernel, [(16, 128)], pieces, [], "token", False, micros)[0]
 
 
 def per_device(image, filters, bias, upstream):
@@ -339,7 +350,7 @@
     bands = lax.axis_size("band")
     taps, outs, local = filters.shape
     rows, cols = image.shape[1:]
-    if n != 4 or local % 128 or cols % 256 or rows < 3 or outs % (32 * bands) or bands < 4:
+    if n != 4 or local % 128 or cols % 256 or rows != 4 or outs % (32 * bands) or bands < 4:
         return plain(image, filters, bias, upstream)
     me = lax.axis_index("chan")
     band = lax.axis_index("band")
@@ -356,41 +367,61 @@
 
     upstream, image = [jnp.transpose(v, (1, 2, 0)) for v in (upstream, image)]
     parts = [(i, r) for i in range(2) for r in (0, rows - 1)]
-    edge = cut(place, [upstream, image], bias[None], parts, "cut_edge", 0)
-    near, across = after((near, across), edge)
-    edge = exchange(*edge)
-    parts = [(0, r) for r in range(1, rows - 1)]
-    first = exchange(*cut(place, [upstream], bias[None], parts, "cut_first", 0))
-    second = exchange(*cut(place, [image], bias[None], parts, "cut_second", 0))
-    mark = token(first, 18)
+    sent = cut(place, [upstream, image], bias[None], parts, 25)
+    (near, across) = after((near, across), sent)
+    pieces = exchange(*sent)
+    parts = [(i, r) for i in range(2) for r in range(1, rows - 1)]
+    sent = cut(place, after([upstream, image], pieces[1]), bias[None], parts, 25)
+    pieces = after(pieces, sent)
+    inners = exchange(*sent)
 
     steps = halving(bands)[:-1]
     near, near_order = gather(near, steps)
     across, across_order = gather(across, steps[::-1])
     held = [near, swap(near, "band", 1), across, swap(across, "band", 1)]
-    weights, extra = kernel(
+    filters = kernel(
         lambda *refs: assemble_kernel((near_order, across_order), *refs),
         [(taps * outs, 2 * local), (taps * 2 * local, 2 * local)],
         [place, filters, *held],
         [],
         "assemble",
         True,
-        2,
-    )
-    rim = (8 * (width + 8), local)
-    body = lambda *refs: rim_kernel(width, *refs)
-    rims = neighbours(*kernel(body, [rim] * 2, edge, [], "rim", False, 16))
-
-    out = [(rows * width, local)] * 2
-    source = [(3, (rows + 2) * width, 4 * local)]
-    args = [*edge, *first, *rims, weights, mark]
-    mine, other = kernel(backward_kernel, out, args, source, "backward", False, 10)
-    other = swap(other, "chan", 1)
-    image_grad = home(place, mine, other, rows)
-    args = [*edge, *after(second, mine), *rims, weights, extra]
-    mine, sent = kernel(forward_kernel, out, args, source, "forward", False, 5)
-    other = swap(after(sent, other), "chan", 1)
-    return home(place, mine, other, rows), image_grad
+        9,
+    )
+    pitch = width + 8
+    body = lambda *refs: rim_kernel(pitch, *refs)
+    rims = neighbours(*kernel(body, [(8 * pitch, local)] * 2, pieces, [], "rim", False, 40))
+
+    size = rows * width
+    totals = kernel(
+        outer_kernel,
+        [(size, 2 * local)] * 2,
+        [*pieces, *rims, *filters],
+        [(3, size, 4 * local)] * 2,
+        "outer",
+        False,
+        6,
+        jnp.float32,
+    )
+    lines = jnp.concatenate([p[width + 2 : width + 3] for p in pieces[:2]]).astype(jnp.float32)
+    inners = after(inners, totals)
+    mark = [token(inners, 0)]
+    kept, came = [], []
+    for which in range(2):
+        mine, other = kernel(
+            lambda *refs: inner_kernel(which, *refs),
+            [(size, local)] * 2,
+            [*inners, totals[which], *filters, lines, *mark],
+            [(3, size // 2, 4 * local)],
+            "inner",
+            False,
+            9,
+        )
+        kept.append(mine)
+        came.append(swap(other, "chan", 1))
+    image_grad = home(place, kept[0], came[0], rows)
+    kept[1] = after(kept[1], image_grad)
+    return home(place, kept[1], came[1], rows), image_grad
 
 
 def solution(mesh):

time: 91.3 us -> 90.2 us (0.988)
  the two profiles are of different devices: /device:TPU:0 before, /device:TPU:3 now
where the time goes in v11:
time: 90.2 us; the launch traced here: 90 us
  starting transfers between devices  39.9 us (44%)
  waiting for transfers between devices  32.5 us (36%)
  Pallas kernels  11.9 us (13%)
  local copies, waits for them, and re-layouts  4.54 us (5%)
    ppermute x17, starting transfers between devices, swap(): return lax.ppermute(value, axis, [(j, j ^ step) for j in range(size)])  34.7 us
    ppermute x17, waiting for transfers between devices, swap(): return lax.ppermute(value, axis, [(j, j ^ step) for j in range(size)])  20.9 us
    pallas_call x10, Pallas kernels, kernel(): pl.pallas_call(body, out_shape=[jax.ShapeDtypeStruct(s, kind) for s in sh...  11.9 us
    ppermute x2, waiting for transfers between devices, neighbours(): return (lax.ppermute(last, 'band', up), lax.ppermute(first, 'band', down))  11.6 us
    ppermute x2, starting transfers between devices, neighbours(): return (lax.ppermute(last, 'band', up), lax.ppermute(first, 'band', down))  5.27 us
    unnamed x8, local copies, waits for them, and re-layouts  1.89 us
  transfers between devices with their start and end apart: 19, of which 9 were waited for; matrix products, arithmetic and copies ran while one was open for 4% of the time, Pallas kernels for 10%

profile of v11, /device:TPU:3, one launch (start us, length us, event | category | flops | bytes accessed | tf_op | source)
XLA Modules:
  0.0 90.0 jit_solution(15321164906549980000)
XLA Ops:
  0.6 0.0 copy-start.2
  0.7 1.0 %constant_dynamic-slice_fusion = bf16[9,32,128]{2,1,0:T(8,128)(2,1)S(1)} fusion(bf16[9,512,128]{2,1,0:T(8,128)(2,1)} %refs_1_.1, s32[]{:T(128)S(6)} %select_n.7), kind=kLoop, calls=%fused_computation.7 | loop fusion | bytes 147460 | tf_op jit(solution)/shard_map/dynamic_slice | solution.py:364
  1.6 3.3 %collective-permute-start.10 = (bf16[288,128]{1,0:T(8,128)(2,1)S(1)}, bf16[288,128]{1,0:T(8,128)(2,1)S(1)}, u32[]{:S(2)}, u32[]{:S(2)}) collective-permute-start(bf16[288,128]{1,0:T(8,128)(2,1)S(1)} %bitcast.38), channel_id=1, source_target_pairs={{0,3},{1,2},{2,1},{3,0},{4,7},{5,6},{6,5},{7,4},{8,11},{9,10},{10,... | collective-permute-start | bytes 221192 | tf_op jit(solution)/shard_map/ppermute | solution.py:11
  4.9 0.0 collective-permute-start.9
  4.9 0.0 copy-start.1
  4.9 0.9 %constant_dynamic-slice_fusion.1 = bf16[9,64,128]{2,1,0:T(8,128)(2,1)S(1)} fusion(bf16[9,512,128]{2,1,0:T(8,128)(2,1)} %refs_1_.1, s32[]{:T(128)S(6)} %select_n.6), kind=kLoop, calls=%fused_computation.8 | loop fusion | bytes 294916 | tf_op jit(solution)/shard_map/dynamic_slice | solution.py:362
  5.9 0.4 collective-permute-start.8
  6.3 1.5 %copy.6 = bf16[128,4,512]{0,2,1:T(8,128)(2,1)S(1)} copy(bf16[128,4,512]{2,1,0:T(4,128)(2,1)} %param.7) | data formatting | bytes 1048576 | tf_op args[3]
  7.7 0.0 copy-done.2
  7.7 0.4 copy.7
  8.2 0.1 pad_add_fusion.refs_0_.place
  8.2 0.0 copy-done.1
  8.2 0.7 cut.2
  8.9 1.2 %collective-permute-start = (bf16[1056,128]{1,0:T(8,128)(2,1)S(1)}, bf16[1056,128]{1,0:T(8,128)(2,1)S(1)}, u32[]{:S(2)}, u32[]{:S(2)}) collective-permute-start(bf16[1056,128]{1,0:T(8,128)(2,1)S(1)} %get-tuple-element.29), channel_id=1, source_target_pairs={{0,1},{1,0},{2,3},{3,2},{4,5},{5,4},{6,7},{7,6},{8,9},{9,8},{10,11... | collective-permute-start | bytes 811016 | tf_op jit(solution)/shard_map/ppermute | solution.py:11
  10.1 0.0 collective-permute-done.10
  10.1 1.1 %collective-permute-done.9 = bf16[288,128]{1,0:T(8,128)(2,1)S(1)} collective-permute-done((bf16[288,128]{1,0:T(8,128)(2,1)S(1)}, bf16[288,128]{1,0:T(8,128)(2,1)S(1)}, u32[]{:S(2)}, u32[]{:S(2)}) %collective-permute-start.9) | collective-permute-done | bytes 73760 | tf_op jit(solution)/shard_map/ppermute | solution.py:11
  11.3 0.9 collective-permute-done.8
  12.1 0.4 collective-permute-start.14
  12.5 1.1 %collective-permute-start.11 = (bf16[1,576,128]{2,1,0:T(8,128)(2,1)S(1)}, bf16[1,576,128]{2,1,0:T(8,128)(2,1)S(1)}, u32[]{:S(2)}, u32[]{:S(2)}) collective-permute-start(bf16[1,576,128]{2,1,0:T(8,128)(2,1)S(1)} %bitcast.32), channel_id=1, source_target_pairs={{0,16},{4,20},{8,24},{12,28},{16,0},{20,4},{24,8},{28,12},{1,17},{... | collective-permute-start | bytes 442376 | tf_op jit(solution)/shard_map/ppermute | solution.py:11
  13.6 1.1 %collective-permute-start.4 = (bf16[1056,128]{1,0:T(8,128)(2,1)S(1)}, bf16[1056,128]{1,0:T(8,128)(2,1)S(1)}, u32[]{:S(2)}, u32[]{:S(2)}) collective-permute-start(bf16[1056,128]{1,0:T(8,128)(2,1)S(1)} %get-tuple-element.35.refs_0_), channel_id=1, source_target_pairs={{0,2},{1,3},{2,0},{3,1},{4,6},{5,7},{6,4},{7,5},{8,10},{9,11},{10,... | collective-permute-start | bytes 811016 | tf_op jit(solution)/shard_map/ppermute | solution.py:11
  14.7 1.9 %collective-permute-start.5 = (bf16[1056,128]{1,0:T(8,128)(2,1)S(1)}, bf16[1056,128]{1,0:T(8,128)(2,1)S(1)}, u32[]{:S(2)}, u32[]{:S(2)}) collective-permute-start(bf16[1056,128]{1,0:T(8,128)(2,1)S(1)} %get-tuple-element.29), channel_id=1, source_target_pairs={{0,3},{1,2},{2,1},{3,0},{4,7},{5,6},{6,5},{7,4},{8,11},{9,10},{10,... | collective-permute-start | bytes 811016 | tf_op jit(solution)/shard_map/ppermute | solution.py:11
  16.6 3.2 %collective-permute-done.refs_1_ = bf16[1056,128]{1,0:T(8,128)(2,1)S(1)} collective-permute-done((bf16[1056,128]{1,0:T(8,128)(2,1)S(1)}, bf16[1056,128]{1,0:T(8,128)(2,1)S(1)}, u32[]{:S(2)}, u32[]{:S(2)}) %collective-permute-start) | collective-permute-done | bytes 270368 | tf_op jit(solution)/shard_map/ppermute | solution.py:11
  19.8 0.0 collective-permute-done.14
  19.9 2.5 %collective-permute-start.15 = (bf16[2,576,128]{2,1,0:T(8,128)(2,1)S(1)}, bf16[2,576,128]{2,1,0:T(8,128)(2,1)S(1)}, u32[]{:S(2)}, u32[]{:S(2)}) collective-permute-start(bf16[2,576,128]{2,1,0:T(8,128)(2,1)S(1)} %pad_maximum_fusion.3), channel_id=1, source_target_pairs={{0,16},{4,20},{8,24},{12,28},{16,0},{20,4},{24,8},{28,12},{1,17},{... | collective-permute-start | bytes 884744 | tf_op jit(solution)/shard_map/ppermute | solution.py:11
  22.4 0.0 collective-permute-done.11
  22.4 0.1 collective-permute-start.12
  22.5 0.7 cut.3
  23.2 0.1 collective-permute-start.1
  23.3 7.6 %collective-permute-done.4.refs_2_ = bf16[1056,128]{1,0:T(8,128)(2,1)S(1)} collective-permute-done((bf16[1056,128]{1,0:T(8,128)(2,1)S(1)}, bf16[1056,128]{1,0:T(8,128)(2,1)S(1)}, u32[]{:S(2)}, u32[]{:S(2)}) %collective-permute-start.4) | collective-permute-done | bytes 270368 | tf_op jit(solution)/shard_map/ppermute | solution.py:11
  30.9 5.2 %collective-permute-start.3 = (bf16[1056,128]{1,0:T(8,128)(2,1)S(1)}, bf16[1056,128]{1,0:T(8,128)(2,1)S(1)}, u32[]{:S(2)}, u32[]{:S(2)}) collective-permute-start(bf16[1056,128]{1,0:T(8,128)(2,1)S(1)} %get-tuple-element.33), channel_id=1, source_target_pairs={{0,3},{1,2},{2,1},{3,0},{4,7},{5,6},{6,5},{7,4},{8,11},{9,10},{10,... | collective-permute-start | bytes 811016 | tf_op jit(solution)/shard_map/ppermute | solution.py:11
  36.1 0.0 collective-permute-done.5.refs_3_
  36.1 10.7 %collective-permute-start.2 = (bf16[1056,128]{1,0:T(8,128)(2,1)S(1)}, bf16[1056,128]{1,0:T(8,128)(2,1)S(1)}, u32[]{:S(2)}, u32[]{:S(2)}) collective-permute-start(bf16[1056,128]{1,0:T(8,128)(2,1)S(1)} %get-tuple-element.47.refs_0_), channel_id=1, source_target_pairs={{0,2},{1,3},{2,0},{3,1},{4,6},{5,7},{6,4},{7,5},{8,10},{9,11},{10,... | collective-permute-start | bytes 811016 | tf_op jit(solution)/shard_map/ppermute | solution.py:11
  46.8 0.0 collective-permute-done.15
  46.8 0.1 pad_maximum_fusion.1.refs_4_
  46.8 5.1 %collective-permute-start.16 = (bf16[4,576,128]{2,1,0:T(8,128)(2,1)S(1)}, bf16[4,576,128]{2,1,0:T(8,128)(2,1)S(1)}, u32[]{:S(2)}, u32[]{:S(2)}) collective-permute-start(bf16[4,576,128]{2,1,0:T(8,128)(2,1)S(1)} %pad_maximum_fusion.1.refs_4_), channel_id=1, source_target_pairs={{0,4},{4,0},{8,12},{12,8},{16,20},{20,16},{24,28},{28,24},{1,5},{5... | collective-permute-start | bytes 1769480 | tf_op jit(solution)/shard_map/ppermute | solution.py:11
  51.9 0.0 collective-permute-done.12
  51.9 0.1 pad_maximum_fusion.refs_2_
  52.0 0.0 copy-start
  52.0 0.1 collective-permute-start.13
  52.1 0.1 rim.1
  52.2 1.3 %collective-permute-done.16.refs_5_ = bf16[4,576,128]{2,1,0:T(8,128)(2,1)S(1)} collective-permute-done((bf16[4,576,128]{2,1,0:T(8,128)(2,1)S(1)}, bf16[4,576,128]{2,1,0:T(8,128)(2,1)S(1)}, u32[]{:S(2)}, u32[]{:S(2)}) %collective-permute-start.16) | collective-permute-done | bytes 589856 | tf_op jit(solution)/shard_map/ppermute | solution.py:11
  53.6 3.3 %collective-permute-start.6 = (bf16[2112,128]{1,0:T(8,128)(2,1)S(1)}, bf16[2112,128]{1,0:T(8,128)(2,1)S(1)}, u32[]{:S(2)}, u32[]{:S(2)}) collective-permute-start(bf16[2112,128]{1,0:T(8,128)(2,1)S(1)} %get-tuple-element.39), channel_id=1, source_target_pairs={{0,4},{4,8},{8,12},{12,16},{16,20},{20,24},{24,28},{1,5},{5,9},{9,... | collective-permute-start | bytes 1622024 | tf_op jit(solution)/shard_map/ppermute | solution.py:18
  56.9 0.0 collective-permute-done.13.refs_3_
  56.9 1.9 %collective-permute-start.7 = (bf16[2112,128]{1,0:T(8,128)(2,1)S(1)}, bf16[2112,128]{1,0:T(8,128)(2,1)S(1)}, u32[]{:S(2)}, u32[]{:S(2)}) collective-permute-start(bf16[2112,128]{1,0:T(8,128)(2,1)S(1)} %get-tuple-element.40), channel_id=1, source_target_pairs={{4,0},{8,4},{12,8},{16,12},{20,16},{24,20},{28,24},{5,1},{9,5},{13... | collective-permute-start | bytes 1622024 | tf_op jit(solution)/shard_map/ppermute | solution.py:18
  58.9 0.0 copy-done
  58.9 1.3 %assemble.1 = (bf16[4608,256]{1,0:T(8,128)(2,1)S(1)}, bf16[2304,256]{1,0:T(8,128)(2,1)S(1)}) custom-call(s32[2]{0:T(128)S(1)} %pad_add_fusion.refs_0_.place, bf16[9,512,128]{2,1,0:T(8,128)(2,1)S(1)} %copy-done, bf16[4,576,128]{2,1,0:T(8,128)(2,1)S(1)} %pad_maximum_fusion.refs_2_, bf16[4,576,128]{2,1,0:T(8,128)(2,1)S(1)} %collective-permute-done.13.refs_3_, ...), custom_call_target="tpu_custom_call" | custom-call | flops 9001048064 | bytes 1048576 | tf_op jit(solution)/shard_map/assemble/pallas_call | solution.py:276
  60.2 6.0 %collective-permute-done.6.refs_4_ = bf16[2112,128]{1,0:T(8,128)(2,1)S(1)} collective-permute-done((bf16[2112,128]{1,0:T(8,128)(2,1)S(1)}, bf16[2112,128]{1,0:T(8,128)(2,1)S(1)}, u32[]{:S(2)}, u32[]{:S(2)}) %collective-permute-start.6) | collective-permute-done | bytes 540704 | tf_op jit(solution)/shard_map/ppermute | solution.py:18
  66.1 5.6 %collective-permute-done.7.refs_5_ = bf16[2112,128]{1,0:T(8,128)(2,1)S(1)} collective-permute-done((bf16[2112,128]{1,0:T(8,128)(2,1)S(1)}, bf16[2112,128]{1,0:T(8,128)(2,1)S(1)}, u32[]{:S(2)}, u32[]{:S(2)}) %collective-permute-start.7) | collective-permute-done | bytes 540704 | tf_op jit(solution)/shard_map/ppermute | solution.py:18
  71.8 3.1 %outer.1 = (f32[1024,256]{1,0:T(8,128)S(1)}, f32[1024,256]{1,0:T(8,128)S(1)}) custom-call(bf16[1056,128]{1,0:T(8,128)(2,1)S(1)} %get-tuple-element.35.refs_0_, bf16[1056,128]{1,0:T(8,128)(2,1)S(1)} %collective-permute-done.refs_1_, bf16[1056,128]{1,0:T(8,128)(2,1)S(1)} %collective-permute-done.4.refs_2_, ...), custom_call_target="tpu_custom_call" | custom-call | flops 6001048576 | bytes 1048576 | tf_op jit(solution)/shard_map/outer/pallas_call | solution.py:276
  74.8 0.0 collective-permute-done.1.refs_1_
  74.8 0.0 collective-permute-done.2.refs_2_
  74.8 0.0 collective-permute-done.3.refs_3_
  74.9 1.7 %inner.3 = (bf16[1024,128]{1,0:T(8,128)(2,1)S(1)}, bf16[1024,128]{1,0:T(8,128)(2,1)S(1)}) custom-call(bf16[1056,128]{1,0:T(8,128)(2,1)S(1)} %get-tuple-element.47.refs_0_, bf16[1056,128]{1,0:T(8,128)(2,1)S(1)} %collective-permute-done.1.refs_1_, bf16[1056,128]{1,0:T(8,128)(2,1)S(1)} %collective-permute-done.2.refs_2_, ...), custom_call_target="tpu_custom_call" | custom-call | flops 9001048064 | bytes 1048576 | tf_op jit(solution)/shard_map/inner/pallas_call | solution.py:276
  76.6 0.1 collective-permute-start.17
  76.6 1.5 %inner.2 = (bf16[1024,128]{1,0:T(8,128)(2,1)S(1)}, bf16[1024,128]{1,0:T(8,128)(2,1)S(1)}) custom-call(bf16[1056,128]{1,0:T(8,128)(2,1)S(1)} %get-tuple-element.47.refs_0_, bf16[1056,128]{1,0:T(8,128)(2,1)S(1)} %collective-permute-done.1.refs_1_, bf16[1056,128]{1,0:T(8,128)(2,1)S(1)} %collective-permute-done.2.refs_2_, ...), custom_call_target="tpu_custom_call" | custom-call | flops 9001048064 | bytes 1048576 | tf_op jit(solution)/shard_map/inner/pallas_call | solution.py:276
  78.2 1.5 %collective-permute-start.18 = (bf16[1024,128]{1,0:T(8,128)(2,1)S(1)}, bf16[1024,128]{1,0:T(8,128)(2,1)S(1)}, u32[]{:S(2)}, u32[]{:S(2)}) collective-permute-start(bf16[1024,128]{1,0:T(8,128)(2,1)S(1)} %get-tuple-element.55), channel_id=1, source_target_pairs={{0,1},{1,0},{2,3},{3,2},{4,5},{5,4},{6,7},{7,6},{8,9},{9,8},{10,11... | collective-permute-start | bytes 786440 | tf_op jit(solution)/shard_map/ppermute | solution.py:11
  79.7 0.2 copy.12
  79.9 5.1 %collective-permute-done.17 = bf16[1024,128]{1,0:T(8,128)(2,1)S(1)} collective-permute-done((bf16[1024,128]{1,0:T(8,128)(2,1)S(1)}, bf16[1024,128]{1,0:T(8,128)(2,1)S(1)}, u32[]{:S(2)}, u32[]{:S(2)}) %collective-permute-start.17) | collective-permute-done | bytes 262176 | tf_op jit(solution)/shard_map/ppermute | solution.py:11
  85.0 0.2 copy.13
  85.2 1.4 %home.2 = bf16[128,4,512]{2,1,0:T(4,128)(2,1)} custom-call(s32[2]{0:T(128)S(1)} %pad_add_fusion.refs_0_.place, bf16[128,4,256]{2,1,0:T(4,128)(2,1)S(1)} %bitcast.18, bf16[128,4,256]{2,1,0:T(4,128)(2,1)S(1)} %bitcast.20), custom_call_target="tpu_custom_call" | custom-call | flops 1048576 | bytes 1048576 | tf_op jit(solution)/shard_map/home/pallas_call | solution.py:276
  86.6 0.2 copy.14
  86.8 1.5 %collective-permute-done.18 = bf16[1024,128]{1,0:T(8,128)(2,1)S(1)} collective-permute-done((bf16[1024,128]{1,0:T(8,128)(2,1)S(1)}, bf16[1024,128]{1,0:T(8,128)(2,1)S(1)}, u32[]{:S(2)}, u32[]{:S(2)}) %collective-permute-start.18) | collective-permute-done | bytes 262176 | tf_op jit(solution)/shard_map/ppermute | solution.py:11
  88.4 0.2 copy.15
  88.5 1.4 %home.3 = bf16[128,4,512]{2,1,0:T(4,128)(2,1)} custom-call(s32[2]{0:T(128)S(1)} %pad_add_fusion.refs_0_.place, bf16[128,4,256]{2,1,0:T(4,128)(2,1)S(1)} %bitcast.17, bf16[128,4,256]{2,1,0:T(4,128)(2,1)S(1)} %bitcast.19), custom_call_target="tpu_custom_call" | custom-call | flops 1048576 | bytes 1048576 | tf_op jit(solution)/shard_map/home/pallas_call | solution.py:276
  (7 shorter events, 0.1 us)
Async XLA Ops:
  0.6 7.1 %copy-start.2 = (bf16[128,4,512]{2,1,0:T(4,128)(2,1)S(1)}, bf16[128,4,512]{2,1,0:T(4,128)(2,1)}, u32[]{:S(2)}) copy-start(bf16[128,4,512]{2,1,0:T(4,128)(2,1)} %param.4) | copy-start | bytes 1572868
  1.6 8.5 %collective-permute-start.10 = (bf16[288,128]{1,0:T(8,128)(2,1)S(1)}, bf16[288,128]{1,0:T(8,128)(2,1)S(1)}, u32[]{:S(2)}, u32[]{:S(2)}) collective-permute-start(bf16[288,128]{1,0:T(8,128)(2,1)S(1)} %bitcast.38), channel_id=1, source_target_pairs={{0,3},{1,2},{2,1},{3,0},{4,7},{5,6},{6,5},{7,4},{8,11},{9,10},{10,... | collective-permute-start | bytes 221192 | tf_op jit(solution)/shard_map/ppermute | solution.py:11
  4.9 6.3 %collective-permute-start.9 = (bf16[288,128]{1,0:T(8,128)(2,1)S(1)}, bf16[288,128]{1,0:T(8,128)(2,1)S(1)}, u32[]{:S(2)}, u32[]{:S(2)}) collective-permute-start(bf16[288,128]{1,0:T(8,128)(2,1)S(1)} %bitcast.39), channel_id=1, source_target_pairs={{0,2},{1,3},{2,0},{3,1},{4,6},{5,7},{6,4},{7,5},{8,10},{9,11},{10,... | collective-permute-start | bytes 221192 | tf_op jit(solution)/shard_map/ppermute | solution.py:11
  4.9 3.3 %copy-start.1 = (bf16[128]{0:T(256)(128)(2,1)S(1)}, bf16[128]{0:T(256)(128)(2,1)}, u32[]{:S(2)}) copy-start(bf16[128]{0:T(256)(128)(2,1)} %param.6) | copy-start | bytes 772
  5.9 6.2 %collective-permute-start.8 = (bf16[576,128]{1,0:T(8,128)(2,1)S(1)}, bf16[576,128]{1,0:T(8,128)(2,1)S(1)}, u32[]{:S(2)}, u32[]{:S(2)}) collective-permute-start(bf16[576,128]{1,0:T(8,128)(2,1)S(1)} %bitcast.37), channel_id=1, source_target_pairs={{0,1},{1,0},{2,3},{3,2},{4,5},{5,4},{6,7},{7,6},{8,9},{9,8},{10,11... | collective-permute-start | bytes 442376 | tf_op jit(solution)/shard_map/ppermute | solution.py:11
  8.9 10.9 %collective-permute-start = (bf16[1056,128]{1,0:T(8,128)(2,1)S(1)}, bf16[1056,128]{1,0:T(8,128)(2,1)S(1)}, u32[]{:S(2)}, u32[]{:S(2)}) collective-permute-start(bf16[1056,128]{1,0:T(8,128)(2,1)S(1)} %get-tuple-element.29), channel_id=1, source_target_pairs={{0,1},{1,0},{2,3},{3,2},{4,5},{5,4},{6,7},{7,6},{8,9},{9,8},{10,11... | collective-permute-start | bytes 811016 | tf_op jit(solution)/shard_map/ppermute | solution.py:11
  12.1 7.7 %collective-permute-start.14 = (bf16[1,576,128]{2,1,0:T(8,128)(2,1)S(1)}, bf16[1,576,128]{2,1,0:T(8,128)(2,1)S(1)}, u32[]{:S(2)}, u32[]{:S(2)}) collective-permute-start(bf16[1,576,128]{2,1,0:T(8,128)(2,1)S(1)} %bitcast.29), channel_id=1, source_target_pairs={{0,8},{4,12},{8,0},{12,4},{16,24},{20,28},{24,16},{28,20},{1,9},{5... | collective-permute-start | bytes 442376 | tf_op jit(solution)/shard_map/ppermute | solution.py:11
  12.5 9.9 %collective-permute-start.11 = (bf16[1,576,128]{2,1,0:T(8,128)(2,1)S(1)}, bf16[1,576,128]{2,1,0:T(8,128)(2,1)S(1)}, u32[]{:S(2)}, u32[]{:S(2)}) collective-permute-start(bf16[1,576,128]{2,1,0:T(8,128)(2,1)S(1)} %bitcast.32), channel_id=1, source_target_pairs={{0,16},{4,20},{8,24},{12,28},{16,0},{20,4},{24,8},{28,12},{1,17},{... | collective-permute-start | bytes 442376 | tf_op jit(solution)/shard_map/ppermute | solution.py:11
  13.6 17.3 %collective-permute-start.4 = (bf16[1056,128]{1,0:T(8,128)(2,1)S(1)}, bf16[1056,128]{1,0:T(8,128)(2,1)S(1)}, u32[]{:S(2)}, u32[]{:S(2)}) collective-permute-start(bf16[1056,128]{1,0:T(8,128)(2,1)S(1)} %get-tuple-element.35.refs_0_), channel_id=1, source_target_pairs={{0,2},{1,3},{2,0},{3,1},{4,6},{5,7},{6,4},{7,5},{8,10},{9,11},{10,... | collective-permute-start | bytes 811016 | tf_op jit(solution)/shard_map/ppermute | solution.py:11
  14.7 21.4 %collective-permute-start.5 = (bf16[1056,128]{1,0:T(8,128)(2,1)S(1)}, bf16[1056,128]{1,0:T(8,128)(2,1)S(1)}, u32[]{:S(2)}, u32[]{:S(2)}) collective-permute-start(bf16[1056,128]{1,0:T(8,128)(2,1)S(1)} %get-tuple-element.29), channel_id=1, source_target_pairs={{0,3},{1,2},{2,1},{3,0},{4,7},{5,6},{6,5},{7,4},{8,11},{9,10},{10,... | collective-permute-start | bytes 811016 | tf_op jit(solution)/shard_map/ppermute | solution.py:11
  19.9 26.9 %collective-permute-start.15 = (bf16[2,576,128]{2,1,0:T(8,128)(2,1)S(1)}, bf16[2,576,128]{2,1,0:T(8,128)(2,1)S(1)}, u32[]{:S(2)}, u32[]{:S(2)}) collective-permute-start(bf16[2,576,128]{2,1,0:T(8,128)(2,1)S(1)} %pad_maximum_fusion.3), channel_id=1, source_target_pairs={{0,16},{4,20},{8,24},{12,28},{16,0},{20,4},{24,8},{28,12},{1,17},{... | collective-permute-start | bytes 884744 | tf_op jit(solution)/shard_map/ppermute | solution.py:11
  22.4 29.5 %collective-permute-start.12 = (bf16[2,576,128]{2,1,0:T(8,128)(2,1)S(1)}, bf16[2,576,128]{2,1,0:T(8,128)(2,1)S(1)}, u32[]{:S(2)}, u32[]{:S(2)}) collective-permute-start(bf16[2,576,128]{2,1,0:T(8,128)(2,1)S(1)} %pad_maximum_fusion.2), channel_id=1, source_target_pairs={{0,8},{4,12},{8,0},{12,4},{16,24},{20,28},{24,16},{28,20},{1,9},{5... | collective-permute-start | bytes 884744 | tf_op jit(solution)/shard_map/ppermute | solution.py:11
  23.2 51.7 %collective-permute-start.1 = (bf16[1056,128]{1,0:T(8,128)(2,1)S(1)}, bf16[1056,128]{1,0:T(8,128)(2,1)S(1)}, u32[]{:S(2)}, u32[]{:S(2)}) collective-permute-start(bf16[1056,128]{1,0:T(8,128)(2,1)S(1)} %get-tuple-element.33), channel_id=1, source_target_pairs={{0,1},{1,0},{2,3},{3,2},{4,5},{5,4},{6,7},{7,6},{8,9},{9,8},{10,11... | collective-permute-start | bytes 811016 | tf_op jit(solution)/shard_map/ppermute | solution.py:11
  30.9 44.0 %collective-permute-start.3 = (bf16[1056,128]{1,0:T(8,128)(2,1)S(1)}, bf16[1056,128]{1,0:T(8,128)(2,1)S(1)}, u32[]{:S(2)}, u32[]{:S(2)}) collective-permute-start(bf16[1056,128]{1,0:T(8,128)(2,1)S(1)} %get-tuple-element.33), channel_id=1, source_target_pairs={{0,3},{1,2},{2,1},{3,0},{4,7},{5,6},{6,5},{7,4},{8,11},{9,10},{10,... | collective-permute-start | bytes 811016 | tf_op jit(solution)/shard_map/ppermute | solution.py:11
  36.1 38.8 %collective-permute-start.2 = (bf16[1056,128]{1,0:T(8,128)(2,1)S(1)}, bf16[1056,128]{1,0:T(8,128)(2,1)S(1)}, u32[]{:S(2)}, u32[]{:S(2)}) collective-permute-start(bf16[1056,128]{1,0:T(8,128)(2,1)S(1)} %get-tuple-element.47.refs_0_), channel_id=1, source_target_pairs={{0,2},{1,3},{2,0},{3,1},{4,6},{5,7},{6,4},{7,5},{8,10},{9,11},{10,... | collective-permute-start | bytes 811016 | tf_op jit(solution)/shard_map/ppermute | solution.py:11
  46.8 6.7 %collective-permute-start.16 = (bf16[4,576,128]{2,1,0:T(8,128)(2,1)S(1)}, bf16[4,576,128]{2,1,0:T(8,128)(2,1)S(1)}, u32[]{:S(2)}, u32[]{:S(2)}) collective-permute-start(bf16[4,576,128]{2,1,0:T(8,128)(2,1)S(1)} %pad_maximum_fusion.1.refs_4_), channel_id=1, source_target_pairs={{0,4},{4,0},{8,12},{12,8},{16,20},{20,16},{24,28},{28,24},{1,5},{5... | collective-permute-start | bytes 1769480 | tf_op jit(solution)/shard_map/ppermute | solution.py:11
  52.0 6.9 %copy-start = (bf16[9,512,128]{2,1,0:T(8,128)(2,1)S(1)}, bf16[9,512,128]{2,1,0:T(8,128)(2,1)}, u32[]{:S(2)}) copy-start(bf16[9,512,128]{2,1,0:T(8,128)(2,1)} %refs_1_.1) | copy-start | bytes 3538948
  52.0 4.9 %collective-permute-start.13 = (bf16[4,576,128]{2,1,0:T(8,128)(2,1)S(1)}, bf16[4,576,128]{2,1,0:T(8,128)(2,1)S(1)}, u32[]{:S(2)}, u32[]{:S(2)}) collective-permute-start(bf16[4,576,128]{2,1,0:T(8,128)(2,1)S(1)} %pad_maximum_fusion.refs_2_), channel_id=1, source_target_pairs={{0,4},{4,0},{8,12},{12,8},{16,20},{20,16},{24,28},{28,24},{1,5},{5... | collective-permute-start | bytes 1769480 | tf_op jit(solution)/shard_map/ppermute | solution.py:11
  53.6 12.6 %collective-permute-start.6 = (bf16[2112,128]{1,0:T(8,128)(2,1)S(1)}, bf16[2112,128]{1,0:T(8,128)(2,1)S(1)}, u32[]{:S(2)}, u32[]{:S(2)}) collective-permute-start(bf16[2112,128]{1,0:T(8,128)(2,1)S(1)} %get-tuple-element.39), channel_id=1, source_target_pairs={{0,4},{4,8},{8,12},{12,16},{16,20},{20,24},{24,28},{1,5},{5,9},{9,... | collective-permute-start | bytes 1622024 | tf_op jit(solution)/shard_map/ppermute | solution.py:18
  56.9 14.8 %collective-permute-start.7 = (bf16[2112,128]{1,0:T(8,128)(2,1)S(1)}, bf16[2112,128]{1,0:T(8,128)(2,1)S(1)}, u32[]{:S(2)}, u32[]{:S(2)}) collective-permute-start(bf16[2112,128]{1,0:T(8,128)(2,1)S(1)} %get-tuple-element.40), channel_id=1, source_target_pairs={{4,0},{8,4},{12,8},{16,12},{20,16},{24,20},{28,24},{5,1},{9,5},{13... | collective-permute-start | bytes 1622024 | tf_op jit(solution)/shard_map/ppermute | solution.py:18
  76.6 8.5 %collective-permute-start.17 = (bf16[1024,128]{1,0:T(8,128)(2,1)S(1)}, bf16[1024,128]{1,0:T(8,128)(2,1)S(1)}, u32[]{:S(2)}, u32[]{:S(2)}) collective-permute-start(bf16[1024,128]{1,0:T(8,128)(2,1)S(1)} %get-tuple-element.53), channel_id=1, source_target_pairs={{0,1},{1,0},{2,3},{3,2},{4,5},{5,4},{6,7},{7,6},{8,9},{9,8},{10,11... | collective-permute-start | bytes 786440 | tf_op jit(solution)/shard_map/ppermute | solution.py:11
  78.2 10.2 %collective-permute-start.18 = (bf16[1024,128]{1,0:T(8,128)(2,1)S(1)}, bf16[1024,128]{1,0:T(8,128)(2,1)S(1)}, u32[]{:S(2)}, u32[]{:S(2)}) collective-permute-start(bf16[1024,128]{1,0:T(8,128)(2,1)S(1)} %get-tuple-element.55), channel_id=1, source_target_pairs={{0,1},{1,0},{2,3},{3,2},{4,5},{5,4},{6,7},{7,6},{8,9},{9,8},{10,11... | collective-permute-start | bytes 786440 | tf_op jit(solution)/shard_map/ppermute | solution.py:11

commit v12 on v11

--- a/solution.py
+++ b/solution.py
@@ -243,7 +243,7 @@
     row = size // 2
     local = mine.shape[1]
     pitch = row + 8
-    fill(source, [[(p, (2 * which + r) * pitch) for p in inners] for r in range(2)])
+    fill(source, [[(p, r * pitch) for p in inners] for r in range(2)])
     top = middle = bottom = None
     for across in range(3):
         terms = [
@@ -294,7 +294,7 @@
 
 def exchange(mine, other, near=None):
     sent = {1: other if near is None else near, 2: mine, 3: other}
-    held = {k: swap(sent[k], "chan", k) for k in (2, 3, 1)}
+    held = {k: swap(sent[k], "chan", k) for k in (1, 2, 3)}
     return [mine, held[1], held[2], held[3]]
 
 
@@ -318,23 +318,36 @@
     return steps
 
 
-def home_kernel(place, mine, other, out):
-    width = mine.shape[2]
-    side = place[0] & 1
-    for t in range(2):
-
-        @pl.when(side == t)
-        def _():
-            out[:, :, t * width : (t + 1) * width] = mine[...]
-            out[:, :, (1 - t) * width : (2 - t) * width] = other[...]
+def place_kernel(slot, piece, *refs):
+    refs[-1][...] = piece[...]
+
+
+def put(slot, piece, whole, cols):
+    channels, rows, width = piece.shape
+    block = pl.BlockSpec((channels, rows, width), lambda i, slot: (0, 0, 0))
+    spot = pl.BlockSpec((channels, rows, width), lambda i, slot: (0, 0, slot[0]))
+    return pl.pallas_call(
+        place_kernel,
+        out_shape=jax.ShapeDtypeStruct((channels, rows, cols), jnp.bfloat16),
+        grid_spec=pltpu.PrefetchScalarGridSpec(
+            num_scalar_prefetch=1,
+            grid=(1,),
+            in_specs=[block] + [ANY] * len(whole),
+            out_specs=spot,
+        ),
+        input_output_aliases={2: 0} if whole else {},
+        cost_estimate=cost(0),
+        name="put",
+    )(slot, piece, *whole)
 
 
 def home(place, mine, other, rows):
-    turn = lambda p: jnp.transpose(p.reshape(rows, -1, p.shape[1]), (2, 0, 1))
-    mine, other = turn(mine), turn(other)
-    channels, rows, width = mine.shape
-    shape = (channels, rows, 2 * width)
-    return kernel(home_kernel, [shape], [place, mine, other], [], "home", True)[0]
+    side = place[:1] & 1
+    mine, other = [
+        jnp.transpose(p.reshape(rows, -1, p.shape[1]), (2, 0, 1)) for p in (mine, other)
+    ]
+    cols = 2 * mine.shape[2]
+    return put(1 - side, other, [put(side, mine, [], cols)], cols)
 
 
 def token_kernel(*refs):
@@ -367,18 +380,22 @@
 
     upstream, image = [jnp.transpose(v, (1, 2, 0)) for v in (upstream, image)]
     parts = [(i, r) for i in range(2) for r in (0, rows - 1)]
-    sent = cut(place, [upstream, image], bias[None], parts, 25)
-    (near, across) = after((near, across), sent)
+    sent = cut(place, [upstream, image], bias[None], parts, 6)
     pieces = exchange(*sent)
-    parts = [(i, r) for i in range(2) for r in range(1, rows - 1)]
-    sent = cut(place, after([upstream, image], pieces[1]), bias[None], parts, 25)
+    inner = [[(i, r) for r in range(1, rows - 1)] for i in range(2)]
+    sent = cut(place, after([upstream, image], pieces[3]), bias[None], inner[0], 25)
     pieces = after(pieces, sent)
-    inners = exchange(*sent)
+    first = exchange(*sent)
+    sent = cut(place, after([upstream, image], first[1:]), bias[None], inner[1], 18)
+    first = after(first, sent)
+    second = exchange(*sent)
 
     steps = halving(bands)[:-1]
     near, near_order = gather(near, steps)
     across, across_order = gather(across, steps[::-1])
-    held = [near, swap(near, "band", 1), across, swap(across, "band", 1)]
+    near, across = after((near, across), pieces[1])
+    there = swap(jnp.concatenate([near, across], axis=1), "band", 1)
+    held = [near, there[:, : near.shape[1]], across, there[:, near.shape[1] :]]
     filters = kernel(
         lambda *refs: assemble_kernel((near_order, across_order), *refs),
         [(taps * outs, 2 * local), (taps * 2 * local, 2 * local)],
@@ -386,11 +403,12 @@
         [],
         "assemble",
         True,
-        9,
+        2,
     )
     pitch = width + 8
     body = lambda *refs: rim_kernel(pitch, *refs)
-    rims = neighbours(*kernel(body, [(8 * pitch, local)] * 2, pieces, [], "rim", False, 40))
+    packed = kernel(body, [(8 * pitch, local)] * 2, pieces, [], "rim", False, 0)
+    rims = neighbours(*packed)
 
     size = rows * width
     totals = kernel(
@@ -400,24 +418,26 @@
         [(3, size, 4 * local)] * 2,
         "outer",
         False,
-        6,
+        2,
         jnp.float32,
     )
     lines = jnp.concatenate([p[width + 2 : width + 3] for p in pieces[:2]]).astype(jnp.float32)
-    inners = after(inners, totals)
-    mark = [token(inners, 0)]
+    marks = [[], []]
+    marks[0].append(token(first, 2))
     kept, came = [], []
     for which in range(2):
         mine, other = kernel(
             lambda *refs: inner_kernel(which, *refs),
             [(size, local)] * 2,
-            [*inners, totals[which], *filters, lines, *mark],
+            [*(first, second)[which], totals[which], *filters, lines, *marks[which]],
             [(3, size // 2, 4 * local)],
             "inner",
             False,
             9,
         )
         kept.append(mine)
+        if not which:
+            second = after(second, mine)
         came.append(swap(other, "chan", 1))
     image_grad = home(place, kept[0], came[0], rows)
     kept[1] = after(kept[1], image_grad)

time: 90.2 us -> 81.3 us (0.901)
  the two profiles are of different devices: /device:TPU:3 before, /device:TPU:0 now
where the time goes in v12:
time: 81.3 us; the launch traced here: 81 us
  waiting for transfers between devices  28.9 us (36%)
  starting transfers between devices  28.1 us (35%)
  Pallas kernels  16.3 us (20%)
  local copies, waits for them, and re-layouts  6.45 us (8%)
  between operations  0.91 us (1%)
    ppermute x19, waiting for transfers between devices, swap(): return lax.ppermute(value, axis, [(j, j ^ step) for j in range(size)])  28.9 us
    ppermute x19, starting transfers between devices, swap(): return lax.ppermute(value, axis, [(j, j ^ step) for j in range(size)])  25.5 us
    pallas_call x9, Pallas kernels, kernel(): pl.pallas_call(body, out_shape=[jax.ShapeDtypeStruct(s, kind) for s in sh...  9.63 us
    pallas_call x4, Pallas kernels, put(): pl.pallas_call(place_kernel, out_shape=jax.ShapeDtypeStruct((channels, ro...  6.67 us
    reshape x4, local copies, waits for them, and re-layouts, home(): p.reshape(rows, -1, p.shape[1])  3.51 us
    ppermute x2, starting transfers between devices, neighbours(): return (lax.ppermute(last, 'band', up), lax.ppermute(first, 'band', down))  2.59 us
    unnamed x8, local copies, waits for them, and re-layouts  1.89 us
  transfers between devices with their start and end apart: 21, of which 7 were waited for; matrix products, arithmetic and copies ran while one was open for 6% of the time, Pallas kernels for 18%

profile of v12, /device:TPU:0, one launch (start us, length us, event | category | flops | bytes accessed | tf_op | source)
XLA Modules:
  0.0 81.0 jit_solution(13676455805833588168)
XLA Ops:
  0.7 1.0 %constant_dynamic-slice_fusion = bf16[9,32,128]{2,1,0:T(8,128)(2,1)S(1)} fusion(bf16[9,512,128]{2,1,0:T(8,128)(2,1)} %refs_1_.1, s32[]{:T(128)S(6)} %select_n.7), kind=kLoop, calls=%fused_computation.8 | loop fusion | bytes 147460 | tf_op jit(solution)/shard_map/dynamic_slice | solution.py:377
  1.6 4.0 %collective-permute-start.14 = (bf16[288,128]{1,0:T(8,128)(2,1)S(1)}, bf16[288,128]{1,0:T(8,128)(2,1)S(1)}, u32[]{:S(2)}, u32[]{:S(2)}) collective-permute-start(bf16[288,128]{1,0:T(8,128)(2,1)S(1)} %bitcast.39), channel_id=1, source_target_pairs={{0,2},{1,3},{2,0},{3,1},{4,6},{5,7},{6,4},{7,5},{8,10},{9,11},{10,... | collective-permute-start | bytes 221192 | tf_op jit(solution)/shard_map/ppermute | solution.py:11
  5.6 1.3 %collective-permute-start.15 = (bf16[288,128]{1,0:T(8,128)(2,1)S(1)}, bf16[288,128]{1,0:T(8,128)(2,1)S(1)}, u32[]{:S(2)}, u32[]{:S(2)}) collective-permute-start(bf16[288,128]{1,0:T(8,128)(2,1)S(1)} %bitcast.40), channel_id=1, source_target_pairs={{0,3},{1,2},{2,1},{3,0},{4,7},{5,6},{6,5},{7,4},{8,11},{9,10},{10,... | collective-permute-start | bytes 221192 | tf_op jit(solution)/shard_map/ppermute | solution.py:11
  7.0 1.5 %copy.8 = bf16[128,4,512]{0,2,1:T(8,128)(2,1)S(1)} copy(bf16[128,4,512]{2,1,0:T(4,128)(2,1)} %param.7) | data formatting | bytes 1048576 | tf_op args[3]
  8.5 0.4 copy.9
  8.9 0.1 pad_add_fusion.refs_0_
  9.0 0.7 cut.3
  9.7 2.5 %collective-permute-start = (bf16[1056,128]{1,0:T(8,128)(2,1)S(1)}, bf16[1056,128]{1,0:T(8,128)(2,1)S(1)}, u32[]{:S(2)}, u32[]{:S(2)}) collective-permute-start(bf16[1056,128]{1,0:T(8,128)(2,1)S(1)} %get-tuple-element.37), channel_id=1, source_target_pairs={{0,3},{1,2},{2,1},{3,0},{4,7},{5,6},{6,5},{7,4},{8,11},{9,10},{10,... | collective-permute-start | bytes 811016 | tf_op jit(solution)/shard_map/ppermute | solution.py:11
  12.2 0.1 collective-permute-start.11
  12.3 0.0 collective-permute-done.14
  12.3 0.0 collective-permute-done.15
  12.3 1.6 %collective-permute-start.16 = (bf16[1,576,128]{2,1,0:T(8,128)(2,1)S(1)}, bf16[1,576,128]{2,1,0:T(8,128)(2,1)S(1)}, u32[]{:S(2)}, u32[]{:S(2)}) collective-permute-start(bf16[1,576,128]{2,1,0:T(8,128)(2,1)S(1)} %maximum_bitcast_fusion), channel_id=1, source_target_pairs={{0,8},{4,12},{8,0},{12,4},{16,24},{20,28},{24,16},{28,20},{1,9},{5... | collective-permute-start | bytes 442376 | tf_op jit(solution)/shard_map/ppermute | solution.py:11
  13.9 8.6 %collective-permute-done.11 = bf16[576,128]{1,0:T(8,128)(2,1)S(1)} collective-permute-done((bf16[576,128]{1,0:T(8,128)(2,1)S(1)}, bf16[576,128]{1,0:T(8,128)(2,1)S(1)}, u32[]{:S(2)}, u32[]{:S(2)}) %collective-permute-start.11) | collective-permute-done | bytes 147488 | tf_op jit(solution)/shard_map/ppermute | solution.py:11
  22.5 1.5 %collective-permute-start.12 = (bf16[1,576,128]{2,1,0:T(8,128)(2,1)S(1)}, bf16[1,576,128]{2,1,0:T(8,128)(2,1)S(1)}, u32[]{:S(2)}, u32[]{:S(2)}) collective-permute-start(bf16[1,576,128]{2,1,0:T(8,128)(2,1)S(1)} %bitcast.33), channel_id=1, source_target_pairs={{0,16},{4,20},{8,24},{12,28},{16,0},{20,4},{24,8},{28,12},{1,17},{... | collective-permute-start | bytes 442376 | tf_op jit(solution)/shard_map/ppermute | solution.py:11
  24.0 0.6 collective-permute-start.7
  24.6 1.7 %collective-permute-start.8 = (bf16[1056,128]{1,0:T(8,128)(2,1)S(1)}, bf16[1056,128]{1,0:T(8,128)(2,1)S(1)}, u32[]{:S(2)}, u32[]{:S(2)}) collective-permute-start(bf16[1056,128]{1,0:T(8,128)(2,1)S(1)} %get-tuple-element.51.refs_0_), channel_id=1, source_target_pairs={{0,2},{1,3},{2,0},{3,1},{4,6},{5,7},{6,4},{7,5},{8,10},{9,11},{10,... | collective-permute-start | bytes 811016 | tf_op jit(solution)/shard_map/ppermute | solution.py:11
  26.3 0.0 collective-permute-done.16
  26.3 0.6 collective-permute-start.17
  26.9 0.0 collective-permute-done.refs_3_
  26.9 2.1 %collective-permute-done.12 = bf16[1,576,128]{2,1,0:T(8,128)(2,1)S(1)} collective-permute-done((bf16[1,576,128]{2,1,0:T(8,128)(2,1)S(1)}, bf16[1,576,128]{2,1,0:T(8,128)(2,1)S(1)}, u32[]{:S(2)}, u32[]{:S(2)}) %collective-permute-start.12) | collective-permute-done | bytes 147488 | tf_op jit(solution)/shard_map/ppermute | solution.py:11
  29.1 1.6 %collective-permute-start.13 = (bf16[2,576,128]{2,1,0:T(8,128)(2,1)S(1)}, bf16[2,576,128]{2,1,0:T(8,128)(2,1)S(1)}, u32[]{:S(2)}, u32[]{:S(2)}) collective-permute-start(bf16[2,576,128]{2,1,0:T(8,128)(2,1)S(1)} %pad_maximum_fusion.3), channel_id=1, source_target_pairs={{0,8},{4,12},{8,0},{12,4},{16,24},{20,28},{24,16},{28,20},{1,9},{5... | collective-permute-start | bytes 884744 | tf_op jit(solution)/shard_map/ppermute | solution.py:11
  30.6 0.6 cut.4
  31.2 0.1 collective-permute-start.1
  31.3 7.4 %collective-permute-done.7.refs_1_ = bf16[1056,128]{1,0:T(8,128)(2,1)S(1)} collective-permute-done((bf16[1056,128]{1,0:T(8,128)(2,1)S(1)}, bf16[1056,128]{1,0:T(8,128)(2,1)S(1)}, u32[]{:S(2)}, u32[]{:S(2)}) %collective-permute-start.7) | collective-permute-done | bytes 270368 | tf_op jit(solution)/shard_map/ppermute | solution.py:11
  38.7 0.0 collective-permute-start.2
  38.7 1.2 %collective-permute-done.8.refs_2_ = bf16[1056,128]{1,0:T(8,128)(2,1)S(1)} collective-permute-done((bf16[1056,128]{1,0:T(8,128)(2,1)S(1)}, bf16[1056,128]{1,0:T(8,128)(2,1)S(1)}, u32[]{:S(2)}, u32[]{:S(2)}) %collective-permute-start.8) | collective-permute-done | bytes 270368 | tf_op jit(solution)/shard_map/ppermute | solution.py:11
  39.9 0.6 collective-permute-start.3
  40.5 0.1 rim.1
  40.6 2.4 %collective-permute-done.1.refs_1_ = bf16[528,128]{1,0:T(8,128)(2,1)S(1)} collective-permute-done((bf16[528,128]{1,0:T(8,128)(2,1)S(1)}, bf16[528,128]{1,0:T(8,128)(2,1)S(1)}, u32[]{:S(2)}, u32[]{:S(2)}) %collective-permute-start.1) | collective-permute-done | bytes 135200 | tf_op jit(solution)/shard_map/ppermute | solution.py:11
  43.0 1.3 %collective-permute-start.10 = (bf16[2112,128]{1,0:T(8,128)(2,1)S(1)}, bf16[2112,128]{1,0:T(8,128)(2,1)S(1)}, u32[]{:S(2)}, u32[]{:S(2)}) collective-permute-start(bf16[2112,128]{1,0:T(8,128)(2,1)S(1)} %get-tuple-element.56), channel_id=1, source_target_pairs={{4,0},{8,4},{12,8},{16,12},{20,16},{24,20},{28,24},{5,1},{9,5},{13... | collective-permute-start | bytes 1622024 | tf_op jit(solution)/shard_map/ppermute | solution.py:18
  44.2 4.6 %collective-permute-done.2.refs_2_ = bf16[528,128]{1,0:T(8,128)(2,1)S(1)} collective-permute-done((bf16[528,128]{1,0:T(8,128)(2,1)S(1)}, bf16[528,128]{1,0:T(8,128)(2,1)S(1)}, u32[]{:S(2)}, u32[]{:S(2)}) %collective-permute-start.2) | collective-permute-done | bytes 135200 | tf_op jit(solution)/shard_map/ppermute | solution.py:11
  48.8 1.3 %collective-permute-start.9 = (bf16[2112,128]{1,0:T(8,128)(2,1)S(1)}, bf16[2112,128]{1,0:T(8,128)(2,1)S(1)}, u32[]{:S(2)}, u32[]{:S(2)}) collective-permute-start(bf16[2112,128]{1,0:T(8,128)(2,1)S(1)} %get-tuple-element.55), channel_id=1, source_target_pairs={{0,4},{4,8},{8,12},{12,16},{16,20},{20,24},{24,28},{1,5},{5,9},{9,... | collective-permute-start | bytes 1622024 | tf_op jit(solution)/shard_map/ppermute | solution.py:18
  50.2 0.0 collective-permute-done.3.refs_3_
  50.2 0.0 collective-permute-done.17
  50.2 0.1 pad_maximum_fusion.2.refs_4_
  50.2 0.0 collective-permute-done.13
  50.3 0.1 pad_maximum_fusion.1.refs_2_
  50.3 0.1 pad_maximum_fusion
  50.4 2.3 %collective-permute-start.18 = (bf16[4,1152,128]{2,1,0:T(8,128)(2,1)S(1)}, bf16[4,1152,128]{2,1,0:T(8,128)(2,1)S(1)}, u32[]{:S(2)}, u32[]{:S(2)}) collective-permute-start(bf16[4,1152,128]{2,1,0:T(8,128)(2,1)S(1)} %pad_maximum_fusion), channel_id=1, source_target_pairs={{0,4},{4,0},{8,12},{12,8},{16,20},{20,16},{24,28},{28,24},{1,5},{5... | collective-permute-start | bytes 3538952 | tf_op jit(solution)/shard_map/ppermute | solution.py:11
  52.7 0.6 cut.5
  53.3 0.1 collective-permute-start.4
  53.4 3.0 %collective-permute-start.5 = (bf16[528,128]{1,0:T(8,128)(2,1)S(1)}, bf16[528,128]{1,0:T(8,128)(2,1)S(1)}, u32[]{:S(2)}, u32[]{:S(2)}) collective-permute-start(bf16[528,128]{1,0:T(8,128)(2,1)S(1)} %get-tuple-element.63.refs_0_), channel_id=1, source_target_pairs={{0,2},{1,3},{2,0},{3,1},{4,6},{5,7},{6,4},{7,5},{8,10},{9,11},{10,... | collective-permute-start | bytes 405512 | tf_op jit(solution)/shard_map/ppermute | solution.py:11
  56.4 0.0 collective-permute-done.18
  56.4 1.4 %collective-permute-start.6 = (bf16[528,128]{1,0:T(8,128)(2,1)S(1)}, bf16[528,128]{1,0:T(8,128)(2,1)S(1)}, u32[]{:S(2)}, u32[]{:S(2)}) collective-permute-start(bf16[528,128]{1,0:T(8,128)(2,1)S(1)} %get-tuple-element.45), channel_id=1, source_target_pairs={{0,3},{1,2},{2,1},{3,0},{4,7},{5,6},{6,5},{7,4},{8,11},{9,10},{10,... | collective-permute-start | bytes 405512 | tf_op jit(solution)/shard_map/ppermute | solution.py:11
  57.8 0.1 fusion
  57.8 1.3 %assemble.1 = (bf16[4608,256]{1,0:T(8,128)(2,1)S(1)}, bf16[2304,256]{1,0:T(8,128)(2,1)S(1)}) custom-call(s32[2]{0:T(128)S(1)} %pad_add_fusion.refs_0_, bf16[9,512,128]{2,1,0:T(8,128)(2,1)S(1)} %copy-done, bf16[4,576,128]{2,1,0:T(8,128)(2,1)S(1)} %pad_maximum_fusion.1.refs_2_, bf16[4,576,128]{2,1,0:T(8,128)(2,1)S(1)} %get-tuple-element.73.refs_3_, ...), custom_call_target="tpu_custom_call" | custom-call | flops 2001048576 | bytes 1048576 | tf_op jit(solution)/shard_map/assemble/pallas_call | solution.py:276
  59.1 0.0 collective-permute-done.10.refs_5_
  59.1 0.0 collective-permute-done.9.refs_4_
  59.1 3.1 %outer.1 = (f32[1024,256]{1,0:T(8,128)S(1)}, f32[1024,256]{1,0:T(8,128)S(1)}) custom-call(bf16[1056,128]{1,0:T(8,128)(2,1)S(1)} %get-tuple-element.51.refs_0_, bf16[1056,128]{1,0:T(8,128)(2,1)S(1)} %collective-permute-done.7.refs_1_, bf16[1056,128]{1,0:T(8,128)(2,1)S(1)} %collective-permute-done.8.refs_2_, ...), custom_call_target="tpu_custom_call" | custom-call | flops 2001048576 | bytes 1048576 | tf_op jit(solution)/shard_map/outer/pallas_call | solution.py:276
  62.3 1.7 %inner.2 = (bf16[1024,128]{1,0:T(8,128)(2,1)S(1)}, bf16[1024,128]{1,0:T(8,128)(2,1)S(1)}) custom-call(bf16[528,128]{1,0:T(8,128)(2,1)S(1)} %get-tuple-element.46.refs_0_, bf16[528,128]{1,0:T(8,128)(2,1)S(1)} %collective-permute-done.1.refs_1_, bf16[528,128]{1,0:T(8,128)(2,1)S(1)} %collective-permute-done.2.refs_2_, ...), custom_call_target="tpu_custom_call" | custom-call | flops 9001048064 | bytes 1048576 | tf_op jit(solution)/shard_map/inner/pallas_call | solution.py:276
  64.0 0.1 collective-permute-start.20
  64.1 2.6 %collective-permute-done.5.refs_2_ = bf16[528,128]{1,0:T(8,128)(2,1)S(1)} collective-permute-done((bf16[528,128]{1,0:T(8,128)(2,1)S(1)}, bf16[528,128]{1,0:T(8,128)(2,1)S(1)}, u32[]{:S(2)}, u32[]{:S(2)}) %collective-permute-start.5) | collective-permute-done | bytes 135200 | tf_op jit(solution)/shard_map/ppermute | solution.py:11
  66.7 0.0 collective-permute-done.6.refs_3_
  66.7 1.5 %inner.3 = (bf16[1024,128]{1,0:T(8,128)(2,1)S(1)}, bf16[1024,128]{1,0:T(8,128)(2,1)S(1)}) custom-call(bf16[528,128]{1,0:T(8,128)(2,1)S(1)} %get-tuple-element.63.refs_0_, bf16[528,128]{1,0:T(8,128)(2,1)S(1)} %collective-permute-done.4.refs_1_, bf16[528,128]{1,0:T(8,128)(2,1)S(1)} %collective-permute-done.5.refs_2_, ...), custom_call_target="tpu_custom_call" | custom-call | flops 9001048064 | bytes 1048576 | tf_op jit(solution)/shard_map/inner/pallas_call | solution.py:276
  68.2 2.6 %collective-permute-start.19 = (bf16[1024,128]{1,0:T(8,128)(2,1)S(1)}, bf16[1024,128]{1,0:T(8,128)(2,1)S(1)}, u32[]{:S(2)}, u32[]{:S(2)}) collective-permute-start(bf16[1024,128]{1,0:T(8,128)(2,1)S(1)} %get-tuple-element.68), channel_id=1, source_target_pairs={{0,1},{1,0},{2,3},{3,2},{4,5},{5,4},{6,7},{7,6},{8,9},{9,8},{10,11... | collective-permute-start | bytes 786440 | tf_op jit(solution)/shard_map/ppermute | solution.py:11
  70.8 0.9 %copy.16 = bf16[4,256,128]{1,0,2:T(4,128)(2,1)} copy(bf16[4,256,128]{2,1,0:T(8,128)(2,1)S(1)} %bitcast.24) | data formatting | bytes 524288 | tf_op jit(solution)/shard_map/reshape | solution.py:347
  71.7 1.7 %put.4.refs_0_ = bf16[128,4,512]{2,1,0:T(4,128)(2,1)} custom-call(s32[1]{0:T(128)S(6)} %and.6.slot, bf16[128,4,256]{2,1,0:T(4,128)(2,1)} %bitcast.32), custom_call_target="tpu_custom_call" | custom-call | flops 1048576 | bytes 1048576 | tf_op jit(solution)/shard_map/put/pallas_call | solution.py:329
  73.3 0.9 %copy.15 = bf16[4,256,128]{1,0,2:T(4,128)(2,1)} copy(bf16[4,256,128]{2,1,0:T(8,128)(2,1)S(1)} %bitcast.36) | data formatting | bytes 524288 | tf_op jit(solution)/shard_map/reshape | solution.py:347
  74.2 1.7 %put.5 = bf16[128,4,512]{2,1,0:T(4,128)(2,1)} custom-call(s32[1]{0:T(128)S(6)} %sub.7.slot, bf16[128,4,256]{2,1,0:T(4,128)(2,1)} %bitcast.30, bf16[128,4,512]{2,1,0:T(4,128)(2,1)} %put.4.refs_0_), custom_call_target="tpu_custom_call", output_to_operand_aliasing={{}: (2, {})} | custom-call | flops 1048576 | bytes 1048576 | tf_op jit(solution)/shard_map/put/pallas_call | solution.py:329
  75.9 0.9 %copy.17 = bf16[4,256,128]{1,0,2:T(4,128)(2,1)} copy(bf16[4,256,128]{2,1,0:T(8,128)(2,1)S(1)} %bitcast.25) | data formatting | bytes 524288 | tf_op jit(solution)/shard_map/reshape | solution.py:347
  76.8 1.7 %put.6.refs_0_ = bf16[128,4,512]{2,1,0:T(4,128)(2,1)} custom-call(s32[1]{0:T(128)S(6)} %and.6.slot, bf16[128,4,256]{2,1,0:T(4,128)(2,1)} %bitcast.31), custom_call_target="tpu_custom_call" | custom-call | flops 1048576 | bytes 1048576 | tf_op jit(solution)/shard_map/put/pallas_call | solution.py:329
  78.4 0.0 collective-permute-done.19
  78.4 0.9 %copy.14 = bf16[4,256,128]{1,0,2:T(4,128)(2,1)} copy(bf16[4,256,128]{2,1,0:T(8,128)(2,1)S(1)} %bitcast.37) | data formatting | bytes 524288 | tf_op jit(solution)/shard_map/reshape | solution.py:347
  79.3 1.7 %put.7 = bf16[128,4,512]{2,1,0:T(4,128)(2,1)} custom-call(s32[1]{0:T(128)S(6)} %sub.7.slot, bf16[128,4,256]{2,1,0:T(4,128)(2,1)} %bitcast.29, bf16[128,4,512]{2,1,0:T(4,128)(2,1)} %put.6.refs_0_), custom_call_target="tpu_custom_call", output_to_operand_aliasing={{}: (2, {})} | custom-call | flops 1048576 | bytes 1048576 | tf_op jit(solution)/shard_map/put/pallas_call | solution.py:329
  (16 shorter events, 0.1 us)
Async XLA Ops:
  0.6 7.8 %copy-start.2 = (bf16[128,4,512]{2,1,0:T(4,128)(2,1)S(1)}, bf16[128,4,512]{2,1,0:T(4,128)(2,1)}, u32[]{:S(2)}) copy-start(bf16[128,4,512]{2,1,0:T(4,128)(2,1)} %param.4) | copy-start | bytes 1572868
  0.6 8.3 %copy-start.1 = (bf16[128]{0:T(256)(128)(2,1)S(1)}, bf16[128]{0:T(256)(128)(2,1)}, u32[]{:S(2)}) copy-start(bf16[128]{0:T(256)(128)(2,1)} %param.6) | copy-start | bytes 772
  1.6 10.7 %collective-permute-start.14 = (bf16[288,128]{1,0:T(8,128)(2,1)S(1)}, bf16[288,128]{1,0:T(8,128)(2,1)S(1)}, u32[]{:S(2)}, u32[]{:S(2)}) collective-permute-start(bf16[288,128]{1,0:T(8,128)(2,1)S(1)} %bitcast.39), channel_id=1, source_target_pairs={{0,2},{1,3},{2,0},{3,1},{4,6},{5,7},{6,4},{7,5},{8,10},{9,11},{10,... | collective-permute-start | bytes 221192 | tf_op jit(solution)/shard_map/ppermute | solution.py:11
  5.6 6.7 %collective-permute-start.15 = (bf16[288,128]{1,0:T(8,128)(2,1)S(1)}, bf16[288,128]{1,0:T(8,128)(2,1)S(1)}, u32[]{:S(2)}, u32[]{:S(2)}) collective-permute-start(bf16[288,128]{1,0:T(8,128)(2,1)S(1)} %bitcast.40), channel_id=1, source_target_pairs={{0,3},{1,2},{2,1},{3,0},{4,7},{5,6},{6,5},{7,4},{8,11},{9,10},{10,... | collective-permute-start | bytes 221192 | tf_op jit(solution)/shard_map/ppermute | solution.py:11
  9.0 3.2 %copy-start = (bf16[9,512,128]{2,1,0:T(8,128)(2,1)S(1)}, bf16[9,512,128]{2,1,0:T(8,128)(2,1)}, u32[]{:S(2)}) copy-start(bf16[9,512,128]{2,1,0:T(8,128)(2,1)} %refs_1_.1) | copy-start | bytes 3538948
  9.7 17.2 %collective-permute-start = (bf16[1056,128]{1,0:T(8,128)(2,1)S(1)}, bf16[1056,128]{1,0:T(8,128)(2,1)S(1)}, u32[]{:S(2)}, u32[]{:S(2)}) collective-permute-start(bf16[1056,128]{1,0:T(8,128)(2,1)S(1)} %get-tuple-element.37), channel_id=1, source_target_pairs={{0,3},{1,2},{2,1},{3,0},{4,7},{5,6},{6,5},{7,4},{8,11},{9,10},{10,... | collective-permute-start | bytes 811016 | tf_op jit(solution)/shard_map/ppermute | solution.py:11
  12.2 10.2 %collective-permute-start.11 = (bf16[576,128]{1,0:T(8,128)(2,1)S(1)}, bf16[576,128]{1,0:T(8,128)(2,1)S(1)}, u32[]{:S(2)}, u32[]{:S(2)}) collective-permute-start(bf16[576,128]{1,0:T(8,128)(2,1)S(1)} %bitcast.38), channel_id=1, source_target_pairs={{0,1},{1,0},{2,3},{3,2},{4,5},{5,4},{6,7},{7,6},{8,9},{9,8},{10,11... | collective-permute-start | bytes 442376 | tf_op jit(solution)/shard_map/ppermute | solution.py:11
  12.3 13.9 %collective-permute-start.16 = (bf16[1,576,128]{2,1,0:T(8,128)(2,1)S(1)}, bf16[1,576,128]{2,1,0:T(8,128)(2,1)S(1)}, u32[]{:S(2)}, u32[]{:S(2)}) collective-permute-start(bf16[1,576,128]{2,1,0:T(8,128)(2,1)S(1)} %maximum_bitcast_fusion), channel_id=1, source_target_pairs={{0,8},{4,12},{8,0},{12,4},{16,24},{20,28},{24,16},{28,20},{1,9},{5... | collective-permute-start | bytes 442376 | tf_op jit(solution)/shard_map/ppermute | solution.py:11
  22.5 6.6 %collective-permute-start.12 = (bf16[1,576,128]{2,1,0:T(8,128)(2,1)S(1)}, bf16[1,576,128]{2,1,0:T(8,128)(2,1)S(1)}, u32[]{:S(2)}, u32[]{:S(2)}) collective-permute-start(bf16[1,576,128]{2,1,0:T(8,128)(2,1)S(1)} %bitcast.33), channel_id=1, source_target_pairs={{0,16},{4,20},{8,24},{12,28},{16,0},{20,4},{24,8},{28,12},{1,17},{... | collective-permute-start | bytes 442376 | tf_op jit(solution)/shard_map/ppermute | solution.py:11
  24.0 14.7 %collective-permute-start.7 = (bf16[1056,128]{1,0:T(8,128)(2,1)S(1)}, bf16[1056,128]{1,0:T(8,128)(2,1)S(1)}, u32[]{:S(2)}, u32[]{:S(2)}) collective-permute-start(bf16[1056,128]{1,0:T(8,128)(2,1)S(1)} %get-tuple-element.37), channel_id=1, source_target_pairs={{0,1},{1,0},{2,3},{3,2},{4,5},{5,4},{6,7},{7,6},{8,9},{9,8},{10,11... | collective-permute-start | bytes 811016 | tf_op jit(solution)/shard_map/ppermute | solution.py:11
  24.6 15.3 %collective-permute-start.8 = (bf16[1056,128]{1,0:T(8,128)(2,1)S(1)}, bf16[1056,128]{1,0:T(8,128)(2,1)S(1)}, u32[]{:S(2)}, u32[]{:S(2)}) collective-permute-start(bf16[1056,128]{1,0:T(8,128)(2,1)S(1)} %get-tuple-element.51.refs_0_), channel_id=1, source_target_pairs={{0,2},{1,3},{2,0},{3,1},{4,6},{5,7},{6,4},{7,5},{8,10},{9,11},{10,... | collective-permute-start | bytes 811016 | tf_op jit(solution)/shard_map/ppermute | solution.py:11
  26.3 23.9 %collective-permute-start.17 = (bf16[2,576,128]{2,1,0:T(8,128)(2,1)S(1)}, bf16[2,576,128]{2,1,0:T(8,128)(2,1)S(1)}, u32[]{:S(2)}, u32[]{:S(2)}) collective-permute-start(bf16[2,576,128]{2,1,0:T(8,128)(2,1)S(1)} %pad_maximum_fusion.4), channel_id=1, source_target_pairs={{0,16},{4,20},{8,24},{12,28},{16,0},{20,4},{24,8},{28,12},{1,17},{... | collective-permute-start | bytes 884744 | tf_op jit(solution)/shard_map/ppermute | solution.py:11
  29.1 21.2 %collective-permute-start.13 = (bf16[2,576,128]{2,1,0:T(8,128)(2,1)S(1)}, bf16[2,576,128]{2,1,0:T(8,128)(2,1)S(1)}, u32[]{:S(2)}, u32[]{:S(2)}) collective-permute-start(bf16[2,576,128]{2,1,0:T(8,128)(2,1)S(1)} %pad_maximum_fusion.3), channel_id=1, source_target_pairs={{0,8},{4,12},{8,0},{12,4},{16,24},{20,28},{24,16},{28,20},{1,9},{5... | collective-permute-start | bytes 884744 | tf_op jit(solution)/shard_map/ppermute | solution.py:11
  31.2 11.7 %collective-permute-start.1 = (bf16[528,128]{1,0:T(8,128)(2,1)S(1)}, bf16[528,128]{1,0:T(8,128)(2,1)S(1)}, u32[]{:S(2)}, u32[]{:S(2)}) collective-permute-start(bf16[528,128]{1,0:T(8,128)(2,1)S(1)} %get-tuple-element.40), channel_id=1, source_target_pairs={{0,1},{1,0},{2,3},{3,2},{4,5},{5,4},{6,7},{7,6},{8,9},{9,8},{10,11... | collective-permute-start | bytes 405512 | tf_op jit(solution)/shard_map/ppermute | solution.py:11
  38.7 10.1 %collective-permute-start.2 = (bf16[528,128]{1,0:T(8,128)(2,1)S(1)}, bf16[528,128]{1,0:T(8,128)(2,1)S(1)}, u32[]{:S(2)}, u32[]{:S(2)}) collective-permute-start(bf16[528,128]{1,0:T(8,128)(2,1)S(1)} %get-tuple-element.46.refs_0_), channel_id=1, source_target_pairs={{0,2},{1,3},{2,0},{3,1},{4,6},{5,7},{6,4},{7,5},{8,10},{9,11},{10,... | collective-permute-start | bytes 405512 | tf_op jit(solution)/shard_map/ppermute | solution.py:11
  39.9 10.3 %collective-permute-start.3 = (bf16[528,128]{1,0:T(8,128)(2,1)S(1)}, bf16[528,128]{1,0:T(8,128)(2,1)S(1)}, u32[]{:S(2)}, u32[]{:S(2)}) collective-permute-start(bf16[528,128]{1,0:T(8,128)(2,1)S(1)} %get-tuple-element.40), channel_id=1, source_target_pairs={{0,3},{1,2},{2,1},{3,0},{4,7},{5,6},{6,5},{7,4},{8,11},{9,10},{10,... | collective-permute-start | bytes 405512 | tf_op jit(solution)/shard_map/ppermute | solution.py:11
  43.0 16.2 %collective-permute-start.10 = (bf16[2112,128]{1,0:T(8,128)(2,1)S(1)}, bf16[2112,128]{1,0:T(8,128)(2,1)S(1)}, u32[]{:S(2)}, u32[]{:S(2)}) collective-permute-start(bf16[2112,128]{1,0:T(8,128)(2,1)S(1)} %get-tuple-element.56), channel_id=1, source_target_pairs={{4,0},{8,4},{12,8},{16,12},{20,16},{24,20},{28,24},{5,1},{9,5},{13... | collective-permute-start | bytes 1622024 | tf_op jit(solution)/shard_map/ppermute | solution.py:18
  48.8 10.3 %collective-permute-start.9 = (bf16[2112,128]{1,0:T(8,128)(2,1)S(1)}, bf16[2112,128]{1,0:T(8,128)(2,1)S(1)}, u32[]{:S(2)}, u32[]{:S(2)}) collective-permute-start(bf16[2112,128]{1,0:T(8,128)(2,1)S(1)} %get-tuple-element.55), channel_id=1, source_target_pairs={{0,4},{4,8},{8,12},{12,16},{16,20},{20,24},{24,28},{1,5},{5,9},{9,... | collective-permute-start | bytes 1622024 | tf_op jit(solution)/shard_map/ppermute | solution.py:18
  50.4 6.0 %collective-permute-start.18 = (bf16[4,1152,128]{2,1,0:T(8,128)(2,1)S(1)}, bf16[4,1152,128]{2,1,0:T(8,128)(2,1)S(1)}, u32[]{:S(2)}, u32[]{:S(2)}) collective-permute-start(bf16[4,1152,128]{2,1,0:T(8,128)(2,1)S(1)} %pad_maximum_fusion), channel_id=1, source_target_pairs={{0,4},{4,0},{8,12},{12,8},{16,20},{20,16},{24,28},{28,24},{1,5},{5... | collective-permute-start | bytes 3538952 | tf_op jit(solution)/shard_map/ppermute | solution.py:11
  53.3 10.8 %collective-permute-start.4 = (bf16[528,128]{1,0:T(8,128)(2,1)S(1)}, bf16[528,128]{1,0:T(8,128)(2,1)S(1)}, u32[]{:S(2)}, u32[]{:S(2)}) collective-permute-start(bf16[528,128]{1,0:T(8,128)(2,1)S(1)} %get-tuple-element.45), channel_id=1, source_target_pairs={{0,1},{1,0},{2,3},{3,2},{4,5},{5,4},{6,7},{7,6},{8,9},{9,8},{10,11... | collective-permute-start | bytes 405512 | tf_op jit(solution)/shard_map/ppermute | solution.py:11
  53.4 13.3 %collective-permute-start.5 = (bf16[528,128]{1,0:T(8,128)(2,1)S(1)}, bf16[528,128]{1,0:T(8,128)(2,1)S(1)}, u32[]{:S(2)}, u32[]{:S(2)}) collective-permute-start(bf16[528,128]{1,0:T(8,128)(2,1)S(1)} %get-tuple-element.63.refs_0_), channel_id=1, source_target_pairs={{0,2},{1,3},{2,0},{3,1},{4,6},{5,7},{6,4},{7,5},{8,10},{9,11},{10,... | collective-permute-start | bytes 405512 | tf_op jit(solution)/shard_map/ppermute | solution.py:11
  56.4 10.3 %collective-permute-start.6 = (bf16[528,128]{1,0:T(8,128)(2,1)S(1)}, bf16[528,128]{1,0:T(8,128)(2,1)S(1)}, u32[]{:S(2)}, u32[]{:S(2)}) collective-permute-start(bf16[528,128]{1,0:T(8,128)(2,1)S(1)} %get-tuple-element.45), channel_id=1, source_target_pairs={{0,3},{1,2},{2,1},{3,0},{4,7},{5,6},{6,5},{7,4},{8,11},{9,10},{10,... | collective-permute-start | bytes 405512 | tf_op jit(solution)/shard_map/ppermute | solution.py:11
  64.0 9.4 %collective-permute-start.20 = (bf16[1024,128]{1,0:T(8,128)(2,1)S(1)}, bf16[1024,128]{1,0:T(8,128)(2,1)S(1)}, u32[]{:S(2)}, u32[]{:S(2)}) collective-permute-start(bf16[1024,128]{1,0:T(8,128)(2,1)S(1)} %get-tuple-element.70), channel_id=1, source_target_pairs={{0,1},{1,0},{2,3},{3,2},{4,5},{5,4},{6,7},{7,6},{8,9},{9,8},{10,11... | collective-permute-start | bytes 786440 | tf_op jit(solution)/shard_map/ppermute | solution.py:11
  68.2 10.2 %collective-permute-start.19 = (bf16[1024,128]{1,0:T(8,128)(2,1)S(1)}, bf16[1024,128]{1,0:T(8,128)(2,1)S(1)}, u32[]{:S(2)}, u32[]{:S(2)}) collective-permute-start(bf16[1024,128]{1,0:T(8,128)(2,1)S(1)} %get-tuple-element.68), channel_id=1, source_target_pairs={{0,1},{1,0},{2,3},{3,2},{4,5},{5,4},{6,7},{7,6},{8,9},{9,8},{10,11... | collective-permute-start | bytes 786440 | tf_op jit(solution)/shard_map/ppermute | solution.py:11

commit v13 on v12

--- a/solution.py
+++ b/solution.py
@@ -294,7 +294,7 @@
 
 def exchange(mine, other, near=None):
     sent = {1: other if near is None else near, 2: mine, 3: other}
-    held = {k: swap(sent[k], "chan", k) for k in (1, 2, 3)}
+    held = {k: swap(sent[k], "chan", k) for k in (2, 3, 1)}
     return [mine, held[1], held[2], held[3]]
 
 
@@ -324,7 +324,6 @@
 
 def put(slot, piece, whole, cols):
     channels, rows, width = piece.shape
-    block = pl.BlockSpec((channels, rows, width), lambda i, slot: (0, 0, 0))
     spot = pl.BlockSpec((channels, rows, width), lambda i, slot: (0, 0, slot[0]))
     return pl.pallas_call(
         place_kernel,
@@ -332,7 +331,7 @@
         grid_spec=pltpu.PrefetchScalarGridSpec(
             num_scalar_prefetch=1,
             grid=(1,),
-            in_specs=[block] + [ANY] * len(whole),
+            in_specs=[VMEM] + [ANY] * len(whole),
             out_specs=spot,
         ),
         input_output_aliases={2: 0} if whole else {},
@@ -386,7 +385,7 @@
     sent = cut(place, after([upstream, image], pieces[3]), bias[None], inner[0], 25)
     pieces = after(pieces, sent)
     first = exchange(*sent)
-    sent = cut(place, after([upstream, image], first[1:]), bias[None], inner[1], 18)
+    sent = cut(place, after([upstream, image], first[1:]), bias[None], inner[1], 13)
     first = after(first, sent)
     second = exchange(*sent)
 
@@ -394,8 +393,7 @@
     near, near_order = gather(near, steps)
     across, across_order = gather(across, steps[::-1])
     near, across = after((near, across), pieces[1])
-    there = swap(jnp.concatenate([near, across], axis=1), "band", 1)
-    held = [near, there[:, : near.shape[1]], across, there[:, near.shape[1] :]]
+    held = [near, swap(near, "band", 1), across, swap(across, "band", 1)]
     filters = kernel(
         lambda *refs: assemble_kernel((near_order, across_order), *refs),
         [(taps * outs, 2 * local), (taps * 2 * local, 2 * local)],
@@ -403,7 +401,7 @@
         [],
         "assemble",
         True,
-        2,
+        0,
     )
     pitch = width + 8
     body = lambda *refs: rim_kernel(pitch, *refs)
@@ -418,12 +416,12 @@
         [(3, size, 4 * local)] * 2,
         "outer",
         False,
-        2,
+        40,
         jnp.float32,
     )
     lines = jnp.concatenate([p[width + 2 : width + 3] for p in pieces[:2]]).astype(jnp.float32)
     marks = [[], []]
-    marks[0].append(token(first, 2))
+    first = after(first, totals)
     kept, came = [], []
     for which in range(2):
         mine, other = kernel(
@@ -433,14 +431,14 @@
             [(3, size // 2, 4 * local)],
             "inner",
             False,
-            9,
+            40,
         )
         kept.append(mine)
         if not which:
             second = after(second, mine)
         came.append(swap(other, "chan", 1))
     image_grad = home(place, kept[0], came[0], rows)
-    kept[1] = after(kept[1], image_grad)
+    came[1] = after(came[1], image_grad)
     return home(place, kept[1], came[1], rows), image_grad
 
 

time: 81.3 us -> 82.4 us (1.014)
  waiting for transfers between devices: 28.9 us -> 30.5 us
    ppermute x19 -> x20, waiting for transfers between devices: 28.9 us -> 30.5 us  [swap(): return lax.ppermute(value, axis, [(j, j ^ step) for j in range(size)])]
    ppermute x19 -> x20, starting transfers between devices: 25.5 us -> 25.1 us  [swap(): return lax.ppermute(value, axis, [(j, j ^ step) for j in range(size)])]
    pallas_call x9 -> x8, Pallas kernels: 9.63 us -> 9.62 us  [kernel(): pl.pallas_call(body, out_shape=[jax.ShapeDtypeStruct(s, kind) for s in sh...]
  transfers between devices with their start and end apart: 21 -> 22, of which waited for: 7 -> 8; matrix products, arithmetic and copies ran while one was open for 6% -> 6% of each run, Pallas kernels for 18% -> 18%
where the time goes in v13:
time: 82.4 us; the launch traced here: 82 us
  waiting for transfers between devices  30.5 us (37%)
  starting transfers between devices  27.7 us (34%)
  Pallas kernels  16.3 us (20%)
  local copies, waits for them, and re-layouts  6.36 us (8%)
  between operations  0.9 us (1%)
    ppermute x20, waiting for transfers between devices, swap(): return lax.ppermute(value, axis, [(j, j ^ step) for j in range(size)])  30.5 us
    ppermute x20, starting transfers between devices, swap(): return lax.ppermute(value, axis, [(j, j ^ step) for j in range(size)])  25.1 us
    pallas_call x8, Pallas kernels, kernel(): pl.pallas_call(body, out_shape=[jax.ShapeDtypeStruct(s, kind) for s in sh...  9.62 us
    pallas_call x4, Pallas kernels, put(): pl.pallas_call(place_kernel, out_shape=jax.ShapeDtypeStruct((channels, ro...  6.67 us
    reshape x4, local copies, waits for them, and re-layouts, home(): p.reshape(rows, -1, p.shape[1])  3.5 us
    ppermute x2, starting transfers between devices, neighbours(): return (lax.ppermute(last, 'band', up), lax.ppermute(first, 'band', down))  2.59 us
    unnamed x8, local copies, waits for them, and re-layouts  1.89 us
  transfers between devices with their start and end apart: 22, of which 8 were waited for; matrix products, arithmetic and copies ran while one was open for 6% of the time, Pallas kernels for 18%

profile of v13, /device:TPU:0, one launch (start us, length us, event | category | flops | bytes accessed | tf_op | source)
XLA Modules:
  0.0 82.0 jit_solution(7747041492716234642)
XLA Ops:
  0.7 1.0 %constant_dynamic-slice_fusion = bf16[9,32,128]{2,1,0:T(8,128)(2,1)S(1)} fusion(bf16[9,512,128]{2,1,0:T(8,128)(2,1)} %refs_1_.1, s32[]{:T(128)S(6)} %select_n.7), kind=kLoop, calls=%fused_computation.7 | loop fusion | bytes 147460 | tf_op jit(solution)/shard_map/dynamic_slice | solution.py:376
  1.6 4.0 %collective-permute-start.14 = (bf16[288,128]{1,0:T(8,128)(2,1)S(1)}, bf16[288,128]{1,0:T(8,128)(2,1)S(1)}, u32[]{:S(2)}, u32[]{:S(2)}) collective-permute-start(bf16[288,128]{1,0:T(8,128)(2,1)S(1)} %bitcast.39), channel_id=1, source_target_pairs={{0,2},{1,3},{2,0},{3,1},{4,6},{5,7},{6,4},{7,5},{8,10},{9,11},{10,... | collective-permute-start | bytes 221192 | tf_op jit(solution)/shard_map/ppermute | solution.py:11
  5.6 1.3 %collective-permute-start.15 = (bf16[288,128]{1,0:T(8,128)(2,1)S(1)}, bf16[288,128]{1,0:T(8,128)(2,1)S(1)}, u32[]{:S(2)}, u32[]{:S(2)}) collective-permute-start(bf16[288,128]{1,0:T(8,128)(2,1)S(1)} %bitcast.40), channel_id=1, source_target_pairs={{0,3},{1,2},{2,1},{3,0},{4,7},{5,6},{6,5},{7,4},{8,11},{9,10},{10,... | collective-permute-start | bytes 221192 | tf_op jit(solution)/shard_map/ppermute | solution.py:11
  7.0 1.5 %copy.8 = bf16[128,4,512]{0,2,1:T(8,128)(2,1)S(1)} copy(bf16[128,4,512]{2,1,0:T(4,128)(2,1)} %param.7) | data formatting | bytes 1048576 | tf_op args[3]
  8.5 0.4 copy.9
  8.9 0.1 pad_add_fusion.refs_0_
  9.0 0.7 cut.3
  9.7 2.5 %collective-permute-start = (bf16[1056,128]{1,0:T(8,128)(2,1)S(1)}, bf16[1056,128]{1,0:T(8,128)(2,1)S(1)}, u32[]{:S(2)}, u32[]{:S(2)}) collective-permute-start(bf16[1056,128]{1,0:T(8,128)(2,1)S(1)} %get-tuple-element.41), channel_id=1, source_target_pairs={{0,3},{1,2},{2,1},{3,0},{4,7},{5,6},{6,5},{7,4},{8,11},{9,10},{10,... | collective-permute-start | bytes 811016 | tf_op jit(solution)/shard_map/ppermute | solution.py:11
  12.2 0.1 collective-permute-start.11
  12.3 0.0 collective-permute-done.14
  12.3 0.0 collective-permute-done.15
  12.3 1.6 %collective-permute-start.16 = (bf16[1,576,128]{2,1,0:T(8,128)(2,1)S(1)}, bf16[1,576,128]{2,1,0:T(8,128)(2,1)S(1)}, u32[]{:S(2)}, u32[]{:S(2)}) collective-permute-start(bf16[1,576,128]{2,1,0:T(8,128)(2,1)S(1)} %maximum_bitcast_fusion), channel_id=1, source_target_pairs={{0,8},{4,12},{8,0},{12,4},{16,24},{20,28},{24,16},{28,20},{1,9},{5... | collective-permute-start | bytes 442376 | tf_op jit(solution)/shard_map/ppermute | solution.py:11
  13.9 8.6 %collective-permute-done.11 = bf16[576,128]{1,0:T(8,128)(2,1)S(1)} collective-permute-done((bf16[576,128]{1,0:T(8,128)(2,1)S(1)}, bf16[576,128]{1,0:T(8,128)(2,1)S(1)}, u32[]{:S(2)}, u32[]{:S(2)}) %collective-permute-start.11) | collective-permute-done | bytes 147488 | tf_op jit(solution)/shard_map/ppermute | solution.py:11
  22.5 1.5 %collective-permute-start.12 = (bf16[1,576,128]{2,1,0:T(8,128)(2,1)S(1)}, bf16[1,576,128]{2,1,0:T(8,128)(2,1)S(1)}, u32[]{:S(2)}, u32[]{:S(2)}) collective-permute-start(bf16[1,576,128]{2,1,0:T(8,128)(2,1)S(1)} %bitcast.33), channel_id=1, source_target_pairs={{0,16},{4,20},{8,24},{12,28},{16,0},{20,4},{24,8},{28,12},{1,17},{... | collective-permute-start | bytes 442376 | tf_op jit(solution)/shard_map/ppermute | solution.py:11
  24.0 0.6 collective-permute-start.7
  24.6 1.7 %collective-permute-start.8 = (bf16[1056,128]{1,0:T(8,128)(2,1)S(1)}, bf16[1056,128]{1,0:T(8,128)(2,1)S(1)}, u32[]{:S(2)}, u32[]{:S(2)}) collective-permute-start(bf16[1056,128]{1,0:T(8,128)(2,1)S(1)} %get-tuple-element.55.refs_0_), channel_id=1, source_target_pairs={{0,2},{1,3},{2,0},{3,1},{4,6},{5,7},{6,4},{7,5},{8,10},{9,11},{10,... | collective-permute-start | bytes 811016 | tf_op jit(solution)/shard_map/ppermute | solution.py:11
  26.3 0.0 collective-permute-done.16
  26.3 0.6 collective-permute-start.17
  26.9 0.0 collective-permute-done.refs_3_
  26.9 2.1 %collective-permute-done.12 = bf16[1,576,128]{2,1,0:T(8,128)(2,1)S(1)} collective-permute-done((bf16[1,576,128]{2,1,0:T(8,128)(2,1)S(1)}, bf16[1,576,128]{2,1,0:T(8,128)(2,1)S(1)}, u32[]{:S(2)}, u32[]{:S(2)}) %collective-permute-start.12) | collective-permute-done | bytes 147488 | tf_op jit(solution)/shard_map/ppermute | solution.py:11
  29.1 1.6 %collective-permute-start.13 = (bf16[2,576,128]{2,1,0:T(8,128)(2,1)S(1)}, bf16[2,576,128]{2,1,0:T(8,128)(2,1)S(1)}, u32[]{:S(2)}, u32[]{:S(2)}) collective-permute-start(bf16[2,576,128]{2,1,0:T(8,128)(2,1)S(1)} %pad_maximum_fusion.2), channel_id=1, source_target_pairs={{0,8},{4,12},{8,0},{12,4},{16,24},{20,28},{24,16},{28,20},{1,9},{5... | collective-permute-start | bytes 884744 | tf_op jit(solution)/shard_map/ppermute | solution.py:11
  30.6 0.6 cut.4
  31.2 0.1 collective-permute-start.1
  31.3 7.4 %collective-permute-done.7.refs_1_ = bf16[1056,128]{1,0:T(8,128)(2,1)S(1)} collective-permute-done((bf16[1056,128]{1,0:T(8,128)(2,1)S(1)}, bf16[1056,128]{1,0:T(8,128)(2,1)S(1)}, u32[]{:S(2)}, u32[]{:S(2)}) %collective-permute-start.7) | collective-permute-done | bytes 270368 | tf_op jit(solution)/shard_map/ppermute | solution.py:11
  38.7 0.0 collective-permute-start.2
  38.7 1.2 %collective-permute-done.8.refs_2_ = bf16[1056,128]{1,0:T(8,128)(2,1)S(1)} collective-permute-done((bf16[1056,128]{1,0:T(8,128)(2,1)S(1)}, bf16[1056,128]{1,0:T(8,128)(2,1)S(1)}, u32[]{:S(2)}, u32[]{:S(2)}) %collective-permute-start.8) | collective-permute-done | bytes 270368 | tf_op jit(solution)/shard_map/ppermute | solution.py:11
  39.9 0.6 collective-permute-start.3
  40.5 0.1 rim.1
  40.6 2.4 %collective-permute-done.1.refs_1_ = bf16[528,128]{1,0:T(8,128)(2,1)S(1)} collective-permute-done((bf16[528,128]{1,0:T(8,128)(2,1)S(1)}, bf16[528,128]{1,0:T(8,128)(2,1)S(1)}, u32[]{:S(2)}, u32[]{:S(2)}) %collective-permute-start.1) | collective-permute-done | bytes 135200 | tf_op jit(solution)/shard_map/ppermute | solution.py:11
  43.0 1.3 %collective-permute-start.10 = (bf16[2112,128]{1,0:T(8,128)(2,1)S(1)}, bf16[2112,128]{1,0:T(8,128)(2,1)S(1)}, u32[]{:S(2)}, u32[]{:S(2)}) collective-permute-start(bf16[2112,128]{1,0:T(8,128)(2,1)S(1)} %get-tuple-element.60), channel_id=1, source_target_pairs={{4,0},{8,4},{12,8},{16,12},{20,16},{24,20},{28,24},{5,1},{9,5},{13... | collective-permute-start | bytes 1622024 | tf_op jit(solution)/shard_map/ppermute | solution.py:18
  44.2 4.6 %collective-permute-done.2.refs_2_ = bf16[528,128]{1,0:T(8,128)(2,1)S(1)} collective-permute-done((bf16[528,128]{1,0:T(8,128)(2,1)S(1)}, bf16[528,128]{1,0:T(8,128)(2,1)S(1)}, u32[]{:S(2)}, u32[]{:S(2)}) %collective-permute-start.2) | collective-permute-done | bytes 135200 | tf_op jit(solution)/shard_map/ppermute | solution.py:11
  48.8 1.3 %collective-permute-start.9 = (bf16[2112,128]{1,0:T(8,128)(2,1)S(1)}, bf16[2112,128]{1,0:T(8,128)(2,1)S(1)}, u32[]{:S(2)}, u32[]{:S(2)}) collective-permute-start(bf16[2112,128]{1,0:T(8,128)(2,1)S(1)} %get-tuple-element.59), channel_id=1, source_target_pairs={{0,4},{4,8},{8,12},{12,16},{16,20},{20,24},{24,28},{1,5},{5,9},{9,... | collective-permute-start | bytes 1622024 | tf_op jit(solution)/shard_map/ppermute | solution.py:18
  50.2 0.0 collective-permute-done.3.refs_3_
  50.2 0.0 collective-permute-done.17
  50.2 0.1 pad_maximum_fusion.1.refs_4_
  50.2 0.0 collective-permute-done.13
  50.3 0.1 pad_maximum_fusion.refs_2_
  50.3 2.3 %collective-permute-start.18 = (bf16[4,576,128]{2,1,0:T(8,128)(2,1)S(1)}, bf16[4,576,128]{2,1,0:T(8,128)(2,1)S(1)}, u32[]{:S(2)}, u32[]{:S(2)}) collective-permute-start(bf16[4,576,128]{2,1,0:T(8,128)(2,1)S(1)} %pad_maximum_fusion.refs_2_), channel_id=1, source_target_pairs={{0,4},{4,0},{8,12},{12,8},{16,20},{20,16},{24,28},{28,24},{1,5},{5... | collective-permute-start | bytes 1769480 | tf_op jit(solution)/shard_map/ppermute | solution.py:11
  52.6 0.1 collective-permute-start.19
  52.7 0.6 cut.5
  53.3 0.1 collective-permute-start.4
  53.4 0.8 %collective-permute-done.18.refs_3_ = bf16[4,576,128]{2,1,0:T(8,128)(2,1)S(1)} collective-permute-done((bf16[4,576,128]{2,1,0:T(8,128)(2,1)S(1)}, bf16[4,576,128]{2,1,0:T(8,128)(2,1)S(1)}, u32[]{:S(2)}, u32[]{:S(2)}) %collective-permute-start.18) | collective-permute-done | bytes 589856 | tf_op jit(solution)/shard_map/ppermute | solution.py:11
  54.2 2.2 %collective-permute-start.5 = (bf16[528,128]{1,0:T(8,128)(2,1)S(1)}, bf16[528,128]{1,0:T(8,128)(2,1)S(1)}, u32[]{:S(2)}, u32[]{:S(2)}) collective-permute-start(bf16[528,128]{1,0:T(8,128)(2,1)S(1)} %get-tuple-element.72.refs_0_), channel_id=1, source_target_pairs={{0,2},{1,3},{2,0},{3,1},{4,6},{5,7},{6,4},{7,5},{8,10},{9,11},{10,... | collective-permute-start | bytes 405512 | tf_op jit(solution)/shard_map/ppermute | solution.py:11
  56.4 0.0 collective-permute-done.19.refs_5_
  56.4 1.4 %collective-permute-start.6 = (bf16[528,128]{1,0:T(8,128)(2,1)S(1)}, bf16[528,128]{1,0:T(8,128)(2,1)S(1)}, u32[]{:S(2)}, u32[]{:S(2)}) collective-permute-start(bf16[528,128]{1,0:T(8,128)(2,1)S(1)} %get-tuple-element.49), channel_id=1, source_target_pairs={{0,3},{1,2},{2,1},{3,0},{4,7},{5,6},{6,5},{7,4},{8,11},{9,10},{10,... | collective-permute-start | bytes 405512 | tf_op jit(solution)/shard_map/ppermute | solution.py:11
  57.7 1.3 %assemble.1 = (bf16[4608,256]{1,0:T(8,128)(2,1)S(1)}, bf16[2304,256]{1,0:T(8,128)(2,1)S(1)}) custom-call(s32[2]{0:T(128)S(1)} %pad_add_fusion.refs_0_, bf16[9,512,128]{2,1,0:T(8,128)(2,1)S(1)} %copy-done, bf16[4,576,128]{2,1,0:T(8,128)(2,1)S(1)} %pad_maximum_fusion.refs_2_, bf16[4,576,128]{2,1,0:T(8,128)(2,1)S(1)} %collective-permute-done.18.refs_3_, ...), custom_call_target="tpu_custom_call" | custom-call | flops 1048576 | bytes 1048576 | tf_op jit(solution)/shard_map/assemble/pallas_call | solution.py:276
  59.0 0.0 collective-permute-done.10.refs_5_
  59.0 0.0 collective-permute-done.9.refs_4_
  59.1 3.1 %outer.1 = (f32[1024,256]{1,0:T(8,128)S(1)}, f32[1024,256]{1,0:T(8,128)S(1)}) custom-call(bf16[1056,128]{1,0:T(8,128)(2,1)S(1)} %get-tuple-element.55.refs_0_, bf16[1056,128]{1,0:T(8,128)(2,1)S(1)} %collective-permute-done.7.refs_1_, bf16[1056,128]{1,0:T(8,128)(2,1)S(1)} %collective-permute-done.8.refs_2_, ...), custom_call_target="tpu_custom_call" | custom-call | flops 40001048576 | bytes 1048576 | tf_op jit(solution)/shard_map/outer/pallas_call | solution.py:276
  62.2 1.7 %inner.2 = (bf16[1024,128]{1,0:T(8,128)(2,1)S(1)}, bf16[1024,128]{1,0:T(8,128)(2,1)S(1)}) custom-call(bf16[528,128]{1,0:T(8,128)(2,1)S(1)} %get-tuple-element.67.refs_0_, bf16[528,128]{1,0:T(8,128)(2,1)S(1)} %collective-permute-done.1.refs_1_, bf16[528,128]{1,0:T(8,128)(2,1)S(1)} %collective-permute-done.2.refs_2_, ...), custom_call_target="tpu_custom_call" | custom-call | flops 40001048576 | bytes 1048576 | tf_op jit(solution)/shard_map/inner/pallas_call | solution.py:276
  63.9 0.1 collective-permute-start.21
  64.0 0.0 collective-permute-done.4.refs_1_
  64.0 3.4 %collective-permute-done.5.refs_2_ = bf16[528,128]{1,0:T(8,128)(2,1)S(1)} collective-permute-done((bf16[528,128]{1,0:T(8,128)(2,1)S(1)}, bf16[528,128]{1,0:T(8,128)(2,1)S(1)}, u32[]{:S(2)}, u32[]{:S(2)}) %collective-permute-start.5) | collective-permute-done | bytes 135200 | tf_op jit(solution)/shard_map/ppermute | solution.py:11
  67.4 1.5 %inner.3 = (bf16[1024,128]{1,0:T(8,128)(2,1)S(1)}, bf16[1024,128]{1,0:T(8,128)(2,1)S(1)}) custom-call(bf16[528,128]{1,0:T(8,128)(2,1)S(1)} %get-tuple-element.72.refs_0_, bf16[528,128]{1,0:T(8,128)(2,1)S(1)} %collective-permute-done.4.refs_1_, bf16[528,128]{1,0:T(8,128)(2,1)S(1)} %collective-permute-done.5.refs_2_, ...), custom_call_target="tpu_custom_call" | custom-call | flops 40001048576 | bytes 1048576 | tf_op jit(solution)/shard_map/inner/pallas_call | solution.py:276
  68.9 3.0 %collective-permute-start.20 = (bf16[1024,128]{1,0:T(8,128)(2,1)S(1)}, bf16[1024,128]{1,0:T(8,128)(2,1)S(1)}, u32[]{:S(2)}, u32[]{:S(2)}) collective-permute-start(bf16[1024,128]{1,0:T(8,128)(2,1)S(1)} %get-tuple-element.76), channel_id=1, source_target_pairs={{0,1},{1,0},{2,3},{3,2},{4,5},{5,4},{6,7},{7,6},{8,9},{9,8},{10,11... | collective-permute-start | bytes 786440 | tf_op jit(solution)/shard_map/ppermute | solution.py:11
  71.9 0.9 %copy.15 = bf16[4,256,128]{1,0,2:T(4,128)(2,1)} copy(bf16[4,256,128]{2,1,0:T(8,128)(2,1)S(1)} %bitcast.24) | data formatting | bytes 524288 | tf_op jit(solution)/shard_map/reshape | solution.py:346
  72.7 0.9 %copy.17 = bf16[4,256,128]{1,0,2:T(4,128)(2,1)} copy(bf16[4,256,128]{2,1,0:T(8,128)(2,1)S(1)} %bitcast.25) | data formatting | bytes 524288 | tf_op jit(solution)/shard_map/reshape | solution.py:346
  73.6 1.7 %put.4.refs_0_ = bf16[128,4,512]{2,1,0:T(4,128)(2,1)} custom-call(s32[1]{0:T(128)S(6)} %and.6.slot, bf16[128,4,256]{2,1,0:T(4,128)(2,1)} %bitcast.31), custom_call_target="tpu_custom_call" | custom-call | flops 1048576 | bytes 1048576 | tf_op jit(solution)/shard_map/put/pallas_call | solution.py:328
  75.3 1.7 %put.6.refs_0_ = bf16[128,4,512]{2,1,0:T(4,128)(2,1)} custom-call(s32[1]{0:T(128)S(6)} %and.6.slot, bf16[128,4,256]{2,1,0:T(4,128)(2,1)} %bitcast.32), custom_call_target="tpu_custom_call" | custom-call | flops 1048576 | bytes 1048576 | tf_op jit(solution)/shard_map/put/pallas_call | solution.py:328
  77.0 0.0 collective-permute-done.21
  77.0 0.9 %copy.14 = bf16[4,256,128]{1,0,2:T(4,128)(2,1)} copy(bf16[4,256,128]{2,1,0:T(8,128)(2,1)S(1)} %bitcast.36) | data formatting | bytes 524288 | tf_op jit(solution)/shard_map/reshape | solution.py:346
  77.8 1.7 %put.5 = bf16[128,4,512]{2,1,0:T(4,128)(2,1)} custom-call(s32[1]{0:T(128)S(6)} %sub.7.slot, bf16[128,4,256]{2,1,0:T(4,128)(2,1)} %bitcast.30, bf16[128,4,512]{2,1,0:T(4,128)(2,1)} %put.4.refs_0_), custom_call_target="tpu_custom_call", output_to_operand_aliasing={{}: (2, {})} | custom-call | flops 1048576 | bytes 1048576 | tf_op jit(solution)/shard_map/put/pallas_call | solution.py:328
  79.5 0.9 %copy.16 = bf16[4,256,128]{1,0,2:T(4,128)(2,1)} copy(bf16[4,256,128]{2,1,0:T(8,128)(2,1)S(1)} %bitcast.37) | data formatting | bytes 524288 | tf_op jit(solution)/shard_map/reshape | solution.py:346
  80.4 1.7 %put.7 = bf16[128,4,512]{2,1,0:T(4,128)(2,1)} custom-call(s32[1]{0:T(128)S(6)} %sub.7.slot, bf16[128,4,256]{2,1,0:T(4,128)(2,1)} %bitcast.29, bf16[128,4,512]{2,1,0:T(4,128)(2,1)} %put.6.refs_0_), custom_call_target="tpu_custom_call", output_to_operand_aliasing={{}: (2, {})} | custom-call | flops 1048576 | bytes 1048576 | tf_op jit(solution)/shard_map/put/pallas_call | solution.py:328
  (15 shorter events, 0.1 us)
Async XLA Ops:
  0.6 7.8 %copy-start.2 = (bf16[128,4,512]{2,1,0:T(4,128)(2,1)S(1)}, bf16[128,4,512]{2,1,0:T(4,128)(2,1)}, u32[]{:S(2)}) copy-start(bf16[128,4,512]{2,1,0:T(4,128)(2,1)} %param.4) | copy-start | bytes 1572868
  0.6 8.3 %copy-start.1 = (bf16[128]{0:T(256)(128)(2,1)S(1)}, bf16[128]{0:T(256)(128)(2,1)}, u32[]{:S(2)}) copy-start(bf16[128]{0:T(256)(128)(2,1)} %param.6) | copy-start | bytes 772
  1.6 10.7 %collective-permute-start.14 = (bf16[288,128]{1,0:T(8,128)(2,1)S(1)}, bf16[288,128]{1,0:T(8,128)(2,1)S(1)}, u32[]{:S(2)}, u32[]{:S(2)}) collective-permute-start(bf16[288,128]{1,0:T(8,128)(2,1)S(1)} %bitcast.39), channel_id=1, source_target_pairs={{0,2},{1,3},{2,0},{3,1},{4,6},{5,7},{6,4},{7,5},{8,10},{9,11},{10,... | collective-permute-start | bytes 221192 | tf_op jit(solution)/shard_map/ppermute | solution.py:11
  5.6 6.7 %collective-permute-start.15 = (bf16[288,128]{1,0:T(8,128)(2,1)S(1)}, bf16[288,128]{1,0:T(8,128)(2,1)S(1)}, u32[]{:S(2)}, u32[]{:S(2)}) collective-permute-start(bf16[288,128]{1,0:T(8,128)(2,1)S(1)} %bitcast.40), channel_id=1, source_target_pairs={{0,3},{1,2},{2,1},{3,0},{4,7},{5,6},{6,5},{7,4},{8,11},{9,10},{10,... | collective-permute-start | bytes 221192 | tf_op jit(solution)/shard_map/ppermute | solution.py:11
  9.0 3.2 %copy-start = (bf16[9,512,128]{2,1,0:T(8,128)(2,1)S(1)}, bf16[9,512,128]{2,1,0:T(8,128)(2,1)}, u32[]{:S(2)}) copy-start(bf16[9,512,128]{2,1,0:T(8,128)(2,1)} %refs_1_.1) | copy-start | bytes 3538948
  9.7 17.2 %collective-permute-start = (bf16[1056,128]{1,0:T(8,128)(2,1)S(1)}, bf16[1056,128]{1,0:T(8,128)(2,1)S(1)}, u32[]{:S(2)}, u32[]{:S(2)}) collective-permute-start(bf16[1056,128]{1,0:T(8,128)(2,1)S(1)} %get-tuple-element.41), channel_id=1, source_target_pairs={{0,3},{1,2},{2,1},{3,0},{4,7},{5,6},{6,5},{7,4},{8,11},{9,10},{10,... | collective-permute-start | bytes 811016 | tf_op jit(solution)/shard_map/ppermute | solution.py:11
  12.2 10.2 %collective-permute-start.11 = (bf16[576,128]{1,0:T(8,128)(2,1)S(1)}, bf16[576,128]{1,0:T(8,128)(2,1)S(1)}, u32[]{:S(2)}, u32[]{:S(2)}) collective-permute-start(bf16[576,128]{1,0:T(8,128)(2,1)S(1)} %bitcast.38), channel_id=1, source_target_pairs={{0,1},{1,0},{2,3},{3,2},{4,5},{5,4},{6,7},{7,6},{8,9},{9,8},{10,11... | collective-permute-start | bytes 442376 | tf_op jit(solution)/shard_map/ppermute | solution.py:11
  12.3 13.9 %collective-permute-start.16 = (bf16[1,576,128]{2,1,0:T(8,128)(2,1)S(1)}, bf16[1,576,128]{2,1,0:T(8,128)(2,1)S(1)}, u32[]{:S(2)}, u32[]{:S(2)}) collective-permute-start(bf16[1,576,128]{2,1,0:T(8,128)(2,1)S(1)} %maximum_bitcast_fusion), channel_id=1, source_target_pairs={{0,8},{4,12},{8,0},{12,4},{16,24},{20,28},{24,16},{28,20},{1,9},{5... | collective-permute-start | bytes 442376 | tf_op jit(solution)/shard_map/ppermute | solution.py:11
  22.5 6.6 %collective-permute-start.12 = (bf16[1,576,128]{2,1,0:T(8,128)(2,1)S(1)}, bf16[1,576,128]{2,1,0:T(8,128)(2,1)S(1)}, u32[]{:S(2)}, u32[]{:S(2)}) collective-permute-start(bf16[1,576,128]{2,1,0:T(8,128)(2,1)S(1)} %bitcast.33), channel_id=1, source_target_pairs={{0,16},{4,20},{8,24},{12,28},{16,0},{20,4},{24,8},{28,12},{1,17},{... | collective-permute-start | bytes 442376 | tf_op jit(solution)/shard_map/ppermute | solution.py:11
  24.0 14.7 %collective-permute-start.7 = (bf16[1056,128]{1,0:T(8,128)(2,1)S(1)}, bf16[1056,128]{1,0:T(8,128)(2,1)S(1)}, u32[]{:S(2)}, u32[]{:S(2)}) collective-permute-start(bf16[1056,128]{1,0:T(8,128)(2,1)S(1)} %get-tuple-element.41), channel_id=1, source_target_pairs={{0,1},{1,0},{2,3},{3,2},{4,5},{5,4},{6,7},{7,6},{8,9},{9,8},{10,11... | collective-permute-start | bytes 811016 | tf_op jit(solution)/shard_map/ppermute | solution.py:11
  24.6 15.3 %collective-permute-start.8 = (bf16[1056,128]{1,0:T(8,128)(2,1)S(1)}, bf16[1056,128]{1,0:T(8,128)(2,1)S(1)}, u32[]{:S(2)}, u32[]{:S(2)}) collective-permute-start(bf16[1056,128]{1,0:T(8,128)(2,1)S(1)} %get-tuple-element.55.refs_0_), channel_id=1, source_target_pairs={{0,2},{1,3},{2,0},{3,1},{4,6},{5,7},{6,4},{7,5},{8,10},{9,11},{10,... | collective-permute-start | bytes 811016 | tf_op jit(solution)/shard_map/ppermute | solution.py:11
  26.3 23.9 %collective-permute-start.17 = (bf16[2,576,128]{2,1,0:T(8,128)(2,1)S(1)}, bf16[2,576,128]{2,1,0:T(8,128)(2,1)S(1)}, u32[]{:S(2)}, u32[]{:S(2)}) collective-permute-start(bf16[2,576,128]{2,1,0:T(8,128)(2,1)S(1)} %pad_maximum_fusion.3), channel_id=1, source_target_pairs={{0,16},{4,20},{8,24},{12,28},{16,0},{20,4},{24,8},{28,12},{1,17},{... | collective-permute-start | bytes 884744 | tf_op jit(solution)/shard_map/ppermute | solution.py:11
  29.1 21.2 %collective-permute-start.13 = (bf16[2,576,128]{2,1,0:T(8,128)(2,1)S(1)}, bf16[2,576,128]{2,1,0:T(8,128)(2,1)S(1)}, u32[]{:S(2)}, u32[]{:S(2)}) collective-permute-start(bf16[2,576,128]{2,1,0:T(8,128)(2,1)S(1)} %pad_maximum_fusion.2), channel_id=1, source_target_pairs={{0,8},{4,12},{8,0},{12,4},{16,24},{20,28},{24,16},{28,20},{1,9},{5... | collective-permute-start | bytes 884744 | tf_op jit(solution)/shard_map/ppermute | solution.py:11
  31.2 11.7 %collective-permute-start.1 = (bf16[528,128]{1,0:T(8,128)(2,1)S(1)}, bf16[528,128]{1,0:T(8,128)(2,1)S(1)}, u32[]{:S(2)}, u32[]{:S(2)}) collective-permute-start(bf16[528,128]{1,0:T(8,128)(2,1)S(1)} %get-tuple-element.44), channel_id=1, source_target_pairs={{0,1},{1,0},{2,3},{3,2},{4,5},{5,4},{6,7},{7,6},{8,9},{9,8},{10,11... | collective-permute-start | bytes 405512 | tf_op jit(solution)/shard_map/ppermute | solution.py:11
  38.7 10.1 %collective-permute-start.2 = (bf16[528,128]{1,0:T(8,128)(2,1)S(1)}, bf16[528,128]{1,0:T(8,128)(2,1)S(1)}, u32[]{:S(2)}, u32[]{:S(2)}) collective-permute-start(bf16[528,128]{1,0:T(8,128)(2,1)S(1)} %get-tuple-element.67.refs_0_), channel_id=1, source_target_pairs={{0,2},{1,3},{2,0},{3,1},{4,6},{5,7},{6,4},{7,5},{8,10},{9,11},{10,... | collective-permute-start | bytes 405512 | tf_op jit(solution)/shard_map/ppermute | solution.py:11
  39.9 10.3 %collective-permute-start.3 = (bf16[528,128]{1,0:T(8,128)(2,1)S(1)}, bf16[528,128]{1,0:T(8,128)(2,1)S(1)}, u32[]{:S(2)}, u32[]{:S(2)}) collective-permute-start(bf16[528,128]{1,0:T(8,128)(2,1)S(1)} %get-tuple-element.44), channel_id=1, source_target_pairs={{0,3},{1,2},{2,1},{3,0},{4,7},{5,6},{6,5},{7,4},{8,11},{9,10},{10,... | collective-permute-start | bytes 405512 | tf_op jit(solution)/shard_map/ppermute | solution.py:11
  43.0 16.1 %collective-permute-start.10 = (bf16[2112,128]{1,0:T(8,128)(2,1)S(1)}, bf16[2112,128]{1,0:T(8,128)(2,1)S(1)}, u32[]{:S(2)}, u32[]{:S(2)}) collective-permute-start(bf16[2112,128]{1,0:T(8,128)(2,1)S(1)} %get-tuple-element.60), channel_id=1, source_target_pairs={{4,0},{8,4},{12,8},{16,12},{20,16},{24,20},{28,24},{5,1},{9,5},{13... | collective-permute-start | bytes 1622024 | tf_op jit(solution)/shard_map/ppermute | solution.py:18
  48.8 10.2 %collective-permute-start.9 = (bf16[2112,128]{1,0:T(8,128)(2,1)S(1)}, bf16[2112,128]{1,0:T(8,128)(2,1)S(1)}, u32[]{:S(2)}, u32[]{:S(2)}) collective-permute-start(bf16[2112,128]{1,0:T(8,128)(2,1)S(1)} %get-tuple-element.59), channel_id=1, source_target_pairs={{0,4},{4,8},{8,12},{12,16},{16,20},{20,24},{24,28},{1,5},{5,9},{9,... | collective-permute-start | bytes 1622024 | tf_op jit(solution)/shard_map/ppermute | solution.py:18
  50.3 3.9 %collective-permute-start.18 = (bf16[4,576,128]{2,1,0:T(8,128)(2,1)S(1)}, bf16[4,576,128]{2,1,0:T(8,128)(2,1)S(1)}, u32[]{:S(2)}, u32[]{:S(2)}) collective-permute-start(bf16[4,576,128]{2,1,0:T(8,128)(2,1)S(1)} %pad_maximum_fusion.refs_2_), channel_id=1, source_target_pairs={{0,4},{4,0},{8,12},{12,8},{16,20},{20,16},{24,28},{28,24},{1,5},{5... | collective-permute-start | bytes 1769480 | tf_op jit(solution)/shard_map/ppermute | solution.py:11
  52.6 3.8 %collective-permute-start.19 = (bf16[4,576,128]{2,1,0:T(8,128)(2,1)S(1)}, bf16[4,576,128]{2,1,0:T(8,128)(2,1)S(1)}, u32[]{:S(2)}, u32[]{:S(2)}) collective-permute-start(bf16[4,576,128]{2,1,0:T(8,128)(2,1)S(1)} %pad_maximum_fusion.1.refs_4_), channel_id=1, source_target_pairs={{0,4},{4,0},{8,12},{12,8},{16,20},{20,16},{24,28},{28,24},{1,5},{5... | collective-permute-start | bytes 1769480 | tf_op jit(solution)/shard_map/ppermute | solution.py:11
  53.3 10.7 %collective-permute-start.4 = (bf16[528,128]{1,0:T(8,128)(2,1)S(1)}, bf16[528,128]{1,0:T(8,128)(2,1)S(1)}, u32[]{:S(2)}, u32[]{:S(2)}) collective-permute-start(bf16[528,128]{1,0:T(8,128)(2,1)S(1)} %get-tuple-element.49), channel_id=1, source_target_pairs={{0,1},{1,0},{2,3},{3,2},{4,5},{5,4},{6,7},{7,6},{8,9},{9,8},{10,11... | collective-permute-start | bytes 405512 | tf_op jit(solution)/shard_map/ppermute | solution.py:11
  54.2 13.2 %collective-permute-start.5 = (bf16[528,128]{1,0:T(8,128)(2,1)S(1)}, bf16[528,128]{1,0:T(8,128)(2,1)S(1)}, u32[]{:S(2)}, u32[]{:S(2)}) collective-permute-start(bf16[528,128]{1,0:T(8,128)(2,1)S(1)} %get-tuple-element.72.refs_0_), channel_id=1, source_target_pairs={{0,2},{1,3},{2,0},{3,1},{4,6},{5,7},{6,4},{7,5},{8,10},{9,11},{10,... | collective-permute-start | bytes 405512 | tf_op jit(solution)/shard_map/ppermute | solution.py:11
  56.4 11.0 %collective-permute-start.6 = (bf16[528,128]{1,0:T(8,128)(2,1)S(1)}, bf16[528,128]{1,0:T(8,128)(2,1)S(1)}, u32[]{:S(2)}, u32[]{:S(2)}) collective-permute-start(bf16[528,128]{1,0:T(8,128)(2,1)S(1)} %get-tuple-element.49), channel_id=1, source_target_pairs={{0,3},{1,2},{2,1},{3,0},{4,7},{5,6},{6,5},{7,4},{8,11},{9,10},{10,... | collective-permute-start | bytes 405512 | tf_op jit(solution)/shard_map/ppermute | solution.py:11
  63.9 13.1 %collective-permute-start.21 = (bf16[1024,128]{1,0:T(8,128)(2,1)S(1)}, bf16[1024,128]{1,0:T(8,128)(2,1)S(1)}, u32[]{:S(2)}, u32[]{:S(2)}) collective-permute-start(bf16[1024,128]{1,0:T(8,128)(2,1)S(1)} %get-tuple-element.77), channel_id=1, source_target_pairs={{0,1},{1,0},{2,3},{3,2},{4,5},{5,4},{6,7},{7,6},{8,9},{9,8},{10,11... | collective-permute-start | bytes 786440 | tf_op jit(solution)/shard_map/ppermute | solution.py:11
  68.9 10.6 %collective-permute-start.20 = (bf16[1024,128]{1,0:T(8,128)(2,1)S(1)}, bf16[1024,128]{1,0:T(8,128)(2,1)S(1)}, u32[]{:S(2)}, u32[]{:S(2)}) collective-permute-start(bf16[1024,128]{1,0:T(8,128)(2,1)S(1)} %get-tuple-element.76), channel_id=1, source_target_pairs={{0,1},{1,0},{2,3},{3,2},{4,5},{5,4},{6,7},{7,6},{8,9},{9,8},{10,11... | collective-permute-start | bytes 786440 | tf_op jit(solution)/shard_map/ppermute | solution.py:11

commit v14 on v11

--- a/solution.py
+++ b/solution.py
@@ -243,7 +243,7 @@
     row = size // 2
     local = mine.shape[1]
     pitch = row + 8
-    fill(source, [[(p, (2 * which + r) * pitch) for p in inners] for r in range(2)])
+    fill(source, [[(p, r * pitch) for p in inners] for r in range(2)])
     top = middle = bottom = None
     for across in range(3):
         terms = [
@@ -294,7 +294,7 @@
 
 def exchange(mine, other, near=None):
     sent = {1: other if near is None else near, 2: mine, 3: other}
-    held = {k: swap(sent[k], "chan", k) for k in (2, 3, 1)}
+    held = {k: swap(sent[k], "chan", k) for k in (1, 2, 3)}
     return [mine, held[1], held[2], held[3]]
 
 
@@ -367,18 +367,22 @@
 
     upstream, image = [jnp.transpose(v, (1, 2, 0)) for v in (upstream, image)]
     parts = [(i, r) for i in range(2) for r in (0, rows - 1)]
-    sent = cut(place, [upstream, image], bias[None], parts, 25)
-    (near, across) = after((near, across), sent)
+    sent = cut(place, [upstream, image], bias[None], parts, 6)
     pieces = exchange(*sent)
-    parts = [(i, r) for i in range(2) for r in range(1, rows - 1)]
-    sent = cut(place, after([upstream, image], pieces[1]), bias[None], parts, 25)
+    inner = [[(i, r) for r in range(1, rows - 1)] for i in range(2)]
+    sent = cut(place, after([upstream, image], pieces[3]), bias[None], inner[0], 25)
     pieces = after(pieces, sent)
-    inners = exchange(*sent)
+    first = exchange(*sent)
+    sent = cut(place, after([upstream, image], first[1:]), bias[None], inner[1], 18)
+    first = after(first, sent)
+    second = exchange(*sent)
 
     steps = halving(bands)[:-1]
     near, near_order = gather(near, steps)
     across, across_order = gather(across, steps[::-1])
-    held = [near, swap(near, "band", 1), across, swap(across, "band", 1)]
+    near, across = after((near, across), pieces[1])
+    there = swap(jnp.concatenate([near, across], axis=1), "band", 1)
+    held = [near, there[:, : near.shape[1]], across, there[:, near.shape[1] :]]
     filters = kernel(
         lambda *refs: assemble_kernel((near_order, across_order), *refs),
         [(taps * outs, 2 * local), (taps * 2 * local, 2 * local)],
@@ -386,11 +390,12 @@
         [],
         "assemble",
         True,
-        9,
+        2,
     )
     pitch = width + 8
     body = lambda *refs: rim_kernel(pitch, *refs)
-    rims = neighbours(*kernel(body, [(8 * pitch, local)] * 2, pieces, [], "rim", False, 40))
+    packed = kernel(body, [(8 * pitch, local)] * 2, pieces, [], "rim", False, 0)
+    rims = neighbours(*packed)
 
     size = rows * width
     totals = kernel(
@@ -400,24 +405,26 @@
         [(3, size, 4 * local)] * 2,
         "outer",
         False,
-        6,
+        2,
         jnp.float32,
     )
     lines = jnp.concatenate([p[width + 2 : width + 3] for p in pieces[:2]]).astype(jnp.float32)
-    inners = after(inners, totals)
-    mark = [token(inners, 0)]
+    marks = [[], []]
+    marks[0].append(token(first, 2))
     kept, came = [], []
     for which in range(2):
         mine, other = kernel(
             lambda *refs: inner_kernel(which, *refs),
             [(size, local)] * 2,
-            [*inners, totals[which], *filters, lines, *mark],
+            [*(first, second)[which], totals[which], *filters, lines, *marks[which]],
             [(3, size // 2, 4 * local)],
             "inner",
             False,
             9,
         )
         kept.append(mine)
+        if not which:
+            second = after(second, mine)
         came.append(swap(other, "chan", 1))
     image_grad = home(place, kept[0], came[0], rows)
     kept[1] = after(kept[1], image_grad)

time: 90.2 us -> 79.7 us (0.88)
  the two profiles are of different devices: /device:TPU:3 before, /device:TPU:0 now
where the time goes in v14:
time: 79.7 us; the launch traced here: 79.5 us
  waiting for transfers between devices  33.9 us (43%)
  starting transfers between devices  28.1 us (35%)
  Pallas kernels  12.5 us (16%)
  local copies, waits for them, and re-layouts  3.69 us (5%)
  between operations  0.93 us (1%)
    ppermute x19, waiting for transfers between devices, swap(): return lax.ppermute(value, axis, [(j, j ^ step) for j in range(size)])  33.9 us
    ppermute x19, starting transfers between devices, swap(): return lax.ppermute(value, axis, [(j, j ^ step) for j in range(size)])  25.5 us
    pallas_call x11, Pallas kernels, kernel(): pl.pallas_call(body, out_shape=[jax.ShapeDtypeStruct(s, kind) for s in sh...  12.5 us
    ppermute x2, starting transfers between devices, neighbours(): return (lax.ppermute(last, 'band', up), lax.ppermute(first, 'band', down))  2.59 us
    unnamed x8, local copies, waits for them, and re-layouts  1.89 us
  transfers between devices with their start and end apart: 21, of which 9 were waited for; matrix products, arithmetic and copies ran while one was open for 4% of the time, Pallas kernels for 14%

profile of v14, /device:TPU:0, one launch (start us, length us, event | category | flops | bytes accessed | tf_op | source)
XLA Modules:
  0.0 79.5 jit_solution(1309951158166078837)
XLA Ops:
  0.7 1.0 %constant_dynamic-slice_fusion = bf16[9,32,128]{2,1,0:T(8,128)(2,1)S(1)} fusion(bf16[9,512,128]{2,1,0:T(8,128)(2,1)} %refs_1_.1, s32[]{:T(128)S(6)} %select_n.7), kind=kLoop, calls=%fused_computation.8 | loop fusion | bytes 147460 | tf_op jit(solution)/shard_map/dynamic_slice | solution.py:364
  1.6 4.0 %collective-permute-start.14 = (bf16[288,128]{1,0:T(8,128)(2,1)S(1)}, bf16[288,128]{1,0:T(8,128)(2,1)S(1)}, u32[]{:S(2)}, u32[]{:S(2)}) collective-permute-start(bf16[288,128]{1,0:T(8,128)(2,1)S(1)} %bitcast.39), channel_id=1, source_target_pairs={{0,2},{1,3},{2,0},{3,1},{4,6},{5,7},{6,4},{7,5},{8,10},{9,11},{10,... | collective-permute-start | bytes 221192 | tf_op jit(solution)/shard_map/ppermute | solution.py:11
  5.6 1.3 %collective-permute-start.15 = (bf16[288,128]{1,0:T(8,128)(2,1)S(1)}, bf16[288,128]{1,0:T(8,128)(2,1)S(1)}, u32[]{:S(2)}, u32[]{:S(2)}) collective-permute-start(bf16[288,128]{1,0:T(8,128)(2,1)S(1)} %bitcast.40), channel_id=1, source_target_pairs={{0,3},{1,2},{2,1},{3,0},{4,7},{5,6},{6,5},{7,4},{8,11},{9,10},{10,... | collective-permute-start | bytes 221192 | tf_op jit(solution)/shard_map/ppermute | solution.py:11
  7.0 1.5 %copy.6 = bf16[128,4,512]{0,2,1:T(8,128)(2,1)S(1)} copy(bf16[128,4,512]{2,1,0:T(4,128)(2,1)} %param.7) | data formatting | bytes 1048576 | tf_op args[3]
  8.5 0.4 copy.7
  8.9 0.1 pad_add_fusion.refs_0_.place
  9.0 0.7 cut.3
  9.7 2.5 %collective-permute-start = (bf16[1056,128]{1,0:T(8,128)(2,1)S(1)}, bf16[1056,128]{1,0:T(8,128)(2,1)S(1)}, u32[]{:S(2)}, u32[]{:S(2)}) collective-permute-start(bf16[1056,128]{1,0:T(8,128)(2,1)S(1)} %get-tuple-element.37), channel_id=1, source_target_pairs={{0,3},{1,2},{2,1},{3,0},{4,7},{5,6},{6,5},{7,4},{8,11},{9,10},{10,... | collective-permute-start | bytes 811016 | tf_op jit(solution)/shard_map/ppermute | solution.py:11
  12.2 0.1 collective-permute-start.11
  12.3 0.0 collective-permute-done.14
  12.3 0.0 collective-permute-done.15
  12.3 1.6 %collective-permute-start.16 = (bf16[1,576,128]{2,1,0:T(8,128)(2,1)S(1)}, bf16[1,576,128]{2,1,0:T(8,128)(2,1)S(1)}, u32[]{:S(2)}, u32[]{:S(2)}) collective-permute-start(bf16[1,576,128]{2,1,0:T(8,128)(2,1)S(1)} %maximum_bitcast_fusion), channel_id=1, source_target_pairs={{0,8},{4,12},{8,0},{12,4},{16,24},{20,28},{24,16},{28,20},{1,9},{5... | collective-permute-start | bytes 442376 | tf_op jit(solution)/shard_map/ppermute | solution.py:11
  13.9 8.6 %collective-permute-done.11 = bf16[576,128]{1,0:T(8,128)(2,1)S(1)} collective-permute-done((bf16[576,128]{1,0:T(8,128)(2,1)S(1)}, bf16[576,128]{1,0:T(8,128)(2,1)S(1)}, u32[]{:S(2)}, u32[]{:S(2)}) %collective-permute-start.11) | collective-permute-done | bytes 147488 | tf_op jit(solution)/shard_map/ppermute | solution.py:11
  22.5 1.5 %collective-permute-start.12 = (bf16[1,576,128]{2,1,0:T(8,128)(2,1)S(1)}, bf16[1,576,128]{2,1,0:T(8,128)(2,1)S(1)}, u32[]{:S(2)}, u32[]{:S(2)}) collective-permute-start(bf16[1,576,128]{2,1,0:T(8,128)(2,1)S(1)} %bitcast.33), channel_id=1, source_target_pairs={{0,16},{4,20},{8,24},{12,28},{16,0},{20,4},{24,8},{28,12},{1,17},{... | collective-permute-start | bytes 442376 | tf_op jit(solution)/shard_map/ppermute | solution.py:11
  24.0 0.6 collective-permute-start.7
  24.6 1.7 %collective-permute-start.8 = (bf16[1056,128]{1,0:T(8,128)(2,1)S(1)}, bf16[1056,128]{1,0:T(8,128)(2,1)S(1)}, u32[]{:S(2)}, u32[]{:S(2)}) collective-permute-start(bf16[1056,128]{1,0:T(8,128)(2,1)S(1)} %get-tuple-element.51.refs_0_), channel_id=1, source_target_pairs={{0,2},{1,3},{2,0},{3,1},{4,6},{5,7},{6,4},{7,5},{8,10},{9,11},{10,... | collective-permute-start | bytes 811016 | tf_op jit(solution)/shard_map/ppermute | solution.py:11
  26.3 0.0 collective-permute-done.16
  26.3 0.6 collective-permute-start.17
  26.9 0.0 collective-permute-done.refs_3_
  26.9 2.1 %collective-permute-done.12 = bf16[1,576,128]{2,1,0:T(8,128)(2,1)S(1)} collective-permute-done((bf16[1,576,128]{2,1,0:T(8,128)(2,1)S(1)}, bf16[1,576,128]{2,1,0:T(8,128)(2,1)S(1)}, u32[]{:S(2)}, u32[]{:S(2)}) %collective-permute-start.12) | collective-permute-done | bytes 147488 | tf_op jit(solution)/shard_map/ppermute | solution.py:11
  29.1 1.6 %collective-permute-start.13 = (bf16[2,576,128]{2,1,0:T(8,128)(2,1)S(1)}, bf16[2,576,128]{2,1,0:T(8,128)(2,1)S(1)}, u32[]{:S(2)}, u32[]{:S(2)}) collective-permute-start(bf16[2,576,128]{2,1,0:T(8,128)(2,1)S(1)} %pad_maximum_fusion.3), channel_id=1, source_target_pairs={{0,8},{4,12},{8,0},{12,4},{16,24},{20,28},{24,16},{28,20},{1,9},{5... | collective-permute-start | bytes 884744 | tf_op jit(solution)/shard_map/ppermute | solution.py:11
  30.6 0.6 cut.4
  31.2 0.1 collective-permute-start.1
  31.3 7.4 %collective-permute-done.7.refs_1_ = bf16[1056,128]{1,0:T(8,128)(2,1)S(1)} collective-permute-done((bf16[1056,128]{1,0:T(8,128)(2,1)S(1)}, bf16[1056,128]{1,0:T(8,128)(2,1)S(1)}, u32[]{:S(2)}, u32[]{:S(2)}) %collective-permute-start.7) | collective-permute-done | bytes 270368 | tf_op jit(solution)/shard_map/ppermute | solution.py:11
  38.7 0.0 collective-permute-start.2
  38.7 1.2 %collective-permute-done.8.refs_2_ = bf16[1056,128]{1,0:T(8,128)(2,1)S(1)} collective-permute-done((bf16[1056,128]{1,0:T(8,128)(2,1)S(1)}, bf16[1056,128]{1,0:T(8,128)(2,1)S(1)}, u32[]{:S(2)}, u32[]{:S(2)}) %collective-permute-start.8) | collective-permute-done | bytes 270368 | tf_op jit(solution)/shard_map/ppermute | solution.py:11
  39.9 0.6 collective-permute-start.3
  40.5 0.1 rim.1
  40.6 2.4 %collective-permute-done.1.refs_1_ = bf16[528,128]{1,0:T(8,128)(2,1)S(1)} collective-permute-done((bf16[528,128]{1,0:T(8,128)(2,1)S(1)}, bf16[528,128]{1,0:T(8,128)(2,1)S(1)}, u32[]{:S(2)}, u32[]{:S(2)}) %collective-permute-start.1) | collective-permute-done | bytes 135200 | tf_op jit(solution)/shard_map/ppermute | solution.py:11
  43.0 1.3 %collective-permute-start.10 = (bf16[2112,128]{1,0:T(8,128)(2,1)S(1)}, bf16[2112,128]{1,0:T(8,128)(2,1)S(1)}, u32[]{:S(2)}, u32[]{:S(2)}) collective-permute-start(bf16[2112,128]{1,0:T(8,128)(2,1)S(1)} %get-tuple-element.56), channel_id=1, source_target_pairs={{4,0},{8,4},{12,8},{16,12},{20,16},{24,20},{28,24},{5,1},{9,5},{13... | collective-permute-start | bytes 1622024 | tf_op jit(solution)/shard_map/ppermute | solution.py:18
  44.2 4.6 %collective-permute-done.2.refs_2_ = bf16[528,128]{1,0:T(8,128)(2,1)S(1)} collective-permute-done((bf16[528,128]{1,0:T(8,128)(2,1)S(1)}, bf16[528,128]{1,0:T(8,128)(2,1)S(1)}, u32[]{:S(2)}, u32[]{:S(2)}) %collective-permute-start.2) | collective-permute-done | bytes 135200 | tf_op jit(solution)/shard_map/ppermute | solution.py:11
  48.8 1.3 %collective-permute-start.9 = (bf16[2112,128]{1,0:T(8,128)(2,1)S(1)}, bf16[2112,128]{1,0:T(8,128)(2,1)S(1)}, u32[]{:S(2)}, u32[]{:S(2)}) collective-permute-start(bf16[2112,128]{1,0:T(8,128)(2,1)S(1)} %get-tuple-element.55), channel_id=1, source_target_pairs={{0,4},{4,8},{8,12},{12,16},{16,20},{20,24},{24,28},{1,5},{5,9},{9,... | collective-permute-start | bytes 1622024 | tf_op jit(solution)/shard_map/ppermute | solution.py:18
  50.2 0.0 collective-permute-done.3.refs_3_
  50.2 0.0 collective-permute-done.17
  50.2 0.1 pad_maximum_fusion.2.refs_4_
  50.2 0.0 collective-permute-done.13
  50.3 0.1 pad_maximum_fusion.1.refs_2_
  50.3 0.1 pad_maximum_fusion
  50.4 2.3 %collective-permute-start.18 = (bf16[4,1152,128]{2,1,0:T(8,128)(2,1)S(1)}, bf16[4,1152,128]{2,1,0:T(8,128)(2,1)S(1)}, u32[]{:S(2)}, u32[]{:S(2)}) collective-permute-start(bf16[4,1152,128]{2,1,0:T(8,128)(2,1)S(1)} %pad_maximum_fusion), channel_id=1, source_target_pairs={{0,4},{4,0},{8,12},{12,8},{16,20},{20,16},{24,28},{28,24},{1,5},{5... | collective-permute-start | bytes 3538952 | tf_op jit(solution)/shard_map/ppermute | solution.py:11
  52.7 0.6 cut.5
  53.3 0.1 collective-permute-start.4
  53.4 3.0 %collective-permute-start.5 = (bf16[528,128]{1,0:T(8,128)(2,1)S(1)}, bf16[528,128]{1,0:T(8,128)(2,1)S(1)}, u32[]{:S(2)}, u32[]{:S(2)}) collective-permute-start(bf16[528,128]{1,0:T(8,128)(2,1)S(1)} %get-tuple-element.63.refs_0_), channel_id=1, source_target_pairs={{0,2},{1,3},{2,0},{3,1},{4,6},{5,7},{6,4},{7,5},{8,10},{9,11},{10,... | collective-permute-start | bytes 405512 | tf_op jit(solution)/shard_map/ppermute | solution.py:11
  56.4 0.0 collective-permute-done.18
  56.4 1.4 %collective-permute-start.6 = (bf16[528,128]{1,0:T(8,128)(2,1)S(1)}, bf16[528,128]{1,0:T(8,128)(2,1)S(1)}, u32[]{:S(2)}, u32[]{:S(2)}) collective-permute-start(bf16[528,128]{1,0:T(8,128)(2,1)S(1)} %get-tuple-element.45), channel_id=1, source_target_pairs={{0,3},{1,2},{2,1},{3,0},{4,7},{5,6},{6,5},{7,4},{8,11},{9,10},{10,... | collective-permute-start | bytes 405512 | tf_op jit(solution)/shard_map/ppermute | solution.py:11
  57.8 0.1 fusion
  57.8 1.3 %assemble.1 = (bf16[4608,256]{1,0:T(8,128)(2,1)S(1)}, bf16[2304,256]{1,0:T(8,128)(2,1)S(1)}) custom-call(s32[2]{0:T(128)S(1)} %pad_add_fusion.refs_0_.place, bf16[9,512,128]{2,1,0:T(8,128)(2,1)S(1)} %copy-done, bf16[4,576,128]{2,1,0:T(8,128)(2,1)S(1)} %pad_maximum_fusion.1.refs_2_, bf16[4,576,128]{2,1,0:T(8,128)(2,1)S(1)} %get-tuple-element.73.refs_3_, ...), custom_call_target="tpu_custom_call" | custom-call | flops 2001048576 | bytes 1048576 | tf_op jit(solution)/shard_map/assemble/pallas_call | solution.py:276
  59.1 0.0 collective-permute-done.10.refs_5_
  59.1 0.0 collective-permute-done.9.refs_4_
  59.1 3.1 %outer.1 = (f32[1024,256]{1,0:T(8,128)S(1)}, f32[1024,256]{1,0:T(8,128)S(1)}) custom-call(bf16[1056,128]{1,0:T(8,128)(2,1)S(1)} %get-tuple-element.51.refs_0_, bf16[1056,128]{1,0:T(8,128)(2,1)S(1)} %collective-permute-done.7.refs_1_, bf16[1056,128]{1,0:T(8,128)(2,1)S(1)} %collective-permute-done.8.refs_2_, ...), custom_call_target="tpu_custom_call" | custom-call | flops 2001048576 | bytes 1048576 | tf_op jit(solution)/shard_map/outer/pallas_call | solution.py:276
  62.3 1.7 %inner.2 = (bf16[1024,128]{1,0:T(8,128)(2,1)S(1)}, bf16[1024,128]{1,0:T(8,128)(2,1)S(1)}) custom-call(bf16[528,128]{1,0:T(8,128)(2,1)S(1)} %get-tuple-element.46.refs_0_, bf16[528,128]{1,0:T(8,128)(2,1)S(1)} %collective-permute-done.1.refs_1_, bf16[528,128]{1,0:T(8,128)(2,1)S(1)} %collective-permute-done.2.refs_2_, ...), custom_call_target="tpu_custom_call" | custom-call | flops 9001048064 | bytes 1048576 | tf_op jit(solution)/shard_map/inner/pallas_call | solution.py:276
  64.0 0.1 collective-permute-start.19
  64.0 0.0 collective-permute-done.4.refs_1_
  64.0 2.6 %collective-permute-done.5.refs_2_ = bf16[528,128]{1,0:T(8,128)(2,1)S(1)} collective-permute-done((bf16[528,128]{1,0:T(8,128)(2,1)S(1)}, bf16[528,128]{1,0:T(8,128)(2,1)S(1)}, u32[]{:S(2)}, u32[]{:S(2)}) %collective-permute-start.5) | collective-permute-done | bytes 135200 | tf_op jit(solution)/shard_map/ppermute | solution.py:11
  66.7 0.0 collective-permute-done.6.refs_3_
  66.7 1.5 %inner.3 = (bf16[1024,128]{1,0:T(8,128)(2,1)S(1)}, bf16[1024,128]{1,0:T(8,128)(2,1)S(1)}) custom-call(bf16[528,128]{1,0:T(8,128)(2,1)S(1)} %get-tuple-element.63.refs_0_, bf16[528,128]{1,0:T(8,128)(2,1)S(1)} %collective-permute-done.4.refs_1_, bf16[528,128]{1,0:T(8,128)(2,1)S(1)} %collective-permute-done.5.refs_2_, ...), custom_call_target="tpu_custom_call" | custom-call | flops 9001048064 | bytes 1048576 | tf_op jit(solution)/shard_map/inner/pallas_call | solution.py:276
  68.2 2.6 %collective-permute-start.20 = (bf16[1024,128]{1,0:T(8,128)(2,1)S(1)}, bf16[1024,128]{1,0:T(8,128)(2,1)S(1)}, u32[]{:S(2)}, u32[]{:S(2)}) collective-permute-start(bf16[1024,128]{1,0:T(8,128)(2,1)S(1)} %get-tuple-element.71), channel_id=1, source_target_pairs={{0,1},{1,0},{2,3},{3,2},{4,5},{5,4},{6,7},{7,6},{8,9},{9,8},{10,11... | collective-permute-start | bytes 786440 | tf_op jit(solution)/shard_map/ppermute | solution.py:11
  70.8 0.2 copy.12
  71.0 2.2 %collective-permute-done.19 = bf16[1024,128]{1,0:T(8,128)(2,1)S(1)} collective-permute-done((bf16[1024,128]{1,0:T(8,128)(2,1)S(1)}, bf16[1024,128]{1,0:T(8,128)(2,1)S(1)}, u32[]{:S(2)}, u32[]{:S(2)}) %collective-permute-start.19) | collective-permute-done | bytes 262176 | tf_op jit(solution)/shard_map/ppermute | solution.py:11
  73.2 0.2 copy.13
  73.4 1.4 %home.2 = bf16[128,4,512]{2,1,0:T(4,128)(2,1)} custom-call(s32[2]{0:T(128)S(1)} %pad_add_fusion.refs_0_.place, bf16[128,4,256]{2,1,0:T(4,128)(2,1)S(1)} %bitcast.19, bf16[128,4,256]{2,1,0:T(4,128)(2,1)S(1)} %bitcast.21), custom_call_target="tpu_custom_call" | custom-call | flops 1048576 | bytes 1048576 | tf_op jit(solution)/shard_map/home/pallas_call | solution.py:276
  74.8 0.2 copy.14
  75.0 2.8 %collective-permute-done.20 = bf16[1024,128]{1,0:T(8,128)(2,1)S(1)} collective-permute-done((bf16[1024,128]{1,0:T(8,128)(2,1)S(1)}, bf16[1024,128]{1,0:T(8,128)(2,1)S(1)}, u32[]{:S(2)}, u32[]{:S(2)}) %collective-permute-start.20) | collective-permute-done | bytes 262176 | tf_op jit(solution)/shard_map/ppermute | solution.py:11
  77.8 0.2 copy.15
  78.0 1.4 %home.3 = bf16[128,4,512]{2,1,0:T(4,128)(2,1)} custom-call(s32[2]{0:T(128)S(1)} %pad_add_fusion.refs_0_.place, bf16[128,4,256]{2,1,0:T(4,128)(2,1)S(1)} %bitcast.18, bf16[128,4,256]{2,1,0:T(4,128)(2,1)S(1)} %bitcast.20), custom_call_target="tpu_custom_call" | custom-call | flops 1048576 | bytes 1048576 | tf_op jit(solution)/shard_map/home/pallas_call | solution.py:276
  (14 shorter events, 0.1 us)
Async XLA Ops:
  0.6 7.8 %copy-start.2 = (bf16[128,4,512]{2,1,0:T(4,128)(2,1)S(1)}, bf16[128,4,512]{2,1,0:T(4,128)(2,1)}, u32[]{:S(2)}) copy-start(bf16[128,4,512]{2,1,0:T(4,128)(2,1)} %param.4) | copy-start | bytes 1572868
  0.6 8.3 %copy-start.1 = (bf16[128]{0:T(256)(128)(2,1)S(1)}, bf16[128]{0:T(256)(128)(2,1)}, u32[]{:S(2)}) copy-start(bf16[128]{0:T(256)(128)(2,1)} %param.6) | copy-start | bytes 772
  1.6 10.7 %collective-permute-start.14 = (bf16[288,128]{1,0:T(8,128)(2,1)S(1)}, bf16[288,128]{1,0:T(8,128)(2,1)S(1)}, u32[]{:S(2)}, u32[]{:S(2)}) collective-permute-start(bf16[288,128]{1,0:T(8,128)(2,1)S(1)} %bitcast.39), channel_id=1, source_target_pairs={{0,2},{1,3},{2,0},{3,1},{4,6},{5,7},{6,4},{7,5},{8,10},{9,11},{10,... | collective-permute-start | bytes 221192 | tf_op jit(solution)/shard_map/ppermute | solution.py:11
  5.6 6.7 %collective-permute-start.15 = (bf16[288,128]{1,0:T(8,128)(2,1)S(1)}, bf16[288,128]{1,0:T(8,128)(2,1)S(1)}, u32[]{:S(2)}, u32[]{:S(2)}) collective-permute-start(bf16[288,128]{1,0:T(8,128)(2,1)S(1)} %bitcast.40), channel_id=1, source_target_pairs={{0,3},{1,2},{2,1},{3,0},{4,7},{5,6},{6,5},{7,4},{8,11},{9,10},{10,... | collective-permute-start | bytes 221192 | tf_op jit(solution)/shard_map/ppermute | solution.py:11
  9.0 3.2 %copy-start = (bf16[9,512,128]{2,1,0:T(8,128)(2,1)S(1)}, bf16[9,512,128]{2,1,0:T(8,128)(2,1)}, u32[]{:S(2)}) copy-start(bf16[9,512,128]{2,1,0:T(8,128)(2,1)} %refs_1_.1) | copy-start | bytes 3538948
  9.7 17.2 %collective-permute-start = (bf16[1056,128]{1,0:T(8,128)(2,1)S(1)}, bf16[1056,128]{1,0:T(8,128)(2,1)S(1)}, u32[]{:S(2)}, u32[]{:S(2)}) collective-permute-start(bf16[1056,128]{1,0:T(8,128)(2,1)S(1)} %get-tuple-element.37), channel_id=1, source_target_pairs={{0,3},{1,2},{2,1},{3,0},{4,7},{5,6},{6,5},{7,4},{8,11},{9,10},{10,... | collective-permute-start | bytes 811016 | tf_op jit(solution)/shard_map/ppermute | solution.py:11
  12.2 10.2 %collective-permute-start.11 = (bf16[576,128]{1,0:T(8,128)(2,1)S(1)}, bf16[576,128]{1,0:T(8,128)(2,1)S(1)}, u32[]{:S(2)}, u32[]{:S(2)}) collective-permute-start(bf16[576,128]{1,0:T(8,128)(2,1)S(1)} %bitcast.38), channel_id=1, source_target_pairs={{0,1},{1,0},{2,3},{3,2},{4,5},{5,4},{6,7},{7,6},{8,9},{9,8},{10,11... | collective-permute-start | bytes 442376 | tf_op jit(solution)/shard_map/ppermute | solution.py:11
  12.3 13.9 %collective-permute-start.16 = (bf16[1,576,128]{2,1,0:T(8,128)(2,1)S(1)}, bf16[1,576,128]{2,1,0:T(8,128)(2,1)S(1)}, u32[]{:S(2)}, u32[]{:S(2)}) collective-permute-start(bf16[1,576,128]{2,1,0:T(8,128)(2,1)S(1)} %maximum_bitcast_fusion), channel_id=1, source_target_pairs={{0,8},{4,12},{8,0},{12,4},{16,24},{20,28},{24,16},{28,20},{1,9},{5... | collective-permute-start | bytes 442376 | tf_op jit(solution)/shard_map/ppermute | solution.py:11
  22.5 6.6 %collective-permute-start.12 = (bf16[1,576,128]{2,1,0:T(8,128)(2,1)S(1)}, bf16[1,576,128]{2,1,0:T(8,128)(2,1)S(1)}, u32[]{:S(2)}, u32[]{:S(2)}) collective-permute-start(bf16[1,576,128]{2,1,0:T(8,128)(2,1)S(1)} %bitcast.33), channel_id=1, source_target_pairs={{0,16},{4,20},{8,24},{12,28},{16,0},{20,4},{24,8},{28,12},{1,17},{... | collective-permute-start | bytes 442376 | tf_op jit(solution)/shard_map/ppermute | solution.py:11
  24.0 14.7 %collective-permute-start.7 = (bf16[1056,128]{1,0:T(8,128)(2,1)S(1)}, bf16[1056,128]{1,0:T(8,128)(2,1)S(1)}, u32[]{:S(2)}, u32[]{:S(2)}) collective-permute-start(bf16[1056,128]{1,0:T(8,128)(2,1)S(1)} %get-tuple-element.37), channel_id=1, source_target_pairs={{0,1},{1,0},{2,3},{3,2},{4,5},{5,4},{6,7},{7,6},{8,9},{9,8},{10,11... | collective-permute-start | bytes 811016 | tf_op jit(solution)/shard_map/ppermute | solution.py:11
  24.6 15.3 %collective-permute-start.8 = (bf16[1056,128]{1,0:T(8,128)(2,1)S(1)}, bf16[1056,128]{1,0:T(8,128)(2,1)S(1)}, u32[]{:S(2)}, u32[]{:S(2)}) collective-permute-start(bf16[1056,128]{1,0:T(8,128)(2,1)S(1)} %get-tuple-element.51.refs_0_), channel_id=1, source_target_pairs={{0,2},{1,3},{2,0},{3,1},{4,6},{5,7},{6,4},{7,5},{8,10},{9,11},{10,... | collective-permute-start | bytes 811016 | tf_op jit(solution)/shard_map/ppermute | solution.py:11
  26.3 23.9 %collective-permute-start.17 = (bf16[2,576,128]{2,1,0:T(8,128)(2,1)S(1)}, bf16[2,576,128]{2,1,0:T(8,128)(2,1)S(1)}, u32[]{:S(2)}, u32[]{:S(2)}) collective-permute-start(bf16[2,576,128]{2,1,0:T(8,128)(2,1)S(1)} %pad_maximum_fusion.4), channel_id=1, source_target_pairs={{0,16},{4,20},{8,24},{12,28},{16,0},{20,4},{24,8},{28,12},{1,17},{... | collective-permute-start | bytes 884744 | tf_op jit(solution)/shard_map/ppermute | solution.py:11
  29.1 21.2 %collective-permute-start.13 = (bf16[2,576,128]{2,1,0:T(8,128)(2,1)S(1)}, bf16[2,576,128]{2,1,0:T(8,128)(2,1)S(1)}, u32[]{:S(2)}, u32[]{:S(2)}) collective-permute-start(bf16[2,576,128]{2,1,0:T(8,128)(2,1)S(1)} %pad_maximum_fusion.3), channel_id=1, source_target_pairs={{0,8},{4,12},{8,0},{12,4},{16,24},{20,28},{24,16},{28,20},{1,9},{5... | collective-permute-start | bytes 884744 | tf_op jit(solution)/shard_map/ppermute | solution.py:11
  31.2 11.7 %collective-permute-start.1 = (bf16[528,128]{1,0:T(8,128)(2,1)S(1)}, bf16[528,128]{1,0:T(8,128)(2,1)S(1)}, u32[]{:S(2)}, u32[]{:S(2)}) collective-permute-start(bf16[528,128]{1,0:T(8,128)(2,1)S(1)} %get-tuple-element.40), channel_id=1, source_target_pairs={{0,1},{1,0},{2,3},{3,2},{4,5},{5,4},{6,7},{7,6},{8,9},{9,8},{10,11... | collective-permute-start | bytes 405512 | tf_op jit(solution)/shard_map/ppermute | solution.py:11
  38.7 10.1 %collective-permute-start.2 = (bf16[528,128]{1,0:T(8,128)(2,1)S(1)}, bf16[528,128]{1,0:T(8,128)(2,1)S(1)}, u32[]{:S(2)}, u32[]{:S(2)}) collective-permute-start(bf16[528,128]{1,0:T(8,128)(2,1)S(1)} %get-tuple-element.46.refs_0_), channel_id=1, source_target_pairs={{0,2},{1,3},{2,0},{3,1},{4,6},{5,7},{6,4},{7,5},{8,10},{9,11},{10,... | collective-permute-start | bytes 405512 | tf_op jit(solution)/shard_map/ppermute | solution.py:11
  39.9 10.3 %collective-permute-start.3 = (bf16[528,128]{1,0:T(8,128)(2,1)S(1)}, bf16[528,128]{1,0:T(8,128)(2,1)S(1)}, u32[]{:S(2)}, u32[]{:S(2)}) collective-permute-start(bf16[528,128]{1,0:T(8,128)(2,1)S(1)} %get-tuple-element.40), channel_id=1, source_target_pairs={{0,3},{1,2},{2,1},{3,0},{4,7},{5,6},{6,5},{7,4},{8,11},{9,10},{10,... | collective-permute-start | bytes 405512 | tf_op jit(solution)/shard_map/ppermute | solution.py:11
  43.0 16.2 %collective-permute-start.10 = (bf16[2112,128]{1,0:T(8,128)(2,1)S(1)}, bf16[2112,128]{1,0:T(8,128)(2,1)S(1)}, u32[]{:S(2)}, u32[]{:S(2)}) collective-permute-start(bf16[2112,128]{1,0:T(8,128)(2,1)S(1)} %get-tuple-element.56), channel_id=1, source_target_pairs={{4,0},{8,4},{12,8},{16,12},{20,16},{24,20},{28,24},{5,1},{9,5},{13... | collective-permute-start | bytes 1622024 | tf_op jit(solution)/shard_map/ppermute | solution.py:18
  48.8 10.3 %collective-permute-start.9 = (bf16[2112,128]{1,0:T(8,128)(2,1)S(1)}, bf16[2112,128]{1,0:T(8,128)(2,1)S(1)}, u32[]{:S(2)}, u32[]{:S(2)}) collective-permute-start(bf16[2112,128]{1,0:T(8,128)(2,1)S(1)} %get-tuple-element.55), channel_id=1, source_target_pairs={{0,4},{4,8},{8,12},{12,16},{16,20},{20,24},{24,28},{1,5},{5,9},{9,... | collective-permute-start | bytes 1622024 | tf_op jit(solution)/shard_map/ppermute | solution.py:18
  50.4 6.0 %collective-permute-start.18 = (bf16[4,1152,128]{2,1,0:T(8,128)(2,1)S(1)}, bf16[4,1152,128]{2,1,0:T(8,128)(2,1)S(1)}, u32[]{:S(2)}, u32[]{:S(2)}) collective-permute-start(bf16[4,1152,128]{2,1,0:T(8,128)(2,1)S(1)} %pad_maximum_fusion), channel_id=1, source_target_pairs={{0,4},{4,0},{8,12},{12,8},{16,20},{20,16},{24,28},{28,24},{1,5},{5... | collective-permute-start | bytes 3538952 | tf_op jit(solution)/shard_map/ppermute | solution.py:11
  53.3 10.7 %collective-permute-start.4 = (bf16[528,128]{1,0:T(8,128)(2,1)S(1)}, bf16[528,128]{1,0:T(8,128)(2,1)S(1)}, u32[]{:S(2)}, u32[]{:S(2)}) collective-permute-start(bf16[528,128]{1,0:T(8,128)(2,1)S(1)} %get-tuple-element.45), channel_id=1, source_target_pairs={{0,1},{1,0},{2,3},{3,2},{4,5},{5,4},{6,7},{7,6},{8,9},{9,8},{10,11... | collective-permute-start | bytes 405512 | tf_op jit(solution)/shard_map/ppermute | solution.py:11
  53.4 13.3 %collective-permute-start.5 = (bf16[528,128]{1,0:T(8,128)(2,1)S(1)}, bf16[528,128]{1,0:T(8,128)(2,1)S(1)}, u32[]{:S(2)}, u32[]{:S(2)}) collective-permute-start(bf16[528,128]{1,0:T(8,128)(2,1)S(1)} %get-tuple-element.63.refs_0_), channel_id=1, source_target_pairs={{0,2},{1,3},{2,0},{3,1},{4,6},{5,7},{6,4},{7,5},{8,10},{9,11},{10,... | collective-permute-start | bytes 405512 | tf_op jit(solution)/shard_map/ppermute | solution.py:11
  56.4 10.3 %collective-permute-start.6 = (bf16[528,128]{1,0:T(8,128)(2,1)S(1)}, bf16[528,128]{1,0:T(8,128)(2,1)S(1)}, u32[]{:S(2)}, u32[]{:S(2)}) collective-permute-start(bf16[528,128]{1,0:T(8,128)(2,1)S(1)} %get-tuple-element.45), channel_id=1, source_target_pairs={{0,3},{1,2},{2,1},{3,0},{4,7},{5,6},{6,5},{7,4},{8,11},{9,10},{10,... | collective-permute-start | bytes 405512 | tf_op jit(solution)/shard_map/ppermute | solution.py:11
  64.0 9.2 %collective-permute-start.19 = (bf16[1024,128]{1,0:T(8,128)(2,1)S(1)}, bf16[1024,128]{1,0:T(8,128)(2,1)S(1)}, u32[]{:S(2)}, u32[]{:S(2)}) collective-permute-start(bf16[1024,128]{1,0:T(8,128)(2,1)S(1)} %get-tuple-element.69), channel_id=1, source_target_pairs={{0,1},{1,0},{2,3},{3,2},{4,5},{5,4},{6,7},{7,6},{8,9},{9,8},{10,11... | collective-permute-start | bytes 786440 | tf_op jit(solution)/shard_map/ppermute | solution.py:11
  68.2 9.7 %collective-permute-start.20 = (bf16[1024,128]{1,0:T(8,128)(2,1)S(1)}, bf16[1024,128]{1,0:T(8,128)(2,1)S(1)}, u32[]{:S(2)}, u32[]{:S(2)}) collective-permute-start(bf16[1024,128]{1,0:T(8,128)(2,1)S(1)} %get-tuple-element.71), channel_id=1, source_target_pairs={{0,1},{1,0},{2,3},{3,2},{4,5},{5,4},{6,7},{7,6},{8,9},{9,8},{10,11... | collective-permute-start | bytes 786440 | tf_op jit(solution)/shard_map/ppermute | solution.py:11

commit v15 on v14

--- a/solution.py
+++ b/solution.py
@@ -373,9 +373,9 @@
     sent = cut(place, after([upstream, image], pieces[3]), bias[None], inner[0], 25)
     pieces = after(pieces, sent)
     first = exchange(*sent)
-    sent = cut(place, after([upstream, image], first[1:]), bias[None], inner[1], 18)
+    sent = cut(place, after([upstream, image], first[1:]), bias[None], inner[1], 9)
     first = after(first, sent)
-    second = exchange(*sent)
+    late = sent
 
     steps = halving(bands)[:-1]
     near, near_order = gather(near, steps)
@@ -383,6 +383,8 @@
     near, across = after((near, across), pieces[1])
     there = swap(jnp.concatenate([near, across], axis=1), "band", 1)
     held = [near, there[:, : near.shape[1]], across, there[:, near.shape[1] :]]
+    second = [late[0], None, swap(late[0], "chan", 2), swap(late[1], "chan", 3)]
+    second[1] = swap(after(late[1], held), "chan", 1)
     filters = kernel(
         lambda *refs: assemble_kernel((near_order, across_order), *refs),
         [(taps * outs, 2 * local), (taps * 2 * local, 2 * local)],
@@ -410,7 +412,7 @@
     )
     lines = jnp.concatenate([p[width + 2 : width + 3] for p in pieces[:2]]).astype(jnp.float32)
     marks = [[], []]
-    marks[0].append(token(first, 2))
+    marks[0].append(token(first, 9))
     kept, came = [], []
     for which in range(2):
         mine, other = kernel(

time: 79.7 us -> 79 us (level)
  waiting for transfers between devices: 33.9 us -> 31.9 us
  starting transfers between devices: 28.1 us -> 29.5 us
    ppermute x19, waiting for transfers between devices: 33.9 us -> 31.9 us  [swap(): return lax.ppermute(value, axis, [(j, j ^ step) for j in range(size)])]
    ppermute x19, starting transfers between devices: 25.5 us -> 26.8 us  [swap(): return lax.ppermute(value, axis, [(j, j ^ step) for j in range(size)])]
  transfers between devices with their start and end apart: 21 -> 21, of which waited for: 9 -> 10; matrix products, arithmetic and copies ran while one was open for 4% -> 4% of each run, Pallas kernels for 14% -> 14%
where the time goes in v15:
time: 79 us; the launch traced here: 78.7 us
  waiting for transfers between devices  31.9 us (40%)
  starting transfers between devices  29.5 us (37%)
  Pallas kernels  12.5 us (16%)
  local copies, waits for them, and re-layouts  3.69 us (5%)
  between operations  0.89 us (1%)
    ppermute x19, waiting for transfers between devices, swap(): return lax.ppermute(value, axis, [(j, j ^ step) for j in range(size)])  31.9 us
    ppermute x19, starting transfers between devices, swap(): return lax.ppermute(value, axis, [(j, j ^ step) for j in range(size)])  26.8 us
    pallas_call x11, Pallas kernels, kernel(): pl.pallas_call(body, out_shape=[jax.ShapeDtypeStruct(s, kind) for s in sh...  12.5 us
    ppermute x2, starting transfers between devices, neighbours(): return (lax.ppermute(last, 'band', up), lax.ppermute(first, 'band', down))  2.6 us
    unnamed x8, local copies, waits for them, and re-layouts  1.89 us
  transfers between devices with their start and end apart: 21, of which 10 were waited for; matrix products, arithmetic and copies ran while one was open for 4% of the time, Pallas kernels for 14%

profile of v15, /device:TPU:0, one launch (start us, length us, event | category | flops | bytes accessed | tf_op | source)
XLA Modules:
  0.0 78.7 jit_solution(6023961750382364747)
XLA Ops:
  0.7 1.0 %constant_dynamic-slice_fusion = bf16[9,32,128]{2,1,0:T(8,128)(2,1)S(1)} fusion(bf16[9,512,128]{2,1,0:T(8,128)(2,1)} %refs_1_.1, s32[]{:T(128)S(6)} %select_n.7), kind=kLoop, calls=%fused_computation.8 | loop fusion | bytes 147460 | tf_op jit(solution)/shard_map/dynamic_slice | solution.py:364
  1.6 5.0 %collective-permute-start.8 = (bf16[288,128]{1,0:T(8,128)(2,1)S(1)}, bf16[288,128]{1,0:T(8,128)(2,1)S(1)}, u32[]{:S(2)}, u32[]{:S(2)}) collective-permute-start(bf16[288,128]{1,0:T(8,128)(2,1)S(1)} %bitcast.39), channel_id=1, source_target_pairs={{0,3},{1,2},{2,1},{3,0},{4,7},{5,6},{6,5},{7,4},{8,11},{9,10},{10,... | collective-permute-start | bytes 221192 | tf_op jit(solution)/shard_map/ppermute | solution.py:11
  6.7 0.0 collective-permute-start.7
  6.7 1.5 %copy.6 = bf16[128,4,512]{0,2,1:T(8,128)(2,1)S(1)} copy(bf16[128,4,512]{2,1,0:T(4,128)(2,1)} %param.7) | data formatting | bytes 1048576 | tf_op args[3]
  8.1 0.4 copy.7
  8.5 0.1 pad_add_fusion.refs_0_.place
  8.6 0.7 cut.3
  9.3 2.0 %collective-permute-start = (bf16[1056,128]{1,0:T(8,128)(2,1)S(1)}, bf16[1056,128]{1,0:T(8,128)(2,1)S(1)}, u32[]{:S(2)}, u32[]{:S(2)}) collective-permute-start(bf16[1056,128]{1,0:T(8,128)(2,1)S(1)} %get-tuple-element.38), channel_id=1, source_target_pairs={{0,3},{1,2},{2,1},{3,0},{4,7},{5,6},{6,5},{7,4},{8,11},{9,10},{10,... | collective-permute-start | bytes 811016 | tf_op jit(solution)/shard_map/ppermute | solution.py:11
  11.3 1.6 %collective-permute-start.4 = (bf16[576,128]{1,0:T(8,128)(2,1)S(1)}, bf16[576,128]{1,0:T(8,128)(2,1)S(1)}, u32[]{:S(2)}, u32[]{:S(2)}) collective-permute-start(bf16[576,128]{1,0:T(8,128)(2,1)S(1)} %bitcast.38), channel_id=1, source_target_pairs={{0,1},{1,0},{2,3},{3,2},{4,5},{5,4},{6,7},{7,6},{8,9},{9,8},{10,11... | collective-permute-start | bytes 442376 | tf_op jit(solution)/shard_map/ppermute | solution.py:11
  13.0 0.0 collective-permute-done.8
  13.0 0.3 collective-permute-done.7
  13.2 1.6 %collective-permute-start.9 = (bf16[1,576,128]{2,1,0:T(8,128)(2,1)S(1)}, bf16[1,576,128]{2,1,0:T(8,128)(2,1)S(1)}, u32[]{:S(2)}, u32[]{:S(2)}) collective-permute-start(bf16[1,576,128]{2,1,0:T(8,128)(2,1)S(1)} %maximum_bitcast_fusion), channel_id=1, source_target_pairs={{0,8},{4,12},{8,0},{12,4},{16,24},{20,28},{24,16},{28,20},{1,9},{5... | collective-permute-start | bytes 442376 | tf_op jit(solution)/shard_map/ppermute | solution.py:11
  14.8 7.3 %collective-permute-done.4 = bf16[576,128]{1,0:T(8,128)(2,1)S(1)} collective-permute-done((bf16[576,128]{1,0:T(8,128)(2,1)S(1)}, bf16[576,128]{1,0:T(8,128)(2,1)S(1)}, u32[]{:S(2)}, u32[]{:S(2)}) %collective-permute-start.4) | collective-permute-done | bytes 147488 | tf_op jit(solution)/shard_map/ppermute | solution.py:11
  22.1 1.5 %collective-permute-start.5 = (bf16[1,576,128]{2,1,0:T(8,128)(2,1)S(1)}, bf16[1,576,128]{2,1,0:T(8,128)(2,1)S(1)}, u32[]{:S(2)}, u32[]{:S(2)}) collective-permute-start(bf16[1,576,128]{2,1,0:T(8,128)(2,1)S(1)} %bitcast.33), channel_id=1, source_target_pairs={{0,16},{4,20},{8,24},{12,28},{16,0},{20,4},{24,8},{28,12},{1,17},{... | collective-permute-start | bytes 442376 | tf_op jit(solution)/shard_map/ppermute | solution.py:11
  23.6 0.2 collective-permute-start.11
  23.7 2.9 %collective-permute-start.12 = (bf16[1056,128]{1,0:T(8,128)(2,1)S(1)}, bf16[1056,128]{1,0:T(8,128)(2,1)S(1)}, u32[]{:S(2)}, u32[]{:S(2)}) collective-permute-start(bf16[1056,128]{1,0:T(8,128)(2,1)S(1)} %get-tuple-element.56.refs_0_), channel_id=1, source_target_pairs={{0,2},{1,3},{2,0},{3,1},{4,6},{5,7},{6,4},{7,5},{8,10},{9,11},{10,... | collective-permute-start | bytes 811016 | tf_op jit(solution)/shard_map/ppermute | solution.py:11
  26.6 0.0 collective-permute-done.9
  26.7 0.6 collective-permute-start.10
  27.2 0.0 collective-permute-done.refs_3_
  27.2 0.2 collective-permute-done.5
  27.5 1.6 %collective-permute-start.6 = (bf16[2,576,128]{2,1,0:T(8,128)(2,1)S(1)}, bf16[2,576,128]{2,1,0:T(8,128)(2,1)S(1)}, u32[]{:S(2)}, u32[]{:S(2)}) collective-permute-start(bf16[2,576,128]{2,1,0:T(8,128)(2,1)S(1)} %pad_maximum_fusion.3), channel_id=1, source_target_pairs={{0,8},{4,12},{8,0},{12,4},{16,24},{20,28},{24,16},{28,20},{1,9},{5... | collective-permute-start | bytes 884744 | tf_op jit(solution)/shard_map/ppermute | solution.py:11
  29.1 0.6 cut.4
  29.7 0.1 collective-permute-start.1
  29.8 8.8 %collective-permute-done.11.refs_1_ = bf16[1056,128]{1,0:T(8,128)(2,1)S(1)} collective-permute-done((bf16[1056,128]{1,0:T(8,128)(2,1)S(1)}, bf16[1056,128]{1,0:T(8,128)(2,1)S(1)}, u32[]{:S(2)}, u32[]{:S(2)}) %collective-permute-start.11) | collective-permute-done | bytes 270368 | tf_op jit(solution)/shard_map/ppermute | solution.py:11
  38.6 0.0 collective-permute-start.2
  38.6 0.0 collective-permute-done.12.refs_2_
  38.6 2.8 %collective-permute-start.3 = (bf16[528,128]{1,0:T(8,128)(2,1)S(1)}, bf16[528,128]{1,0:T(8,128)(2,1)S(1)}, u32[]{:S(2)}, u32[]{:S(2)}) collective-permute-start(bf16[528,128]{1,0:T(8,128)(2,1)S(1)} %get-tuple-element.41), channel_id=1, source_target_pairs={{0,3},{1,2},{2,1},{3,0},{4,7},{5,6},{6,5},{7,4},{8,11},{9,10},{10,... | collective-permute-start | bytes 405512 | tf_op jit(solution)/shard_map/ppermute | solution.py:11
  41.4 0.1 rim.1
  41.5 0.0 collective-permute-done.1.refs_1_
  41.5 1.3 %collective-permute-start.17 = (bf16[2112,128]{1,0:T(8,128)(2,1)S(1)}, bf16[2112,128]{1,0:T(8,128)(2,1)S(1)}, u32[]{:S(2)}, u32[]{:S(2)}) collective-permute-start(bf16[2112,128]{1,0:T(8,128)(2,1)S(1)} %get-tuple-element.59), channel_id=1, source_target_pairs={{0,4},{4,8},{8,12},{12,16},{16,20},{20,24},{24,28},{1,5},{5,9},{9,... | collective-permute-start | bytes 1622024 | tf_op jit(solution)/shard_map/ppermute | solution.py:18
  42.8 6.5 %collective-permute-done.2.refs_2_ = bf16[528,128]{1,0:T(8,128)(2,1)S(1)} collective-permute-done((bf16[528,128]{1,0:T(8,128)(2,1)S(1)}, bf16[528,128]{1,0:T(8,128)(2,1)S(1)}, u32[]{:S(2)}, u32[]{:S(2)}) %collective-permute-start.2) | collective-permute-done | bytes 135200 | tf_op jit(solution)/shard_map/ppermute | solution.py:11
  49.3 1.3 %collective-permute-start.18 = (bf16[2112,128]{1,0:T(8,128)(2,1)S(1)}, bf16[2112,128]{1,0:T(8,128)(2,1)S(1)}, u32[]{:S(2)}, u32[]{:S(2)}) collective-permute-start(bf16[2112,128]{1,0:T(8,128)(2,1)S(1)} %get-tuple-element.60), channel_id=1, source_target_pairs={{4,0},{8,4},{12,8},{16,12},{20,16},{24,20},{28,24},{5,1},{9,5},{13... | collective-permute-start | bytes 1622024 | tf_op jit(solution)/shard_map/ppermute | solution.py:18
  50.6 0.0 collective-permute-done.3.refs_3_
  50.6 0.0 collective-permute-done.10
  50.6 0.1 pad_maximum_fusion.2.refs_4_
  50.7 0.0 collective-permute-done.6
  50.7 0.1 pad_maximum_fusion.1.refs_2_
  50.7 0.1 pad_maximum_fusion
  50.8 1.2 %collective-permute-start.13 = (bf16[4,1152,128]{2,1,0:T(8,128)(2,1)S(1)}, bf16[4,1152,128]{2,1,0:T(8,128)(2,1)S(1)}, u32[]{:S(2)}, u32[]{:S(2)}) collective-permute-start(bf16[4,1152,128]{2,1,0:T(8,128)(2,1)S(1)} %pad_maximum_fusion), channel_id=1, source_target_pairs={{0,4},{4,0},{8,12},{12,8},{16,20},{20,16},{24,28},{28,24},{1,5},{5... | collective-permute-start | bytes 3538952 | tf_op jit(solution)/shard_map/ppermute | solution.py:11
  52.0 0.6 cut.5
  52.6 0.1 collective-permute-start.15
  52.7 1.9 %collective-permute-start.16 = (bf16[528,128]{1,0:T(8,128)(2,1)S(1)}, bf16[528,128]{1,0:T(8,128)(2,1)S(1)}, u32[]{:S(2)}, u32[]{:S(2)}) collective-permute-start(bf16[528,128]{1,0:T(8,128)(2,1)S(1)} %get-tuple-element.51), channel_id=1, source_target_pairs={{0,3},{1,2},{2,1},{3,0},{4,7},{5,6},{6,5},{7,4},{8,11},{9,10},{10,... | collective-permute-start | bytes 405512 | tf_op jit(solution)/shard_map/ppermute | solution.py:11
  54.7 0.1 collective-permute-done.13
  54.8 0.1 fusion
  54.9 1.5 %collective-permute-start.14 = (bf16[528,128]{1,0:T(8,128)(2,1)S(1)}, bf16[528,128]{1,0:T(8,128)(2,1)S(1)}, u32[]{:S(2)}, u32[]{:S(2)}) collective-permute-start(bf16[528,128]{1,0:T(8,128)(2,1)S(1)} %get-tuple-element.51), channel_id=1, source_target_pairs={{0,1},{1,0},{2,3},{3,2},{4,5},{5,4},{6,7},{7,6},{8,9},{9,8},{10,11... | collective-permute-start | bytes 405512 | tf_op jit(solution)/shard_map/ppermute | solution.py:11
  56.4 1.3 %assemble.1 = (bf16[4608,256]{1,0:T(8,128)(2,1)S(1)}, bf16[2304,256]{1,0:T(8,128)(2,1)S(1)}) custom-call(s32[2]{0:T(128)S(1)} %pad_add_fusion.refs_0_.place, bf16[9,512,128]{2,1,0:T(8,128)(2,1)S(1)} %copy-done, bf16[4,576,128]{2,1,0:T(8,128)(2,1)S(1)} %pad_maximum_fusion.1.refs_2_, bf16[4,576,128]{2,1,0:T(8,128)(2,1)S(1)} %get-tuple-element.75.refs_3_, ...), custom_call_target="tpu_custom_call" | custom-call | flops 2001048576 | bytes 1048576 | tf_op jit(solution)/shard_map/assemble/pallas_call | solution.py:276
  57.6 0.0 collective-permute-done.17.refs_4_
  57.6 0.0 collective-permute-done.18.refs_5_
  57.7 3.1 %outer.1 = (f32[1024,256]{1,0:T(8,128)S(1)}, f32[1024,256]{1,0:T(8,128)S(1)}) custom-call(bf16[1056,128]{1,0:T(8,128)(2,1)S(1)} %get-tuple-element.56.refs_0_, bf16[1056,128]{1,0:T(8,128)(2,1)S(1)} %collective-permute-done.11.refs_1_, bf16[1056,128]{1,0:T(8,128)(2,1)S(1)} %collective-permute-done.12.refs_2_, ...), custom_call_target="tpu_custom_call" | custom-call | flops 2001048576 | bytes 1048576 | tf_op jit(solution)/shard_map/outer/pallas_call | solution.py:276
  60.8 1.7 %inner.2 = (bf16[1024,128]{1,0:T(8,128)(2,1)S(1)}, bf16[1024,128]{1,0:T(8,128)(2,1)S(1)}) custom-call(bf16[528,128]{1,0:T(8,128)(2,1)S(1)} %get-tuple-element.52.refs_0_, bf16[528,128]{1,0:T(8,128)(2,1)S(1)} %collective-permute-done.1.refs_1_, bf16[528,128]{1,0:T(8,128)(2,1)S(1)} %collective-permute-done.2.refs_2_, ...), custom_call_target="tpu_custom_call" | custom-call | flops 9001048064 | bytes 1048576 | tf_op jit(solution)/shard_map/inner/pallas_call | solution.py:276
  62.5 0.7 collective-permute-start.19
  63.1 1.4 %collective-permute-done.15.refs_2_ = bf16[528,128]{1,0:T(8,128)(2,1)S(1)} collective-permute-done((bf16[528,128]{1,0:T(8,128)(2,1)S(1)}, bf16[528,128]{1,0:T(8,128)(2,1)S(1)}, u32[]{:S(2)}, u32[]{:S(2)}) %collective-permute-start.15) | collective-permute-done | bytes 135200 | tf_op jit(solution)/shard_map/ppermute | solution.py:11
  64.5 0.0 collective-permute-done.16.refs_3_
  64.6 1.7 %collective-permute-done.14.refs_1_ = bf16[528,128]{1,0:T(8,128)(2,1)S(1)} collective-permute-done((bf16[528,128]{1,0:T(8,128)(2,1)S(1)}, bf16[528,128]{1,0:T(8,128)(2,1)S(1)}, u32[]{:S(2)}, u32[]{:S(2)}) %collective-permute-start.14) | collective-permute-done | bytes 135200 | tf_op jit(solution)/shard_map/ppermute | solution.py:11
  66.2 1.5 %inner.3 = (bf16[1024,128]{1,0:T(8,128)(2,1)S(1)}, bf16[1024,128]{1,0:T(8,128)(2,1)S(1)}) custom-call(bf16[528,128]{1,0:T(8,128)(2,1)S(1)} %get-tuple-element.65.refs_0_, bf16[528,128]{1,0:T(8,128)(2,1)S(1)} %collective-permute-done.14.refs_1_, bf16[528,128]{1,0:T(8,128)(2,1)S(1)} %collective-permute-done.15.refs_2_, ...), custom_call_target="tpu_custom_call" | custom-call | flops 9001048064 | bytes 1048576 | tf_op jit(solution)/shard_map/inner/pallas_call | solution.py:276
  67.8 1.7 %collective-permute-start.20 = (bf16[1024,128]{1,0:T(8,128)(2,1)S(1)}, bf16[1024,128]{1,0:T(8,128)(2,1)S(1)}, u32[]{:S(2)}, u32[]{:S(2)}) collective-permute-start(bf16[1024,128]{1,0:T(8,128)(2,1)S(1)} %get-tuple-element.73), channel_id=1, source_target_pairs={{0,1},{1,0},{2,3},{3,2},{4,5},{5,4},{6,7},{7,6},{8,9},{9,8},{10,11... | collective-permute-start | bytes 786440 | tf_op jit(solution)/shard_map/ppermute | solution.py:11
  69.5 0.2 copy.12
  69.7 0.8 collective-permute-done.19
  70.5 0.2 copy.13
  70.7 1.4 %home.2 = bf16[128,4,512]{2,1,0:T(4,128)(2,1)} custom-call(s32[2]{0:T(128)S(1)} %pad_add_fusion.refs_0_.place, bf16[128,4,256]{2,1,0:T(4,128)(2,1)S(1)} %bitcast.19, bf16[128,4,256]{2,1,0:T(4,128)(2,1)S(1)} %bitcast.21), custom_call_target="tpu_custom_call" | custom-call | flops 1048576 | bytes 1048576 | tf_op jit(solution)/shard_map/home/pallas_call | solution.py:276
  72.1 0.2 copy.14
  72.3 4.8 %collective-permute-done.20 = bf16[1024,128]{1,0:T(8,128)(2,1)S(1)} collective-permute-done((bf16[1024,128]{1,0:T(8,128)(2,1)S(1)}, bf16[1024,128]{1,0:T(8,128)(2,1)S(1)}, u32[]{:S(2)}, u32[]{:S(2)}) %collective-permute-start.20) | collective-permute-done | bytes 262176 | tf_op jit(solution)/shard_map/ppermute | solution.py:11
  77.1 0.2 copy.15
  77.3 1.4 %home.3 = bf16[128,4,512]{2,1,0:T(4,128)(2,1)} custom-call(s32[2]{0:T(128)S(1)} %pad_add_fusion.refs_0_.place, bf16[128,4,256]{2,1,0:T(4,128)(2,1)S(1)} %bitcast.18, bf16[128,4,256]{2,1,0:T(4,128)(2,1)S(1)} %bitcast.20), custom_call_target="tpu_custom_call" | custom-call | flops 1048576 | bytes 1048576 | tf_op jit(solution)/shard_map/home/pallas_call | solution.py:276
  (14 shorter events, 0.1 us)
Async XLA Ops:
  0.6 7.5 %copy-start.2 = (bf16[128,4,512]{2,1,0:T(4,128)(2,1)S(1)}, bf16[128,4,512]{2,1,0:T(4,128)(2,1)}, u32[]{:S(2)}) copy-start(bf16[128,4,512]{2,1,0:T(4,128)(2,1)} %param.4) | copy-start | bytes 1572868
  0.6 8.0 %copy-start.1 = (bf16[128]{0:T(256)(128)(2,1)S(1)}, bf16[128]{0:T(256)(128)(2,1)}, u32[]{:S(2)}) copy-start(bf16[128]{0:T(256)(128)(2,1)} %param.6) | copy-start | bytes 772
  1.6 11.4 %collective-permute-start.8 = (bf16[288,128]{1,0:T(8,128)(2,1)S(1)}, bf16[288,128]{1,0:T(8,128)(2,1)S(1)}, u32[]{:S(2)}, u32[]{:S(2)}) collective-permute-start(bf16[288,128]{1,0:T(8,128)(2,1)S(1)} %bitcast.39), channel_id=1, source_target_pairs={{0,3},{1,2},{2,1},{3,0},{4,7},{5,6},{6,5},{7,4},{8,11},{9,10},{10,... | collective-permute-start | bytes 221192 | tf_op jit(solution)/shard_map/ppermute | solution.py:11
  6.7 6.6 %collective-permute-start.7 = (bf16[288,128]{1,0:T(8,128)(2,1)S(1)}, bf16[288,128]{1,0:T(8,128)(2,1)S(1)}, u32[]{:S(2)}, u32[]{:S(2)}) collective-permute-start(bf16[288,128]{1,0:T(8,128)(2,1)S(1)} %bitcast.40), channel_id=1, source_target_pairs={{0,2},{1,3},{2,0},{3,1},{4,6},{5,7},{6,4},{7,5},{8,10},{9,11},{10,... | collective-permute-start | bytes 221192 | tf_op jit(solution)/shard_map/ppermute | solution.py:11
  8.6 2.7 %copy-start = (bf16[9,512,128]{2,1,0:T(8,128)(2,1)S(1)}, bf16[9,512,128]{2,1,0:T(8,128)(2,1)}, u32[]{:S(2)}) copy-start(bf16[9,512,128]{2,1,0:T(8,128)(2,1)} %refs_1_.1) | copy-start | bytes 3538948
  9.3 17.9 %collective-permute-start = (bf16[1056,128]{1,0:T(8,128)(2,1)S(1)}, bf16[1056,128]{1,0:T(8,128)(2,1)S(1)}, u32[]{:S(2)}, u32[]{:S(2)}) collective-permute-start(bf16[1056,128]{1,0:T(8,128)(2,1)S(1)} %get-tuple-element.38), channel_id=1, source_target_pairs={{0,3},{1,2},{2,1},{3,0},{4,7},{5,6},{6,5},{7,4},{8,11},{9,10},{10,... | collective-permute-start | bytes 811016 | tf_op jit(solution)/shard_map/ppermute | solution.py:11
  11.3 10.7 %collective-permute-start.4 = (bf16[576,128]{1,0:T(8,128)(2,1)S(1)}, bf16[576,128]{1,0:T(8,128)(2,1)S(1)}, u32[]{:S(2)}, u32[]{:S(2)}) collective-permute-start(bf16[576,128]{1,0:T(8,128)(2,1)S(1)} %bitcast.38), channel_id=1, source_target_pairs={{0,1},{1,0},{2,3},{3,2},{4,5},{5,4},{6,7},{7,6},{8,9},{9,8},{10,11... | collective-permute-start | bytes 442376 | tf_op jit(solution)/shard_map/ppermute | solution.py:11
  13.2 13.4 %collective-permute-start.9 = (bf16[1,576,128]{2,1,0:T(8,128)(2,1)S(1)}, bf16[1,576,128]{2,1,0:T(8,128)(2,1)S(1)}, u32[]{:S(2)}, u32[]{:S(2)}) collective-permute-start(bf16[1,576,128]{2,1,0:T(8,128)(2,1)S(1)} %maximum_bitcast_fusion), channel_id=1, source_target_pairs={{0,8},{4,12},{8,0},{12,4},{16,24},{20,28},{24,16},{28,20},{1,9},{5... | collective-permute-start | bytes 442376 | tf_op jit(solution)/shard_map/ppermute | solution.py:11
  22.1 5.4 %collective-permute-start.5 = (bf16[1,576,128]{2,1,0:T(8,128)(2,1)S(1)}, bf16[1,576,128]{2,1,0:T(8,128)(2,1)S(1)}, u32[]{:S(2)}, u32[]{:S(2)}) collective-permute-start(bf16[1,576,128]{2,1,0:T(8,128)(2,1)S(1)} %bitcast.33), channel_id=1, source_target_pairs={{0,16},{4,20},{8,24},{12,28},{16,0},{20,4},{24,8},{28,12},{1,17},{... | collective-permute-start | bytes 442376 | tf_op jit(solution)/shard_map/ppermute | solution.py:11
  23.6 15.0 %collective-permute-start.11 = (bf16[1056,128]{1,0:T(8,128)(2,1)S(1)}, bf16[1056,128]{1,0:T(8,128)(2,1)S(1)}, u32[]{:S(2)}, u32[]{:S(2)}) collective-permute-start(bf16[1056,128]{1,0:T(8,128)(2,1)S(1)} %get-tuple-element.38), channel_id=1, source_target_pairs={{0,1},{1,0},{2,3},{3,2},{4,5},{5,4},{6,7},{7,6},{8,9},{9,8},{10,11... | collective-permute-start | bytes 811016 | tf_op jit(solution)/shard_map/ppermute | solution.py:11
  23.7 14.8 %collective-permute-start.12 = (bf16[1056,128]{1,0:T(8,128)(2,1)S(1)}, bf16[1056,128]{1,0:T(8,128)(2,1)S(1)}, u32[]{:S(2)}, u32[]{:S(2)}) collective-permute-start(bf16[1056,128]{1,0:T(8,128)(2,1)S(1)} %get-tuple-element.56.refs_0_), channel_id=1, source_target_pairs={{0,2},{1,3},{2,0},{3,1},{4,6},{5,7},{6,4},{7,5},{8,10},{9,11},{10,... | collective-permute-start | bytes 811016 | tf_op jit(solution)/shard_map/ppermute | solution.py:11
  26.7 23.9 %collective-permute-start.10 = (bf16[2,576,128]{2,1,0:T(8,128)(2,1)S(1)}, bf16[2,576,128]{2,1,0:T(8,128)(2,1)S(1)}, u32[]{:S(2)}, u32[]{:S(2)}) collective-permute-start(bf16[2,576,128]{2,1,0:T(8,128)(2,1)S(1)} %pad_maximum_fusion.4), channel_id=1, source_target_pairs={{0,16},{4,20},{8,24},{12,28},{16,0},{20,4},{24,8},{28,12},{1,17},{... | collective-permute-start | bytes 884744 | tf_op jit(solution)/shard_map/ppermute | solution.py:11
  27.5 23.2 %collective-permute-start.6 = (bf16[2,576,128]{2,1,0:T(8,128)(2,1)S(1)}, bf16[2,576,128]{2,1,0:T(8,128)(2,1)S(1)}, u32[]{:S(2)}, u32[]{:S(2)}) collective-permute-start(bf16[2,576,128]{2,1,0:T(8,128)(2,1)S(1)} %pad_maximum_fusion.3), channel_id=1, source_target_pairs={{0,8},{4,12},{8,0},{12,4},{16,24},{20,28},{24,16},{28,20},{1,9},{5... | collective-permute-start | bytes 884744 | tf_op jit(solution)/shard_map/ppermute | solution.py:11
  29.7 11.8 %collective-permute-start.1 = (bf16[528,128]{1,0:T(8,128)(2,1)S(1)}, bf16[528,128]{1,0:T(8,128)(2,1)S(1)}, u32[]{:S(2)}, u32[]{:S(2)}) collective-permute-start(bf16[528,128]{1,0:T(8,128)(2,1)S(1)} %get-tuple-element.41), channel_id=1, source_target_pairs={{0,1},{1,0},{2,3},{3,2},{4,5},{5,4},{6,7},{7,6},{8,9},{9,8},{10,11... | collective-permute-start | bytes 405512 | tf_op jit(solution)/shard_map/ppermute | solution.py:11
  38.6 10.7 %collective-permute-start.2 = (bf16[528,128]{1,0:T(8,128)(2,1)S(1)}, bf16[528,128]{1,0:T(8,128)(2,1)S(1)}, u32[]{:S(2)}, u32[]{:S(2)}) collective-permute-start(bf16[528,128]{1,0:T(8,128)(2,1)S(1)} %get-tuple-element.52.refs_0_), channel_id=1, source_target_pairs={{0,2},{1,3},{2,0},{3,1},{4,6},{5,7},{6,4},{7,5},{8,10},{9,11},{10,... | collective-permute-start | bytes 405512 | tf_op jit(solution)/shard_map/ppermute | solution.py:11
  38.6 12.0 %collective-permute-start.3 = (bf16[528,128]{1,0:T(8,128)(2,1)S(1)}, bf16[528,128]{1,0:T(8,128)(2,1)S(1)}, u32[]{:S(2)}, u32[]{:S(2)}) collective-permute-start(bf16[528,128]{1,0:T(8,128)(2,1)S(1)} %get-tuple-element.41), channel_id=1, source_target_pairs={{0,3},{1,2},{2,1},{3,0},{4,7},{5,6},{6,5},{7,4},{8,11},{9,10},{10,... | collective-permute-start | bytes 405512 | tf_op jit(solution)/shard_map/ppermute | solution.py:11
  41.5 16.2 %collective-permute-start.17 = (bf16[2112,128]{1,0:T(8,128)(2,1)S(1)}, bf16[2112,128]{1,0:T(8,128)(2,1)S(1)}, u32[]{:S(2)}, u32[]{:S(2)}) collective-permute-start(bf16[2112,128]{1,0:T(8,128)(2,1)S(1)} %get-tuple-element.59), channel_id=1, source_target_pairs={{0,4},{4,8},{8,12},{12,16},{16,20},{20,24},{24,28},{1,5},{5,9},{9,... | collective-permute-start | bytes 1622024 | tf_op jit(solution)/shard_map/ppermute | solution.py:18
  49.3 8.4 %collective-permute-start.18 = (bf16[2112,128]{1,0:T(8,128)(2,1)S(1)}, bf16[2112,128]{1,0:T(8,128)(2,1)S(1)}, u32[]{:S(2)}, u32[]{:S(2)}) collective-permute-start(bf16[2112,128]{1,0:T(8,128)(2,1)S(1)} %get-tuple-element.60), channel_id=1, source_target_pairs={{4,0},{8,4},{12,8},{16,12},{20,16},{24,20},{28,24},{5,1},{9,5},{13... | collective-permute-start | bytes 1622024 | tf_op jit(solution)/shard_map/ppermute | solution.py:18
  50.8 4.0 %collective-permute-start.13 = (bf16[4,1152,128]{2,1,0:T(8,128)(2,1)S(1)}, bf16[4,1152,128]{2,1,0:T(8,128)(2,1)S(1)}, u32[]{:S(2)}, u32[]{:S(2)}) collective-permute-start(bf16[4,1152,128]{2,1,0:T(8,128)(2,1)S(1)} %pad_maximum_fusion), channel_id=1, source_target_pairs={{0,4},{4,0},{8,12},{12,8},{16,20},{20,16},{24,28},{28,24},{1,5},{5... | collective-permute-start | bytes 3538952 | tf_op jit(solution)/shard_map/ppermute | solution.py:11
  52.6 11.9 %collective-permute-start.15 = (bf16[528,128]{1,0:T(8,128)(2,1)S(1)}, bf16[528,128]{1,0:T(8,128)(2,1)S(1)}, u32[]{:S(2)}, u32[]{:S(2)}) collective-permute-start(bf16[528,128]{1,0:T(8,128)(2,1)S(1)} %get-tuple-element.65.refs_0_), channel_id=1, source_target_pairs={{0,2},{1,3},{2,0},{3,1},{4,6},{5,7},{6,4},{7,5},{8,10},{9,11},{10,... | collective-permute-start | bytes 405512 | tf_op jit(solution)/shard_map/ppermute | solution.py:11
  52.7 11.8 %collective-permute-start.16 = (bf16[528,128]{1,0:T(8,128)(2,1)S(1)}, bf16[528,128]{1,0:T(8,128)(2,1)S(1)}, u32[]{:S(2)}, u32[]{:S(2)}) collective-permute-start(bf16[528,128]{1,0:T(8,128)(2,1)S(1)} %get-tuple-element.51), channel_id=1, source_target_pairs={{0,3},{1,2},{2,1},{3,0},{4,7},{5,6},{6,5},{7,4},{8,11},{9,10},{10,... | collective-permute-start | bytes 405512 | tf_op jit(solution)/shard_map/ppermute | solution.py:11
  54.9 11.4 %collective-permute-start.14 = (bf16[528,128]{1,0:T(8,128)(2,1)S(1)}, bf16[528,128]{1,0:T(8,128)(2,1)S(1)}, u32[]{:S(2)}, u32[]{:S(2)}) collective-permute-start(bf16[528,128]{1,0:T(8,128)(2,1)S(1)} %get-tuple-element.51), channel_id=1, source_target_pairs={{0,1},{1,0},{2,3},{3,2},{4,5},{5,4},{6,7},{7,6},{8,9},{9,8},{10,11... | collective-permute-start | bytes 405512 | tf_op jit(solution)/shard_map/ppermute | solution.py:11
  62.5 8.0 %collective-permute-start.19 = (bf16[1024,128]{1,0:T(8,128)(2,1)S(1)}, bf16[1024,128]{1,0:T(8,128)(2,1)S(1)}, u32[]{:S(2)}, u32[]{:S(2)}) collective-permute-start(bf16[1024,128]{1,0:T(8,128)(2,1)S(1)} %get-tuple-element.71), channel_id=1, source_target_pairs={{0,1},{1,0},{2,3},{3,2},{4,5},{5,4},{6,7},{7,6},{8,9},{9,8},{10,11... | collective-permute-start | bytes 786440 | tf_op jit(solution)/shard_map/ppermute | solution.py:11
  67.8 9.3 %collective-permute-start.20 = (bf16[1024,128]{1,0:T(8,128)(2,1)S(1)}, bf16[1024,128]{1,0:T(8,128)(2,1)S(1)}, u32[]{:S(2)}, u32[]{:S(2)}) collective-permute-start(bf16[1024,128]{1,0:T(8,128)(2,1)S(1)} %get-tuple-element.73), channel_id=1, source_target_pairs={{0,1},{1,0},{2,3},{3,2},{4,5},{5,4},{6,7},{7,6},{8,9},{9,8},{10,11... | collective-permute-start | bytes 786440 | tf_op jit(solution)/shard_map/ppermute | solution.py:11

commit v16 on v15

--- a/solution.py
+++ b/solution.py
@@ -320,21 +320,30 @@
 
 def home_kernel(place, mine, other, out):
     width = mine.shape[2]
+    block = out.shape[0]
+    part = pl.ds(pl.program_id(0) * block, block)
     side = place[0] & 1
     for t in range(2):
 
         @pl.when(side == t)
         def _():
-            out[:, :, t * width : (t + 1) * width] = mine[...]
-            out[:, :, (1 - t) * width : (2 - t) * width] = other[...]
+            out[:, :, t * width : (t + 1) * width] = mine[part]
+            out[:, :, (1 - t) * width : (2 - t) * width] = other[part]
 
 
 def home(place, mine, other, rows):
     turn = lambda p: jnp.transpose(p.reshape(rows, -1, p.shape[1]), (2, 0, 1))
     mine, other = turn(mine), turn(other)
     channels, rows, width = mine.shape
-    shape = (channels, rows, 2 * width)
-    return kernel(home_kernel, [shape], [place, mine, other], [], "home", True)[0]
+    return pl.pallas_call(
+        home_kernel,
+        out_shape=jax.ShapeDtypeStruct((channels, rows, 2 * width), jnp.bfloat16),
+        grid=(4,),
+        in_specs=[SMEM, VMEM, VMEM],
+        out_specs=pl.BlockSpec((channels // 4, rows, 2 * width), lambda i: (i, 0, 0)),
+        cost_estimate=cost(0),
+        name="home",
+    )(place, mine, other)
 
 
 def token_kernel(*refs):

time: 79 us -> 80.7 us (1.022)
  waiting for transfers between devices: 31.9 us -> 28.7 us
  local copies, waits for them, and re-layouts: 3.69 us -> 6.44 us
  Pallas kernels: 12.5 us -> 14.6 us
    pallas_call x0 -> x2, Pallas kernels: none -> 4.97 us  [home(): pl.pallas_call(home_kernel, out_shape=jax.ShapeDtypeStruct((channels, row...]
    ppermute x19, waiting for transfers between devices: 31.9 us -> 28.7 us  [swap(): return lax.ppermute(value, axis, [(j, j ^ step) for j in range(size)])]
    pallas_call x11 -> x9, Pallas kernels: 12.5 us -> 9.63 us  [kernel(): pl.pallas_call(body, out_shape=[jax.ShapeDtypeStruct(s, kind) for s in sh...]
    reshape x4, local copies, waits for them, and re-layouts: 0.75 us -> 3.5 us  [home(): turn = lambda p: jnp.transpose(p.reshape(rows, -1, p.shape[1]), (2, 0, 1))]
    unnamed x8 -> x10, local copies, waits for them, and re-layouts: 1.89 us -> 1.89 us
  transfers between devices with their start and end apart: 21 -> 21, of which waited for: 10 -> 9; matrix products, arithmetic and copies ran while one was open for 4% -> 6% of each run, Pallas kernels for 14% -> 15%
where the time goes in v16:
time: 80.7 us; the launch traced here: 80.5 us
  starting transfers between devices  29.5 us (37%)
  waiting for transfers between devices  28.7 us (36%)
  Pallas kernels  14.6 us (18%)
  local copies, waits for them, and re-layouts  6.44 us (8%)
  between operations  0.88 us (1%)
    ppermute x19, waiting for transfers between devices, swap(): return lax.ppermute(value, axis, [(j, j ^ step) for j in range(size)])  28.7 us
    ppermute x19, starting transfers between devices, swap(): return lax.ppermute(value, axis, [(j, j ^ step) for j in range(size)])  26.9 us
    pallas_call x9, Pallas kernels, kernel(): pl.pallas_call(body, out_shape=[jax.ShapeDtypeStruct(s, kind) for s in sh...  9.63 us
    pallas_call x2, Pallas kernels, home(): pl.pallas_call(home_kernel, out_shape=jax.ShapeDtypeStruct((channels, row...  4.97 us
    reshape x4, local copies, waits for them, and re-layouts, home(): turn = lambda p: jnp.transpose(p.reshape(rows, -1, p.shape[1]), (2, 0, 1))  3.5 us
    ppermute x2, starting transfers between devices, neighbours(): return (lax.ppermute(last, 'band', up), lax.ppermute(first, 'band', down))  2.6 us
    unnamed x10, local copies, waits for them, and re-layouts  1.89 us
  transfers between devices with their start and end apart: 21, of which 9 were waited for; matrix products, arithmetic and copies ran while one was open for 6% of the time, Pallas kernels for 15%

profile of v16, /device:TPU:0, one launch (start us, length us, event | category | flops | bytes accessed | tf_op | source)
XLA Modules:
  0.0 80.5 jit_solution(3697423003217239092)
XLA Ops:
  0.7 1.0 %constant_dynamic-slice_fusion = bf16[9,32,128]{2,1,0:T(8,128)(2,1)S(1)} fusion(bf16[9,512,128]{2,1,0:T(8,128)(2,1)} %refs_1_.1, s32[]{:T(128)S(6)} %select_n.7), kind=kLoop, calls=%fused_computation.8 | loop fusion | bytes 147460 | tf_op jit(solution)/shard_map/dynamic_slice | solution.py:373
  1.6 5.0 %collective-permute-start.8 = (bf16[288,128]{1,0:T(8,128)(2,1)S(1)}, bf16[288,128]{1,0:T(8,128)(2,1)S(1)}, u32[]{:S(2)}, u32[]{:S(2)}) collective-permute-start(bf16[288,128]{1,0:T(8,128)(2,1)S(1)} %bitcast.39), channel_id=1, source_target_pairs={{0,3},{1,2},{2,1},{3,0},{4,7},{5,6},{6,5},{7,4},{8,11},{9,10},{10,... | collective-permute-start | bytes 221192 | tf_op jit(solution)/shard_map/ppermute | solution.py:11
  6.7 0.0 collective-permute-start.7
  6.7 1.5 %copy.6 = bf16[128,4,512]{0,2,1:T(8,128)(2,1)S(1)} copy(bf16[128,4,512]{2,1,0:T(4,128)(2,1)} %param.7) | data formatting | bytes 1048576 | tf_op args[3]
  8.1 0.4 copy.7
  8.5 0.1 pad_add_fusion.refs_0_.place
  8.6 0.7 cut.3
  9.3 2.0 %collective-permute-start = (bf16[1056,128]{1,0:T(8,128)(2,1)S(1)}, bf16[1056,128]{1,0:T(8,128)(2,1)S(1)}, u32[]{:S(2)}, u32[]{:S(2)}) collective-permute-start(bf16[1056,128]{1,0:T(8,128)(2,1)S(1)} %get-tuple-element.38), channel_id=1, source_target_pairs={{0,3},{1,2},{2,1},{3,0},{4,7},{5,6},{6,5},{7,4},{8,11},{9,10},{10,... | collective-permute-start | bytes 811016 | tf_op jit(solution)/shard_map/ppermute | solution.py:11
  11.3 1.6 %collective-permute-start.4 = (bf16[576,128]{1,0:T(8,128)(2,1)S(1)}, bf16[576,128]{1,0:T(8,128)(2,1)S(1)}, u32[]{:S(2)}, u32[]{:S(2)}) collective-permute-start(bf16[576,128]{1,0:T(8,128)(2,1)S(1)} %bitcast.38), channel_id=1, source_target_pairs={{0,1},{1,0},{2,3},{3,2},{4,5},{5,4},{6,7},{7,6},{8,9},{9,8},{10,11... | collective-permute-start | bytes 442376 | tf_op jit(solution)/shard_map/ppermute | solution.py:11
  13.0 0.0 collective-permute-done.8
  13.0 0.3 collective-permute-done.7
  13.2 1.6 %collective-permute-start.9 = (bf16[1,576,128]{2,1,0:T(8,128)(2,1)S(1)}, bf16[1,576,128]{2,1,0:T(8,128)(2,1)S(1)}, u32[]{:S(2)}, u32[]{:S(2)}) collective-permute-start(bf16[1,576,128]{2,1,0:T(8,128)(2,1)S(1)} %maximum_bitcast_fusion), channel_id=1, source_target_pairs={{0,8},{4,12},{8,0},{12,4},{16,24},{20,28},{24,16},{28,20},{1,9},{5... | collective-permute-start | bytes 442376 | tf_op jit(solution)/shard_map/ppermute | solution.py:11
  14.8 7.3 %collective-permute-done.4 = bf16[576,128]{1,0:T(8,128)(2,1)S(1)} collective-permute-done((bf16[576,128]{1,0:T(8,128)(2,1)S(1)}, bf16[576,128]{1,0:T(8,128)(2,1)S(1)}, u32[]{:S(2)}, u32[]{:S(2)}) %collective-permute-start.4) | collective-permute-done | bytes 147488 | tf_op jit(solution)/shard_map/ppermute | solution.py:11
  22.1 1.5 %collective-permute-start.5 = (bf16[1,576,128]{2,1,0:T(8,128)(2,1)S(1)}, bf16[1,576,128]{2,1,0:T(8,128)(2,1)S(1)}, u32[]{:S(2)}, u32[]{:S(2)}) collective-permute-start(bf16[1,576,128]{2,1,0:T(8,128)(2,1)S(1)} %bitcast.33), channel_id=1, source_target_pairs={{0,16},{4,20},{8,24},{12,28},{16,0},{20,4},{24,8},{28,12},{1,17},{... | collective-permute-start | bytes 442376 | tf_op jit(solution)/shard_map/ppermute | solution.py:11
  23.6 0.2 collective-permute-start.11
  23.7 2.9 %collective-permute-start.12 = (bf16[1056,128]{1,0:T(8,128)(2,1)S(1)}, bf16[1056,128]{1,0:T(8,128)(2,1)S(1)}, u32[]{:S(2)}, u32[]{:S(2)}) collective-permute-start(bf16[1056,128]{1,0:T(8,128)(2,1)S(1)} %get-tuple-element.56.refs_0_), channel_id=1, source_target_pairs={{0,2},{1,3},{2,0},{3,1},{4,6},{5,7},{6,4},{7,5},{8,10},{9,11},{10,... | collective-permute-start | bytes 811016 | tf_op jit(solution)/shard_map/ppermute | solution.py:11
  26.6 0.0 collective-permute-done.9
  26.7 0.6 collective-permute-start.10
  27.2 0.0 collective-permute-done.refs_3_
  27.2 0.2 collective-permute-done.5
  27.5 1.6 %collective-permute-start.6 = (bf16[2,576,128]{2,1,0:T(8,128)(2,1)S(1)}, bf16[2,576,128]{2,1,0:T(8,128)(2,1)S(1)}, u32[]{:S(2)}, u32[]{:S(2)}) collective-permute-start(bf16[2,576,128]{2,1,0:T(8,128)(2,1)S(1)} %pad_maximum_fusion.3), channel_id=1, source_target_pairs={{0,8},{4,12},{8,0},{12,4},{16,24},{20,28},{24,16},{28,20},{1,9},{5... | collective-permute-start | bytes 884744 | tf_op jit(solution)/shard_map/ppermute | solution.py:11
  29.0 0.6 cut.4
  29.7 0.1 collective-permute-start.1
  29.8 8.8 %collective-permute-done.11.refs_1_ = bf16[1056,128]{1,0:T(8,128)(2,1)S(1)} collective-permute-done((bf16[1056,128]{1,0:T(8,128)(2,1)S(1)}, bf16[1056,128]{1,0:T(8,128)(2,1)S(1)}, u32[]{:S(2)}, u32[]{:S(2)}) %collective-permute-start.11) | collective-permute-done | bytes 270368 | tf_op jit(solution)/shard_map/ppermute | solution.py:11
  38.6 0.0 collective-permute-start.2
  38.6 0.0 collective-permute-done.12.refs_2_
  38.6 2.8 %collective-permute-start.3 = (bf16[528,128]{1,0:T(8,128)(2,1)S(1)}, bf16[528,128]{1,0:T(8,128)(2,1)S(1)}, u32[]{:S(2)}, u32[]{:S(2)}) collective-permute-start(bf16[528,128]{1,0:T(8,128)(2,1)S(1)} %get-tuple-element.41), channel_id=1, source_target_pairs={{0,3},{1,2},{2,1},{3,0},{4,7},{5,6},{6,5},{7,4},{8,11},{9,10},{10,... | collective-permute-start | bytes 405512 | tf_op jit(solution)/shard_map/ppermute | solution.py:11
  41.4 0.1 rim.1
  41.5 0.0 collective-permute-done.1.refs_1_
  41.5 1.3 %collective-permute-start.17 = (bf16[2112,128]{1,0:T(8,128)(2,1)S(1)}, bf16[2112,128]{1,0:T(8,128)(2,1)S(1)}, u32[]{:S(2)}, u32[]{:S(2)}) collective-permute-start(bf16[2112,128]{1,0:T(8,128)(2,1)S(1)} %get-tuple-element.59), channel_id=1, source_target_pairs={{0,4},{4,8},{8,12},{12,16},{16,20},{20,24},{24,28},{1,5},{5,9},{9,... | collective-permute-start | bytes 1622024 | tf_op jit(solution)/shard_map/ppermute | solution.py:18
  42.8 6.4 %collective-permute-done.2.refs_2_ = bf16[528,128]{1,0:T(8,128)(2,1)S(1)} collective-permute-done((bf16[528,128]{1,0:T(8,128)(2,1)S(1)}, bf16[528,128]{1,0:T(8,128)(2,1)S(1)}, u32[]{:S(2)}, u32[]{:S(2)}) %collective-permute-start.2) | collective-permute-done | bytes 135200 | tf_op jit(solution)/shard_map/ppermute | solution.py:11
  49.3 1.3 %collective-permute-start.18 = (bf16[2112,128]{1,0:T(8,128)(2,1)S(1)}, bf16[2112,128]{1,0:T(8,128)(2,1)S(1)}, u32[]{:S(2)}, u32[]{:S(2)}) collective-permute-start(bf16[2112,128]{1,0:T(8,128)(2,1)S(1)} %get-tuple-element.60), channel_id=1, source_target_pairs={{4,0},{8,4},{12,8},{16,12},{20,16},{24,20},{28,24},{5,1},{9,5},{13... | collective-permute-start | bytes 1622024 | tf_op jit(solution)/shard_map/ppermute | solution.py:18
  50.6 0.0 collective-permute-done.3.refs_3_
  50.6 0.0 collective-permute-done.10
  50.6 0.1 pad_maximum_fusion.2.refs_4_
  50.6 0.0 collective-permute-done.6
  50.7 0.1 pad_maximum_fusion.1.refs_2_
  50.7 0.1 pad_maximum_fusion
  50.8 1.2 %collective-permute-start.13 = (bf16[4,1152,128]{2,1,0:T(8,128)(2,1)S(1)}, bf16[4,1152,128]{2,1,0:T(8,128)(2,1)S(1)}, u32[]{:S(2)}, u32[]{:S(2)}) collective-permute-start(bf16[4,1152,128]{2,1,0:T(8,128)(2,1)S(1)} %pad_maximum_fusion), channel_id=1, source_target_pairs={{0,4},{4,0},{8,12},{12,8},{16,20},{20,16},{24,28},{28,24},{1,5},{5... | collective-permute-start | bytes 3538952 | tf_op jit(solution)/shard_map/ppermute | solution.py:11
  52.0 0.6 cut.5
  52.6 0.1 collective-permute-start.15
  52.7 1.9 %collective-permute-start.16 = (bf16[528,128]{1,0:T(8,128)(2,1)S(1)}, bf16[528,128]{1,0:T(8,128)(2,1)S(1)}, u32[]{:S(2)}, u32[]{:S(2)}) collective-permute-start(bf16[528,128]{1,0:T(8,128)(2,1)S(1)} %get-tuple-element.51), channel_id=1, source_target_pairs={{0,3},{1,2},{2,1},{3,0},{4,7},{5,6},{6,5},{7,4},{8,11},{9,10},{10,... | collective-permute-start | bytes 405512 | tf_op jit(solution)/shard_map/ppermute | solution.py:11
  54.6 0.1 collective-permute-done.13
  54.8 0.1 fusion
  54.9 1.5 %collective-permute-start.14 = (bf16[528,128]{1,0:T(8,128)(2,1)S(1)}, bf16[528,128]{1,0:T(8,128)(2,1)S(1)}, u32[]{:S(2)}, u32[]{:S(2)}) collective-permute-start(bf16[528,128]{1,0:T(8,128)(2,1)S(1)} %get-tuple-element.51), channel_id=1, source_target_pairs={{0,1},{1,0},{2,3},{3,2},{4,5},{5,4},{6,7},{7,6},{8,9},{9,8},{10,11... | collective-permute-start | bytes 405512 | tf_op jit(solution)/shard_map/ppermute | solution.py:11
  56.3 1.3 %assemble.1 = (bf16[4608,256]{1,0:T(8,128)(2,1)S(1)}, bf16[2304,256]{1,0:T(8,128)(2,1)S(1)}) custom-call(s32[2]{0:T(128)S(1)} %pad_add_fusion.refs_0_.place, bf16[9,512,128]{2,1,0:T(8,128)(2,1)S(1)} %copy-done, bf16[4,576,128]{2,1,0:T(8,128)(2,1)S(1)} %pad_maximum_fusion.1.refs_2_, bf16[4,576,128]{2,1,0:T(8,128)(2,1)S(1)} %get-tuple-element.75.refs_3_, ...), custom_call_target="tpu_custom_call" | custom-call | flops 2001048576 | bytes 1048576 | tf_op jit(solution)/shard_map/assemble/pallas_call | solution.py:276
  57.6 0.0 collective-permute-done.17.refs_4_
  57.6 0.0 collective-permute-done.18.refs_5_
  57.6 3.1 %outer.1 = (f32[1024,256]{1,0:T(8,128)S(1)}, f32[1024,256]{1,0:T(8,128)S(1)}) custom-call(bf16[1056,128]{1,0:T(8,128)(2,1)S(1)} %get-tuple-element.56.refs_0_, bf16[1056,128]{1,0:T(8,128)(2,1)S(1)} %collective-permute-done.11.refs_1_, bf16[1056,128]{1,0:T(8,128)(2,1)S(1)} %collective-permute-done.12.refs_2_, ...), custom_call_target="tpu_custom_call" | custom-call | flops 2001048576 | bytes 1048576 | tf_op jit(solution)/shard_map/outer/pallas_call | solution.py:276
  60.8 1.7 %inner.2 = (bf16[1024,128]{1,0:T(8,128)(2,1)S(1)}, bf16[1024,128]{1,0:T(8,128)(2,1)S(1)}) custom-call(bf16[528,128]{1,0:T(8,128)(2,1)S(1)} %get-tuple-element.52.refs_0_, bf16[528,128]{1,0:T(8,128)(2,1)S(1)} %collective-permute-done.1.refs_1_, bf16[528,128]{1,0:T(8,128)(2,1)S(1)} %collective-permute-done.2.refs_2_, ...), custom_call_target="tpu_custom_call" | custom-call | flops 9001048064 | bytes 1048576 | tf_op jit(solution)/shard_map/inner/pallas_call | solution.py:276
  62.5 0.7 collective-permute-start.19
  63.1 1.4 %collective-permute-done.15.refs_2_ = bf16[528,128]{1,0:T(8,128)(2,1)S(1)} collective-permute-done((bf16[528,128]{1,0:T(8,128)(2,1)S(1)}, bf16[528,128]{1,0:T(8,128)(2,1)S(1)}, u32[]{:S(2)}, u32[]{:S(2)}) %collective-permute-start.15) | collective-permute-done | bytes 135200 | tf_op jit(solution)/shard_map/ppermute | solution.py:11
  64.5 0.0 collective-permute-done.16.refs_3_
  64.5 1.7 %collective-permute-done.14.refs_1_ = bf16[528,128]{1,0:T(8,128)(2,1)S(1)} collective-permute-done((bf16[528,128]{1,0:T(8,128)(2,1)S(1)}, bf16[528,128]{1,0:T(8,128)(2,1)S(1)}, u32[]{:S(2)}, u32[]{:S(2)}) %collective-permute-start.14) | collective-permute-done | bytes 135200 | tf_op jit(solution)/shard_map/ppermute | solution.py:11
  66.2 1.5 %inner.3 = (bf16[1024,128]{1,0:T(8,128)(2,1)S(1)}, bf16[1024,128]{1,0:T(8,128)(2,1)S(1)}) custom-call(bf16[528,128]{1,0:T(8,128)(2,1)S(1)} %get-tuple-element.65.refs_0_, bf16[528,128]{1,0:T(8,128)(2,1)S(1)} %collective-permute-done.14.refs_1_, bf16[528,128]{1,0:T(8,128)(2,1)S(1)} %collective-permute-done.15.refs_2_, ...), custom_call_target="tpu_custom_call" | custom-call | flops 9001048064 | bytes 1048576 | tf_op jit(solution)/shard_map/inner/pallas_call | solution.py:276
  67.8 1.7 %collective-permute-start.20 = (bf16[1024,128]{1,0:T(8,128)(2,1)S(1)}, bf16[1024,128]{1,0:T(8,128)(2,1)S(1)}, u32[]{:S(2)}, u32[]{:S(2)}) collective-permute-start(bf16[1024,128]{1,0:T(8,128)(2,1)S(1)} %get-tuple-element.73), channel_id=1, source_target_pairs={{0,1},{1,0},{2,3},{3,2},{4,5},{5,4},{6,7},{7,6},{8,9},{9,8},{10,11... | collective-permute-start | bytes 786440 | tf_op jit(solution)/shard_map/ppermute | solution.py:11
  69.5 0.9 %copy.12 = bf16[4,256,128]{1,0,2:T(4,128)(2,1)} copy(bf16[4,256,128]{2,1,0:T(8,128)(2,1)S(1)} %bitcast.24) | data formatting | bytes 524288 | tf_op jit(solution)/shard_map/reshape | solution.py:335
  70.4 0.0 collective-permute-done.19
  70.4 0.9 %copy.13 = bf16[4,256,128]{1,0,2:T(4,128)(2,1)} copy(bf16[4,256,128]{2,1,0:T(8,128)(2,1)S(1)} %bitcast.36) | data formatting | bytes 524288 | tf_op jit(solution)/shard_map/reshape | solution.py:335
  71.3 2.5 %home.2 = bf16[128,4,512]{2,1,0:T(4,128)(2,1)} custom-call(s32[2]{0:T(128)} %copy-done.1, bf16[128,4,256]{2,1,0:T(4,128)(2,1)} %bitcast.30, bf16[128,4,256]{2,1,0:T(4,128)(2,1)} %bitcast.32), custom_call_target="tpu_custom_call" | custom-call | flops 1048576 | bytes 1048576 | tf_op jit(solution)/shard_map/home/pallas_call | solution.py:338
  73.8 0.9 %copy.14 = bf16[4,256,128]{1,0,2:T(4,128)(2,1)} copy(bf16[4,256,128]{2,1,0:T(8,128)(2,1)S(1)} %bitcast.25) | data formatting | bytes 524288 | tf_op jit(solution)/shard_map/reshape | solution.py:335
  74.7 2.4 %collective-permute-done.20 = bf16[1024,128]{1,0:T(8,128)(2,1)S(1)} collective-permute-done((bf16[1024,128]{1,0:T(8,128)(2,1)S(1)}, bf16[1024,128]{1,0:T(8,128)(2,1)S(1)}, u32[]{:S(2)}, u32[]{:S(2)}) %collective-permute-start.20) | collective-permute-done | bytes 262176 | tf_op jit(solution)/shard_map/ppermute | solution.py:11
  77.1 0.9 %copy.15 = bf16[4,256,128]{1,0,2:T(4,128)(2,1)} copy(bf16[4,256,128]{2,1,0:T(8,128)(2,1)S(1)} %bitcast.37) | data formatting | bytes 524288 | tf_op jit(solution)/shard_map/reshape | solution.py:335
  78.0 2.5 %home.3 = bf16[128,4,512]{2,1,0:T(4,128)(2,1)} custom-call(s32[2]{0:T(128)} %copy-done.1, bf16[128,4,256]{2,1,0:T(4,128)(2,1)} %bitcast.29, bf16[128,4,256]{2,1,0:T(4,128)(2,1)} %bitcast.31), custom_call_target="tpu_custom_call" | custom-call | flops 1048576 | bytes 1048576 | tf_op jit(solution)/shard_map/home/pallas_call | solution.py:338
  (16 shorter events, 0.1 us)
Async XLA Ops:
  0.6 7.5 %copy-start.3 = (bf16[128,4,512]{2,1,0:T(4,128)(2,1)S(1)}, bf16[128,4,512]{2,1,0:T(4,128)(2,1)}, u32[]{:S(2)}) copy-start(bf16[128,4,512]{2,1,0:T(4,128)(2,1)} %param.4) | copy-start | bytes 1572868
  0.6 8.0 %copy-start.2 = (bf16[128]{0:T(256)(128)(2,1)S(1)}, bf16[128]{0:T(256)(128)(2,1)}, u32[]{:S(2)}) copy-start(bf16[128]{0:T(256)(128)(2,1)} %param.6) | copy-start | bytes 772
  1.6 11.4 %collective-permute-start.8 = (bf16[288,128]{1,0:T(8,128)(2,1)S(1)}, bf16[288,128]{1,0:T(8,128)(2,1)S(1)}, u32[]{:S(2)}, u32[]{:S(2)}) collective-permute-start(bf16[288,128]{1,0:T(8,128)(2,1)S(1)} %bitcast.39), channel_id=1, source_target_pairs={{0,3},{1,2},{2,1},{3,0},{4,7},{5,6},{6,5},{7,4},{8,11},{9,10},{10,... | collective-permute-start | bytes 221192 | tf_op jit(solution)/shard_map/ppermute | solution.py:11
  6.7 6.6 %collective-permute-start.7 = (bf16[288,128]{1,0:T(8,128)(2,1)S(1)}, bf16[288,128]{1,0:T(8,128)(2,1)S(1)}, u32[]{:S(2)}, u32[]{:S(2)}) collective-permute-start(bf16[288,128]{1,0:T(8,128)(2,1)S(1)} %bitcast.40), channel_id=1, source_target_pairs={{0,2},{1,3},{2,0},{3,1},{4,6},{5,7},{6,4},{7,5},{8,10},{9,11},{10,... | collective-permute-start | bytes 221192 | tf_op jit(solution)/shard_map/ppermute | solution.py:11
  8.6 47.7 %copy-start.1 = (s32[2]{0:T(128)}, s32[2]{0:T(128)S(1)}, u32[]{:S(2)}) copy-start(s32[2]{0:T(128)S(1)} %pad_add_fusion.refs_0_.place) | copy-start | bytes 28
  8.6 2.7 %copy-start = (bf16[9,512,128]{2,1,0:T(8,128)(2,1)S(1)}, bf16[9,512,128]{2,1,0:T(8,128)(2,1)}, u32[]{:S(2)}) copy-start(bf16[9,512,128]{2,1,0:T(8,128)(2,1)} %refs_1_.1) | copy-start | bytes 3538948
  9.3 17.9 %collective-permute-start = (bf16[1056,128]{1,0:T(8,128)(2,1)S(1)}, bf16[1056,128]{1,0:T(8,128)(2,1)S(1)}, u32[]{:S(2)}, u32[]{:S(2)}) collective-permute-start(bf16[1056,128]{1,0:T(8,128)(2,1)S(1)} %get-tuple-element.38), channel_id=1, source_target_pairs={{0,3},{1,2},{2,1},{3,0},{4,7},{5,6},{6,5},{7,4},{8,11},{9,10},{10,... | collective-permute-start | bytes 811016 | tf_op jit(solution)/shard_map/ppermute | solution.py:11
  11.3 10.7 %collective-permute-start.4 = (bf16[576,128]{1,0:T(8,128)(2,1)S(1)}, bf16[576,128]{1,0:T(8,128)(2,1)S(1)}, u32[]{:S(2)}, u32[]{:S(2)}) collective-permute-start(bf16[576,128]{1,0:T(8,128)(2,1)S(1)} %bitcast.38), channel_id=1, source_target_pairs={{0,1},{1,0},{2,3},{3,2},{4,5},{5,4},{6,7},{7,6},{8,9},{9,8},{10,11... | collective-permute-start | bytes 442376 | tf_op jit(solution)/shard_map/ppermute | solution.py:11
  13.2 13.4 %collective-permute-start.9 = (bf16[1,576,128]{2,1,0:T(8,128)(2,1)S(1)}, bf16[1,576,128]{2,1,0:T(8,128)(2,1)S(1)}, u32[]{:S(2)}, u32[]{:S(2)}) collective-permute-start(bf16[1,576,128]{2,1,0:T(8,128)(2,1)S(1)} %maximum_bitcast_fusion), channel_id=1, source_target_pairs={{0,8},{4,12},{8,0},{12,4},{16,24},{20,28},{24,16},{28,20},{1,9},{5... | collective-permute-start | bytes 442376 | tf_op jit(solution)/shard_map/ppermute | solution.py:11
  22.1 5.4 %collective-permute-start.5 = (bf16[1,576,128]{2,1,0:T(8,128)(2,1)S(1)}, bf16[1,576,128]{2,1,0:T(8,128)(2,1)S(1)}, u32[]{:S(2)}, u32[]{:S(2)}) collective-permute-start(bf16[1,576,128]{2,1,0:T(8,128)(2,1)S(1)} %bitcast.33), channel_id=1, source_target_pairs={{0,16},{4,20},{8,24},{12,28},{16,0},{20,4},{24,8},{28,12},{1,17},{... | collective-permute-start | bytes 442376 | tf_op jit(solution)/shard_map/ppermute | solution.py:11
  23.6 15.0 %collective-permute-start.11 = (bf16[1056,128]{1,0:T(8,128)(2,1)S(1)}, bf16[1056,128]{1,0:T(8,128)(2,1)S(1)}, u32[]{:S(2)}, u32[]{:S(2)}) collective-permute-start(bf16[1056,128]{1,0:T(8,128)(2,1)S(1)} %get-tuple-element.38), channel_id=1, source_target_pairs={{0,1},{1,0},{2,3},{3,2},{4,5},{5,4},{6,7},{7,6},{8,9},{9,8},{10,11... | collective-permute-start | bytes 811016 | tf_op jit(solution)/shard_map/ppermute | solution.py:11
  23.7 14.8 %collective-permute-start.12 = (bf16[1056,128]{1,0:T(8,128)(2,1)S(1)}, bf16[1056,128]{1,0:T(8,128)(2,1)S(1)}, u32[]{:S(2)}, u32[]{:S(2)}) collective-permute-start(bf16[1056,128]{1,0:T(8,128)(2,1)S(1)} %get-tuple-element.56.refs_0_), channel_id=1, source_target_pairs={{0,2},{1,3},{2,0},{3,1},{4,6},{5,7},{6,4},{7,5},{8,10},{9,11},{10,... | collective-permute-start | bytes 811016 | tf_op jit(solution)/shard_map/ppermute | solution.py:11
  26.7 23.9 %collective-permute-start.10 = (bf16[2,576,128]{2,1,0:T(8,128)(2,1)S(1)}, bf16[2,576,128]{2,1,0:T(8,128)(2,1)S(1)}, u32[]{:S(2)}, u32[]{:S(2)}) collective-permute-start(bf16[2,576,128]{2,1,0:T(8,128)(2,1)S(1)} %pad_maximum_fusion.4), channel_id=1, source_target_pairs={{0,16},{4,20},{8,24},{12,28},{16,0},{20,4},{24,8},{28,12},{1,17},{... | collective-permute-start | bytes 884744 | tf_op jit(solution)/shard_map/ppermute | solution.py:11
  27.5 23.2 %collective-permute-start.6 = (bf16[2,576,128]{2,1,0:T(8,128)(2,1)S(1)}, bf16[2,576,128]{2,1,0:T(8,128)(2,1)S(1)}, u32[]{:S(2)}, u32[]{:S(2)}) collective-permute-start(bf16[2,576,128]{2,1,0:T(8,128)(2,1)S(1)} %pad_maximum_fusion.3), channel_id=1, source_target_pairs={{0,8},{4,12},{8,0},{12,4},{16,24},{20,28},{24,16},{28,20},{1,9},{5... | collective-permute-start | bytes 884744 | tf_op jit(solution)/shard_map/ppermute | solution.py:11
  29.7 11.8 %collective-permute-start.1 = (bf16[528,128]{1,0:T(8,128)(2,1)S(1)}, bf16[528,128]{1,0:T(8,128)(2,1)S(1)}, u32[]{:S(2)}, u32[]{:S(2)}) collective-permute-start(bf16[528,128]{1,0:T(8,128)(2,1)S(1)} %get-tuple-element.41), channel_id=1, source_target_pairs={{0,1},{1,0},{2,3},{3,2},{4,5},{5,4},{6,7},{7,6},{8,9},{9,8},{10,11... | collective-permute-start | bytes 405512 | tf_op jit(solution)/shard_map/ppermute | solution.py:11
  38.6 10.7 %collective-permute-start.2 = (bf16[528,128]{1,0:T(8,128)(2,1)S(1)}, bf16[528,128]{1,0:T(8,128)(2,1)S(1)}, u32[]{:S(2)}, u32[]{:S(2)}) collective-permute-start(bf16[528,128]{1,0:T(8,128)(2,1)S(1)} %get-tuple-element.52.refs_0_), channel_id=1, source_target_pairs={{0,2},{1,3},{2,0},{3,1},{4,6},{5,7},{6,4},{7,5},{8,10},{9,11},{10,... | collective-permute-start | bytes 405512 | tf_op jit(solution)/shard_map/ppermute | solution.py:11
  38.6 12.0 %collective-permute-start.3 = (bf16[528,128]{1,0:T(8,128)(2,1)S(1)}, bf16[528,128]{1,0:T(8,128)(2,1)S(1)}, u32[]{:S(2)}, u32[]{:S(2)}) collective-permute-start(bf16[528,128]{1,0:T(8,128)(2,1)S(1)} %get-tuple-element.41), channel_id=1, source_target_pairs={{0,3},{1,2},{2,1},{3,0},{4,7},{5,6},{6,5},{7,4},{8,11},{9,10},{10,... | collective-permute-start | bytes 405512 | tf_op jit(solution)/shard_map/ppermute | solution.py:11
  41.5 16.1 %collective-permute-start.17 = (bf16[2112,128]{1,0:T(8,128)(2,1)S(1)}, bf16[2112,128]{1,0:T(8,128)(2,1)S(1)}, u32[]{:S(2)}, u32[]{:S(2)}) collective-permute-start(bf16[2112,128]{1,0:T(8,128)(2,1)S(1)} %get-tuple-element.59), channel_id=1, source_target_pairs={{0,4},{4,8},{8,12},{12,16},{16,20},{20,24},{24,28},{1,5},{5,9},{9,... | collective-permute-start | bytes 1622024 | tf_op jit(solution)/shard_map/ppermute | solution.py:18
  49.3 8.4 %collective-permute-start.18 = (bf16[2112,128]{1,0:T(8,128)(2,1)S(1)}, bf16[2112,128]{1,0:T(8,128)(2,1)S(1)}, u32[]{:S(2)}, u32[]{:S(2)}) collective-permute-start(bf16[2112,128]{1,0:T(8,128)(2,1)S(1)} %get-tuple-element.60), channel_id=1, source_target_pairs={{4,0},{8,4},{12,8},{16,12},{20,16},{24,20},{28,24},{5,1},{9,5},{13... | collective-permute-start | bytes 1622024 | tf_op jit(solution)/shard_map/ppermute | solution.py:18
  50.8 4.0 %collective-permute-start.13 = (bf16[4,1152,128]{2,1,0:T(8,128)(2,1)S(1)}, bf16[4,1152,128]{2,1,0:T(8,128)(2,1)S(1)}, u32[]{:S(2)}, u32[]{:S(2)}) collective-permute-start(bf16[4,1152,128]{2,1,0:T(8,128)(2,1)S(1)} %pad_maximum_fusion), channel_id=1, source_target_pairs={{0,4},{4,0},{8,12},{12,8},{16,20},{20,16},{24,28},{28,24},{1,5},{5... | collective-permute-start | bytes 3538952 | tf_op jit(solution)/shard_map/ppermute | solution.py:11
  52.6 11.9 %collective-permute-start.15 = (bf16[528,128]{1,0:T(8,128)(2,1)S(1)}, bf16[528,128]{1,0:T(8,128)(2,1)S(1)}, u32[]{:S(2)}, u32[]{:S(2)}) collective-permute-start(bf16[528,128]{1,0:T(8,128)(2,1)S(1)} %get-tuple-element.65.refs_0_), channel_id=1, source_target_pairs={{0,2},{1,3},{2,0},{3,1},{4,6},{5,7},{6,4},{7,5},{8,10},{9,11},{10,... | collective-permute-start | bytes 405512 | tf_op jit(solution)/shard_map/ppermute | solution.py:11
  52.7 11.8 %collective-permute-start.16 = (bf16[528,128]{1,0:T(8,128)(2,1)S(1)}, bf16[528,128]{1,0:T(8,128)(2,1)S(1)}, u32[]{:S(2)}, u32[]{:S(2)}) collective-permute-start(bf16[528,128]{1,0:T(8,128)(2,1)S(1)} %get-tuple-element.51), channel_id=1, source_target_pairs={{0,3},{1,2},{2,1},{3,0},{4,7},{5,6},{6,5},{7,4},{8,11},{9,10},{10,... | collective-permute-start | bytes 405512 | tf_op jit(solution)/shard_map/ppermute | solution.py:11
  54.9 11.4 %collective-permute-start.14 = (bf16[528,128]{1,0:T(8,128)(2,1)S(1)}, bf16[528,128]{1,0:T(8,128)(2,1)S(1)}, u32[]{:S(2)}, u32[]{:S(2)}) collective-permute-start(bf16[528,128]{1,0:T(8,128)(2,1)S(1)} %get-tuple-element.51), channel_id=1, source_target_pairs={{0,1},{1,0},{2,3},{3,2},{4,5},{5,4},{6,7},{7,6},{8,9},{9,8},{10,11... | collective-permute-start | bytes 405512 | tf_op jit(solution)/shard_map/ppermute | solution.py:11
  62.5 8.0 %collective-permute-start.19 = (bf16[1024,128]{1,0:T(8,128)(2,1)S(1)}, bf16[1024,128]{1,0:T(8,128)(2,1)S(1)}, u32[]{:S(2)}, u32[]{:S(2)}) collective-permute-start(bf16[1024,128]{1,0:T(8,128)(2,1)S(1)} %get-tuple-element.71), channel_id=1, source_target_pairs={{0,1},{1,0},{2,3},{3,2},{4,5},{5,4},{6,7},{7,6},{8,9},{9,8},{10,11... | collective-permute-start | bytes 786440 | tf_op jit(solution)/shard_map/ppermute | solution.py:11
  67.8 9.3 %collective-permute-start.20 = (bf16[1024,128]{1,0:T(8,128)(2,1)S(1)}, bf16[1024,128]{1,0:T(8,128)(2,1)S(1)}, u32[]{:S(2)}, u32[]{:S(2)}) collective-permute-start(bf16[1024,128]{1,0:T(8,128)(2,1)S(1)} %get-tuple-element.73), channel_id=1, source_target_pairs={{0,1},{1,0},{2,3},{3,2},{4,5},{5,4},{6,7},{7,6},{8,9},{9,8},{10,11... | collective-permute-start | bytes 786440 | tf_op jit(solution)/shard_map/ppermute | solution.py:11

commit v17 on v14

--- a/solution.py
+++ b/solution.py
@@ -363,7 +363,8 @@
     start = (1 - half) * (outs // 2) + band * (share // 2)
     across = lax.dynamic_slice_in_dim(filters, start, share // 2, axis=1).reshape(-1, local)
     near = swap(near, "chan", 1)
-    across = jnp.concatenate([swap(across, "chan", k) for k in (2, 3)])
+    across = swap(across, "chan", 2)
+    across = jnp.concatenate([across, swap(across, "chan", 1)])
 
     upstream, image = [jnp.transpose(v, (1, 2, 0)) for v in (upstream, image)]
     parts = [(i, r) for i in range(2) for r in (0, rows - 1)]
@@ -380,7 +381,6 @@
     steps = halving(bands)[:-1]
     near, near_order = gather(near, steps)
     across, across_order = gather(across, steps[::-1])
-    near, across = after((near, across), pieces[1])
     there = swap(jnp.concatenate([near, across], axis=1), "band", 1)
     held = [near, there[:, : near.shape[1]], across, there[:, near.shape[1] :]]
     filters = kernel(

time: 79.7 us -> 79.7 us (level)
  starting transfers between devices: 28.1 us -> 32.2 us
  waiting for transfers between devices: 33.9 us -> 29.9 us
    ppermute x19, starting transfers between devices: 25.5 us -> 29.6 us  [swap(): return lax.ppermute(value, axis, [(j, j ^ step) for j in range(size)])]
    ppermute x19, waiting for transfers between devices: 33.9 us -> 29.9 us  [swap(): return lax.ppermute(value, axis, [(j, j ^ step) for j in range(size)])]
  transfers between devices with their start and end apart: 21 -> 21, of which waited for: 9 -> 8; matrix products, arithmetic and copies ran while one was open for 4% -> 4% of each run, Pallas kernels for 14% -> 14%
where the time goes in v17:
time: 79.7 us; the launch traced here: 79.5 us
  starting transfers between devices  32.2 us (40%)
  waiting for transfers between devices  29.9 us (38%)
  Pallas kernels  12.5 us (16%)
  local copies, waits for them, and re-layouts  3.69 us (5%)
  between operations  0.9 us (1%)
    ppermute x19, waiting for transfers between devices, swap(): return lax.ppermute(value, axis, [(j, j ^ step) for j in range(size)])  29.9 us
    ppermute x19, starting transfers between devices, swap(): return lax.ppermute(value, axis, [(j, j ^ step) for j in range(size)])  29.6 us
    pallas_call x11, Pallas kernels, kernel(): pl.pallas_call(body, out_shape=[jax.ShapeDtypeStruct(s, kind) for s in sh...  12.5 us
    ppermute x2, starting transfers between devices, neighbours(): return (lax.ppermute(last, 'band', up), lax.ppermute(first, 'band', down))  2.6 us
    unnamed x8, local copies, waits for them, and re-layouts  1.89 us
  transfers between devices with their start and end apart: 21, of which 8 were waited for; matrix products, arithmetic and copies ran while one was open for 4% of the time, Pallas kernels for 14%

profile of v17, /device:TPU:0, one launch (start us, length us, event | category | flops | bytes accessed | tf_op | source)
XLA Modules:
  0.0 79.5 jit_solution(13655337684325608450)
XLA Ops:
  0.7 1.0 %constant_dynamic-slice_fusion = bf16[9,32,128]{2,1,0:T(8,128)(2,1)S(1)} fusion(bf16[9,512,128]{2,1,0:T(8,128)(2,1)} %refs_1_.1, s32[]{:T(128)S(6)} %select_n.7), kind=kLoop, calls=%fused_computation.8 | loop fusion | bytes 147460 | tf_op jit(solution)/shard_map/dynamic_slice | solution.py:364
  1.6 4.0 %collective-permute-start.14 = (bf16[288,128]{1,0:T(8,128)(2,1)S(1)}, bf16[288,128]{1,0:T(8,128)(2,1)S(1)}, u32[]{:S(2)}, u32[]{:S(2)}) collective-permute-start(bf16[288,128]{1,0:T(8,128)(2,1)S(1)} %bitcast.40), channel_id=1, source_target_pairs={{0,2},{1,3},{2,0},{3,1},{4,6},{5,7},{6,4},{7,5},{8,10},{9,11},{10,... | collective-permute-start | bytes 221192 | tf_op jit(solution)/shard_map/ppermute | solution.py:11
  5.6 1.5 %copy.6 = bf16[128,4,512]{0,2,1:T(8,128)(2,1)S(1)} copy(bf16[128,4,512]{2,1,0:T(4,128)(2,1)} %param.7) | data formatting | bytes 1048576 | tf_op args[3]
  7.1 0.4 copy.7
  7.5 0.1 pad_add_fusion.refs_0_.place
  7.6 0.7 cut.3
  8.3 1.4 %collective-permute-start = (bf16[1056,128]{1,0:T(8,128)(2,1)S(1)}, bf16[1056,128]{1,0:T(8,128)(2,1)S(1)}, u32[]{:S(2)}, u32[]{:S(2)}) collective-permute-start(bf16[1056,128]{1,0:T(8,128)(2,1)S(1)} %get-tuple-element.35), channel_id=1, source_target_pairs={{0,3},{1,2},{2,1},{3,0},{4,7},{5,6},{6,5},{7,4},{8,11},{9,10},{10,... | collective-permute-start | bytes 811016 | tf_op jit(solution)/shard_map/ppermute | solution.py:11
  9.7 0.0 collective-permute-done.14
  9.7 0.7 collective-permute-start.15
  10.5 1.3 %collective-permute-start.11 = (bf16[576,128]{1,0:T(8,128)(2,1)S(1)}, bf16[576,128]{1,0:T(8,128)(2,1)S(1)}, u32[]{:S(2)}, u32[]{:S(2)}) collective-permute-start(bf16[576,128]{1,0:T(8,128)(2,1)S(1)} %bitcast.39), channel_id=1, source_target_pairs={{0,1},{1,0},{2,3},{3,2},{4,5},{5,4},{6,7},{7,6},{8,9},{9,8},{10,11... | collective-permute-start | bytes 442376 | tf_op jit(solution)/shard_map/ppermute | solution.py:11
  11.8 8.1 %collective-permute-done.15 = bf16[288,128]{1,0:T(8,128)(2,1)S(1)} collective-permute-done((bf16[288,128]{1,0:T(8,128)(2,1)S(1)}, bf16[288,128]{1,0:T(8,128)(2,1)S(1)}, u32[]{:S(2)}, u32[]{:S(2)}) %collective-permute-start.15) | collective-permute-done | bytes 73760 | tf_op jit(solution)/shard_map/ppermute | solution.py:11
  19.9 1.6 %collective-permute-start.16 = (bf16[1,576,128]{2,1,0:T(8,128)(2,1)S(1)}, bf16[1,576,128]{2,1,0:T(8,128)(2,1)S(1)}, u32[]{:S(2)}, u32[]{:S(2)}) collective-permute-start(bf16[1,576,128]{2,1,0:T(8,128)(2,1)S(1)} %maximum_bitcast_fusion), channel_id=1, source_target_pairs={{0,8},{4,12},{8,0},{12,4},{16,24},{20,28},{24,16},{28,20},{1,9},{5... | collective-permute-start | bytes 442376 | tf_op jit(solution)/shard_map/ppermute | solution.py:11
  21.5 0.6 collective-permute-done.11
  22.1 1.5 %collective-permute-start.12 = (bf16[1,576,128]{2,1,0:T(8,128)(2,1)S(1)}, bf16[1,576,128]{2,1,0:T(8,128)(2,1)S(1)}, u32[]{:S(2)}, u32[]{:S(2)}) collective-permute-start(bf16[1,576,128]{2,1,0:T(8,128)(2,1)S(1)} %bitcast.33), channel_id=1, source_target_pairs={{0,16},{4,20},{8,24},{12,28},{16,0},{20,4},{24,8},{28,12},{1,17},{... | collective-permute-start | bytes 442376 | tf_op jit(solution)/shard_map/ppermute | solution.py:11
  23.7 0.4 collective-permute-start.7
  24.0 2.4 %collective-permute-start.8 = (bf16[1056,128]{1,0:T(8,128)(2,1)S(1)}, bf16[1056,128]{1,0:T(8,128)(2,1)S(1)}, u32[]{:S(2)}, u32[]{:S(2)}) collective-permute-start(bf16[1056,128]{1,0:T(8,128)(2,1)S(1)} %get-tuple-element.49.refs_0_), channel_id=1, source_target_pairs={{0,2},{1,3},{2,0},{3,1},{4,6},{5,7},{6,4},{7,5},{8,10},{9,11},{10,... | collective-permute-start | bytes 811016 | tf_op jit(solution)/shard_map/ppermute | solution.py:11
  26.4 0.0 collective-permute-done.refs_3_
  26.4 0.0 collective-permute-done.16
  26.4 0.6 collective-permute-start.17
  27.0 0.3 collective-permute-done.12
  27.3 1.6 %collective-permute-start.13 = (bf16[2,576,128]{2,1,0:T(8,128)(2,1)S(1)}, bf16[2,576,128]{2,1,0:T(8,128)(2,1)S(1)}, u32[]{:S(2)}, u32[]{:S(2)}) collective-permute-start(bf16[2,576,128]{2,1,0:T(8,128)(2,1)S(1)} %pad_maximum_fusion.2), channel_id=1, source_target_pairs={{0,8},{4,12},{8,0},{12,4},{16,24},{20,28},{24,16},{28,20},{1,9},{5... | collective-permute-start | bytes 884744 | tf_op jit(solution)/shard_map/ppermute | solution.py:11
  28.9 0.6 cut.4
  29.5 0.4 collective-permute-start.1
  29.9 8.3 %collective-permute-done.7.refs_1_ = bf16[1056,128]{1,0:T(8,128)(2,1)S(1)} collective-permute-done((bf16[1056,128]{1,0:T(8,128)(2,1)S(1)}, bf16[1056,128]{1,0:T(8,128)(2,1)S(1)}, u32[]{:S(2)}, u32[]{:S(2)}) %collective-permute-start.7) | collective-permute-done | bytes 270368 | tf_op jit(solution)/shard_map/ppermute | solution.py:11
  38.2 0.3 collective-permute-start.2
  38.5 0.0 collective-permute-done.8.refs_2_
  38.5 4.0 %collective-permute-start.3 = (bf16[528,128]{1,0:T(8,128)(2,1)S(1)}, bf16[528,128]{1,0:T(8,128)(2,1)S(1)}, u32[]{:S(2)}, u32[]{:S(2)}) collective-permute-start(bf16[528,128]{1,0:T(8,128)(2,1)S(1)} %get-tuple-element.38), channel_id=1, source_target_pairs={{0,3},{1,2},{2,1},{3,0},{4,7},{5,6},{6,5},{7,4},{8,11},{9,10},{10,... | collective-permute-start | bytes 405512 | tf_op jit(solution)/shard_map/ppermute | solution.py:11
  42.4 0.1 rim.1
  42.5 0.0 collective-permute-done.1.refs_1_
  42.6 1.3 %collective-permute-start.10 = (bf16[2112,128]{1,0:T(8,128)(2,1)S(1)}, bf16[2112,128]{1,0:T(8,128)(2,1)S(1)}, u32[]{:S(2)}, u32[]{:S(2)}) collective-permute-start(bf16[2112,128]{1,0:T(8,128)(2,1)S(1)} %get-tuple-element.54), channel_id=1, source_target_pairs={{4,0},{8,4},{12,8},{16,12},{20,16},{24,20},{28,24},{5,1},{9,5},{13... | collective-permute-start | bytes 1622024 | tf_op jit(solution)/shard_map/ppermute | solution.py:18
  43.9 5.3 %collective-permute-done.2.refs_2_ = bf16[528,128]{1,0:T(8,128)(2,1)S(1)} collective-permute-done((bf16[528,128]{1,0:T(8,128)(2,1)S(1)}, bf16[528,128]{1,0:T(8,128)(2,1)S(1)}, u32[]{:S(2)}, u32[]{:S(2)}) %collective-permute-start.2) | collective-permute-done | bytes 135200 | tf_op jit(solution)/shard_map/ppermute | solution.py:11
  49.2 1.3 %collective-permute-start.9 = (bf16[2112,128]{1,0:T(8,128)(2,1)S(1)}, bf16[2112,128]{1,0:T(8,128)(2,1)S(1)}, u32[]{:S(2)}, u32[]{:S(2)}) collective-permute-start(bf16[2112,128]{1,0:T(8,128)(2,1)S(1)} %get-tuple-element.53), channel_id=1, source_target_pairs={{0,4},{4,8},{8,12},{12,16},{16,20},{20,24},{24,28},{1,5},{5,9},{9,... | collective-permute-start | bytes 1622024 | tf_op jit(solution)/shard_map/ppermute | solution.py:18
  50.5 0.0 collective-permute-done.3.refs_3_
  50.5 0.0 collective-permute-done.17
  50.5 0.0 collective-permute-done.13
  50.5 0.1 maximum_maximum_fusion
  50.6 2.3 %collective-permute-start.18 = (bf16[4,1152,128]{2,1,0:T(8,128)(2,1)S(1)}, bf16[4,1152,128]{2,1,0:T(8,128)(2,1)S(1)}, u32[]{:S(2)}, u32[]{:S(2)}) collective-permute-start(bf16[4,1152,128]{2,1,0:T(8,128)(2,1)S(1)} %maximum_maximum_fusion), channel_id=1, source_target_pairs={{0,4},{4,0},{8,12},{12,8},{16,20},{20,16},{24,28},{28,24},{1,5},{5... | collective-permute-start | bytes 3538952 | tf_op jit(solution)/shard_map/ppermute | solution.py:11
  52.9 0.6 cut.5
  53.5 0.1 collective-permute-start.4
  53.6 1.9 %collective-permute-start.5 = (bf16[528,128]{1,0:T(8,128)(2,1)S(1)}, bf16[528,128]{1,0:T(8,128)(2,1)S(1)}, u32[]{:S(2)}, u32[]{:S(2)}) collective-permute-start(bf16[528,128]{1,0:T(8,128)(2,1)S(1)} %get-tuple-element.59.refs_0_), channel_id=1, source_target_pairs={{0,2},{1,3},{2,0},{3,1},{4,6},{5,7},{6,4},{7,5},{8,10},{9,11},{10,... | collective-permute-start | bytes 405512 | tf_op jit(solution)/shard_map/ppermute | solution.py:11
  55.5 0.1 pad_maximum_fusion.1.refs_4_
  55.5 0.1 pad_maximum_fusion.refs_2_
  55.6 0.0 collective-permute-done.18
  55.6 2.6 %collective-permute-start.6 = (bf16[528,128]{1,0:T(8,128)(2,1)S(1)}, bf16[528,128]{1,0:T(8,128)(2,1)S(1)}, u32[]{:S(2)}, u32[]{:S(2)}) collective-permute-start(bf16[528,128]{1,0:T(8,128)(2,1)S(1)} %get-tuple-element.43), channel_id=1, source_target_pairs={{0,3},{1,2},{2,1},{3,0},{4,7},{5,6},{6,5},{7,4},{8,11},{9,10},{10,... | collective-permute-start | bytes 405512 | tf_op jit(solution)/shard_map/ppermute | solution.py:11
  58.2 0.1 fusion
  58.2 1.3 %assemble.1 = (bf16[4608,256]{1,0:T(8,128)(2,1)S(1)}, bf16[2304,256]{1,0:T(8,128)(2,1)S(1)}) custom-call(s32[2]{0:T(128)S(1)} %pad_add_fusion.refs_0_.place, bf16[9,512,128]{2,1,0:T(8,128)(2,1)S(1)} %copy-done, bf16[4,576,128]{2,1,0:T(8,128)(2,1)S(1)} %pad_maximum_fusion.refs_2_, bf16[4,576,128]{2,1,0:T(8,128)(2,1)S(1)} %get-tuple-element.69.refs_3_, ...), custom_call_target="tpu_custom_call" | custom-call | flops 2001048576 | bytes 1048576 | tf_op jit(solution)/shard_map/assemble/pallas_call | solution.py:276
  59.5 0.0 collective-permute-done.10.refs_5_
  59.6 0.0 collective-permute-done.9.refs_4_
  59.6 3.1 %outer.1 = (f32[1024,256]{1,0:T(8,128)S(1)}, f32[1024,256]{1,0:T(8,128)S(1)}) custom-call(bf16[1056,128]{1,0:T(8,128)(2,1)S(1)} %get-tuple-element.49.refs_0_, bf16[1056,128]{1,0:T(8,128)(2,1)S(1)} %collective-permute-done.7.refs_1_, bf16[1056,128]{1,0:T(8,128)(2,1)S(1)} %collective-permute-done.8.refs_2_, ...), custom_call_target="tpu_custom_call" | custom-call | flops 2001048576 | bytes 1048576 | tf_op jit(solution)/shard_map/outer/pallas_call | solution.py:276
  62.7 1.7 %inner.2 = (bf16[1024,128]{1,0:T(8,128)(2,1)S(1)}, bf16[1024,128]{1,0:T(8,128)(2,1)S(1)}) custom-call(bf16[528,128]{1,0:T(8,128)(2,1)S(1)} %get-tuple-element.44.refs_0_, bf16[528,128]{1,0:T(8,128)(2,1)S(1)} %collective-permute-done.1.refs_1_, bf16[528,128]{1,0:T(8,128)(2,1)S(1)} %collective-permute-done.2.refs_2_, ...), custom_call_target="tpu_custom_call" | custom-call | flops 9001048064 | bytes 1048576 | tf_op jit(solution)/shard_map/inner/pallas_call | solution.py:276
  64.4 0.1 collective-permute-start.19
  64.4 0.0 collective-permute-done.4.refs_1_
  64.5 2.4 %collective-permute-done.5.refs_2_ = bf16[528,128]{1,0:T(8,128)(2,1)S(1)} collective-permute-done((bf16[528,128]{1,0:T(8,128)(2,1)S(1)}, bf16[528,128]{1,0:T(8,128)(2,1)S(1)}, u32[]{:S(2)}, u32[]{:S(2)}) %collective-permute-start.5) | collective-permute-done | bytes 135200 | tf_op jit(solution)/shard_map/ppermute | solution.py:11
  66.8 0.0 collective-permute-done.6.refs_3_
  66.8 1.5 %inner.3 = (bf16[1024,128]{1,0:T(8,128)(2,1)S(1)}, bf16[1024,128]{1,0:T(8,128)(2,1)S(1)}) custom-call(bf16[528,128]{1,0:T(8,128)(2,1)S(1)} %get-tuple-element.59.refs_0_, bf16[528,128]{1,0:T(8,128)(2,1)S(1)} %collective-permute-done.4.refs_1_, bf16[528,128]{1,0:T(8,128)(2,1)S(1)} %collective-permute-done.5.refs_2_, ...), custom_call_target="tpu_custom_call" | custom-call | flops 9001048064 | bytes 1048576 | tf_op jit(solution)/shard_map/inner/pallas_call | solution.py:276
  68.4 2.6 %collective-permute-start.20 = (bf16[1024,128]{1,0:T(8,128)(2,1)S(1)}, bf16[1024,128]{1,0:T(8,128)(2,1)S(1)}, u32[]{:S(2)}, u32[]{:S(2)}) collective-permute-start(bf16[1024,128]{1,0:T(8,128)(2,1)S(1)} %get-tuple-element.67), channel_id=1, source_target_pairs={{0,1},{1,0},{2,3},{3,2},{4,5},{5,4},{6,7},{7,6},{8,9},{9,8},{10,11... | collective-permute-start | bytes 786440 | tf_op jit(solution)/shard_map/ppermute | solution.py:11
  71.0 0.2 copy.12
  71.1 2.3 %collective-permute-done.19 = bf16[1024,128]{1,0:T(8,128)(2,1)S(1)} collective-permute-done((bf16[1024,128]{1,0:T(8,128)(2,1)S(1)}, bf16[1024,128]{1,0:T(8,128)(2,1)S(1)}, u32[]{:S(2)}, u32[]{:S(2)}) %collective-permute-start.19) | collective-permute-done | bytes 262176 | tf_op jit(solution)/shard_map/ppermute | solution.py:11
  73.4 0.2 copy.13
  73.6 1.4 %home.2 = bf16[128,4,512]{2,1,0:T(4,128)(2,1)} custom-call(s32[2]{0:T(128)S(1)} %pad_add_fusion.refs_0_.place, bf16[128,4,256]{2,1,0:T(4,128)(2,1)S(1)} %bitcast.19, bf16[128,4,256]{2,1,0:T(4,128)(2,1)S(1)} %bitcast.21), custom_call_target="tpu_custom_call" | custom-call | flops 1048576 | bytes 1048576 | tf_op jit(solution)/shard_map/home/pallas_call | solution.py:276
  75.1 0.2 copy.14
  75.3 2.6 %collective-permute-done.20 = bf16[1024,128]{1,0:T(8,128)(2,1)S(1)} collective-permute-done((bf16[1024,128]{1,0:T(8,128)(2,1)S(1)}, bf16[1024,128]{1,0:T(8,128)(2,1)S(1)}, u32[]{:S(2)}, u32[]{:S(2)}) %collective-permute-start.20) | collective-permute-done | bytes 262176 | tf_op jit(solution)/shard_map/ppermute | solution.py:11
  77.9 0.2 copy.15
  78.1 1.4 %home.3 = bf16[128,4,512]{2,1,0:T(4,128)(2,1)} custom-call(s32[2]{0:T(128)S(1)} %pad_add_fusion.refs_0_.place, bf16[128,4,256]{2,1,0:T(4,128)(2,1)S(1)} %bitcast.18, bf16[128,4,256]{2,1,0:T(4,128)(2,1)S(1)} %bitcast.20), custom_call_target="tpu_custom_call" | custom-call | flops 1048576 | bytes 1048576 | tf_op jit(solution)/shard_map/home/pallas_call | solution.py:276
  (14 shorter events, 0.1 us)
Async XLA Ops:
  0.6 6.5 %copy-start.2 = (bf16[128,4,512]{2,1,0:T(4,128)(2,1)S(1)}, bf16[128,4,512]{2,1,0:T(4,128)(2,1)}, u32[]{:S(2)}) copy-start(bf16[128,4,512]{2,1,0:T(4,128)(2,1)} %param.4) | copy-start | bytes 1572868
  0.6 7.0 %copy-start.1 = (bf16[128]{0:T(256)(128)(2,1)S(1)}, bf16[128]{0:T(256)(128)(2,1)}, u32[]{:S(2)}) copy-start(bf16[128]{0:T(256)(128)(2,1)} %param.6) | copy-start | bytes 772
  1.6 8.1 %collective-permute-start.14 = (bf16[288,128]{1,0:T(8,128)(2,1)S(1)}, bf16[288,128]{1,0:T(8,128)(2,1)S(1)}, u32[]{:S(2)}, u32[]{:S(2)}) collective-permute-start(bf16[288,128]{1,0:T(8,128)(2,1)S(1)} %bitcast.40), channel_id=1, source_target_pairs={{0,2},{1,3},{2,0},{3,1},{4,6},{5,7},{6,4},{7,5},{8,10},{9,11},{10,... | collective-permute-start | bytes 221192 | tf_op jit(solution)/shard_map/ppermute | solution.py:11
  7.6 2.9 %copy-start = (bf16[9,512,128]{2,1,0:T(8,128)(2,1)S(1)}, bf16[9,512,128]{2,1,0:T(8,128)(2,1)}, u32[]{:S(2)}) copy-start(bf16[9,512,128]{2,1,0:T(8,128)(2,1)} %refs_1_.1) | copy-start | bytes 3538948
  8.3 18.1 %collective-permute-start = (bf16[1056,128]{1,0:T(8,128)(2,1)S(1)}, bf16[1056,128]{1,0:T(8,128)(2,1)S(1)}, u32[]{:S(2)}, u32[]{:S(2)}) collective-permute-start(bf16[1056,128]{1,0:T(8,128)(2,1)S(1)} %get-tuple-element.35), channel_id=1, source_target_pairs={{0,3},{1,2},{2,1},{3,0},{4,7},{5,6},{6,5},{7,4},{8,11},{9,10},{10,... | collective-permute-start | bytes 811016 | tf_op jit(solution)/shard_map/ppermute | solution.py:11
  9.7 10.2 %collective-permute-start.15 = (bf16[288,128]{1,0:T(8,128)(2,1)S(1)}, bf16[288,128]{1,0:T(8,128)(2,1)S(1)}, u32[]{:S(2)}, u32[]{:S(2)}) collective-permute-start(bf16[288,128]{1,0:T(8,128)(2,1)S(1)} %collective-permute-done.14), channel_id=1, source_target_pairs={{0,1},{1,0},{2,3},{3,2},{4,5},{5,4},{6,7},{7,6},{8,9},{9,8},{10,11... | collective-permute-start | bytes 221192 | tf_op jit(solution)/shard_map/ppermute | solution.py:11
  10.5 11.6 %collective-permute-start.11 = (bf16[576,128]{1,0:T(8,128)(2,1)S(1)}, bf16[576,128]{1,0:T(8,128)(2,1)S(1)}, u32[]{:S(2)}, u32[]{:S(2)}) collective-permute-start(bf16[576,128]{1,0:T(8,128)(2,1)S(1)} %bitcast.39), channel_id=1, source_target_pairs={{0,1},{1,0},{2,3},{3,2},{4,5},{5,4},{6,7},{7,6},{8,9},{9,8},{10,11... | collective-permute-start | bytes 442376 | tf_op jit(solution)/shard_map/ppermute | solution.py:11
  19.9 6.5 %collective-permute-start.16 = (bf16[1,576,128]{2,1,0:T(8,128)(2,1)S(1)}, bf16[1,576,128]{2,1,0:T(8,128)(2,1)S(1)}, u32[]{:S(2)}, u32[]{:S(2)}) collective-permute-start(bf16[1,576,128]{2,1,0:T(8,128)(2,1)S(1)} %maximum_bitcast_fusion), channel_id=1, source_target_pairs={{0,8},{4,12},{8,0},{12,4},{16,24},{20,28},{24,16},{28,20},{1,9},{5... | collective-permute-start | bytes 442376 | tf_op jit(solution)/shard_map/ppermute | solution.py:11
  22.1 5.1 %collective-permute-start.12 = (bf16[1,576,128]{2,1,0:T(8,128)(2,1)S(1)}, bf16[1,576,128]{2,1,0:T(8,128)(2,1)S(1)}, u32[]{:S(2)}, u32[]{:S(2)}) collective-permute-start(bf16[1,576,128]{2,1,0:T(8,128)(2,1)S(1)} %bitcast.33), channel_id=1, source_target_pairs={{0,16},{4,20},{8,24},{12,28},{16,0},{20,4},{24,8},{28,12},{1,17},{... | collective-permute-start | bytes 442376 | tf_op jit(solution)/shard_map/ppermute | solution.py:11
  23.7 14.5 %collective-permute-start.7 = (bf16[1056,128]{1,0:T(8,128)(2,1)S(1)}, bf16[1056,128]{1,0:T(8,128)(2,1)S(1)}, u32[]{:S(2)}, u32[]{:S(2)}) collective-permute-start(bf16[1056,128]{1,0:T(8,128)(2,1)S(1)} %get-tuple-element.35), channel_id=1, source_target_pairs={{0,1},{1,0},{2,3},{3,2},{4,5},{5,4},{6,7},{7,6},{8,9},{9,8},{10,11... | collective-permute-start | bytes 811016 | tf_op jit(solution)/shard_map/ppermute | solution.py:11
  24.0 14.5 %collective-permute-start.8 = (bf16[1056,128]{1,0:T(8,128)(2,1)S(1)}, bf16[1056,128]{1,0:T(8,128)(2,1)S(1)}, u32[]{:S(2)}, u32[]{:S(2)}) collective-permute-start(bf16[1056,128]{1,0:T(8,128)(2,1)S(1)} %get-tuple-element.49.refs_0_), channel_id=1, source_target_pairs={{0,2},{1,3},{2,0},{3,1},{4,6},{5,7},{6,4},{7,5},{8,10},{9,11},{10,... | collective-permute-start | bytes 811016 | tf_op jit(solution)/shard_map/ppermute | solution.py:11
  26.4 24.1 %collective-permute-start.17 = (bf16[2,576,128]{2,1,0:T(8,128)(2,1)S(1)}, bf16[2,576,128]{2,1,0:T(8,128)(2,1)S(1)}, u32[]{:S(2)}, u32[]{:S(2)}) collective-permute-start(bf16[2,576,128]{2,1,0:T(8,128)(2,1)S(1)} %pad_maximum_fusion.3), channel_id=1, source_target_pairs={{0,16},{4,20},{8,24},{12,28},{16,0},{20,4},{24,8},{28,12},{1,17},{... | collective-permute-start | bytes 884744 | tf_op jit(solution)/shard_map/ppermute | solution.py:11
  27.3 23.2 %collective-permute-start.13 = (bf16[2,576,128]{2,1,0:T(8,128)(2,1)S(1)}, bf16[2,576,128]{2,1,0:T(8,128)(2,1)S(1)}, u32[]{:S(2)}, u32[]{:S(2)}) collective-permute-start(bf16[2,576,128]{2,1,0:T(8,128)(2,1)S(1)} %pad_maximum_fusion.2), channel_id=1, source_target_pairs={{0,8},{4,12},{8,0},{12,4},{16,24},{20,28},{24,16},{28,20},{1,9},{5... | collective-permute-start | bytes 884744 | tf_op jit(solution)/shard_map/ppermute | solution.py:11
  29.5 13.0 %collective-permute-start.1 = (bf16[528,128]{1,0:T(8,128)(2,1)S(1)}, bf16[528,128]{1,0:T(8,128)(2,1)S(1)}, u32[]{:S(2)}, u32[]{:S(2)}) collective-permute-start(bf16[528,128]{1,0:T(8,128)(2,1)S(1)} %get-tuple-element.38), channel_id=1, source_target_pairs={{0,1},{1,0},{2,3},{3,2},{4,5},{5,4},{6,7},{7,6},{8,9},{9,8},{10,11... | collective-permute-start | bytes 405512 | tf_op jit(solution)/shard_map/ppermute | solution.py:11
  38.2 11.0 %collective-permute-start.2 = (bf16[528,128]{1,0:T(8,128)(2,1)S(1)}, bf16[528,128]{1,0:T(8,128)(2,1)S(1)}, u32[]{:S(2)}, u32[]{:S(2)}) collective-permute-start(bf16[528,128]{1,0:T(8,128)(2,1)S(1)} %get-tuple-element.44.refs_0_), channel_id=1, source_target_pairs={{0,2},{1,3},{2,0},{3,1},{4,6},{5,7},{6,4},{7,5},{8,10},{9,11},{10,... | collective-permute-start | bytes 405512 | tf_op jit(solution)/shard_map/ppermute | solution.py:11
  38.5 12.0 %collective-permute-start.3 = (bf16[528,128]{1,0:T(8,128)(2,1)S(1)}, bf16[528,128]{1,0:T(8,128)(2,1)S(1)}, u32[]{:S(2)}, u32[]{:S(2)}) collective-permute-start(bf16[528,128]{1,0:T(8,128)(2,1)S(1)} %get-tuple-element.38), channel_id=1, source_target_pairs={{0,3},{1,2},{2,1},{3,0},{4,7},{5,6},{6,5},{7,4},{8,11},{9,10},{10,... | collective-permute-start | bytes 405512 | tf_op jit(solution)/shard_map/ppermute | solution.py:11
  42.6 17.0 %collective-permute-start.10 = (bf16[2112,128]{1,0:T(8,128)(2,1)S(1)}, bf16[2112,128]{1,0:T(8,128)(2,1)S(1)}, u32[]{:S(2)}, u32[]{:S(2)}) collective-permute-start(bf16[2112,128]{1,0:T(8,128)(2,1)S(1)} %get-tuple-element.54), channel_id=1, source_target_pairs={{4,0},{8,4},{12,8},{16,12},{20,16},{24,20},{28,24},{5,1},{9,5},{13... | collective-permute-start | bytes 1622024 | tf_op jit(solution)/shard_map/ppermute | solution.py:18
  49.2 10.4 %collective-permute-start.9 = (bf16[2112,128]{1,0:T(8,128)(2,1)S(1)}, bf16[2112,128]{1,0:T(8,128)(2,1)S(1)}, u32[]{:S(2)}, u32[]{:S(2)}) collective-permute-start(bf16[2112,128]{1,0:T(8,128)(2,1)S(1)} %get-tuple-element.53), channel_id=1, source_target_pairs={{0,4},{4,8},{8,12},{12,16},{16,20},{20,24},{24,28},{1,5},{5,9},{9,... | collective-permute-start | bytes 1622024 | tf_op jit(solution)/shard_map/ppermute | solution.py:18
  50.6 5.0 %collective-permute-start.18 = (bf16[4,1152,128]{2,1,0:T(8,128)(2,1)S(1)}, bf16[4,1152,128]{2,1,0:T(8,128)(2,1)S(1)}, u32[]{:S(2)}, u32[]{:S(2)}) collective-permute-start(bf16[4,1152,128]{2,1,0:T(8,128)(2,1)S(1)} %maximum_maximum_fusion), channel_id=1, source_target_pairs={{0,4},{4,0},{8,12},{12,8},{16,20},{20,16},{24,28},{28,24},{1,5},{5... | collective-permute-start | bytes 3538952 | tf_op jit(solution)/shard_map/ppermute | solution.py:11
  53.5 10.9 %collective-permute-start.4 = (bf16[528,128]{1,0:T(8,128)(2,1)S(1)}, bf16[528,128]{1,0:T(8,128)(2,1)S(1)}, u32[]{:S(2)}, u32[]{:S(2)}) collective-permute-start(bf16[528,128]{1,0:T(8,128)(2,1)S(1)} %get-tuple-element.43), channel_id=1, source_target_pairs={{0,1},{1,0},{2,3},{3,2},{4,5},{5,4},{6,7},{7,6},{8,9},{9,8},{10,11... | collective-permute-start | bytes 405512 | tf_op jit(solution)/shard_map/ppermute | solution.py:11
  53.6 13.2 %collective-permute-start.5 = (bf16[528,128]{1,0:T(8,128)(2,1)S(1)}, bf16[528,128]{1,0:T(8,128)(2,1)S(1)}, u32[]{:S(2)}, u32[]{:S(2)}) collective-permute-start(bf16[528,128]{1,0:T(8,128)(2,1)S(1)} %get-tuple-element.59.refs_0_), channel_id=1, source_target_pairs={{0,2},{1,3},{2,0},{3,1},{4,6},{5,7},{6,4},{7,5},{8,10},{9,11},{10,... | collective-permute-start | bytes 405512 | tf_op jit(solution)/shard_map/ppermute | solution.py:11
  55.6 11.2 %collective-permute-start.6 = (bf16[528,128]{1,0:T(8,128)(2,1)S(1)}, bf16[528,128]{1,0:T(8,128)(2,1)S(1)}, u32[]{:S(2)}, u32[]{:S(2)}) collective-permute-start(bf16[528,128]{1,0:T(8,128)(2,1)S(1)} %get-tuple-element.43), channel_id=1, source_target_pairs={{0,3},{1,2},{2,1},{3,0},{4,7},{5,6},{6,5},{7,4},{8,11},{9,10},{10,... | collective-permute-start | bytes 405512 | tf_op jit(solution)/shard_map/ppermute | solution.py:11
  64.4 9.1 %collective-permute-start.19 = (bf16[1024,128]{1,0:T(8,128)(2,1)S(1)}, bf16[1024,128]{1,0:T(8,128)(2,1)S(1)}, u32[]{:S(2)}, u32[]{:S(2)}) collective-permute-start(bf16[1024,128]{1,0:T(8,128)(2,1)S(1)} %get-tuple-element.65), channel_id=1, source_target_pairs={{0,1},{1,0},{2,3},{3,2},{4,5},{5,4},{6,7},{7,6},{8,9},{9,8},{10,11... | collective-permute-start | bytes 786440 | tf_op jit(solution)/shard_map/ppermute | solution.py:11
  68.4 9.5 %collective-permute-start.20 = (bf16[1024,128]{1,0:T(8,128)(2,1)S(1)}, bf16[1024,128]{1,0:T(8,128)(2,1)S(1)}, u32[]{:S(2)}, u32[]{:S(2)}) collective-permute-start(bf16[1024,128]{1,0:T(8,128)(2,1)S(1)} %get-tuple-element.67), channel_id=1, source_target_pairs={{0,1},{1,0},{2,3},{3,2},{4,5},{5,4},{6,7},{7,6},{8,9},{9,8},{10,11... | collective-permute-start | bytes 786440 | tf_op jit(solution)/shard_map/ppermute | solution.py:11
